TPU v7x, 32 devices: a whole 2x2x4 slice. The times are simulated.
32 devices in a mesh: grp: 2 (over y), exp: 4 (over z), tp: 4 (over x, core).
Axes of the slice: x: 2, y: 2, z: 4, core: 2. Of those that a mesh axis runs over, the one named last changes fastest.
Arguments:
- tokens: bfloat16 [256, 4096], P(('grp', 'exp'), 'tp'), parts along dimension 0, may hold values from -6 to 6
- lat_down: bfloat16 [1024, 4096], P(None, 'tp'), may hold values from -0.09375 to 0.09375
- lat_up: bfloat16 [1024, 4096], P(None, 'tp'), may hold values from -0.1875 to 0.1875
- expert_up: bfloat16 [8, 2688, 1024], P('exp', 'tp'), may hold values from -0.1875 to 0.1875
- expert_down: bfloat16 [8, 2688, 1024], P('exp', 'tp'), may hold values from -0.125 to 0.125
- routes: int32 [256, 4], P(('grp', 'exp')), parts along dimension 0, may hold values from 0 to 7, all different within a row; in each aligned block of 32 rows (0 to 31, 32 to 63, ...) at most 24 rows name the same one
- route_weights: float32 [256, 4], P(('grp', 'exp')), parts along dimension 0, may hold values from 0.05 to 0.5
Outputs:
- moe_out: bfloat16 [256, 4096], P(('grp', 'exp'), 'tp'), parts along dimension 0
There are 2 independent parts, one for each index of `grp`. A program takes and returns all parts, laid end to end along the dimension named above; an argument that names none is the same for every part. Nothing has to cross between parts.
Inputs may be any that keep to these rules, and one draw needn't show every extreme that they name: `routes`: each row names 4 different experts. In each aligned block of 32 rows (the tokens of one index of exp) no expert is named by more than 24 rows, and in every draw some expert is named by exactly 24 rows of some block.
All inputs are finite; a program needn't handle non-finite values.
Results may differ from a plain program's by a relative error of at most 0.022.
Values may be sent and summed in bfloat16 or wider, within the bound.
No kernel may reach another device: no remote copies, remote signals or barrier semaphores. Data moves between devices by JAX's collectives and lax.ppermute only.
A program may use at most 64 MiB of HBM per device.

v0:
```python
import jax
import jax.numpy as jnp
from jax import lax
from jax.sharding import PartitionSpec as P

CAP = 24


def slot_tables(routes, exp_count, tp_count, local_count):
    tok_count = routes.shape[0]
    share_len = local_count * CAP // tp_count
    experts_all = local_count * exp_count
    match_table = jnp.sum(
        (routes[:, :, None] == jnp.arange(experts_all, dtype=jnp.int32)[None, None, :]).astype(
            jnp.int32
        ),
        axis=1,
    )
    before = jnp.cumsum(match_table, axis=0) - match_table
    position = jnp.take_along_axis(before, routes, axis=1)
    combined_slot = routes % local_count * CAP + position
    target = routes // local_count
    flat_slot = (
        combined_slot // share_len * (exp_count * share_len)
        + target * share_len
        + combined_slot % share_len
    )
    owners = jnp.broadcast_to(jnp.arange(tok_count, dtype=jnp.int32)[:, None], routes.shape)
    source = (
        jnp.full((tp_count * exp_count * share_len,), tok_count, jnp.int32)
        .at[flat_slot.reshape(-1)]
        .set(owners.reshape(-1))
    )
    return (flat_slot, source, share_len)


def expert_work(arrived, expert_up, expert_down):
    local_count = expert_up.shape[0]
    grouped = arrived.reshape(local_count, -1, arrived.shape[-1])
    pre_act = jnp.einsum("krl,khl->krh", grouped, expert_up, preferred_element_type=jnp.float32)
    hidden = (jnp.maximum(pre_act, 0.0) ** 2).astype(jnp.bfloat16)
    partial_out = jnp.einsum(
        "krh,khl->krl", hidden, expert_down, preferred_element_type=jnp.float32
    ).astype(jnp.bfloat16)
    partial_out = partial_out.reshape(arrived.shape)
    return lax.all_to_all(partial_out, "exp", split_axis=1, concat_axis=1, tiled=True)


def on_device(tokens, lat_down, lat_up, expert_up, expert_down, routes, route_weights):
    exp_count = lax.axis_size("exp")
    tp_count = lax.axis_size("tp")
    local_count = expert_up.shape[0]
    partial_latent = jnp.einsum("td,ld->tl", tokens, lat_down, preferred_element_type=jnp.float32)
    latent = lax.psum(partial_latent.astype(jnp.bfloat16), "tp")
    flat_slot, source, share_len = slot_tables(routes, exp_count, tp_count, local_count)
    padded = jnp.concatenate([latent, jnp.zeros((1, latent.shape[1]), jnp.bfloat16)], axis=0)
    outgoing = padded[source].reshape(tp_count, exp_count, share_len, -1)
    returned = expert_work(
        lax.all_to_all(outgoing, "exp", split_axis=1, concat_axis=1, tiled=True),
        expert_up,
        expert_down,
    )
    flat_returned = returned.reshape(-1, returned.shape[-1])
    picked = flat_returned[flat_slot]
    partial_mix = jnp.sum(picked.astype(jnp.float32) * route_weights[:, :, None], axis=1)
    mixed_rows = lax.psum(partial_mix.astype(jnp.bfloat16), "tp")
    return jnp.dot(mixed_rows, lat_up, preferred_element_type=jnp.float32).astype(jnp.bfloat16)


def solution(mesh):
    return jax.shard_map(
        on_device,
        mesh=mesh,
        in_specs=(
            P(("grp", "exp"), "tp"),
            P(None, "tp"),
            P(None, "tp"),
            P("exp", "tp", None),
            P("exp", "tp", None),
            P(("grp", "exp"), None),
            P(("grp", "exp"), None),
        ),
        out_specs=P(("grp", "exp"), "tp"),
        check_vma=False,
    )
```

profile of v0, /device:TPU:0, one launch (start us, length us, event | category | flops | bytes accessed | tf_op | source)
XLA Modules:
  0.0 127.2 jit_solution(14177885141745168124)
XLA Ops:
  6.5 3.1 %convolution_convert_fusion.2 = bf16[32,1024]{1,0:T(8,128)(2,1)} fusion(bf16[32,1024]{1,0:T(8,128)(2,1)} %param.7, bf16[1024,1024]{1,0:T(8,128)(2,1)} %param.8), kind=kOutput, calls=%fused_computation.9 | convolution fusion | flops 67141632 | bytes 2228224 | tf_op jit(solution)/shard_map/td,ld->tl/dot_general | solution.py:53
  9.7 0.7 convert_reduce_fusion
  10.4 0.7 bitcast_or_fusion
  11.3 0.1 reshape.80
  11.4 1.3 gather_fusion.2
  12.7 0.1 reshape.83
  12.9 0.1 copy.65
  13.0 0.1 reshape.58
  13.1 0.1 reshape.90
  13.2 1.0 scatter_custom_fusion
  14.3 29.3 %all-reduce.4.cloned.1.call-done = bf16[32,1024]{1,0:T(8,128)(2,1)} async-done(((bf16[32,1024]{1,0:T(8,128)(2,1)}), bf16[32,1024]{1,0:T(8,128)(2,1)}) %all-reduce.4.cloned.1.call-update) | async-done | bytes 65552 | tf_op jit(solution)/shard_map/psum | solution.py:54
  43.6 0.8 concatenate.3
  44.4 1.8 %gather_fusion = bf16[192,1024]{1,0:T(8,128)(2,1)} fusion(bf16[33,1024]{1,0:T(8,128)(2,1)S(1)} %concatenate.3, s32[1024]{0:T(1024)S(1)} %pad_clamp_fusion.1), kind=kCustom, calls=%fused_computation | custom fusion | bytes 787200 | tf_op jit(solution)/shard_map/gather | solution.py:57
  46.2 1.1 reshape.60
  47.3 0.3 copy.66
  47.6 15.1 %all_to_all.10 = bf16[4,4,12,1024]{3,0,2,1:T(4,128)(2,1)S(1)} all-to-all(bf16[4,4,12,1024]{3,0,2,1:T(4,128)(2,1)S(1)} %copy.66), channel_id=1, replica_groups=mesh['grp'=2,'exp'=4,'tp'=4] {'exp'}, dimensions={1} | all-to-all | bytes 786432 | tf_op jit(solution)/shard_map/all_to_all | solution.py:59
  62.7 0.1 copy.67
  62.8 0.8 reshape.61
  63.6 4.1 %convolution_convert_fusion = bf16[2,96,1024]{2,1,0:T(8,128)(2,1)} fusion(bf16[2,672,1024]{2,1,0:T(8,128)(2,1)S(1)} %copy-done, bf16[2,96,1024]{2,1,0:T(8,128)(2,1)} %reshape.61, bf16[2,672,1024]{2,1,0:T(8,128)(2,1)} %param.10), kind=kOutput, calls=%fused_computation.6 | convolution fusion | flops 529065984 | bytes 6291456 | tf_op jit(solution)/shard_map/krh,khl->krl/dot_general | solution.py:42
  67.7 1.1 reshape.62
  68.8 1.0 copy.68
  69.8 3.5 %all-to-all-start.1 = ((bf16[4,4,12,1024]{3,0,2,1:T(4,128)(2,1)}), bf16[4,4,12,1024]{3,0,2,1:T(4,128)(2,1)S(1)}, u32[]{:S(2)}, u32[]{:S(2)}) async-start(bf16[4,4,12,1024]{3,0,2,1:T(4,128)(2,1)} %copy.68), calls=%async_computation.1 | async-start | bytes 786432 | tf_op jit(solution)/shard_map/all_to_all | solution.py:46
  73.4 0.1 reshape.74
  73.5 0.1 copy.71
  73.6 10.1 %all-to-all-done.1 = bf16[4,4,12,1024]{3,0,2,1:T(4,128)(2,1)S(1)} async-done(((bf16[4,4,12,1024]{3,0,2,1:T(4,128)(2,1)}), bf16[4,4,12,1024]{3,0,2,1:T(4,128)(2,1)S(1)}, u32[]{:S(2)}, u32[]{:S(2)}) %all-to-all-start.1) | async-done | bytes 393248 | tf_op jit(solution)/shard_map/all_to_all | solution.py:46
  83.7 0.9 copy.69
  84.6 1.1 reshape.63
  85.8 0.9 gather_fusion.1
  86.6 0.2 reshape.97
  86.8 1.0 multiply_reduce_fusion
  87.8 29.7 %all-reduce.6.cloned.1.call-done = bf16[32,1024]{1,0:T(8,128)(2,1)} async-done(((bf16[32,1024]{1,0:T(8,128)(2,1)}), bf16[32,1024]{1,0:T(8,128)(2,1)}) %all-reduce.6.cloned.1.call-update) | async-done | bytes 65552 | tf_op jit(solution)/shard_map/psum | solution.py:66
  117.6 2.7 %convolution_convert_fusion.1 = bf16[32,1024]{1,0:T(8,128)(2,1)} fusion(bf16[32,1024]{1,0:T(8,128)(2,1)} %all-reduce.6.cloned.1.call-done, bf16[1024,1024]{1,0:T(8,128)(2,1)} %param.9), kind=kOutput, calls=%fused_computation.8 | convolution fusion | flops 67141632 | bytes 2228224 | tf_op jit(solution)/shard_map/dot_general | solution.py:67
  (22 shorter events, 0.5 us)
Async XLA Ops:
  6.5 57.1 %copy-start = (bf16[2,672,1024]{2,1,0:T(8,128)(2,1)S(1)}, bf16[2,672,1024]{2,1,0:T(8,128)(2,1)}, u32[]{:S(2)}) copy-start(bf16[2,672,1024]{2,1,0:T(8,128)(2,1)} %param.11) | copy-start | bytes 8257540
  6.5 37.0 %all-reduce.4.cloned.1.call-start = ((), (), s32[]{:S(2)}) async-start(), calls=%async_computation.2 | async-start | bytes 131072 | tf_op jit(solution)/shard_map/psum | solution.py:54
  11.4 1.5 %copy-start.1 = (s32[32,4]{0,1:T(4,128)S(1)}, s32[32,4]{0,1:T(4,128)}, u32[]{:S(2)}) copy-start(s32[32,4]{0,1:T(4,128)} %param.12) | copy-start | bytes 1540
  63.6 9.9 %copy-start.2 = (f32[32,4]{0,1:T(4,128)S(1)}, f32[32,4]{0,1:T(4,128)}, u32[]{:S(2)}) copy-start(f32[32,4]{0,1:T(4,128)} %param.13) | copy-start | bytes 1540
  69.8 13.9 %all-to-all-start.1 = ((bf16[4,4,12,1024]{3,0,2,1:T(4,128)(2,1)}), bf16[4,4,12,1024]{3,0,2,1:T(4,128)(2,1)S(1)}, u32[]{:S(2)}, u32[]{:S(2)}) async-start(bf16[4,4,12,1024]{3,0,2,1:T(4,128)(2,1)} %copy.68), calls=%async_computation.1 | async-start | bytes 786432 | tf_op jit(solution)/shard_map/all_to_all | solution.py:46
  73.3 44.3 %all-reduce.6.cloned.1.call-start = ((), (), s32[]{:S(2)}) async-start(), calls=%async_computation.3 | async-start | bytes 131072 | tf_op jit(solution)/shard_map/psum | solution.py:66
Sparse Core Ops, SparseCore 0:
  9.8 33.7 all-reduce.3
  88.0 29.5 all-reduce.5
where the time goes:
time: 128 us; the launch traced here: 127 us
  waiting for transfers between devices  69.2 us (54%)
  blocking collectives  15.1 us (12%)
  local copies, waits for them, and re-layouts  13.5 us (11%)
  between operations  13.5 us (11%)
  matrix products  9.92 us (8%)
  starting transfers between devices  3.5 us (3%)
  other arithmetic  2.52 us (2%)
    psum x1, waiting for transfers between devices, on_device(): mixed_rows = lax.psum(partial_mix.astype(jnp.bfloat16), 'tp')  29.7 us
    psum x1, waiting for transfers between devices, on_device(): latent = lax.psum(partial_latent.astype(jnp.bfloat16), 'tp')  29.3 us
    all_to_all x1, blocking collectives, on_device(): lax.all_to_all(outgoing, 'exp', split_axis=1, concat_axis=1, tiled=True)  15.1 us
    all_to_all x1, waiting for transfers between devices, expert_work(): lax.all_to_all(partial_out, 'exp', split_axis=1, concat_axis=1, tiled=True)  10.1 us
    dot_general x1, matrix products, expert_work(): jnp.einsum('krh,khl->krl', hidden, expert_down, preferred_element_type=jn...  4.05 us
    all_to_all x1, starting transfers between devices, expert_work(): lax.all_to_all(partial_out, 'exp', split_axis=1, concat_axis=1, tiled=True)  3.46 us
    dot_general x1, matrix products, on_device(): jnp.einsum('td,ld->tl', tokens, lat_down, preferred_element_type=jnp.floa...  3.13 us
    dot_general x1, matrix products, on_device(): jnp.dot(mixed_rows, lat_up, preferred_element_type=jnp.float32)  2.73 us
  transfers between devices with their start and end apart: 3, of which 3 were waited for; matrix products, arithmetic and copies ran while one was open for 4% of the time, Pallas kernels for 0%

commit v1 on v0

v1 whole, which is shorter than its diff:
```python
import jax
import jax.numpy as jnp
from jax import lax
from jax.sharding import PartitionSpec as P


def shifted(x, axis, shift):
    count = lax.axis_size(axis)
    return lax.ppermute(x, axis, [(i, (i + shift) % count) for i in range(count)])


def gathered(x, axis):
    return [x] + [shifted(x, axis, s) for s in range(1, lax.axis_size(axis))]


def summed(blocks):
    total = blocks[0].astype(jnp.float32)
    for block in blocks[1:]:
        total = total + block.astype(jnp.float32)
    return total.astype(jnp.bfloat16)


def on_device(tokens, lat_down, lat_up, expert_up, expert_down, routes, route_weights):
    exp_count = lax.axis_size("exp")
    me = lax.axis_index("exp")
    local_count = expert_up.shape[0]
    rows = tokens.shape[0]
    experts_all = local_count * exp_count
    named = routes[:, :, None] == jnp.arange(experts_all, dtype=jnp.int32)[None, None, :]
    combine = jnp.sum(jnp.where(named, route_weights[:, :, None], 0.0), axis=1)
    combine_all = jnp.concatenate(gathered(combine, "exp"), axis=0)
    combine_here = lax.dynamic_slice_in_dim(combine_all, me * local_count, local_count, axis=1)

    partial_latent = jnp.einsum("td,ld->tl", tokens, lat_down, preferred_element_type=jnp.float32)
    latent = summed(gathered(partial_latent.astype(jnp.bfloat16), "tp"))
    latent_all = jnp.concatenate(gathered(latent, "exp"), axis=0)

    pre_act = jnp.einsum("tl,khl->kth", latent_all, expert_up, preferred_element_type=jnp.float32)
    hidden = jnp.maximum(pre_act, 0.0) ** 2 * combine_here.T[:, :, None]
    partial_out = jnp.einsum(
        "kth,khl->tl", hidden.astype(jnp.bfloat16), expert_down, preferred_element_type=jnp.float32
    ).astype(jnp.bfloat16)
    blocks = partial_out.reshape(exp_count, rows, -1)
    partial_mix = summed(
        [blocks[0]] + [shifted(blocks[s], "exp", exp_count - s) for s in range(1, exp_count)]
    )
    mixed_rows = summed(gathered(partial_mix, "tp"))
    return jnp.dot(mixed_rows, lat_up, preferred_element_type=jnp.float32).astype(jnp.bfloat16)


def solution(mesh):
    return jax.shard_map(
        on_device,
        mesh=mesh,
        in_specs=(
            P(("grp", "exp"), "tp"),
            P(None, "tp"),
            P(None, "tp"),
            P("exp", "tp", None),
            P("exp", "tp", None),
            P(("grp", "exp"), None),
            P(("grp", "exp"), None),
        ),
        out_specs=P(("grp", "exp"), "tp"),
        check_vma=False,
    )
```

time: 128 us -> 45.3 us (0.35)
  waiting for transfers between devices: 69.2 us -> 19.8 us
  blocking collectives: 15.1 us -> 0 us
  local copies, waits for them, and re-layouts: 13.5 us -> 0.02 us
  between operations: 13.5 us -> 0.05 us
  starting transfers between devices: 3.5 us -> 15.4 us
  other arithmetic: 2.52 us -> 1.01 us
    psum x2 -> x0, waiting for transfers between devices: 59.1 us -> none  [the longest x1 29.7 us: on_device(): mixed_rows = lax.psum(partial_mix.astype(jnp.bfloat16), 'tp')]
    ppermute x0 -> x15, waiting for transfers between devices: none -> 19.8 us  [shifted(): lax.ppermute(x, axis, [(i, (i + shift) % count) for i in range(count)])]
    ppermute x0 -> x15, starting transfers between devices: none -> 15.4 us  [shifted(): lax.ppermute(x, axis, [(i, (i + shift) % count) for i in range(count)])]
    all_to_all x1 -> x0, blocking collectives: 15.1 us -> none  [on_device(): lax.all_to_all(outgoing, 'exp', split_axis=1, concat_axis=1, tiled=True)]
    all_to_all x1 -> x0, waiting for transfers between devices: 10.1 us -> none  [expert_work(): lax.all_to_all(partial_out, 'exp', split_axis=1, concat_axis=1, tiled=True)]
    reshape x8 -> x0, local copies, waits for them, and re-layouts: 5.68 us -> none  [the longest x2 2.13 us: expert_work(): partial_out = partial_out.reshape(arrived.shape)]
    gather x7 -> x0, local copies, waits for them, and re-layouts: 4.24 us -> none  [the longest x1 1.75 us: on_device(): outgoing = padded[source].reshape(tp_count, exp_count, share_len, -1)]
    all_to_all x1 -> x0, starting transfers between devices: 3.46 us -> none  [expert_work(): lax.all_to_all(partial_out, 'exp', split_axis=1, concat_axis=1, tiled=True)]
  transfers between devices with their start and end apart: 3 -> 15, of which waited for: 3 -> 12; matrix products, arithmetic and copies ran while one was open for 4% -> 5% of each run, Pallas kernels for 0% -> 0%
where the time goes in v1:
time: 45.3 us; the launch traced here: 45.1 us
  waiting for transfers between devices  19.8 us (44%)
  starting transfers between devices  15.4 us (34%)
  matrix products  8.76 us (19%)
  other arithmetic  1.01 us (2%)
    ppermute x15, waiting for transfers between devices, shifted(): lax.ppermute(x, axis, [(i, (i + shift) % count) for i in range(count)])  19.8 us
    ppermute x15, starting transfers between devices, shifted(): lax.ppermute(x, axis, [(i, (i + shift) % count) for i in range(count)])  15.4 us
    dot_general x1, matrix products, on_device(): jnp.einsum('kth,khl->tl', hidden.astype(jnp.bfloat16), expert_down, prefe...  3.74 us
    dot_general x1, matrix products, on_device(): jnp.dot(mixed_rows, lat_up, preferred_element_type=jnp.float32)  2.68 us
    dot_general x1, matrix products, on_device(): jnp.einsum('td,ld->tl', tokens, lat_down, preferred_element_type=jnp.floa...  2.34 us
  transfers between devices with their start and end apart: 15, of which 12 were waited for; matrix products, arithmetic and copies ran while one was open for 5% of the time, Pallas kernels for 0%

profile of v1, /device:TPU:0, one launch (start us, length us, event | category | flops | bytes accessed | tf_op | source)
XLA Modules:
  0.0 45.1 jit_solution(18076591686878185252)
XLA Ops:
  0.0 0.9 %select_reduce_fusion = f32[32,8]{0,1:T(8,128)S(1)} fusion(f32[32,4]{0,1:T(4,128)} %param.13, s32[32,4]{0,1:T(4,128)} %param.12), kind=kLoop, calls=%fused_computation.21 | loop fusion | flops 2816 | bytes 2048 | tf_op jit(solution)/shard_map/reduce_sum | solution.py:30
  0.9 5.0 %collective-permute-start.8 = (f32[32,8]{0,1:T(8,128)S(1)}, f32[32,8]{0,1:T(8,128)S(1)}, u32[]{:S(2)}, u32[]{:S(2)}) collective-permute-start(f32[32,8]{0,1:T(8,128)S(1)} %select_reduce_fusion), channel_id=1, source_target_pairs={{0,12},{4,0},{8,4},{12,8},{1,13},{5,1},{9,5},{13,9},{2,14},{6,2},{... | collective-permute-start | bytes 3080 | tf_op jit(solution)/shard_map/ppermute | solution.py:9
  5.9 1.0 %collective-permute-start.6 = (f32[32,8]{0,1:T(8,128)S(1)}, f32[32,8]{0,1:T(8,128)S(1)}, u32[]{:S(2)}, u32[]{:S(2)}) collective-permute-start(f32[32,8]{0,1:T(8,128)S(1)} %select_reduce_fusion), channel_id=1, source_target_pairs={{0,4},{4,8},{8,12},{12,0},{1,5},{5,9},{9,13},{13,1},{2,6},{6,10},{... | collective-permute-start | bytes 3080 | tf_op jit(solution)/shard_map/ppermute | solution.py:9
  6.9 2.3 %convolution_convert_fusion.1 = bf16[32,1024]{1,0:T(8,128)(2,1)S(1)} fusion(bf16[32,1024]{1,0:T(8,128)(2,1)} %param.7, bf16[1024,1024]{1,0:T(8,128)(2,1)} %param.8), kind=kOutput, calls=%fused_computation.8 | convolution fusion | flops 67141632 | bytes 2228224 | tf_op jit(solution)/shard_map/td,ld->tl/dot_general | solution.py:34
  9.3 0.1 collective-permute-start.2
  9.4 1.5 %collective-permute-start.1 = (bf16[32,1024]{1,0:T(8,128)(2,1)S(1)}, bf16[32,1024]{1,0:T(8,128)(2,1)S(1)}, u32[]{:S(2)}, u32[]{:S(2)}) collective-permute-start(bf16[32,1024]{1,0:T(8,128)(2,1)S(1)} %convolution_convert_fusion.1), channel_id=1, source_target_pairs={{0,2},{1,3},{2,0},{3,1},{4,6},{5,7},{6,4},{7,5},{8,10},{9,11},{10,... | collective-permute-start | bytes 196616 | tf_op jit(solution)/shard_map/ppermute | solution.py:9
  10.9 0.0 collective-permute-done.8
  10.9 0.2 collective-permute-start
  11.0 0.3 collective-permute-done.6
  11.3 0.1 pad_maximum_fusion
  11.4 3.6 %collective-permute-done.1 = bf16[32,1024]{1,0:T(8,128)(2,1)S(1)} collective-permute-done((bf16[32,1024]{1,0:T(8,128)(2,1)S(1)}, bf16[32,1024]{1,0:T(8,128)(2,1)S(1)}, u32[]{:S(2)}, u32[]{:S(2)}) %collective-permute-start.1) | collective-permute-done | bytes 65568 | tf_op jit(solution)/shard_map/ppermute | solution.py:9
  15.0 0.2 collective-permute-done
  15.2 2.9 %collective-permute-start.5 = (bf16[32,1024]{1,0:T(8,128)(2,1)S(1)}, bf16[32,1024]{1,0:T(8,128)(2,1)S(1)}, u32[]{:S(2)}, u32[]{:S(2)}) collective-permute-start(bf16[32,1024]{1,0:T(8,128)(2,1)S(1)} %add_convert_fusion.2), channel_id=1, source_target_pairs={{0,12},{4,0},{8,4},{12,8},{1,13},{5,1},{9,5},{13,9},{2,14},{6,2},{... | collective-permute-start | bytes 196616 | tf_op jit(solution)/shard_map/ppermute | solution.py:9
  18.1 1.1 %collective-permute-start.4 = (bf16[32,1024]{1,0:T(8,128)(2,1)S(1)}, bf16[32,1024]{1,0:T(8,128)(2,1)S(1)}, u32[]{:S(2)}, u32[]{:S(2)}) collective-permute-start(bf16[32,1024]{1,0:T(8,128)(2,1)S(1)} %add_convert_fusion.2), channel_id=1, source_target_pairs={{0,8},{4,12},{8,0},{12,4},{1,9},{5,13},{9,1},{13,5},{2,10},{6,14},... | collective-permute-start | bytes 196616 | tf_op jit(solution)/shard_map/ppermute | solution.py:9
  19.2 0.0 collective-permute-start.3
  19.2 0.8 %collective-permute-done.5 = bf16[32,1024]{1,0:T(8,128)(2,1)S(1)} collective-permute-done((bf16[32,1024]{1,0:T(8,128)(2,1)S(1)}, bf16[32,1024]{1,0:T(8,128)(2,1)S(1)}, u32[]{:S(2)}, u32[]{:S(2)}) %collective-permute-start.5) | collective-permute-done | bytes 65568 | tf_op jit(solution)/shard_map/ppermute | solution.py:9
  20.0 3.8 %collective-permute-done.4 = bf16[32,1024]{1,0:T(8,128)(2,1)S(1)} collective-permute-done((bf16[32,1024]{1,0:T(8,128)(2,1)S(1)}, bf16[32,1024]{1,0:T(8,128)(2,1)S(1)}, u32[]{:S(2)}, u32[]{:S(2)}) %collective-permute-start.4) | collective-permute-done | bytes 65568 | tf_op jit(solution)/shard_map/ppermute | solution.py:9
  23.8 1.4 %collective-permute-done.3 = bf16[32,1024]{1,0:T(8,128)(2,1)S(1)} collective-permute-done((bf16[32,1024]{1,0:T(8,128)(2,1)S(1)}, bf16[32,1024]{1,0:T(8,128)(2,1)S(1)}, u32[]{:S(2)}, u32[]{:S(2)}) %collective-permute-start.3) | collective-permute-done | bytes 65568 | tf_op jit(solution)/shard_map/ppermute | solution.py:9
  25.2 3.7 %fusion.4 = bf16[128,1024]{1,0:T(8,128)(2,1)S(1)} fusion(bf16[2,672,1024]{2,1,0:T(8,128)(2,1)S(1)} %copy-done, bf16[2,672,1024]{2,1,0:T(8,128)(2,1)} %param.10, f32[2,128]{1,0:T(2,128)S(1)} %dynamic-slice_bitcast_fusion, bf16[32,1024]{1,0:T(8,128)(2,1)S(1)} %collective-permute-done.5, bf16[32,1024]{1,0:T(8,128)(2,1)S(1)} %collective-permute-done.4, ...), kind=kOutput, calls=%fused_computation.6 | convolution fusion | flops 706510848 | bytes 6030336 | tf_op jit(solution)/shard_map/kth,khl->tl/dot_general | solution.py:40
  29.0 0.4 collective-permute-start.9
  29.4 1.7 %collective-permute-start.11 = (bf16[32,1024]{1,0:T(8,128)(2,1)S(1)}, bf16[32,1024]{1,0:T(8,128)(2,1)S(1)}, u32[]{:S(2)}, u32[]{:S(2)}) collective-permute-start(bf16[32,1024]{1,0:T(8,128)(2,1)S(1)} %get-tuple-element.6), channel_id=1, source_target_pairs={{0,4},{4,8},{8,12},{12,0},{1,5},{5,9},{9,13},{13,1},{2,6},{6,10},{... | collective-permute-start | bytes 196616 | tf_op jit(solution)/shard_map/ppermute | solution.py:9
  31.1 0.2 collective-permute-start.10
  31.3 2.7 %collective-permute-done.9 = bf16[32,1024]{1,0:T(8,128)(2,1)S(1)} collective-permute-done((bf16[32,1024]{1,0:T(8,128)(2,1)S(1)}, bf16[32,1024]{1,0:T(8,128)(2,1)S(1)}, u32[]{:S(2)}, u32[]{:S(2)}) %collective-permute-start.9) | collective-permute-done | bytes 65568 | tf_op jit(solution)/shard_map/ppermute | solution.py:9
  34.0 1.5 %collective-permute-done.11 = bf16[32,1024]{1,0:T(8,128)(2,1)S(1)} collective-permute-done((bf16[32,1024]{1,0:T(8,128)(2,1)S(1)}, bf16[32,1024]{1,0:T(8,128)(2,1)S(1)}, u32[]{:S(2)}, u32[]{:S(2)}) %collective-permute-start.11) | collective-permute-done | bytes 65568 | tf_op jit(solution)/shard_map/ppermute | solution.py:9
  35.5 1.4 %collective-permute-done.10 = bf16[32,1024]{1,0:T(8,128)(2,1)S(1)} collective-permute-done((bf16[32,1024]{1,0:T(8,128)(2,1)S(1)}, bf16[32,1024]{1,0:T(8,128)(2,1)S(1)}, u32[]{:S(2)}, u32[]{:S(2)}) %collective-permute-start.10) | collective-permute-done | bytes 65568 | tf_op jit(solution)/shard_map/ppermute | solution.py:9
  36.9 0.1 collective-permute-start.14
  37.0 1.1 %collective-permute-start.13 = (bf16[32,1024]{1,0:T(8,128)(2,1)S(1)}, bf16[32,1024]{1,0:T(8,128)(2,1)S(1)}, u32[]{:S(2)}, u32[]{:S(2)}) collective-permute-start(bf16[32,1024]{1,0:T(8,128)(2,1)S(1)} %add_convert_fusion.1), channel_id=1, source_target_pairs={{0,2},{1,3},{2,0},{3,1},{4,6},{5,7},{6,4},{7,5},{8,10},{9,11},{10,... | collective-permute-start | bytes 196616 | tf_op jit(solution)/shard_map/ppermute | solution.py:9
  38.1 0.2 collective-permute-start.12
  38.3 0.7 %collective-permute-done.14 = bf16[32,1024]{1,0:T(8,128)(2,1)S(1)} collective-permute-done((bf16[32,1024]{1,0:T(8,128)(2,1)S(1)}, bf16[32,1024]{1,0:T(8,128)(2,1)S(1)}, u32[]{:S(2)}, u32[]{:S(2)}) %collective-permute-start.14) | collective-permute-done | bytes 65568 | tf_op jit(solution)/shard_map/ppermute | solution.py:9
  39.0 3.0 %collective-permute-done.13 = bf16[32,1024]{1,0:T(8,128)(2,1)S(1)} collective-permute-done((bf16[32,1024]{1,0:T(8,128)(2,1)S(1)}, bf16[32,1024]{1,0:T(8,128)(2,1)S(1)}, u32[]{:S(2)}, u32[]{:S(2)}) %collective-permute-start.13) | collective-permute-done | bytes 65568 | tf_op jit(solution)/shard_map/ppermute | solution.py:9
  42.0 0.4 collective-permute-done.12
  42.4 2.7 %convolution_convert_fusion = bf16[32,1024]{1,0:T(8,128)(2,1)} fusion(bf16[1024,1024]{1,0:T(8,128)(2,1)} %param.9, bf16[32,1024]{1,0:T(8,128)(2,1)S(1)} %collective-permute-done.14, bf16[32,1024]{1,0:T(8,128)(2,1)S(1)} %collective-permute-done.13, bf16[32,1024]{1,0:T(8,128)(2,1)S(1)} %collective-permute-done.12, bf16[32,1024]{1,0:T(8,128)(2,1)S(1)} %add_convert_fusion.1), kind=kOutput, calls=%fused_computation.7 | convolution fusion | flops 67403776 | bytes 2424832 | tf_op jit(solution)/shard_map/dot_general | solution.py:48
  (9 shorter events, 0.1 us)
Async XLA Ops:
  0.0 25.2 %copy-start = (bf16[2,672,1024]{2,1,0:T(8,128)(2,1)S(1)}, bf16[2,672,1024]{2,1,0:T(8,128)(2,1)}, u32[]{:S(2)}) copy-start(bf16[2,672,1024]{2,1,0:T(8,128)(2,1)} %param.11) | copy-start | bytes 8257540
  0.9 10.0 %collective-permute-start.8 = (f32[32,8]{0,1:T(8,128)S(1)}, f32[32,8]{0,1:T(8,128)S(1)}, u32[]{:S(2)}, u32[]{:S(2)}) collective-permute-start(f32[32,8]{0,1:T(8,128)S(1)} %select_reduce_fusion), channel_id=1, source_target_pairs={{0,12},{4,0},{8,4},{12,8},{1,13},{5,1},{9,5},{13,9},{2,14},{6,2},{... | collective-permute-start | bytes 3080 | tf_op jit(solution)/shard_map/ppermute | solution.py:9
  5.9 5.1 %collective-permute-start.7 = (f32[32,8]{0,1:T(8,128)S(1)}, f32[32,8]{0,1:T(8,128)S(1)}, u32[]{:S(2)}, u32[]{:S(2)}) collective-permute-start(f32[32,8]{0,1:T(8,128)S(1)} %select_reduce_fusion), channel_id=1, source_target_pairs={{0,8},{4,12},{8,0},{12,4},{1,9},{5,13},{9,1},{13,5},{2,10},{6,14},... | collective-permute-start | bytes 3080 | tf_op jit(solution)/shard_map/ppermute | solution.py:9
  5.9 5.4 %collective-permute-start.6 = (f32[32,8]{0,1:T(8,128)S(1)}, f32[32,8]{0,1:T(8,128)S(1)}, u32[]{:S(2)}, u32[]{:S(2)}) collective-permute-start(f32[32,8]{0,1:T(8,128)S(1)} %select_reduce_fusion), channel_id=1, source_target_pairs={{0,4},{4,8},{8,12},{12,0},{1,5},{5,9},{9,13},{13,1},{2,6},{6,10},{... | collective-permute-start | bytes 3080 | tf_op jit(solution)/shard_map/ppermute | solution.py:9
  9.3 2.1 %collective-permute-start.2 = (bf16[32,1024]{1,0:T(8,128)(2,1)S(1)}, bf16[32,1024]{1,0:T(8,128)(2,1)S(1)}, u32[]{:S(2)}, u32[]{:S(2)}) collective-permute-start(bf16[32,1024]{1,0:T(8,128)(2,1)S(1)} %convolution_convert_fusion.1), channel_id=1, source_target_pairs={{0,3},{1,0},{2,1},{3,2},{4,7},{5,4},{6,5},{7,6},{8,11},{9,8},{10,9... | collective-permute-start | bytes 196616 | tf_op jit(solution)/shard_map/ppermute | solution.py:9
  9.4 5.6 %collective-permute-start.1 = (bf16[32,1024]{1,0:T(8,128)(2,1)S(1)}, bf16[32,1024]{1,0:T(8,128)(2,1)S(1)}, u32[]{:S(2)}, u32[]{:S(2)}) collective-permute-start(bf16[32,1024]{1,0:T(8,128)(2,1)S(1)} %convolution_convert_fusion.1), channel_id=1, source_target_pairs={{0,2},{1,3},{2,0},{3,1},{4,6},{5,7},{6,4},{7,5},{8,10},{9,11},{10,... | collective-permute-start | bytes 196616 | tf_op jit(solution)/shard_map/ppermute | solution.py:9
  10.9 4.3 %collective-permute-start = (bf16[32,1024]{1,0:T(8,128)(2,1)S(1)}, bf16[32,1024]{1,0:T(8,128)(2,1)S(1)}, u32[]{:S(2)}, u32[]{:S(2)}) collective-permute-start(bf16[32,1024]{1,0:T(8,128)(2,1)S(1)} %convolution_convert_fusion.1), channel_id=1, source_target_pairs={{0,1},{1,2},{2,3},{3,0},{4,5},{5,6},{6,7},{7,4},{8,9},{9,10},{10,1... | collective-permute-start | bytes 196616 | tf_op jit(solution)/shard_map/ppermute | solution.py:9
  15.2 4.8 %collective-permute-start.5 = (bf16[32,1024]{1,0:T(8,128)(2,1)S(1)}, bf16[32,1024]{1,0:T(8,128)(2,1)S(1)}, u32[]{:S(2)}, u32[]{:S(2)}) collective-permute-start(bf16[32,1024]{1,0:T(8,128)(2,1)S(1)} %add_convert_fusion.2), channel_id=1, source_target_pairs={{0,12},{4,0},{8,4},{12,8},{1,13},{5,1},{9,5},{13,9},{2,14},{6,2},{... | collective-permute-start | bytes 196616 | tf_op jit(solution)/shard_map/ppermute | solution.py:9
  18.1 5.7 %collective-permute-start.4 = (bf16[32,1024]{1,0:T(8,128)(2,1)S(1)}, bf16[32,1024]{1,0:T(8,128)(2,1)S(1)}, u32[]{:S(2)}, u32[]{:S(2)}) collective-permute-start(bf16[32,1024]{1,0:T(8,128)(2,1)S(1)} %add_convert_fusion.2), channel_id=1, source_target_pairs={{0,8},{4,12},{8,0},{12,4},{1,9},{5,13},{9,1},{13,5},{2,10},{6,14},... | collective-permute-start | bytes 196616 | tf_op jit(solution)/shard_map/ppermute | solution.py:9
  19.2 6.1 %collective-permute-start.3 = (bf16[32,1024]{1,0:T(8,128)(2,1)S(1)}, bf16[32,1024]{1,0:T(8,128)(2,1)S(1)}, u32[]{:S(2)}, u32[]{:S(2)}) collective-permute-start(bf16[32,1024]{1,0:T(8,128)(2,1)S(1)} %add_convert_fusion.2), channel_id=1, source_target_pairs={{0,4},{4,8},{8,12},{12,0},{1,5},{5,9},{9,13},{13,1},{2,6},{6,10},{... | collective-permute-start | bytes 196616 | tf_op jit(solution)/shard_map/ppermute | solution.py:9
  29.0 4.9 %collective-permute-start.9 = (bf16[32,1024]{1,0:T(8,128)(2,1)S(1)}, bf16[32,1024]{1,0:T(8,128)(2,1)S(1)}, u32[]{:S(2)}, u32[]{:S(2)}) collective-permute-start(bf16[32,1024]{1,0:T(8,128)(2,1)S(1)} %get-tuple-element.5), channel_id=1, source_target_pairs={{0,12},{4,0},{8,4},{12,8},{1,13},{5,1},{9,5},{13,9},{2,14},{6,2},{... | collective-permute-start | bytes 196616 | tf_op jit(solution)/shard_map/ppermute | solution.py:9
  29.4 6.1 %collective-permute-start.11 = (bf16[32,1024]{1,0:T(8,128)(2,1)S(1)}, bf16[32,1024]{1,0:T(8,128)(2,1)S(1)}, u32[]{:S(2)}, u32[]{:S(2)}) collective-permute-start(bf16[32,1024]{1,0:T(8,128)(2,1)S(1)} %get-tuple-element.6), channel_id=1, source_target_pairs={{0,4},{4,8},{8,12},{12,0},{1,5},{5,9},{9,13},{13,1},{2,6},{6,10},{... | collective-permute-start | bytes 196616 | tf_op jit(solution)/shard_map/ppermute | solution.py:9
  31.1 5.8 %collective-permute-start.10 = (bf16[32,1024]{1,0:T(8,128)(2,1)S(1)}, bf16[32,1024]{1,0:T(8,128)(2,1)S(1)}, u32[]{:S(2)}, u32[]{:S(2)}) collective-permute-start(bf16[32,1024]{1,0:T(8,128)(2,1)S(1)} %get-tuple-element.7), channel_id=1, source_target_pairs={{0,8},{4,12},{8,0},{12,4},{1,9},{5,13},{9,1},{13,5},{2,10},{6,14},... | collective-permute-start | bytes 196616 | tf_op jit(solution)/shard_map/ppermute | solution.py:9
  36.9 2.0 %collective-permute-start.14 = (bf16[32,1024]{1,0:T(8,128)(2,1)S(1)}, bf16[32,1024]{1,0:T(8,128)(2,1)S(1)}, u32[]{:S(2)}, u32[]{:S(2)}) collective-permute-start(bf16[32,1024]{1,0:T(8,128)(2,1)S(1)} %add_convert_fusion.1), channel_id=1, source_target_pairs={{0,3},{1,0},{2,1},{3,2},{4,7},{5,4},{6,5},{7,6},{8,11},{9,8},{10,9... | collective-permute-start | bytes 196616 | tf_op jit(solution)/shard_map/ppermute | solution.py:9
  37.0 5.0 %collective-permute-start.13 = (bf16[32,1024]{1,0:T(8,128)(2,1)S(1)}, bf16[32,1024]{1,0:T(8,128)(2,1)S(1)}, u32[]{:S(2)}, u32[]{:S(2)}) collective-permute-start(bf16[32,1024]{1,0:T(8,128)(2,1)S(1)} %add_convert_fusion.1), channel_id=1, source_target_pairs={{0,2},{1,3},{2,0},{3,1},{4,6},{5,7},{6,4},{7,5},{8,10},{9,11},{10,... | collective-permute-start | bytes 196616 | tf_op jit(solution)/shard_map/ppermute | solution.py:9
  38.1 4.3 %collective-permute-start.12 = (bf16[32,1024]{1,0:T(8,128)(2,1)S(1)}, bf16[32,1024]{1,0:T(8,128)(2,1)S(1)}, u32[]{:S(2)}, u32[]{:S(2)}) collective-permute-start(bf16[32,1024]{1,0:T(8,128)(2,1)S(1)} %add_convert_fusion.1), channel_id=1, source_target_pairs={{0,1},{1,2},{2,3},{3,0},{4,5},{5,6},{6,7},{7,4},{8,9},{9,10},{10,1... | collective-permute-start | bytes 196616 | tf_op jit(solution)/shard_map/ppermute | solution.py:9

commit v2 on v1

v2 whole, which is shorter than its diff:
```python
import jax
import jax.numpy as jnp
from jax import lax
from jax.sharding import PartitionSpec as P


def swap(blocks, axes):
    return lax.all_to_all(blocks, axes, split_axis=0, concat_axis=0, tiled=True)


def spread(x, axes, count):
    return swap(jnp.broadcast_to(x[None], (count, *x.shape)), axes)


def summed(blocks):
    return jnp.sum(blocks.astype(jnp.float32), axis=0).astype(jnp.bfloat16)


def on_device(tokens, lat_down, lat_up, expert_up, expert_down, routes, route_weights):
    exp_count, tp_count = lax.axis_size("exp"), lax.axis_size("tp")
    local_count = expert_up.shape[0]
    rows, latent_len = tokens.shape[0], lat_down.shape[0]
    part_len = latent_len // tp_count
    experts_all = local_count * exp_count
    named = routes[:, :, None] == jnp.arange(experts_all, dtype=jnp.int32)[None, None, :]
    combine = jnp.sum(jnp.where(named, route_weights[:, :, None], 0.0), axis=1)
    combine_here = swap(combine.reshape(rows, exp_count, local_count).transpose(1, 0, 2), "exp")
    combine_here = combine_here.reshape(exp_count * rows, local_count)

    partial_latent = jnp.einsum("td,ld->tl", tokens, lat_down, preferred_element_type=jnp.float32)
    parts = partial_latent.astype(jnp.bfloat16).reshape(rows, tp_count, part_len).transpose(1, 0, 2)
    latent_part = summed(swap(parts, "tp"))
    latent_all = spread(latent_part, ("exp", "tp"), exp_count * tp_count)
    latent_all = latent_all.reshape(exp_count, tp_count, rows, part_len).transpose(0, 2, 1, 3)
    latent_all = latent_all.reshape(exp_count * rows, latent_len)

    pre_act = jnp.einsum("tl,khl->kth", latent_all, expert_up, preferred_element_type=jnp.float32)
    hidden = jnp.maximum(pre_act, 0.0) ** 2 * combine_here.T[:, :, None]
    partial_out = jnp.einsum(
        "kth,khl->tl", hidden.astype(jnp.bfloat16), expert_down, preferred_element_type=jnp.float32
    ).astype(jnp.bfloat16)
    blocks = partial_out.reshape(exp_count, rows, tp_count, part_len).transpose(0, 2, 1, 3)
    mixed_part = summed(swap(blocks.reshape(exp_count * tp_count, rows, part_len), ("exp", "tp")))
    mixed_rows = spread(mixed_part, "tp", tp_count).transpose(1, 0, 2).reshape(rows, latent_len)
    return jnp.dot(mixed_rows, lat_up, preferred_element_type=jnp.float32).astype(jnp.bfloat16)


def solution(mesh):
    return jax.shard_map(
        on_device,
        mesh=mesh,
        in_specs=(
            P(("grp", "exp"), "tp"),
            P(None, "tp"),
            P(None, "tp"),
            P("exp", "tp", None),
            P("exp", "tp", None),
            P(("grp", "exp"), None),
            P(("grp", "exp"), None),
        ),
        out_specs=P(("grp", "exp"), "tp"),
        check_vma=False,
    )
```

time: 45.3 us -> 63.7 us (1.41)
  blocking collectives: 0 us -> 19.3 us
  starting transfers between devices: 15.4 us -> 13.1 us
  local copies, waits for them, and re-layouts: 0.02 us -> 2.06 us
  waiting for transfers between devices: 19.8 us -> 18.3 us
    ppermute x15 -> x0, waiting for transfers between devices: 19.8 us -> none  [shifted(): lax.ppermute(x, axis, [(i, (i + shift) % count) for i in range(count)])]
    all_to_all x0 -> x2, blocking collectives: none -> 19.3 us  [swap(): return lax.all_to_all(blocks, axes, split_axis=0, concat_axis=0, tiled=True)]
    all_to_all x0 -> x3, waiting for transfers between devices: none -> 18.3 us  [swap(): return lax.all_to_all(blocks, axes, split_axis=0, concat_axis=0, tiled=True)]
    ppermute x15 -> x0, starting transfers between devices: 15.4 us -> none  [shifted(): lax.ppermute(x, axis, [(i, (i + shift) % count) for i in range(count)])]
    all_to_all x0 -> x3, starting transfers between devices: none -> 13.1 us  [swap(): return lax.all_to_all(blocks, axes, split_axis=0, concat_axis=0, tiled=True)]
    reshape x0 -> x6, local copies, waits for them, and re-layouts: none -> 1.12 us  [the longest x1 0.65 us: on_device(): partial_latent.astype(jnp.bfloat16).reshape(rows, tp_count, part_len)]
    broadcast_in_dim x0 -> x2, local copies, waits for them, and re-layouts: none -> 0.72 us  [spread(): return swap(jnp.broadcast_to(x[None], (count, *x.shape)), axes)]
  transfers between devices with their start and end apart: 15 -> 3, of which waited for: 12 -> 3; matrix products, arithmetic and copies ran while one was open for 5% -> 2% of each run, Pallas kernels for 0% -> 0%
where the time goes in v2:
time: 63.7 us; the launch traced here: 63.1 us
  blocking collectives  19.3 us (30%)
  waiting for transfers between devices  18.3 us (29%)
  starting transfers between devices  13.1 us (21%)
  matrix products  8.92 us (14%)
  local copies, waits for them, and re-layouts  2.06 us (3%)
  other arithmetic  1.36 us (2%)
    all_to_all x2, blocking collectives, swap(): return lax.all_to_all(blocks, axes, split_axis=0, concat_axis=0, tiled=True)  19.3 us
    all_to_all x3, waiting for transfers between devices, swap(): return lax.all_to_all(blocks, axes, split_axis=0, concat_axis=0, tiled=True)  18.3 us
    all_to_all x3, starting transfers between devices, swap(): return lax.all_to_all(blocks, axes, split_axis=0, concat_axis=0, tiled=True)  13.1 us
    dot_general x1, matrix products, on_device(): jnp.einsum('kth,khl->tl', hidden.astype(jnp.bfloat16), expert_down, prefe...  3.74 us
    dot_general x1, matrix products, on_device(): jnp.dot(mixed_rows, lat_up, preferred_element_type=jnp.float32)  2.7 us
    dot_general x1, matrix products, on_device(): jnp.einsum('td,ld->tl', tokens, lat_down, preferred_element_type=jnp.floa...  2.49 us
    reduce_sum x1, other arithmetic, on_device(): combine = jnp.sum(jnp.where(named, route_weights[:, :, None], 0.0), axis=1)  1.3 us
  transfers between devices with their start and end apart: 3, of which 3 were waited for; matrix products, arithmetic and copies ran while one was open for 2% of the time, Pallas kernels for 0%

profile of v2, /device:TPU:0, one launch (start us, length us, event | category | flops | bytes accessed | tf_op | source)
XLA Modules:
  0.0 63.1 jit_solution(18308430189576608693)
XLA Ops:
  0.0 0.0 copy-start
  0.0 2.5 %convolution_convert_fusion.1 = bf16[32,1024]{1,0:T(8,128)(2,1)S(1)} fusion(bf16[32,1024]{1,0:T(8,128)(2,1)} %param.7, bf16[1024,1024]{1,0:T(8,128)(2,1)} %param.8), kind=kOutput, calls=%fused_computation.8 | convolution fusion | flops 67141632 | bytes 2228224 | tf_op jit(solution)/shard_map/td,ld->tl/dot_general | solution.py:30
  2.5 0.7 %copy.33 = bf16[4,4,8,256]{3,2,0,1:T(8,128)(2,1)} copy(bf16[4,4,8,256]{3,2,1,0:T(8,128)(2,1)S(1)} %bitcast.44) | data formatting | bytes 131072 | tf_op jit(solution)/shard_map/reshape | solution.py:31
  3.1 4.2 %all-to-all-start = ((bf16[4,32,256]{2,1,0:T(8,128)(2,1)}), bf16[4,32,256]{2,1,0:T(8,128)(2,1)S(1)}, u32[]{:S(2)}, u32[]{:S(2)}) async-start(bf16[4,32,256]{2,1,0:T(8,128)(2,1)} %bitcast.40), calls=%async_computation | async-start | bytes 131072 | tf_op jit(solution)/shard_map/all_to_all | solution.py:8
  7.4 1.3 %select_reduce_fusion = f32[32,8]{0,1:T(8,128)} fusion(f32[32,4]{0,1:T(4,128)} %param.13, s32[32,4]{0,1:T(4,128)} %param.12), kind=kLoop, calls=%fused_computation.12 | loop fusion | flops 2816 | bytes 2048 | tf_op jit(solution)/shard_map/reduce_sum | solution.py:26
  8.7 2.8 %all-to-all-done = bf16[4,32,256]{2,1,0:T(8,128)(2,1)S(1)} async-done(((bf16[4,32,256]{2,1,0:T(8,128)(2,1)}), bf16[4,32,256]{2,1,0:T(8,128)(2,1)S(1)}, u32[]{:S(2)}, u32[]{:S(2)}) %all-to-all-start) | async-done | bytes 65568 | tf_op jit(solution)/shard_map/all_to_all | solution.py:8
  11.5 5.4 %all-to-all-start.2 = ((f32[4,32,2]{1,2,0:T(2,128)}), f32[4,32,2]{1,2,0:T(2,128)S(1)}, u32[]{:S(2)}, u32[]{:S(2)}) async-start(f32[4,32,2]{1,2,0:T(2,128)} %bitcast.5), calls=%async_computation.2 | async-start | bytes 8192 | tf_op jit(solution)/shard_map/all_to_all | solution.py:8
  16.9 5.6 %all-to-all-done.2 = f32[4,32,2]{1,2,0:T(2,128)S(1)} async-done(((f32[4,32,2]{1,2,0:T(2,128)}), f32[4,32,2]{1,2,0:T(2,128)S(1)}, u32[]{:S(2)}, u32[]{:S(2)}) %all-to-all-start.2) | async-done | bytes 1056 | tf_op jit(solution)/shard_map/all_to_all | solution.py:8
  22.4 0.7 %broadcast_in_dim.16 = bf16[16,32,256]{2,1,0:T(8,128)(2,1)} broadcast(bf16[32,256]{1,0:T(8,128)(2,1)S(1)} %reduce_sum.33), dimensions={1,2} | broadcast | bytes 278528 | tf_op jit(solution)/shard_map/broadcast_in_dim | solution.py:12
  23.1 3.5 %all-to-all-start.1 = ((bf16[16,32,256]{2,1,0:T(8,128)(2,1)}), bf16[16,32,256]{2,1,0:T(8,128)(2,1)S(1)}, u32[]{:S(2)}, u32[]{:S(2)}) async-start(bf16[16,32,256]{2,1,0:T(8,128)(2,1)} %broadcast_in_dim.16), calls=%async_computation.1 | async-start | bytes 524288 | tf_op jit(solution)/shard_map/all_to_all | solution.py:8
  26.7 0.1 reshape.33
  26.8 9.9 %all-to-all-done.1 = bf16[16,32,256]{2,1,0:T(8,128)(2,1)S(1)} async-done(((bf16[16,32,256]{2,1,0:T(8,128)(2,1)}), bf16[16,32,256]{2,1,0:T(8,128)(2,1)S(1)}, u32[]{:S(2)}, u32[]{:S(2)}) %all-to-all-start.1) | async-done | bytes 262176 | tf_op jit(solution)/shard_map/all_to_all | solution.py:8
  36.7 0.2 copy.26
  36.9 0.2 reshape.37
  37.1 0.0 copy-done
  37.1 3.7 %fusion.4 = bf16[128,1024]{1,0:T(8,128)(2,1)S(1)} fusion(bf16[2,672,1024]{2,1,0:T(8,128)(2,1)S(1)} %copy-done, bf16[128,1024,1]{1,0,2:T(8,128)(2,1)S(1)} %reshape.37, bf16[2,672,1024]{2,1,0:T(8,128)(2,1)} %param.10, f32[2,128]{1,0:T(2,128)S(1)} %bitcast.46), kind=kOutput, calls=%fused_computation.6 | convolution fusion | flops 705462272 | bytes 6030336 | tf_op jit(solution)/shard_map/kth,khl->tl/dot_general | solution.py:39
  40.8 0.2 reshape.34
  41.0 12.8 %all_to_all.25 = bf16[16,32,256]{2,1,0:T(8,128)(2,1)S(1)} all-to-all(bf16[16,32,256]{2,1,0:T(8,128)(2,1)S(1)} %bitcast.42), channel_id=1, replica_groups=mesh['grp'=2,'exp'=4,'tp'=4] {'exp','tp'}, dimensions={0} | all-to-all | bytes 524288 | tf_op jit(solution)/shard_map/all_to_all | solution.py:8
  53.9 6.5 %all_to_all.26 = bf16[4,32,256]{2,1,0:T(8,128)(2,1)S(1)} all-to-all(bf16[4,32,256]{2,1,0:T(8,128)(2,1)S(1)} %broadcast_in_dim.19), channel_id=1, replica_groups=mesh['grp'=2,'exp'=4,'tp'=4] {'tp'}, dimensions={0} | all-to-all | bytes 131072 | tf_op jit(solution)/shard_map/all_to_all | solution.py:8
  60.4 2.7 %convolution_convert_fusion = bf16[32,1024]{1,0:T(8,128)(2,1)} fusion(bf16[32,1024]{1,0:T(8,128)(2,1)S(1)} %bitcast.43, bf16[1024,1024]{1,0:T(8,128)(2,1)} %param.9), kind=kOutput, calls=%fused_computation.7 | convolution fusion | flops 67141632 | bytes 2228224 | tf_op jit(solution)/shard_map/dot_general | solution.py:45
  (6 shorter events, 0.1 us)
Async XLA Ops:
  0.0 37.1 %copy-start = (bf16[2,672,1024]{2,1,0:T(8,128)(2,1)S(1)}, bf16[2,672,1024]{2,1,0:T(8,128)(2,1)}, u32[]{:S(2)}) copy-start(bf16[2,672,1024]{2,1,0:T(8,128)(2,1)} %param.11) | copy-start | bytes 8257540
  3.1 8.3 %all-to-all-start = ((bf16[4,32,256]{2,1,0:T(8,128)(2,1)}), bf16[4,32,256]{2,1,0:T(8,128)(2,1)S(1)}, u32[]{:S(2)}, u32[]{:S(2)}) async-start(bf16[4,32,256]{2,1,0:T(8,128)(2,1)} %bitcast.40), calls=%async_computation | async-start | bytes 131072 | tf_op jit(solution)/shard_map/all_to_all | solution.py:8
  11.5 10.9 %all-to-all-start.2 = ((f32[4,32,2]{1,2,0:T(2,128)}), f32[4,32,2]{1,2,0:T(2,128)S(1)}, u32[]{:S(2)}, u32[]{:S(2)}) async-start(f32[4,32,2]{1,2,0:T(2,128)} %bitcast.5), calls=%async_computation.2 | async-start | bytes 8192 | tf_op jit(solution)/shard_map/all_to_all | solution.py:8
  23.1 13.5 %all-to-all-start.1 = ((bf16[16,32,256]{2,1,0:T(8,128)(2,1)}), bf16[16,32,256]{2,1,0:T(8,128)(2,1)S(1)}, u32[]{:S(2)}, u32[]{:S(2)}) async-start(bf16[16,32,256]{2,1,0:T(8,128)(2,1)} %broadcast_in_dim.16), calls=%async_computation.1 | async-start | bytes 524288 | tf_op jit(solution)/shard_map/all_to_all | solution.py:8

commit v3 on v2

v3 whole, which is shorter than its diff:
```python
import jax
import jax.numpy as jnp
from jax import lax
from jax.sharding import PartitionSpec as P

BF16, F32 = jnp.bfloat16, jnp.float32


def traded(x, axis, mask):
    return lax.ppermute(x, axis, [(i, i ^ mask) for i in range(lax.axis_size(axis))])


def summed(own, arrived):
    total = own.astype(F32)
    for block in arrived:
        total = total + block.astype(F32)
    return total


def on_device(tokens, lat_down, lat_up, expert_up, expert_down, routes, route_weights):
    exp_count, tp_count = lax.axis_size("exp"), lax.axis_size("tp")
    me = lax.axis_index("exp")
    odd = lax.axis_index("tp") % 2 == 1
    local_count = expert_up.shape[0]
    rows, latent_len = tokens.shape[0], lat_down.shape[0]
    half = latent_len // 2
    experts_all = local_count * exp_count
    pair_masks = [1 << b for b in range(1, tp_count.bit_length() - 1)]

    def mine(x):
        return jnp.where(odd, x[:, half:], x[:, :half])

    def theirs(x):
        return jnp.where(odd, x[:, :half], x[:, half:])

    def whole(own, other):
        return jnp.concatenate([jnp.where(odd, other, own), jnp.where(odd, own, other)], axis=1)

    def pair_sum(x):
        for mask in pair_masks:
            x = summed(x, [traded(x.astype(BF16), "tp", mask)])
        return x

    named = routes[:, :, None] == jnp.arange(experts_all, dtype=jnp.int32)[None, None, :]
    combine = jnp.sum(jnp.where(named, route_weights[:, :, None], 0.0), axis=1)
    high = combine.astype(BF16)
    low = (combine - high.astype(F32)).astype(BF16)
    pad = jnp.zeros((rows, -2 * experts_all % 128), BF16)

    partial_latent = jnp.einsum("td,ld->tl", tokens, lat_down, preferred_element_type=F32)
    latent_half = summed(
        mine(partial_latent), [traded(theirs(partial_latent).astype(BF16), "tp", 1)]
    )
    message = jnp.concatenate([pair_sum(latent_half).astype(BF16), high, low, pad], axis=1)
    messages = [message] + [traded(message, "exp", s) for s in range(1, exp_count)]
    messages = jnp.concatenate(messages, axis=0)
    halves = messages[:, :half]
    latent_all = whole(halves, traded(halves, "tp", 1))
    terms = messages[:, half : half + 2 * experts_all].astype(F32)
    combine_all = terms[:, :experts_all] + terms[:, experts_all:]
    combine_here = lax.dynamic_slice_in_dim(combine_all, me * local_count, local_count, axis=1)

    pre_act = jnp.einsum("tl,khl->kth", latent_all, expert_up, preferred_element_type=F32)
    hidden = jnp.maximum(pre_act, 0.0) ** 2 * combine_here.T[:, :, None]
    partial_out = jnp.einsum(
        "kth,khl->tl", hidden.astype(BF16), expert_down, preferred_element_type=F32
    )
    part_half = summed(
        mine(partial_out), [traded(theirs(partial_out).astype(BF16), "tp", 1)]
    ).astype(BF16)
    blocks = part_half.reshape(exp_count, rows, half)
    mixed_half = summed(blocks[0], [traded(blocks[s], "exp", s) for s in range(1, exp_count)])
    mixed_half = pair_sum(mixed_half).astype(BF16)
    mixed_rows = whole(mixed_half, traded(mixed_half, "tp", 1))
    return jnp.dot(mixed_rows, lat_up, preferred_element_type=F32).astype(BF16)


def solution(mesh):
    return jax.shard_map(
        on_device,
        mesh=mesh,
        in_specs=(
            P(("grp", "exp"), "tp"),
            P(None, "tp"),
            P(None, "tp"),
            P("exp", "tp", None),
            P("exp", "tp", None),
            P(("grp", "exp"), None),
            P(("grp", "exp"), None),
        ),
        out_specs=P(("grp", "exp"), "tp"),
        check_vma=False,
    )
```

time: 63.7 us -> 41.3 us (0.65)
  blocking collectives: 19.3 us -> 0 us
  local copies, waits for them, and re-layouts: 2.06 us -> 0.35 us
  waiting for transfers between devices: 18.3 us -> 16.7 us
    all_to_all x2 -> x0, blocking collectives: 19.3 us -> none  [swap(): return lax.all_to_all(blocks, axes, split_axis=0, concat_axis=0, tiled=True)]
    all_to_all x3 -> x0, waiting for transfers between devices: 18.3 us -> none  [swap(): return lax.all_to_all(blocks, axes, split_axis=0, concat_axis=0, tiled=True)]
    ppermute x0 -> x12, waiting for transfers between devices: none -> 16.7 us  [traded(): lax.ppermute(x, axis, [(i, i ^ mask) for i in range(lax.axis_size(axis))])]
    ppermute x0 -> x12, starting transfers between devices: none -> 13.7 us  [traded(): lax.ppermute(x, axis, [(i, i ^ mask) for i in range(lax.axis_size(axis))])]
    all_to_all x3 -> x0, starting transfers between devices: 13.1 us -> none  [swap(): return lax.all_to_all(blocks, axes, split_axis=0, concat_axis=0, tiled=True)]
    reshape x6 -> x0, local copies, waits for them, and re-layouts: 1.12 us -> none  [the longest x1 0.65 us: on_device(): partial_latent.astype(jnp.bfloat16).reshape(rows, tp_count, part_len)]
    broadcast_in_dim x2 -> x1, local copies, waits for them, and re-layouts: 0.72 us -> 0.01 us  [on_device(): pad = jnp.zeros((rows, -2 * experts_all % 128), BF16)]
  transfers between devices with their start and end apart: 3 -> 12, of which waited for: 3 -> 11; matrix products, arithmetic and copies ran while one was open for 2% -> 3% of each run, Pallas kernels for 0% -> 0%
where the time goes in v3:
time: 41.3 us; the launch traced here: 41.1 us
  waiting for transfers between devices  16.7 us (40%)
  starting transfers between devices  13.7 us (33%)
  matrix products  8.93 us (22%)
  other arithmetic  1.29 us (3%)
    ppermute x12, waiting for transfers between devices, traded(): lax.ppermute(x, axis, [(i, i ^ mask) for i in range(lax.axis_size(axis))])  16.7 us
    ppermute x12, starting transfers between devices, traded(): lax.ppermute(x, axis, [(i, i ^ mask) for i in range(lax.axis_size(axis))])  13.7 us
    dot_general x1, matrix products, on_device(): jnp.einsum('kth,khl->tl', hidden.astype(BF16), expert_down, preferred_ele...  3.74 us
    dot_general x1, matrix products, on_device(): return jnp.dot(mixed_rows, lat_up, preferred_element_type=F32).astype(BF16)  2.7 us
    dot_general x1, matrix products, on_device(): jnp.einsum('td,ld->tl', tokens, lat_down, preferred_element_type=F32)  2.49 us
  transfers between devices with their start and end apart: 12, of which 11 were waited for; matrix products, arithmetic and copies ran while one was open for 3% of the time, Pallas kernels for 0%

profile of v3, /device:TPU:0, one launch (start us, length us, event | category | flops | bytes accessed | tf_op | source)
XLA Modules:
  0.0 41.1 jit_solution(11268237998873925992)
XLA Ops:
  0.0 2.5 %fusion.22 = f32[32,1024]{1,0:T(8,128)S(1)} fusion(bf16[32,1024]{1,0:T(8,128)(2,1)} %param.7, bf16[1024,1024]{1,0:T(8,128)(2,1)} %param.8), kind=kOutput, calls=%fused_computation.41 | convolution fusion | flops 67108864 | bytes 2293760 | tf_op jit(solution)/shard_map/td,ld->tl/dot_general | solution.py:50
  2.5 0.5 %collective-permute-start = (bf16[32,512]{1,0:T(8,128)(2,1)S(1)}, bf16[32,512]{1,0:T(8,128)(2,1)S(1)}, u32[]{:S(2)}, u32[]{:S(2)}) collective-permute-start(bf16[32,512]{1,0:T(8,128)(2,1)S(1)} %select_convert_fusion.1), channel_id=1, source_target_pairs={{0,1},{1,0},{2,3},{3,2},{4,5},{5,4},{6,7},{7,6},{8,9},{9,8},{10,11... | collective-permute-start | bytes 98312 | tf_op jit(solution)/shard_map/ppermute | solution.py:10
  3.0 0.7 %select_reduce_fusion = f32[32,8]{0,1:T(8,128)S(1)} fusion(f32[32,4]{0,1:T(4,128)} %param.13, s32[32,4]{0,1:T(4,128)} %param.12), kind=kLoop, calls=%fused_computation.32 | loop fusion | flops 2816 | bytes 2048 | tf_op jit(solution)/shard_map/reduce_sum | solution.py:45
  3.7 0.2 collective-permute-done
  3.9 2.9 %collective-permute-start.1 = (bf16[32,512]{1,0:T(8,128)(2,1)S(1)}, bf16[32,512]{1,0:T(8,128)(2,1)S(1)}, u32[]{:S(2)}, u32[]{:S(2)}) collective-permute-start(bf16[32,512]{1,0:T(8,128)(2,1)S(1)} %fusion.15), channel_id=1, source_target_pairs={{0,2},{1,3},{2,0},{3,1},{4,6},{5,7},{6,4},{7,5},{8,10},{9,11},{10,... | collective-permute-start | bytes 98312 | tf_op jit(solution)/shard_map/ppermute | solution.py:10
  6.8 0.1 copy.15
  6.9 0.1 copy.14
  7.0 1.7 %collective-permute-done.1 = bf16[32,512]{1,0:T(8,128)(2,1)S(1)} collective-permute-done((bf16[32,512]{1,0:T(8,128)(2,1)S(1)}, bf16[32,512]{1,0:T(8,128)(2,1)S(1)}, u32[]{:S(2)}, u32[]{:S(2)}) %collective-permute-start.1) | collective-permute-done | bytes 32800 | tf_op jit(solution)/shard_map/ppermute | solution.py:10
  8.7 0.1 pad_maximum_fusion.1
  8.8 4.1 %collective-permute-start.4 = (bf16[32,640]{1,0:T(8,128)(2,1)S(1)}, bf16[32,640]{1,0:T(8,128)(2,1)S(1)}, u32[]{:S(2)}, u32[]{:S(2)}) collective-permute-start(bf16[32,640]{1,0:T(8,128)(2,1)S(1)} %pad_maximum_fusion.1), channel_id=1, source_target_pairs={{0,12},{4,8},{8,4},{12,0},{1,13},{5,9},{9,5},{13,1},{2,14},{6,10},... | collective-permute-start | bytes 122888 | tf_op jit(solution)/shard_map/ppermute | solution.py:10
  13.0 0.6 %collective-permute-start.2 = (bf16[32,640]{1,0:T(8,128)(2,1)S(1)}, bf16[32,640]{1,0:T(8,128)(2,1)S(1)}, u32[]{:S(2)}, u32[]{:S(2)}) collective-permute-start(bf16[32,640]{1,0:T(8,128)(2,1)S(1)} %pad_maximum_fusion.1), channel_id=1, source_target_pairs={{0,4},{4,0},{8,12},{12,8},{1,5},{5,1},{9,13},{13,9},{2,6},{6,2},{1... | collective-permute-start | bytes 122888 | tf_op jit(solution)/shard_map/ppermute | solution.py:10
  13.6 1.6 %collective-permute-done.4 = bf16[32,640]{1,0:T(8,128)(2,1)S(1)} collective-permute-done((bf16[32,640]{1,0:T(8,128)(2,1)S(1)}, bf16[32,640]{1,0:T(8,128)(2,1)S(1)}, u32[]{:S(2)}, u32[]{:S(2)}) %collective-permute-start.4) | collective-permute-done | bytes 40992 | tf_op jit(solution)/shard_map/ppermute | solution.py:10
  15.2 2.7 %collective-permute-done.3 = bf16[32,640]{1,0:T(8,128)(2,1)S(1)} collective-permute-done((bf16[32,640]{1,0:T(8,128)(2,1)S(1)}, bf16[32,640]{1,0:T(8,128)(2,1)S(1)}, u32[]{:S(2)}, u32[]{:S(2)}) %collective-permute-start.3) | collective-permute-done | bytes 40992 | tf_op jit(solution)/shard_map/ppermute | solution.py:10
  17.9 0.1 pad_maximum_fusion
  18.0 0.1 collective-permute-start.5
  18.0 0.1 maximum_convert_fusion
  18.1 0.1 fusion.21
  18.2 0.1 fusion.10
  18.4 1.0 %collective-permute-done.5 = bf16[128,512]{1,0:T(8,128)(2,1)S(1)} collective-permute-done((bf16[128,512]{1,0:T(8,128)(2,1)S(1)}, bf16[128,512]{1,0:T(8,128)(2,1)S(1)}, u32[]{:S(2)}, u32[]{:S(2)}) %collective-permute-start.5) | collective-permute-done | bytes 131104 | tf_op jit(solution)/shard_map/ppermute | solution.py:10
  19.4 3.7 %convolution_bitcast_fusion = f32[128,1024]{1,0:T(8,128)S(1)} fusion(bf16[2,672,1024]{2,1,0:T(8,128)(2,1)S(1)} %copy-done, bf16[2,672,1024]{2,1,0:T(8,128)(2,1)} %param.10, f32[2,128]{1,0:T(2,128)S(1)} %copy.16, bf16[128,512]{1,0:T(8,128)(2,1)S(1)} %get-tuple-element.8, bf16[128,512]{1,0:T(8,128)(2,1)S(1)} %get-tuple-element.7), kind=kOutput, calls=%fused_computation.4 | convolution fusion | flops 705855488 | bytes 6292480 | tf_op jit(solution)/shard_map/kth,khl->tl/dot_general | solution.py:65
  23.2 0.2 collective-permute-start.6
  23.4 1.2 %collective-permute-done.6 = bf16[128,512]{1,0:T(8,128)(2,1)S(1)} collective-permute-done((bf16[128,512]{1,0:T(8,128)(2,1)S(1)}, bf16[128,512]{1,0:T(8,128)(2,1)S(1)}, u32[]{:S(2)}, u32[]{:S(2)}) %collective-permute-start.6) | collective-permute-done | bytes 131104 | tf_op jit(solution)/shard_map/ppermute | solution.py:10
  24.7 0.1 collective-permute-start.7
  24.8 3.5 %collective-permute-start.9 = (bf16[32,512]{1,0:T(8,128)(2,1)S(1)}, bf16[32,512]{1,0:T(8,128)(2,1)S(1)}, u32[]{:S(2)}, u32[]{:S(2)}) collective-permute-start(bf16[32,512]{1,0:T(8,128)(2,1)S(1)} %get-tuple-element.10), channel_id=1, source_target_pairs={{0,12},{4,8},{8,4},{12,0},{1,13},{5,9},{9,5},{13,1},{2,14},{6,10},... | collective-permute-start | bytes 98312 | tf_op jit(solution)/shard_map/ppermute | solution.py:10
  28.2 0.4 %collective-permute-done.7 = bf16[32,512]{1,0:T(8,128)(2,1)S(1)} collective-permute-done((bf16[32,512]{1,0:T(8,128)(2,1)S(1)}, bf16[32,512]{1,0:T(8,128)(2,1)S(1)}, u32[]{:S(2)}, u32[]{:S(2)}) %collective-permute-start.7) | collective-permute-done | bytes 32800 | tf_op jit(solution)/shard_map/ppermute | solution.py:10
  28.7 2.2 %collective-permute-done.9 = bf16[32,512]{1,0:T(8,128)(2,1)S(1)} collective-permute-done((bf16[32,512]{1,0:T(8,128)(2,1)S(1)}, bf16[32,512]{1,0:T(8,128)(2,1)S(1)}, u32[]{:S(2)}, u32[]{:S(2)}) %collective-permute-start.9) | collective-permute-done | bytes 32800 | tf_op jit(solution)/shard_map/ppermute | solution.py:10
  30.9 2.2 %collective-permute-done.8 = bf16[32,512]{1,0:T(8,128)(2,1)S(1)} collective-permute-done((bf16[32,512]{1,0:T(8,128)(2,1)S(1)}, bf16[32,512]{1,0:T(8,128)(2,1)S(1)}, u32[]{:S(2)}, u32[]{:S(2)}) %collective-permute-start.8) | collective-permute-done | bytes 32800 | tf_op jit(solution)/shard_map/ppermute | solution.py:10
  33.1 1.6 %collective-permute-start.10 = (bf16[32,512]{1,0:T(8,128)(2,1)S(1)}, bf16[32,512]{1,0:T(8,128)(2,1)S(1)}, u32[]{:S(2)}, u32[]{:S(2)}) collective-permute-start(bf16[32,512]{1,0:T(8,128)(2,1)S(1)} %fusion.14), channel_id=1, source_target_pairs={{0,2},{1,3},{2,0},{3,1},{4,6},{5,7},{6,4},{7,5},{8,10},{9,11},{10,... | collective-permute-start | bytes 98312 | tf_op jit(solution)/shard_map/ppermute | solution.py:10
  34.6 2.4 %collective-permute-done.10 = bf16[32,512]{1,0:T(8,128)(2,1)S(1)} collective-permute-done((bf16[32,512]{1,0:T(8,128)(2,1)S(1)}, bf16[32,512]{1,0:T(8,128)(2,1)S(1)}, u32[]{:S(2)}, u32[]{:S(2)}) %collective-permute-start.10) | collective-permute-done | bytes 32800 | tf_op jit(solution)/shard_map/ppermute | solution.py:10
  37.1 0.1 collective-permute-start.11
  37.2 1.2 %collective-permute-done.11 = bf16[32,512]{1,0:T(8,128)(2,1)S(1)} collective-permute-done((bf16[32,512]{1,0:T(8,128)(2,1)S(1)}, bf16[32,512]{1,0:T(8,128)(2,1)S(1)}, u32[]{:S(2)}, u32[]{:S(2)}) %collective-permute-start.11) | collective-permute-done | bytes 32800 | tf_op jit(solution)/shard_map/ppermute | solution.py:10
  38.4 2.7 %convolution_convert_fusion = bf16[32,1024]{1,0:T(8,128)(2,1)} fusion(bf16[1024,1024]{1,0:T(8,128)(2,1)} %param.9, bf16[32,512]{1,0:T(8,128)(2,1)S(1)} %get-tuple-element.13, bf16[32,512]{1,0:T(8,128)(2,1)S(1)} %get-tuple-element.12), kind=kOutput, calls=%fused_computation.6 | convolution fusion | flops 67272704 | bytes 2228224 | tf_op jit(solution)/shard_map/dot_general | solution.py:75
  (19 shorter events, 0.3 us)
Async XLA Ops:
  0.0 19.4 %copy-start = (bf16[2,672,1024]{2,1,0:T(8,128)(2,1)S(1)}, bf16[2,672,1024]{2,1,0:T(8,128)(2,1)}, u32[]{:S(2)}) copy-start(bf16[2,672,1024]{2,1,0:T(8,128)(2,1)} %param.11) | copy-start | bytes 8257540
  2.5 1.4 %collective-permute-start = (bf16[32,512]{1,0:T(8,128)(2,1)S(1)}, bf16[32,512]{1,0:T(8,128)(2,1)S(1)}, u32[]{:S(2)}, u32[]{:S(2)}) collective-permute-start(bf16[32,512]{1,0:T(8,128)(2,1)S(1)} %select_convert_fusion.1), channel_id=1, source_target_pairs={{0,1},{1,0},{2,3},{3,2},{4,5},{5,4},{6,7},{7,6},{8,9},{9,8},{10,11... | collective-permute-start | bytes 98312 | tf_op jit(solution)/shard_map/ppermute | solution.py:10
  3.9 4.8 %collective-permute-start.1 = (bf16[32,512]{1,0:T(8,128)(2,1)S(1)}, bf16[32,512]{1,0:T(8,128)(2,1)S(1)}, u32[]{:S(2)}, u32[]{:S(2)}) collective-permute-start(bf16[32,512]{1,0:T(8,128)(2,1)S(1)} %fusion.15), channel_id=1, source_target_pairs={{0,2},{1,3},{2,0},{3,1},{4,6},{5,7},{6,4},{7,5},{8,10},{9,11},{10,... | collective-permute-start | bytes 98312 | tf_op jit(solution)/shard_map/ppermute | solution.py:10
  8.8 6.3 %collective-permute-start.4 = (bf16[32,640]{1,0:T(8,128)(2,1)S(1)}, bf16[32,640]{1,0:T(8,128)(2,1)S(1)}, u32[]{:S(2)}, u32[]{:S(2)}) collective-permute-start(bf16[32,640]{1,0:T(8,128)(2,1)S(1)} %pad_maximum_fusion.1), channel_id=1, source_target_pairs={{0,12},{4,8},{8,4},{12,0},{1,13},{5,9},{9,5},{13,1},{2,14},{6,10},... | collective-permute-start | bytes 122888 | tf_op jit(solution)/shard_map/ppermute | solution.py:10
  13.0 4.9 %collective-permute-start.3 = (bf16[32,640]{1,0:T(8,128)(2,1)S(1)}, bf16[32,640]{1,0:T(8,128)(2,1)S(1)}, u32[]{:S(2)}, u32[]{:S(2)}) collective-permute-start(bf16[32,640]{1,0:T(8,128)(2,1)S(1)} %pad_maximum_fusion.1), channel_id=1, source_target_pairs={{0,8},{4,12},{8,0},{12,4},{1,9},{5,13},{9,1},{13,5},{2,10},{6,14},... | collective-permute-start | bytes 122888 | tf_op jit(solution)/shard_map/ppermute | solution.py:10
  13.0 4.9 %collective-permute-start.2 = (bf16[32,640]{1,0:T(8,128)(2,1)S(1)}, bf16[32,640]{1,0:T(8,128)(2,1)S(1)}, u32[]{:S(2)}, u32[]{:S(2)}) collective-permute-start(bf16[32,640]{1,0:T(8,128)(2,1)S(1)} %pad_maximum_fusion.1), channel_id=1, source_target_pairs={{0,4},{4,0},{8,12},{12,8},{1,5},{5,1},{9,13},{13,9},{2,6},{6,2},{1... | collective-permute-start | bytes 122888 | tf_op jit(solution)/shard_map/ppermute | solution.py:10
  18.0 1.4 %collective-permute-start.5 = (bf16[128,512]{1,0:T(8,128)(2,1)S(1)}, bf16[128,512]{1,0:T(8,128)(2,1)S(1)}, u32[]{:S(2)}, u32[]{:S(2)}) collective-permute-start(bf16[128,512]{1,0:T(8,128)(2,1)S(1)} %slice.58), channel_id=1, source_target_pairs={{0,1},{1,0},{2,3},{3,2},{4,5},{5,4},{6,7},{7,6},{8,9},{9,8},{10,11... | collective-permute-start | bytes 393224 | tf_op jit(solution)/shard_map/ppermute | solution.py:10
  23.2 1.4 %collective-permute-start.6 = (bf16[128,512]{1,0:T(8,128)(2,1)S(1)}, bf16[128,512]{1,0:T(8,128)(2,1)S(1)}, u32[]{:S(2)}, u32[]{:S(2)}) collective-permute-start(bf16[128,512]{1,0:T(8,128)(2,1)S(1)} %select_convert_fusion), channel_id=1, source_target_pairs={{0,1},{1,0},{2,3},{3,2},{4,5},{5,4},{6,7},{7,6},{8,9},{9,8},{10,11... | collective-permute-start | bytes 393224 | tf_op jit(solution)/shard_map/ppermute | solution.py:10
  24.7 4.0 %collective-permute-start.7 = (bf16[32,512]{1,0:T(8,128)(2,1)S(1)}, bf16[32,512]{1,0:T(8,128)(2,1)S(1)}, u32[]{:S(2)}, u32[]{:S(2)}) collective-permute-start(bf16[32,512]{1,0:T(8,128)(2,1)S(1)} %get-tuple-element.9), channel_id=1, source_target_pairs={{0,4},{4,0},{8,12},{12,8},{1,5},{5,1},{9,13},{13,9},{2,6},{6,2},{1... | collective-permute-start | bytes 98312 | tf_op jit(solution)/shard_map/ppermute | solution.py:10
  24.8 6.1 %collective-permute-start.9 = (bf16[32,512]{1,0:T(8,128)(2,1)S(1)}, bf16[32,512]{1,0:T(8,128)(2,1)S(1)}, u32[]{:S(2)}, u32[]{:S(2)}) collective-permute-start(bf16[32,512]{1,0:T(8,128)(2,1)S(1)} %get-tuple-element.10), channel_id=1, source_target_pairs={{0,12},{4,8},{8,4},{12,0},{1,13},{5,9},{9,5},{13,1},{2,14},{6,10},... | collective-permute-start | bytes 98312 | tf_op jit(solution)/shard_map/ppermute | solution.py:10
  28.2 4.8 %collective-permute-start.8 = (bf16[32,512]{1,0:T(8,128)(2,1)S(1)}, bf16[32,512]{1,0:T(8,128)(2,1)S(1)}, u32[]{:S(2)}, u32[]{:S(2)}) collective-permute-start(bf16[32,512]{1,0:T(8,128)(2,1)S(1)} %get-tuple-element.11), channel_id=1, source_target_pairs={{0,8},{4,12},{8,0},{12,4},{1,9},{5,13},{9,1},{13,5},{2,10},{6,14},... | collective-permute-start | bytes 98312 | tf_op jit(solution)/shard_map/ppermute | solution.py:10
  33.1 4.0 %collective-permute-start.10 = (bf16[32,512]{1,0:T(8,128)(2,1)S(1)}, bf16[32,512]{1,0:T(8,128)(2,1)S(1)}, u32[]{:S(2)}, u32[]{:S(2)}) collective-permute-start(bf16[32,512]{1,0:T(8,128)(2,1)S(1)} %fusion.14), channel_id=1, source_target_pairs={{0,2},{1,3},{2,0},{3,1},{4,6},{5,7},{6,4},{7,5},{8,10},{9,11},{10,... | collective-permute-start | bytes 98312 | tf_op jit(solution)/shard_map/ppermute | solution.py:10
  37.1 1.3 %collective-permute-start.11 = (bf16[32,512]{1,0:T(8,128)(2,1)S(1)}, bf16[32,512]{1,0:T(8,128)(2,1)S(1)}, u32[]{:S(2)}, u32[]{:S(2)}) collective-permute-start(bf16[32,512]{1,0:T(8,128)(2,1)S(1)} %add_convert_fusion.1), channel_id=1, source_target_pairs={{0,1},{1,0},{2,3},{3,2},{4,5},{5,4},{6,7},{7,6},{8,9},{9,8},{10,11... | collective-permute-start | bytes 98312 | tf_op jit(solution)/shard_map/ppermute | solution.py:10

commit v4 on v3

v4 whole, which is shorter than its diff:
```python
import jax
import jax.numpy as jnp
from jax import lax
from jax.experimental import pallas as pl
from jax.experimental.pallas import tpu as pltpu
from jax.sharding import PartitionSpec as P

BF16, F32 = jnp.bfloat16, jnp.float32
NT = (((1,), (1,)), ((), ()))
VMEM_LIMIT = 24 << 20


def traded(x, axis, mask):
    return lax.ppermute(x, axis, [(i, i ^ mask) for i in range(lax.axis_size(axis))])


def summed(own, arrived):
    total = own.astype(F32)
    for block in arrived:
        total = total + block.astype(F32)
    return total


def in_vmem(x):
    return pltpu.with_memory_space_constraint(x, pltpu.VMEM)


def params():
    return pltpu.CompilerParams(vmem_limit_bytes=VMEM_LIMIT)


def kernel_call(body, out_shape, args, specs, scratch, flops, moved):
    vmem = pl.BlockSpec(memory_space=pltpu.VMEM)
    return pl.pallas_call(
        body,
        out_shape=out_shape,
        in_specs=[vmem if s is None else pl.BlockSpec(memory_space=s) for s in specs],
        out_specs=jax.tree.map(lambda _: vmem, out_shape),
        scratch_shapes=scratch,
        compiler_params=params(),
        cost_estimate=pl.CostEstimate(flops=flops, bytes_accessed=moved, transcendentals=0),
    )(*args)


CHUNKS = 2


def down_kernel(tokens_ref, weight_ref, theirs_ref, mine_ref, held, sems):
    odd = lax.axis_index("tp") % 2
    half = held.shape[0] // 2
    size = half // CHUNKS
    copies = []
    for i in range(2 * CHUNKS):
        side = (1 - odd) if i < CHUNKS else odd
        start = pl.multiple_of(side * half + i % CHUNKS * size, size)
        copy = pltpu.make_async_copy(
            weight_ref.at[pl.ds(start, size), :], held.at[pl.ds(i * size, size), :], sems.at[i]
        )
        copy.start()
        copies.append(copy)
    x = tokens_ref[...]
    for i in range(2 * CHUNKS):
        copies[i].wait()
        part = lax.dot_general(x, held[i * size : (i + 1) * size, :], NT, preferred_element_type=F32)
        at = i % CHUNKS * size
        if i < CHUNKS:
            theirs_ref[:, at : at + size] = part.astype(BF16)
        else:
            mine_ref[:, at : at + size] = part


def expert_kernel(messages_ref, other_ref, up_ref, down_ref, theirs_ref, mine_ref, latent, hidden):
    odd = lax.axis_index("tp") % 2
    local_count, units, latent_len = up_ref.shape
    half = latent_len // 2
    experts_all = local_count * lax.axis_size("exp")
    first = lax.axis_index("exp") * local_count
    own_at = pl.multiple_of(odd * half, half)
    other_at = pl.multiple_of((1 - odd) * half, half)
    latent[:, pl.ds(own_at, half)] = messages_ref[:, :half]
    latent[:, pl.ds(other_at, half)] = other_ref[...]
    terms = messages_ref[:, half:].astype(F32)
    lane = lax.broadcasted_iota(jnp.int32, terms.shape, 1)
    rows = latent[...]
    for k in range(local_count):
        named = (lane == first + k) | (lane == first + k + experts_all)
        weight = jnp.sum(jnp.where(named, terms, 0.0), axis=1, keepdims=True)
        pre_act = lax.dot_general(rows, up_ref[k], NT, preferred_element_type=F32)
        active = jnp.maximum(pre_act, 0.0)
        hidden[:, k * units : (k + 1) * units] = (active * active * weight).astype(BF16)
    acts = hidden[...]
    theirs_ref[...] = jnp.dot(
        acts, down_ref[:, pl.ds(other_at, half)], preferred_element_type=F32
    ).astype(BF16)
    mine_ref[...] = jnp.dot(acts, down_ref[:, pl.ds(own_at, half)], preferred_element_type=F32)


def up_kernel(mine_ref, other_ref, weight_ref, out_ref):
    odd = lax.axis_index("tp") % 2
    half = mine_ref.shape[1]
    own_at = pl.multiple_of(odd * half, half)
    other_at = pl.multiple_of((1 - odd) * half, half)
    total = jnp.dot(mine_ref[...], weight_ref[pl.ds(own_at, half), :], preferred_element_type=F32)
    total += jnp.dot(other_ref[...], weight_ref[pl.ds(other_at, half), :], preferred_element_type=F32)
    out_ref[...] = total.astype(BF16)


def on_device(tokens, lat_down, lat_up, expert_up, expert_down, routes, route_weights):
    exp_count, tp_count = lax.axis_size("exp"), lax.axis_size("tp")
    local_count, units, latent_len = expert_up.shape
    rows, width = tokens.shape
    half = latent_len // 2
    all_rows = exp_count * rows
    experts_all = local_count * exp_count
    pair_masks = [1 << b for b in range(1, tp_count.bit_length() - 1)]

    def pair_sum(x):
        for mask in pair_masks:
            x = summed(x, [traded(x.astype(BF16), "tp", mask)])
        return x

    named = routes[:, :, None] == jnp.arange(experts_all, dtype=jnp.int32)[None, None, :]
    combine = jnp.sum(jnp.where(named, route_weights[:, :, None], 0.0), axis=1)
    high = combine.astype(BF16)
    low = (combine - high.astype(F32)).astype(BF16)
    pad = jnp.zeros((rows, -2 * experts_all % 128), BF16)

    theirs, mine = kernel_call(
        down_kernel,
        (jax.ShapeDtypeStruct((rows, half), BF16), jax.ShapeDtypeStruct((rows, half), F32)),
        (tokens, lat_down),
        (None, pltpu.HBM),
        [pltpu.VMEM((latent_len, width), BF16), pltpu.SemaphoreType.DMA((2 * CHUNKS,))],
        2 * rows * width * latent_len,
        2 * width * latent_len,
    )
    latent_half = summed(mine, [traded(theirs, "tp", 1)])
    message = jnp.concatenate([pair_sum(latent_half).astype(BF16), high, low, pad], axis=1)
    messages = [message] + [traded(message, "exp", s) for s in range(1, exp_count)]
    messages = jnp.concatenate(messages, axis=0)
    theirs, mine = kernel_call(
        expert_kernel,
        (jax.ShapeDtypeStruct((all_rows, half), BF16), jax.ShapeDtypeStruct((all_rows, half), F32)),
        (
            messages,
            traded(messages[:, :half], "tp", 1),
            in_vmem(expert_up),
            in_vmem(expert_down.reshape(local_count * units, latent_len)),
        ),
        (None,) * 4,
        [
            pltpu.VMEM((all_rows, latent_len), BF16),
            pltpu.VMEM((all_rows, local_count * units), BF16),
        ],
        4 * all_rows * latent_len * local_count * units,
        4 * latent_len * local_count * units,
    )
    part_half = summed(mine, [traded(theirs, "tp", 1)]).astype(BF16)
    blocks = part_half.reshape(exp_count, rows, half)
    mixed_half = summed(blocks[0], [traded(blocks[s], "exp", s) for s in range(1, exp_count)])
    mixed_half = pair_sum(mixed_half).astype(BF16)
    return kernel_call(
        up_kernel,
        jax.ShapeDtypeStruct((rows, lat_up.shape[1]), BF16),
        (mixed_half, traded(mixed_half, "tp", 1), in_vmem(lat_up)),
        (None,) * 3,
        [],
        2 * rows * latent_len * lat_up.shape[1],
        2 * latent_len * lat_up.shape[1],
    )


def solution(mesh):
    return jax.shard_map(
        on_device,
        mesh=mesh,
        in_specs=(
            P(("grp", "exp"), "tp"),
            P(None, "tp"),
            P(None, "tp"),
            P("exp", "tp", None),
            P("exp", "tp", None),
            P(("grp", "exp"), None),
            P(("grp", "exp"), None),
        ),
        out_specs=P(("grp", "exp"), "tp"),
        check_vma=False,
    )
```

time: 41.3 us -> 40.9 us (level)
  matrix products: 8.93 us -> 0 us
  Pallas kernels: 0 us -> 4.32 us
  local copies, waits for them, and re-layouts: 0.35 us -> 4.55 us
    dot_general x3 -> x0, matrix products: 8.93 us -> none  [the longest x1 3.74 us: on_device(): jnp.einsum('kth,khl->tl', hidden.astype(BF16), expert_down, preferred_ele...]
    unnamed x2 -> x10, local copies, waits for them, and re-layouts: 0.01 us -> 4.36 us
    pallas_call x0 -> x3, Pallas kernels: none -> 4.32 us  [kernel_call(): pl.pallas_call(body, out_shape=out_shape, in_specs=[vmem if s is None els...]
  transfers between devices with their start and end apart: 12 -> 12, of which waited for: 11 -> 10; matrix products, arithmetic and copies ran while one was open for 3% -> 2% of each run, Pallas kernels for 0% -> 0%
where the time goes in v4:
time: 40.9 us; the launch traced here: 40.7 us
  waiting for transfers between devices  17.1 us (42%)
  starting transfers between devices  13.6 us (33%)
  local copies, waits for them, and re-layouts  4.55 us (11%)
  Pallas kernels  4.32 us (11%)
  other arithmetic  0.98 us (2%)
    ppermute x12, waiting for transfers between devices, traded(): lax.ppermute(x, axis, [(i, i ^ mask) for i in range(lax.axis_size(axis))])  17.1 us
    ppermute x12, starting transfers between devices, traded(): lax.ppermute(x, axis, [(i, i ^ mask) for i in range(lax.axis_size(axis))])  13.6 us
    unnamed x10, local copies, waits for them, and re-layouts  4.36 us
    pallas_call x3, Pallas kernels, kernel_call(): pl.pallas_call(body, out_shape=out_shape, in_specs=[vmem if s is None els...  4.32 us
  transfers between devices with their start and end apart: 12, of which 10 were waited for; matrix products, arithmetic and copies ran while one was open for 2% of the time, Pallas kernels for 0%

profile of v4, /device:TPU:0, one launch (start us, length us, event | category | flops | bytes accessed | tf_op | source)
XLA Modules:
  0.0 40.7 jit_solution(16564841424430592508)
XLA Ops:
  0.0 1.7 %copy-done.2 = bf16[1024,1024]{1,0:T(8,128)(2,1)S(1)} copy-done((bf16[1024,1024]{1,0:T(8,128)(2,1)S(1)}, bf16[1024,1024]{1,0:T(8,128)(2,1)}, u32[]{:S(2)}) %copy-start.2) | copy-done | bytes 2097176
  1.7 0.8 %copy-done.4 = bf16[32,1024]{1,0:T(8,128)(2,1)S(1)} copy-done((bf16[32,1024]{1,0:T(8,128)(2,1)S(1)}, bf16[32,1024]{1,0:T(8,128)(2,1)}, u32[]{:S(2)}) %copy-start.4) | copy-done | bytes 65560
  2.6 1.8 %shard_map.73 = (bf16[32,512]{1,0:T(8,128)(2,1)S(1)}, f32[32,512]{1,0:T(8,128)S(1)}) custom-call(bf16[32,1024]{1,0:T(8,128)(2,1)S(1)} %copy-done.4, bf16[1024,1024]{1,0:T(8,128)(2,1)S(1)} %copy-done.2), custom_call_target="tpu_custom_call" | custom-call | flops 67108864 | bytes 2097152 | tf_op jit(solution)/shard_map/pallas_call | solution.py:34
  4.3 0.5 %collective-permute-start = (bf16[32,512]{1,0:T(8,128)(2,1)S(1)}, bf16[32,512]{1,0:T(8,128)(2,1)S(1)}, u32[]{:S(2)}, u32[]{:S(2)}) collective-permute-start(bf16[32,512]{1,0:T(8,128)(2,1)S(1)} %get-tuple-element.10), channel_id=1, source_target_pairs={{0,1},{1,0},{2,3},{3,2},{4,5},{5,4},{6,7},{7,6},{8,9},{9,8},{10,11... | collective-permute-start | bytes 98312 | tf_op jit(solution)/shard_map/ppermute | solution.py:14
  4.9 0.7 %select_reduce_fusion = f32[32,8]{0,1:T(8,128)S(1)} fusion(f32[32,4]{0,1:T(4,128)} %param.13, s32[32,4]{0,1:T(4,128)} %param.12), kind=kLoop, calls=%fused_computation.10 | loop fusion | flops 2816 | bytes 2048 | tf_op jit(solution)/shard_map/reduce_sum | solution.py:123
  5.6 0.1 copy.13
  5.7 0.1 copy.14
  5.8 2.9 %collective-permute-start.1 = (bf16[32,512]{1,0:T(8,128)(2,1)S(1)}, bf16[32,512]{1,0:T(8,128)(2,1)S(1)}, u32[]{:S(2)}, u32[]{:S(2)}) collective-permute-start(bf16[32,512]{1,0:T(8,128)(2,1)S(1)} %fusion), channel_id=1, source_target_pairs={{0,2},{1,3},{2,0},{3,1},{4,6},{5,7},{6,4},{7,5},{8,10},{9,11},{10,... | collective-permute-start | bytes 98312 | tf_op jit(solution)/shard_map/ppermute | solution.py:14
  8.6 1.9 %collective-permute-done.1 = bf16[32,512]{1,0:T(8,128)(2,1)S(1)} collective-permute-done((bf16[32,512]{1,0:T(8,128)(2,1)S(1)}, bf16[32,512]{1,0:T(8,128)(2,1)S(1)}, u32[]{:S(2)}, u32[]{:S(2)}) %collective-permute-start.1) | collective-permute-done | bytes 32800 | tf_op jit(solution)/shard_map/ppermute | solution.py:14
  10.6 0.1 pad_maximum_fusion.1
  10.6 4.1 %collective-permute-start.4 = (bf16[32,640]{1,0:T(8,128)(2,1)S(1)}, bf16[32,640]{1,0:T(8,128)(2,1)S(1)}, u32[]{:S(2)}, u32[]{:S(2)}) collective-permute-start(bf16[32,640]{1,0:T(8,128)(2,1)S(1)} %pad_maximum_fusion.1), channel_id=1, source_target_pairs={{0,12},{4,8},{8,4},{12,0},{1,13},{5,9},{9,5},{13,1},{2,14},{6,10},... | collective-permute-start | bytes 122888 | tf_op jit(solution)/shard_map/ppermute | solution.py:14
  14.8 0.6 %collective-permute-start.2 = (bf16[32,640]{1,0:T(8,128)(2,1)S(1)}, bf16[32,640]{1,0:T(8,128)(2,1)S(1)}, u32[]{:S(2)}, u32[]{:S(2)}) collective-permute-start(bf16[32,640]{1,0:T(8,128)(2,1)S(1)} %pad_maximum_fusion.1), channel_id=1, source_target_pairs={{0,4},{4,0},{8,12},{12,8},{1,5},{5,1},{9,13},{13,9},{2,6},{6,2},{1... | collective-permute-start | bytes 122888 | tf_op jit(solution)/shard_map/ppermute | solution.py:14
  15.4 1.6 %collective-permute-done.4 = bf16[32,640]{1,0:T(8,128)(2,1)S(1)} collective-permute-done((bf16[32,640]{1,0:T(8,128)(2,1)S(1)}, bf16[32,640]{1,0:T(8,128)(2,1)S(1)}, u32[]{:S(2)}, u32[]{:S(2)}) %collective-permute-start.4) | collective-permute-done | bytes 40992 | tf_op jit(solution)/shard_map/ppermute | solution.py:14
  17.0 2.7 %collective-permute-done.3 = bf16[32,640]{1,0:T(8,128)(2,1)S(1)} collective-permute-done((bf16[32,640]{1,0:T(8,128)(2,1)S(1)}, bf16[32,640]{1,0:T(8,128)(2,1)S(1)}, u32[]{:S(2)}, u32[]{:S(2)}) %collective-permute-start.3) | collective-permute-done | bytes 40992 | tf_op jit(solution)/shard_map/ppermute | solution.py:14
  19.7 0.1 pad_maximum_fusion.messages_ref
  19.8 0.1 collective-permute-start.5
  19.9 1.3 %collective-permute-done.5.other_ref = bf16[128,512]{1,0:T(8,128)(2,1)S(1)} collective-permute-done((bf16[128,512]{1,0:T(8,128)(2,1)S(1)}, bf16[128,512]{1,0:T(8,128)(2,1)S(1)}, u32[]{:S(2)}, u32[]{:S(2)}) %collective-permute-start.5) | collective-permute-done | bytes 131104 | tf_op jit(solution)/shard_map/ppermute | solution.py:14
  21.2 1.8 %copy-done.1 = bf16[2,672,1024]{2,1,0:T(8,128)(2,1)S(1)} copy-done((bf16[2,672,1024]{2,1,0:T(8,128)(2,1)S(1)}, bf16[2,672,1024]{2,1,0:T(8,128)(2,1)}, u32[]{:S(2)}) %copy-start.1) | copy-done | bytes 2752536
  23.0 1.5 %shard_map.74 = (bf16[128,512]{1,0:T(8,128)(2,1)S(1)}, f32[128,512]{1,0:T(8,128)S(1)}) custom-call(bf16[128,640]{1,0:T(8,128)(2,1)S(1)} %pad_maximum_fusion.messages_ref, bf16[128,512]{1,0:T(8,128)(2,1)S(1)} %collective-permute-done.5.other_ref, bf16[2,672,1024]{2,1,0:T(8,128)(2,1)S(1)} %copy-done, bf16[1344,1024]{1,0:T(8,128)(2,1)S(1)} %bitcast.1), custom_call_target="tpu_custom_call" | custom-call | flops 704643072 | bytes 5505024 | tf_op jit(solution)/shard_map/pallas_call | solution.py:34
  24.5 0.2 collective-permute-start.6
  24.7 1.2 %collective-permute-done.6 = bf16[128,512]{1,0:T(8,128)(2,1)S(1)} collective-permute-done((bf16[128,512]{1,0:T(8,128)(2,1)S(1)}, bf16[128,512]{1,0:T(8,128)(2,1)S(1)}, u32[]{:S(2)}, u32[]{:S(2)}) %collective-permute-start.6) | collective-permute-done | bytes 131104 | tf_op jit(solution)/shard_map/ppermute | solution.py:14
  25.9 0.1 collective-permute-start.7
  26.0 3.5 %collective-permute-start.9 = (bf16[32,512]{1,0:T(8,128)(2,1)S(1)}, bf16[32,512]{1,0:T(8,128)(2,1)S(1)}, u32[]{:S(2)}, u32[]{:S(2)}) collective-permute-start(bf16[32,512]{1,0:T(8,128)(2,1)S(1)} %get-tuple-element.14), channel_id=1, source_target_pairs={{0,12},{4,8},{8,4},{12,0},{1,13},{5,9},{9,5},{13,1},{2,14},{6,10},... | collective-permute-start | bytes 98312 | tf_op jit(solution)/shard_map/ppermute | solution.py:14
  29.5 0.0 collective-permute-start.8
  29.5 0.4 %collective-permute-done.7 = bf16[32,512]{1,0:T(8,128)(2,1)S(1)} collective-permute-done((bf16[32,512]{1,0:T(8,128)(2,1)S(1)}, bf16[32,512]{1,0:T(8,128)(2,1)S(1)}, u32[]{:S(2)}, u32[]{:S(2)}) %collective-permute-start.7) | collective-permute-done | bytes 32800 | tf_op jit(solution)/shard_map/ppermute | solution.py:14
  29.9 2.2 %collective-permute-done.9 = bf16[32,512]{1,0:T(8,128)(2,1)S(1)} collective-permute-done((bf16[32,512]{1,0:T(8,128)(2,1)S(1)}, bf16[32,512]{1,0:T(8,128)(2,1)S(1)}, u32[]{:S(2)}, u32[]{:S(2)}) %collective-permute-start.9) | collective-permute-done | bytes 32800 | tf_op jit(solution)/shard_map/ppermute | solution.py:14
  32.1 2.2 %collective-permute-done.8 = bf16[32,512]{1,0:T(8,128)(2,1)S(1)} collective-permute-done((bf16[32,512]{1,0:T(8,128)(2,1)S(1)}, bf16[32,512]{1,0:T(8,128)(2,1)S(1)}, u32[]{:S(2)}, u32[]{:S(2)}) %collective-permute-start.8) | collective-permute-done | bytes 32800 | tf_op jit(solution)/shard_map/ppermute | solution.py:14
  34.3 1.6 %collective-permute-start.10 = (bf16[32,512]{1,0:T(8,128)(2,1)S(1)}, bf16[32,512]{1,0:T(8,128)(2,1)S(1)}, u32[]{:S(2)}, u32[]{:S(2)}) collective-permute-start(bf16[32,512]{1,0:T(8,128)(2,1)S(1)} %fusion.1), channel_id=1, source_target_pairs={{0,2},{1,3},{2,0},{3,1},{4,6},{5,7},{6,4},{7,5},{8,10},{9,11},{10,... | collective-permute-start | bytes 98312 | tf_op jit(solution)/shard_map/ppermute | solution.py:14
  35.9 2.4 %collective-permute-done.10 = bf16[32,512]{1,0:T(8,128)(2,1)S(1)} collective-permute-done((bf16[32,512]{1,0:T(8,128)(2,1)S(1)}, bf16[32,512]{1,0:T(8,128)(2,1)S(1)}, u32[]{:S(2)}, u32[]{:S(2)}) %collective-permute-start.10) | collective-permute-done | bytes 32800 | tf_op jit(solution)/shard_map/ppermute | solution.py:14
  38.3 0.1 collective-permute-start.11
  38.4 1.2 %collective-permute-done.11.other_ref = bf16[32,512]{1,0:T(8,128)(2,1)S(1)} collective-permute-done((bf16[32,512]{1,0:T(8,128)(2,1)S(1)}, bf16[32,512]{1,0:T(8,128)(2,1)S(1)}, u32[]{:S(2)}, u32[]{:S(2)}) %collective-permute-start.11) | collective-permute-done | bytes 32800 | tf_op jit(solution)/shard_map/ppermute | solution.py:14
  39.6 1.1 %shard_map.75 = bf16[32,1024]{1,0:T(8,128)(2,1)} custom-call(bf16[32,512]{1,0:T(8,128)(2,1)S(1)} %add_convert_fusion.1.mine_ref, bf16[32,512]{1,0:T(8,128)(2,1)S(1)} %collective-permute-done.11.other_ref, bf16[1024,1024]{1,0:T(8,128)(2,1)S(1)} %copy-done.3), custom_call_target="tpu_custom_call" | custom-call | flops 67108864 | bytes 2097152 | tf_op jit(solution)/shard_map/pallas_call | solution.py:34
  (20 shorter events, 0.2 us)
Async XLA Ops:
  0.0 21.2 %copy-start = (bf16[2,672,1024]{2,1,0:T(8,128)(2,1)S(1)}, bf16[2,672,1024]{2,1,0:T(8,128)(2,1)}, u32[]{:S(2)}) copy-start(bf16[2,672,1024]{2,1,0:T(8,128)(2,1)} %up_ref.1) | copy-start | bytes 8257540
  0.0 1.7 %copy-start.2 = (bf16[1024,1024]{1,0:T(8,128)(2,1)S(1)}, bf16[1024,1024]{1,0:T(8,128)(2,1)}, u32[]{:S(2)}) copy-start(bf16[1024,1024]{1,0:T(8,128)(2,1)} %weight_ref.2) | copy-start | bytes 6291460
  1.7 0.8 %copy-start.4 = (bf16[32,1024]{1,0:T(8,128)(2,1)S(1)}, bf16[32,1024]{1,0:T(8,128)(2,1)}, u32[]{:S(2)}) copy-start(bf16[32,1024]{1,0:T(8,128)(2,1)} %tokens_ref.1) | copy-start | bytes 196612
  4.3 1.4 %collective-permute-start = (bf16[32,512]{1,0:T(8,128)(2,1)S(1)}, bf16[32,512]{1,0:T(8,128)(2,1)S(1)}, u32[]{:S(2)}, u32[]{:S(2)}) collective-permute-start(bf16[32,512]{1,0:T(8,128)(2,1)S(1)} %get-tuple-element.10), channel_id=1, source_target_pairs={{0,1},{1,0},{2,3},{3,2},{4,5},{5,4},{6,7},{7,6},{8,9},{9,8},{10,11... | collective-permute-start | bytes 98312 | tf_op jit(solution)/shard_map/ppermute | solution.py:14
  5.8 4.8 %collective-permute-start.1 = (bf16[32,512]{1,0:T(8,128)(2,1)S(1)}, bf16[32,512]{1,0:T(8,128)(2,1)S(1)}, u32[]{:S(2)}, u32[]{:S(2)}) collective-permute-start(bf16[32,512]{1,0:T(8,128)(2,1)S(1)} %fusion), channel_id=1, source_target_pairs={{0,2},{1,3},{2,0},{3,1},{4,6},{5,7},{6,4},{7,5},{8,10},{9,11},{10,... | collective-permute-start | bytes 98312 | tf_op jit(solution)/shard_map/ppermute | solution.py:14
  10.6 6.4 %collective-permute-start.4 = (bf16[32,640]{1,0:T(8,128)(2,1)S(1)}, bf16[32,640]{1,0:T(8,128)(2,1)S(1)}, u32[]{:S(2)}, u32[]{:S(2)}) collective-permute-start(bf16[32,640]{1,0:T(8,128)(2,1)S(1)} %pad_maximum_fusion.1), channel_id=1, source_target_pairs={{0,12},{4,8},{8,4},{12,0},{1,13},{5,9},{9,5},{13,1},{2,14},{6,10},... | collective-permute-start | bytes 122888 | tf_op jit(solution)/shard_map/ppermute | solution.py:14
  14.8 4.9 %collective-permute-start.3 = (bf16[32,640]{1,0:T(8,128)(2,1)S(1)}, bf16[32,640]{1,0:T(8,128)(2,1)S(1)}, u32[]{:S(2)}, u32[]{:S(2)}) collective-permute-start(bf16[32,640]{1,0:T(8,128)(2,1)S(1)} %pad_maximum_fusion.1), channel_id=1, source_target_pairs={{0,8},{4,12},{8,0},{12,4},{1,9},{5,13},{9,1},{13,5},{2,10},{6,14},... | collective-permute-start | bytes 122888 | tf_op jit(solution)/shard_map/ppermute | solution.py:14
  14.8 4.9 %collective-permute-start.2 = (bf16[32,640]{1,0:T(8,128)(2,1)S(1)}, bf16[32,640]{1,0:T(8,128)(2,1)S(1)}, u32[]{:S(2)}, u32[]{:S(2)}) collective-permute-start(bf16[32,640]{1,0:T(8,128)(2,1)S(1)} %pad_maximum_fusion.1), channel_id=1, source_target_pairs={{0,4},{4,0},{8,12},{12,8},{1,5},{5,1},{9,13},{13,9},{2,6},{6,2},{1... | collective-permute-start | bytes 122888 | tf_op jit(solution)/shard_map/ppermute | solution.py:14
  19.8 1.4 %collective-permute-start.5 = (bf16[128,512]{1,0:T(8,128)(2,1)S(1)}, bf16[128,512]{1,0:T(8,128)(2,1)S(1)}, u32[]{:S(2)}, u32[]{:S(2)}) collective-permute-start(bf16[128,512]{1,0:T(8,128)(2,1)S(1)} %slice.24), channel_id=1, source_target_pairs={{0,1},{1,0},{2,3},{3,2},{4,5},{5,4},{6,7},{7,6},{8,9},{9,8},{10,11... | collective-permute-start | bytes 393224 | tf_op jit(solution)/shard_map/ppermute | solution.py:14
  21.2 1.8 %copy-start.1 = (bf16[2,672,1024]{2,1,0:T(8,128)(2,1)S(1)}, bf16[2,672,1024]{2,1,0:T(8,128)(2,1)}, u32[]{:S(2)}) copy-start(bf16[2,672,1024]{2,1,0:T(8,128)(2,1)} %param.11) | copy-start | bytes 8257540
  23.0 16.6 %copy-start.3 = (bf16[1024,1024]{1,0:T(8,128)(2,1)S(1)}, bf16[1024,1024]{1,0:T(8,128)(2,1)}, u32[]{:S(2)}) copy-start(bf16[1024,1024]{1,0:T(8,128)(2,1)} %weight_ref.3) | copy-start | bytes 6291460
  24.5 1.4 %collective-permute-start.6 = (bf16[128,512]{1,0:T(8,128)(2,1)S(1)}, bf16[128,512]{1,0:T(8,128)(2,1)S(1)}, u32[]{:S(2)}, u32[]{:S(2)}) collective-permute-start(bf16[128,512]{1,0:T(8,128)(2,1)S(1)} %get-tuple-element.12), channel_id=1, source_target_pairs={{0,1},{1,0},{2,3},{3,2},{4,5},{5,4},{6,7},{7,6},{8,9},{9,8},{10,11... | collective-permute-start | bytes 393224 | tf_op jit(solution)/shard_map/ppermute | solution.py:14
  25.9 4.0 %collective-permute-start.7 = (bf16[32,512]{1,0:T(8,128)(2,1)S(1)}, bf16[32,512]{1,0:T(8,128)(2,1)S(1)}, u32[]{:S(2)}, u32[]{:S(2)}) collective-permute-start(bf16[32,512]{1,0:T(8,128)(2,1)S(1)} %get-tuple-element.13), channel_id=1, source_target_pairs={{0,4},{4,0},{8,12},{12,8},{1,5},{5,1},{9,13},{13,9},{2,6},{6,2},{1... | collective-permute-start | bytes 98312 | tf_op jit(solution)/shard_map/ppermute | solution.py:14
  26.0 6.1 %collective-permute-start.9 = (bf16[32,512]{1,0:T(8,128)(2,1)S(1)}, bf16[32,512]{1,0:T(8,128)(2,1)S(1)}, u32[]{:S(2)}, u32[]{:S(2)}) collective-permute-start(bf16[32,512]{1,0:T(8,128)(2,1)S(1)} %get-tuple-element.14), channel_id=1, source_target_pairs={{0,12},{4,8},{8,4},{12,0},{1,13},{5,9},{9,5},{13,1},{2,14},{6,10},... | collective-permute-start | bytes 98312 | tf_op jit(solution)/shard_map/ppermute | solution.py:14
  29.5 4.8 %collective-permute-start.8 = (bf16[32,512]{1,0:T(8,128)(2,1)S(1)}, bf16[32,512]{1,0:T(8,128)(2,1)S(1)}, u32[]{:S(2)}, u32[]{:S(2)}) collective-permute-start(bf16[32,512]{1,0:T(8,128)(2,1)S(1)} %get-tuple-element.15), channel_id=1, source_target_pairs={{0,8},{4,12},{8,0},{12,4},{1,9},{5,13},{9,1},{13,5},{2,10},{6,14},... | collective-permute-start | bytes 98312 | tf_op jit(solution)/shard_map/ppermute | solution.py:14
  34.3 4.0 %collective-permute-start.10 = (bf16[32,512]{1,0:T(8,128)(2,1)S(1)}, bf16[32,512]{1,0:T(8,128)(2,1)S(1)}, u32[]{:S(2)}, u32[]{:S(2)}) collective-permute-start(bf16[32,512]{1,0:T(8,128)(2,1)S(1)} %fusion.1), channel_id=1, source_target_pairs={{0,2},{1,3},{2,0},{3,1},{4,6},{5,7},{6,4},{7,5},{8,10},{9,11},{10,... | collective-permute-start | bytes 98312 | tf_op jit(solution)/shard_map/ppermute | solution.py:14
  38.3 1.3 %collective-permute-start.11 = (bf16[32,512]{1,0:T(8,128)(2,1)S(1)}, bf16[32,512]{1,0:T(8,128)(2,1)S(1)}, u32[]{:S(2)}, u32[]{:S(2)}) collective-permute-start(bf16[32,512]{1,0:T(8,128)(2,1)S(1)} %add_convert_fusion.1.mine_ref), channel_id=1, source_target_pairs={{0,1},{1,0},{2,3},{3,2},{4,5},{5,4},{6,7},{7,6},{8,9},{9,8},{10,11... | collective-permute-start | bytes 98312 | tf_op jit(solution)/shard_map/ppermute | solution.py:14

commit v5 on v2

v5 whole, which is shorter than its diff:
```python
import jax
import jax.numpy as jnp
from jax import lax
from jax.experimental import pallas as pl
from jax.experimental.pallas import tpu as pltpu
from jax.sharding import PartitionSpec as P

BF16, F32 = jnp.bfloat16, jnp.float32
NT = (((1,), (1,)), ((), ()))
VMEM_LIMIT = 24 << 20
LANES = 128
CHUNKS = 4


def in_space(x, space):
    return pltpu.with_memory_space_constraint(x, space)


def kernel_call(body, out_shape, args, specs, scratch, flops, moved):
    vmem = pl.BlockSpec(memory_space=pltpu.VMEM)
    return pl.pallas_call(
        body,
        out_shape=out_shape,
        in_specs=[vmem if s is None else pl.BlockSpec(memory_space=s) for s in specs],
        out_specs=jax.tree.map(lambda _: vmem, out_shape),
        scratch_shapes=scratch,
        compiler_params=pltpu.CompilerParams(vmem_limit_bytes=VMEM_LIMIT),
        cost_estimate=pl.CostEstimate(flops=flops, bytes_accessed=moved, transcendentals=0),
    )(*args)


def down_kernel(
    tokens_hbm, weight_hbm, routes_hbm, scale_hbm, send_ref, keep_ref, terms_ref,
    tokens, weight, routes, scale, sems,
):
    size = weight.shape[0] // CHUNKS
    small = [(tokens_hbm, tokens), (routes_hbm, routes), (scale_hbm, scale)]
    small = [pltpu.make_async_copy(a, b, sems.at[i]) for i, (a, b) in enumerate(small)]
    small[0].start()
    chunks = []
    for i in range(CHUNKS):
        at = pl.ds(i * size, size)
        chunks.append(pltpu.make_async_copy(weight_hbm.at[at, :], weight.at[at, :], sems.at[3 + i]))
        chunks[i].start()
        if i == 0:
            small[1].start()
            small[2].start()
    small[1].wait()
    small[2].wait()
    rows = tokens.shape[0]
    width = terms_ref.shape[1]
    row = lax.broadcasted_iota(jnp.int32, (width, rows), 0)
    experts_all = width // 2
    expert = jnp.where(row < experts_all, row, row - experts_all)
    combine = jnp.zeros((width, rows), F32)
    for r in range(routes.shape[0]):
        combine += jnp.where(expert == routes[r : r + 1, :], scale[r : r + 1, :], 0.0)
    high = combine.astype(BF16).astype(F32)
    combine = jnp.where(row < experts_all, high, combine - high)
    combine = jnp.concatenate([combine, jnp.zeros((width, LANES - rows), F32)], axis=1)
    terms_ref[...] = combine.T[:rows, :].astype(BF16)
    small[0].wait()
    x = tokens[...]
    for i in range(CHUNKS):
        chunks[i].wait()
        part = lax.dot_general(x, weight[i * size : (i + 1) * size, :], NT, preferred_element_type=F32)
        send_ref[:, i * size : (i + 1) * size] = part.astype(BF16)
        keep_ref[:, i * size : (i + 1) * size] = part


def load_kernel(after_ref, up_hbm, down_hbm, up_ref, down_ref, sems):
    copies = [
        pltpu.make_async_copy(up_hbm, up_ref, sems.at[0]),
        pltpu.make_async_copy(down_hbm, down_ref, sems.at[1]),
    ]
    for copy in copies:
        copy.start()
    for copy in copies:
        copy.wait()


def expert_kernel(own_ref, other_ref, up_ref, down_ref, theirs_ref, mine_ref, latent, terms, hidden):
    local_count, units, latent_len = up_ref.shape
    side = own_ref.shape[0]
    experts_all = terms.shape[1] // 2
    first = lax.axis_index("exp") * local_count
    for at, ref in ((0, own_ref), (side, other_ref)):
        latent[at : at + side, :] = ref[:, :latent_len]
        terms[at : at + side, :] = ref[:, latent_len:].astype(F32)
    rows = latent[...]
    lane = lax.broadcasted_iota(jnp.int32, terms.shape, 1)
    for k in range(local_count):
        named = (lane == first + k) | (lane == first + k + experts_all)
        weight = jnp.sum(jnp.where(named, terms[...], 0.0), axis=1, keepdims=True)
        pre_act = lax.dot_general(rows, up_ref[k], NT, preferred_element_type=F32)
        active = jnp.maximum(pre_act, 0.0)
        hidden[:, k * units : (k + 1) * units] = (active * active * weight).astype(BF16)
    result = jnp.dot(hidden[...], down_ref[...], preferred_element_type=F32)
    mine_ref[...] = result[:side, :]
    theirs_ref[...] = result[side:, :].astype(BF16)


def up_kernel(keep_ref, other_ref, weight_ref, out_ref):
    mixed = (keep_ref[...] + other_ref[...].astype(F32)).astype(BF16)
    out_ref[...] = jnp.dot(mixed, weight_ref[...], preferred_element_type=F32).astype(BF16)


def on_device(tokens, lat_down, lat_up, expert_up, expert_down, routes, route_weights):
    exp_count, tp_count = lax.axis_size("exp"), lax.axis_size("tp")
    pairs = tp_count // 2
    local_count, units, latent_len = expert_up.shape
    rows, width = tokens.shape
    side_rows = exp_count // 2 * rows
    terms_len = -(-2 * local_count * exp_count // LANES) * LANES

    def from_pair(x):
        return lax.ppermute(x, "tp", [(t, t ^ 1) for t in range(tp_count)])

    def sent(x, step, over):
        def peer(e, t):
            return (e ^ (exp_count - 2 - 2 * step + 1 - t % 2)) * tp_count + (t ^ (2 * over))

        whole = [(e, t) for e in range(exp_count) for t in range(tp_count)]
        return lax.ppermute(x, ("exp", "tp"), [(e * tp_count + t, peer(e, t)) for e, t in whole])

    send, keep, terms = kernel_call(
        down_kernel,
        (
            jax.ShapeDtypeStruct((rows, latent_len), BF16),
            jax.ShapeDtypeStruct((rows, latent_len), F32),
            jax.ShapeDtypeStruct((rows, terms_len), BF16),
        ),
        [in_space(x, pltpu.HBM) for x in (tokens, lat_down, routes.T, route_weights.T)],
        (pltpu.HBM,) * 4,
        [
            pltpu.VMEM((rows, width), BF16),
            pltpu.VMEM((latent_len, width), BF16),
            pltpu.VMEM((routes.shape[1], rows), jnp.int32),
            pltpu.VMEM((routes.shape[1], rows), F32),
            pltpu.SemaphoreType.DMA((3 + CHUNKS,)),
        ],
        2 * rows * width * latent_len,
        2 * width * latent_len,
    )
    latent_part = (keep + from_pair(send).astype(F32)).astype(BF16)
    message = jnp.concatenate([latent_part, terms], axis=1)
    down_rows = expert_down.reshape(local_count * units, latent_len)
    up_here, down_here = kernel_call(
        load_kernel,
        (pltpu.VMEM(expert_up.shape, BF16), pltpu.VMEM(down_rows.shape, BF16)),
        (message, in_space(expert_up, pltpu.HBM), in_space(down_rows, pltpu.HBM)),
        (pl.ANY, pltpu.HBM, pltpu.HBM),
        [pltpu.SemaphoreType.DMA((2,))],
        0,
        4 * latent_len * local_count * units,
    )
    arrived = [
        [sent(latent_part if over else message, step, over) for over in range(pairs)]
        for step in range(exp_count // 2)
    ]
    arrived, up_here, down_here = lax.optimization_barrier((arrived, up_here, down_here))
    own = []
    for blocks in arrived:
        latent = sum(a[:, :latent_len].astype(F32) for a in blocks).astype(BF16)
        own.append(jnp.concatenate([latent, blocks[0][:, latent_len:]], axis=1))
    own = jnp.concatenate(own, axis=0)
    theirs, mine = kernel_call(
        expert_kernel,
        (
            jax.ShapeDtypeStruct((side_rows, latent_len), BF16),
            jax.ShapeDtypeStruct((side_rows, latent_len), F32),
        ),
        (own, from_pair(own), in_space(up_here, pltpu.VMEM), in_space(down_here, pltpu.VMEM)),
        (None,) * 4,
        [
            pltpu.VMEM((2 * side_rows, latent_len), BF16),
            pltpu.VMEM((2 * side_rows, terms_len), F32),
            pltpu.VMEM((2 * side_rows, local_count * units), BF16),
        ],
        8 * side_rows * latent_len * local_count * units,
        4 * latent_len * local_count * units,
    )
    part = (mine + from_pair(theirs).astype(F32)).astype(BF16)
    arrived = []
    for step in range(exp_count // 2):
        block = part[step * rows : (step + 1) * rows]
        arrived += [sent(block, step, over) for over in range(pairs)]
    keep = sum(a.astype(F32) for a in arrived)
    return kernel_call(
        up_kernel,
        jax.ShapeDtypeStruct((rows, lat_up.shape[1]), BF16),
        (keep, from_pair(keep.astype(BF16)), in_space(lat_up, pltpu.VMEM)),
        (None,) * 3,
        [],
        2 * rows * latent_len * lat_up.shape[1],
        2 * latent_len * lat_up.shape[1],
    )


def solution(mesh):
    return jax.shard_map(
        on_device,
        mesh=mesh,
        in_specs=(
            P(("grp", "exp"), "tp"),
            P(None, "tp"),
            P(None, "tp"),
            P("exp", "tp", None),
            P("exp", "tp", None),
            P(("grp", "exp"), None),
            P(("grp", "exp"), None),
        ),
        out_specs=P(("grp", "exp"), "tp"),
        check_vma=False,
    )
```

time: 63.7 us -> 38.2 us (0.60)
  blocking collectives: 19.3 us -> 0 us
  matrix products: 8.92 us -> 0 us
  waiting for transfers between devices: 18.3 us -> 10.3 us
  Pallas kernels: 0 us -> 7.93 us
  starting transfers between devices: 13.1 us -> 19.5 us
  local copies, waits for them, and re-layouts: 2.06 us -> 0.02 us
  other arithmetic: 1.36 us -> 0.14 us
    ppermute x0 -> x12, starting transfers between devices: none -> 19.5 us  [the longest x8 18.6 us: sent(): lax.ppermute(x, ('exp', 'tp'), [(e * tp_count + t, peer(e, t)) for e, t i...]
    all_to_all x2 -> x0, blocking collectives: 19.3 us -> none  [swap(): return lax.all_to_all(blocks, axes, split_axis=0, concat_axis=0, tiled=True)]
    all_to_all x3 -> x0, waiting for transfers between devices: 18.3 us -> none  [swap(): return lax.all_to_all(blocks, axes, split_axis=0, concat_axis=0, tiled=True)]
    all_to_all x3 -> x0, starting transfers between devices: 13.1 us -> none  [swap(): return lax.all_to_all(blocks, axes, split_axis=0, concat_axis=0, tiled=True)]
    ppermute x0 -> x12, waiting for transfers between devices: none -> 10.3 us  [the longest x8 5.6 us: sent(): lax.ppermute(x, ('exp', 'tp'), [(e * tp_count + t, peer(e, t)) for e, t i...]
    dot_general x3 -> x0, matrix products: 8.92 us -> none  [the longest x1 3.74 us: on_device(): jnp.einsum('kth,khl->tl', hidden.astype(jnp.bfloat16), expert_down, prefe...]
    pallas_call x0 -> x4, Pallas kernels: none -> 7.93 us  [kernel_call(): pl.pallas_call(body, out_shape=out_shape, in_specs=[vmem if s is None els...]
    reduce_sum x3 -> x0, other arithmetic: 1.36 us -> none  [the longest x1 1.3 us: on_device(): combine = jnp.sum(jnp.where(named, route_weights[:, :, None], 0.0), axis=1)]
  transfers between devices with their start and end apart: 3 -> 12, of which waited for: 3 -> 8; matrix products, arithmetic and copies ran while one was open for 2% -> 0% of each run, Pallas kernels for 0% -> 7%
where the time goes in v5:
time: 38.2 us; the launch traced here: 38 us
  starting transfers between devices  19.5 us (51%)
  waiting for transfers between devices  10.3 us (27%)
  Pallas kernels  7.93 us (21%)
    ppermute x8, starting transfers between devices, sent(): lax.ppermute(x, ('exp', 'tp'), [(e * tp_count + t, peer(e, t)) for e, t i...  18.6 us
    pallas_call x4, Pallas kernels, kernel_call(): pl.pallas_call(body, out_shape=out_shape, in_specs=[vmem if s is None els...  7.93 us
    ppermute x8, waiting for transfers between devices, sent(): lax.ppermute(x, ('exp', 'tp'), [(e * tp_count + t, peer(e, t)) for e, t i...  5.6 us
    ppermute x4, waiting for transfers between devices, from_pair(): return lax.ppermute(x, 'tp', [(t, t ^ 1) for t in range(tp_count)])  4.71 us
    ppermute x4, starting transfers between devices, from_pair(): return lax.ppermute(x, 'tp', [(t, t ^ 1) for t in range(tp_count)])  0.87 us
  transfers between devices with their start and end apart: 12, of which 8 were waited for; matrix products, arithmetic and copies ran while one was open for 0% of the time, Pallas kernels for 7%

profile of v5, /device:TPU:0, one launch (start us, length us, event | category | flops | bytes accessed | tf_op | source)
XLA Modules:
  0.0 38.0 jit_solution(3184541146213980349)
XLA Ops:
  0.0 2.7 %shard_map.73 = (bf16[32,1024]{1,0:T(8,128)(2,1)S(1)}, f32[32,1024]{1,0:T(8,128)S(1)}, bf16[32,128]{1,0:T(8,128)(2,1)S(1)}) custom-call(bf16[32,1024]{1,0:T(8,128)(2,1)} %tokens_hbm.1, bf16[1024,1024]{1,0:T(8,128)(2,1)} %weight_hbm.1, s32[4,32]{1,0:T(4,128)} %bitcast.4, f32[4,32]{1,0:T(4,128)} %bitcast.5), custom_call_target="tpu_custom_call" | custom-call | flops 67108864 | bytes 2097152 | tf_op jit(solution)/shard_map/pallas_call | solution.py:21
  2.7 0.5 %collective-permute-start = (bf16[32,1024]{1,0:T(8,128)(2,1)S(1)}, bf16[32,1024]{1,0:T(8,128)(2,1)S(1)}, u32[]{:S(2)}, u32[]{:S(2)}) collective-permute-start(bf16[32,1024]{1,0:T(8,128)(2,1)S(1)} %get-tuple-element.19), channel_id=1, source_target_pairs={{0,1},{1,0},{2,3},{3,2},{4,5},{5,4},{6,7},{7,6},{8,9},{9,8},{10,11... | collective-permute-start | bytes 196616 | tf_op jit(solution)/shard_map/ppermute | solution.py:117
  3.2 0.9 %collective-permute-done = bf16[32,1024]{1,0:T(8,128)(2,1)S(1)} collective-permute-done((bf16[32,1024]{1,0:T(8,128)(2,1)S(1)}, bf16[32,1024]{1,0:T(8,128)(2,1)S(1)}, u32[]{:S(2)}, u32[]{:S(2)}) %collective-permute-start) | collective-permute-done | bytes 65568 | tf_op jit(solution)/shard_map/ppermute | solution.py:117
  4.2 4.8 %collective-permute-start.3 = (bf16[32,1152]{1,0:T(8,128)(2,1)S(1)}, bf16[32,1152]{1,0:T(8,128)(2,1)S(1)}, u32[]{:S(2)}, u32[]{:S(2)}) collective-permute-start(bf16[32,1152]{1,0:T(8,128)(2,1)S(1)} %pad_maximum_fusion.after_ref), channel_id=1, source_target_pairs={{0,4},{1,1},{2,6},{3,3},{4,0},{5,5},{6,2},{7,7},{8,12},{9,9},{10,1... | collective-permute-start | bytes 221192 | tf_op jit(solution)/shard_map/ppermute | solution.py:124
  9.0 2.5 %collective-permute-start.1 = (bf16[32,1152]{1,0:T(8,128)(2,1)S(1)}, bf16[32,1152]{1,0:T(8,128)(2,1)S(1)}, u32[]{:S(2)}, u32[]{:S(2)}) collective-permute-start(bf16[32,1152]{1,0:T(8,128)(2,1)S(1)} %pad_maximum_fusion.after_ref), channel_id=1, source_target_pairs={{0,12},{1,9},{2,14},{3,11},{4,8},{5,13},{6,10},{7,15},{8,4},{9,1},... | collective-permute-start | bytes 221192 | tf_op jit(solution)/shard_map/ppermute | solution.py:124
  11.6 1.6 %collective-permute-start.4 = (bf16[32,1024]{1,0:T(8,128)(2,1)S(1)}, bf16[32,1024]{1,0:T(8,128)(2,1)S(1)}, u32[]{:S(2)}, u32[]{:S(2)}) collective-permute-start(bf16[32,1024]{1,0:T(8,128)(2,1)S(1)} %add_convert_fusion.3), channel_id=1, source_target_pairs={{0,6},{1,3},{2,4},{3,1},{4,2},{5,7},{6,0},{7,5},{8,14},{9,11},{10,... | collective-permute-start | bytes 196616 | tf_op jit(solution)/shard_map/ppermute | solution.py:124
  13.2 0.9 %collective-permute-start.2 = (bf16[32,1024]{1,0:T(8,128)(2,1)S(1)}, bf16[32,1024]{1,0:T(8,128)(2,1)S(1)}, u32[]{:S(2)}, u32[]{:S(2)}) collective-permute-start(bf16[32,1024]{1,0:T(8,128)(2,1)S(1)} %add_convert_fusion.3), channel_id=1, source_target_pairs={{0,14},{1,11},{2,12},{3,9},{4,10},{5,15},{6,8},{7,13},{8,6},{9,3},... | collective-permute-start | bytes 196616 | tf_op jit(solution)/shard_map/ppermute | solution.py:124
  14.1 2.6 %shard_map.74 = (bf16[2,672,1024]{2,1,0:T(8,128)(2,1)S(1)}, bf16[1344,1024]{1,0:T(8,128)(2,1)S(1)}) custom-call(bf16[32,1152]{1,0:T(8,128)(2,1)S(1)} %pad_maximum_fusion.after_ref, bf16[2,672,1024]{2,1,0:T(8,128)(2,1)} %up_hbm.1, bf16[1344,1024]{1,0:T(8,128)(2,1)} %bitcast.3), custom_call_target="tpu_custom_call" | custom-call | bytes 5505024 | tf_op jit(solution)/shard_map/pallas_call | solution.py:21
  16.7 0.6 %collective-permute-done.4 = bf16[32,1024]{1,0:T(8,128)(2,1)S(1)} collective-permute-done((bf16[32,1024]{1,0:T(8,128)(2,1)S(1)}, bf16[32,1024]{1,0:T(8,128)(2,1)S(1)}, u32[]{:S(2)}, u32[]{:S(2)}) %collective-permute-start.4) | collective-permute-done | bytes 65568 | tf_op jit(solution)/shard_map/ppermute | solution.py:124
  17.4 2.7 %collective-permute-done.2 = bf16[32,1024]{1,0:T(8,128)(2,1)S(1)} collective-permute-done((bf16[32,1024]{1,0:T(8,128)(2,1)S(1)}, bf16[32,1024]{1,0:T(8,128)(2,1)S(1)}, u32[]{:S(2)}, u32[]{:S(2)}) %collective-permute-start.2) | collective-permute-done | bytes 65568 | tf_op jit(solution)/shard_map/ppermute | solution.py:124
  20.1 0.0 collective-permute-done.3
  20.1 0.0 collective-permute-done.1
  20.2 0.0 copy-start
  20.2 0.1 collective-permute-start.5
  20.3 1.4 %collective-permute-done.5.other_ref = bf16[64,1152]{1,0:T(8,128)(2,1)S(1)} collective-permute-done((bf16[64,1152]{1,0:T(8,128)(2,1)S(1)}, bf16[64,1152]{1,0:T(8,128)(2,1)S(1)}, u32[]{:S(2)}, u32[]{:S(2)}) %collective-permute-start.5) | collective-permute-done | bytes 147488 | tf_op jit(solution)/shard_map/ppermute | solution.py:117
  21.7 1.5 %shard_map.75 = (bf16[64,1024]{1,0:T(8,128)(2,1)S(1)}, f32[64,1024]{1,0:T(8,128)S(1)}) custom-call(bf16[64,1152]{1,0:T(8,128)(2,1)S(1)} %maximum_maximum_fusion.own_ref, bf16[64,1152]{1,0:T(8,128)(2,1)S(1)} %collective-permute-done.5.other_ref, bf16[2,672,1024]{2,1,0:T(8,128)(2,1)S(1)} %get-tuple-element.27.up_ref, ...), custom_call_target="tpu_custom_call" | custom-call | flops 704643072 | bytes 5505024 | tf_op jit(solution)/shard_map/pallas_call | solution.py:21
  23.2 0.2 collective-permute-start.6
  23.4 1.2 %collective-permute-done.6 = bf16[64,1024]{1,0:T(8,128)(2,1)S(1)} collective-permute-done((bf16[64,1024]{1,0:T(8,128)(2,1)S(1)}, bf16[64,1024]{1,0:T(8,128)(2,1)S(1)}, u32[]{:S(2)}, u32[]{:S(2)}) %collective-permute-start.6) | collective-permute-done | bytes 131104 | tf_op jit(solution)/shard_map/ppermute | solution.py:117
  24.6 1.1 %collective-permute-start.8 = (bf16[32,1024]{1,0:T(8,128)(2,1)S(1)}, bf16[32,1024]{1,0:T(8,128)(2,1)S(1)}, u32[]{:S(2)}, u32[]{:S(2)}) collective-permute-start(bf16[32,1024]{1,0:T(8,128)(2,1)S(1)} %get-tuple-element.33), channel_id=1, source_target_pairs={{0,14},{1,11},{2,12},{3,9},{4,10},{5,15},{6,8},{7,13},{8,6},{9,3},... | collective-permute-start | bytes 196616 | tf_op jit(solution)/shard_map/ppermute | solution.py:124
  25.7 2.8 %collective-permute-start.7 = (bf16[32,1024]{1,0:T(8,128)(2,1)S(1)}, bf16[32,1024]{1,0:T(8,128)(2,1)S(1)}, u32[]{:S(2)}, u32[]{:S(2)}) collective-permute-start(bf16[32,1024]{1,0:T(8,128)(2,1)S(1)} %get-tuple-element.33), channel_id=1, source_target_pairs={{0,12},{1,9},{2,14},{3,11},{4,8},{5,13},{6,10},{7,15},{8,4},{9,1},... | collective-permute-start | bytes 196616 | tf_op jit(solution)/shard_map/ppermute | solution.py:124
  28.5 0.0 collective-permute-start.10
  28.5 4.8 %collective-permute-start.9 = (bf16[32,1024]{1,0:T(8,128)(2,1)S(1)}, bf16[32,1024]{1,0:T(8,128)(2,1)S(1)}, u32[]{:S(2)}, u32[]{:S(2)}) collective-permute-start(bf16[32,1024]{1,0:T(8,128)(2,1)S(1)} %get-tuple-element.34), channel_id=1, source_target_pairs={{0,4},{1,1},{2,6},{3,3},{4,0},{5,5},{6,2},{7,7},{8,12},{9,9},{10,1... | collective-permute-start | bytes 196616 | tf_op jit(solution)/shard_map/ppermute | solution.py:124
  33.3 0.0 collective-permute-done.8
  33.4 0.0 collective-permute-done.7
  33.4 0.9 %collective-permute-done.10 = bf16[32,1024]{1,0:T(8,128)(2,1)S(1)} collective-permute-done((bf16[32,1024]{1,0:T(8,128)(2,1)S(1)}, bf16[32,1024]{1,0:T(8,128)(2,1)S(1)}, u32[]{:S(2)}, u32[]{:S(2)}) %collective-permute-start.10) | collective-permute-done | bytes 65568 | tf_op jit(solution)/shard_map/ppermute | solution.py:124
  34.3 1.3 %collective-permute-done.9 = bf16[32,1024]{1,0:T(8,128)(2,1)S(1)} collective-permute-done((bf16[32,1024]{1,0:T(8,128)(2,1)S(1)}, bf16[32,1024]{1,0:T(8,128)(2,1)S(1)}, u32[]{:S(2)}, u32[]{:S(2)}) %collective-permute-start.9) | collective-permute-done | bytes 65568 | tf_op jit(solution)/shard_map/ppermute | solution.py:124
  35.6 0.1 collective-permute-start.11
  35.7 1.2 %collective-permute-done.11.other_ref = bf16[32,1024]{1,0:T(8,128)(2,1)S(1)} collective-permute-done((bf16[32,1024]{1,0:T(8,128)(2,1)S(1)}, bf16[32,1024]{1,0:T(8,128)(2,1)S(1)}, u32[]{:S(2)}, u32[]{:S(2)}) %collective-permute-start.11) | collective-permute-done | bytes 65568 | tf_op jit(solution)/shard_map/ppermute | solution.py:117
  36.9 0.0 copy-done
  36.9 1.1 %shard_map.76 = bf16[32,1024]{1,0:T(8,128)(2,1)} custom-call(f32[32,1024]{1,0:T(8,128)S(1)} %get-tuple-element.32.keep_ref, bf16[32,1024]{1,0:T(8,128)(2,1)S(1)} %collective-permute-done.11.other_ref, bf16[1024,1024]{1,0:T(8,128)(2,1)S(1)} %copy-done), custom_call_target="tpu_custom_call" | custom-call | flops 67108864 | bytes 2097152 | tf_op jit(solution)/shard_map/pallas_call | solution.py:21
  (9 shorter events, 0.2 us)
Async XLA Ops:
  2.7 1.4 %collective-permute-start = (bf16[32,1024]{1,0:T(8,128)(2,1)S(1)}, bf16[32,1024]{1,0:T(8,128)(2,1)S(1)}, u32[]{:S(2)}, u32[]{:S(2)}) collective-permute-start(bf16[32,1024]{1,0:T(8,128)(2,1)S(1)} %get-tuple-element.19), channel_id=1, source_target_pairs={{0,1},{1,0},{2,3},{3,2},{4,5},{5,4},{6,7},{7,6},{8,9},{9,8},{10,11... | collective-permute-start | bytes 196616 | tf_op jit(solution)/shard_map/ppermute | solution.py:117
  4.2 16.0 %collective-permute-start.3 = (bf16[32,1152]{1,0:T(8,128)(2,1)S(1)}, bf16[32,1152]{1,0:T(8,128)(2,1)S(1)}, u32[]{:S(2)}, u32[]{:S(2)}) collective-permute-start(bf16[32,1152]{1,0:T(8,128)(2,1)S(1)} %pad_maximum_fusion.after_ref), channel_id=1, source_target_pairs={{0,4},{1,1},{2,6},{3,3},{4,0},{5,5},{6,2},{7,7},{8,12},{9,9},{10,1... | collective-permute-start | bytes 221192 | tf_op jit(solution)/shard_map/ppermute | solution.py:124
  9.0 11.1 %collective-permute-start.1 = (bf16[32,1152]{1,0:T(8,128)(2,1)S(1)}, bf16[32,1152]{1,0:T(8,128)(2,1)S(1)}, u32[]{:S(2)}, u32[]{:S(2)}) collective-permute-start(bf16[32,1152]{1,0:T(8,128)(2,1)S(1)} %pad_maximum_fusion.after_ref), channel_id=1, source_target_pairs={{0,12},{1,9},{2,14},{3,11},{4,8},{5,13},{6,10},{7,15},{8,4},{9,1},... | collective-permute-start | bytes 221192 | tf_op jit(solution)/shard_map/ppermute | solution.py:124
  11.6 5.8 %collective-permute-start.4 = (bf16[32,1024]{1,0:T(8,128)(2,1)S(1)}, bf16[32,1024]{1,0:T(8,128)(2,1)S(1)}, u32[]{:S(2)}, u32[]{:S(2)}) collective-permute-start(bf16[32,1024]{1,0:T(8,128)(2,1)S(1)} %add_convert_fusion.3), channel_id=1, source_target_pairs={{0,6},{1,3},{2,4},{3,1},{4,2},{5,7},{6,0},{7,5},{8,14},{9,11},{10,... | collective-permute-start | bytes 196616 | tf_op jit(solution)/shard_map/ppermute | solution.py:124
  13.2 7.0 %collective-permute-start.2 = (bf16[32,1024]{1,0:T(8,128)(2,1)S(1)}, bf16[32,1024]{1,0:T(8,128)(2,1)S(1)}, u32[]{:S(2)}, u32[]{:S(2)}) collective-permute-start(bf16[32,1024]{1,0:T(8,128)(2,1)S(1)} %add_convert_fusion.3), channel_id=1, source_target_pairs={{0,14},{1,11},{2,12},{3,9},{4,10},{5,15},{6,8},{7,13},{8,6},{9,3},... | collective-permute-start | bytes 196616 | tf_op jit(solution)/shard_map/ppermute | solution.py:124
  20.2 16.7 %copy-start = (bf16[1024,1024]{1,0:T(8,128)(2,1)S(1)}, bf16[1024,1024]{1,0:T(8,128)(2,1)}, u32[]{:S(2)}) copy-start(bf16[1024,1024]{1,0:T(8,128)(2,1)} %weight_ref.1) | copy-start | bytes 6291460
  20.2 1.4 %collective-permute-start.5 = (bf16[64,1152]{1,0:T(8,128)(2,1)S(1)}, bf16[64,1152]{1,0:T(8,128)(2,1)S(1)}, u32[]{:S(2)}, u32[]{:S(2)}) collective-permute-start(bf16[64,1152]{1,0:T(8,128)(2,1)S(1)} %maximum_maximum_fusion.own_ref), channel_id=1, source_target_pairs={{0,1},{1,0},{2,3},{3,2},{4,5},{5,4},{6,7},{7,6},{8,9},{9,8},{10,11... | collective-permute-start | bytes 442376 | tf_op jit(solution)/shard_map/ppermute | solution.py:117
  23.2 1.4 %collective-permute-start.6 = (bf16[64,1024]{1,0:T(8,128)(2,1)S(1)}, bf16[64,1024]{1,0:T(8,128)(2,1)S(1)}, u32[]{:S(2)}, u32[]{:S(2)}) collective-permute-start(bf16[64,1024]{1,0:T(8,128)(2,1)S(1)} %get-tuple-element.30), channel_id=1, source_target_pairs={{0,1},{1,0},{2,3},{3,2},{4,5},{5,4},{6,7},{7,6},{8,9},{9,8},{10,11... | collective-permute-start | bytes 393224 | tf_op jit(solution)/shard_map/ppermute | solution.py:117
  24.6 8.7 %collective-permute-start.8 = (bf16[32,1024]{1,0:T(8,128)(2,1)S(1)}, bf16[32,1024]{1,0:T(8,128)(2,1)S(1)}, u32[]{:S(2)}, u32[]{:S(2)}) collective-permute-start(bf16[32,1024]{1,0:T(8,128)(2,1)S(1)} %get-tuple-element.33), channel_id=1, source_target_pairs={{0,14},{1,11},{2,12},{3,9},{4,10},{5,15},{6,8},{7,13},{8,6},{9,3},... | collective-permute-start | bytes 196616 | tf_op jit(solution)/shard_map/ppermute | solution.py:124
  25.7 7.7 %collective-permute-start.7 = (bf16[32,1024]{1,0:T(8,128)(2,1)S(1)}, bf16[32,1024]{1,0:T(8,128)(2,1)S(1)}, u32[]{:S(2)}, u32[]{:S(2)}) collective-permute-start(bf16[32,1024]{1,0:T(8,128)(2,1)S(1)} %get-tuple-element.33), channel_id=1, source_target_pairs={{0,12},{1,9},{2,14},{3,11},{4,8},{5,13},{6,10},{7,15},{8,4},{9,1},... | collective-permute-start | bytes 196616 | tf_op jit(solution)/shard_map/ppermute | solution.py:124
  28.5 5.8 %collective-permute-start.10 = (bf16[32,1024]{1,0:T(8,128)(2,1)S(1)}, bf16[32,1024]{1,0:T(8,128)(2,1)S(1)}, u32[]{:S(2)}, u32[]{:S(2)}) collective-permute-start(bf16[32,1024]{1,0:T(8,128)(2,1)S(1)} %get-tuple-element.34), channel_id=1, source_target_pairs={{0,6},{1,3},{2,4},{3,1},{4,2},{5,7},{6,0},{7,5},{8,14},{9,11},{10,... | collective-permute-start | bytes 196616 | tf_op jit(solution)/shard_map/ppermute | solution.py:124
  28.5 7.1 %collective-permute-start.9 = (bf16[32,1024]{1,0:T(8,128)(2,1)S(1)}, bf16[32,1024]{1,0:T(8,128)(2,1)S(1)}, u32[]{:S(2)}, u32[]{:S(2)}) collective-permute-start(bf16[32,1024]{1,0:T(8,128)(2,1)S(1)} %get-tuple-element.34), channel_id=1, source_target_pairs={{0,4},{1,1},{2,6},{3,3},{4,0},{5,5},{6,2},{7,7},{8,12},{9,9},{10,1... | collective-permute-start | bytes 196616 | tf_op jit(solution)/shard_map/ppermute | solution.py:124
  35.6 1.3 %collective-permute-start.11 = (bf16[32,1024]{1,0:T(8,128)(2,1)S(1)}, bf16[32,1024]{1,0:T(8,128)(2,1)S(1)}, u32[]{:S(2)}, u32[]{:S(2)}) collective-permute-start(bf16[32,1024]{1,0:T(8,128)(2,1)S(1)} %get-tuple-element.31), channel_id=1, source_target_pairs={{0,1},{1,0},{2,3},{3,2},{4,5},{5,4},{6,7},{7,6},{8,9},{9,8},{10,11... | collective-permute-start | bytes 196616 | tf_op jit(solution)/shard_map/ppermute | solution.py:117

commit v6 on v5

--- a/solution.py
+++ b/solution.py
@@ -16,13 +16,14 @@
     return pltpu.with_memory_space_constraint(x, space)
 
 
-def kernel_call(body, out_shape, args, specs, scratch, flops, moved):
+def kernel_call(body, out_shape, args, specs, scratch, flops, moved, out_space=pltpu.VMEM):
     vmem = pl.BlockSpec(memory_space=pltpu.VMEM)
+    out_spec = pl.BlockSpec(memory_space=out_space)
     return pl.pallas_call(
         body,
         out_shape=out_shape,
         in_specs=[vmem if s is None else pl.BlockSpec(memory_space=s) for s in specs],
-        out_specs=jax.tree.map(lambda _: vmem, out_shape),
+        out_specs=jax.tree.map(lambda _: out_spec, out_shape),
         scratch_shapes=scratch,
         compiler_params=pltpu.CompilerParams(vmem_limit_bytes=VMEM_LIMIT),
         cost_estimate=pl.CostEstimate(flops=flops, bytes_accessed=moved, transcendentals=0),
@@ -30,11 +31,11 @@
 
 
 def down_kernel(
-    tokens_hbm, weight_hbm, routes_hbm, scale_hbm, send_ref, keep_ref, terms_ref,
-    tokens, weight, routes, scale, sems,
+    tokens_hbm, weight_hbm, routes_hbm, scale_hbm, send_ref, keep_ref, routes_ref, scale_ref,
+    tokens, weight, sems,
 ):
     size = weight.shape[0] // CHUNKS
-    small = [(tokens_hbm, tokens), (routes_hbm, routes), (scale_hbm, scale)]
+    small = [(tokens_hbm, tokens), (routes_hbm, routes_ref), (scale_hbm, scale_ref)]
     small = [pltpu.make_async_copy(a, b, sems.at[i]) for i, (a, b) in enumerate(small)]
     small[0].start()
     chunks = []
@@ -42,23 +43,8 @@
         at = pl.ds(i * size, size)
         chunks.append(pltpu.make_async_copy(weight_hbm.at[at, :], weight.at[at, :], sems.at[3 + i]))
         chunks[i].start()
-        if i == 0:
-            small[1].start()
-            small[2].start()
-    small[1].wait()
-    small[2].wait()
-    rows = tokens.shape[0]
-    width = terms_ref.shape[1]
-    row = lax.broadcasted_iota(jnp.int32, (width, rows), 0)
-    experts_all = width // 2
-    expert = jnp.where(row < experts_all, row, row - experts_all)
-    combine = jnp.zeros((width, rows), F32)
-    for r in range(routes.shape[0]):
-        combine += jnp.where(expert == routes[r : r + 1, :], scale[r : r + 1, :], 0.0)
-    high = combine.astype(BF16).astype(F32)
-    combine = jnp.where(row < experts_all, high, combine - high)
-    combine = jnp.concatenate([combine, jnp.zeros((width, LANES - rows), F32)], axis=1)
-    terms_ref[...] = combine.T[:rows, :].astype(BF16)
+    small[1].start()
+    small[2].start()
     small[0].wait()
     x = tokens[...]
     for i in range(CHUNKS):
@@ -66,6 +52,22 @@
         part = lax.dot_general(x, weight[i * size : (i + 1) * size, :], NT, preferred_element_type=F32)
         send_ref[:, i * size : (i + 1) * size] = part.astype(BF16)
         keep_ref[:, i * size : (i + 1) * size] = part
+    small[1].wait()
+    small[2].wait()
+
+
+def terms_kernel(routes_ref, scale_ref, terms_ref):
+    rows, width = terms_ref.shape
+    row = lax.broadcasted_iota(jnp.int32, (width, rows), 0)
+    experts_all = width // 2
+    expert = jnp.where(row < experts_all, row, row - experts_all)
+    combine = jnp.zeros((width, rows), F32)
+    for r in range(routes_ref.shape[0]):
+        combine += jnp.where(expert == routes_ref[r : r + 1, :], scale_ref[r : r + 1, :], 0.0)
+    high = combine.astype(BF16).astype(F32)
+    combine = jnp.where(row < experts_all, high, combine - high)
+    combine = jnp.concatenate([combine, jnp.zeros((width, LANES - rows), F32)], axis=1)
+    terms_ref[...] = combine.T[:rows, :].astype(BF16)
 
 
 def load_kernel(after_ref, up_hbm, down_hbm, up_ref, down_ref, sems):
@@ -100,9 +102,17 @@
     theirs_ref[...] = result[side:, :].astype(BF16)
 
 
-def up_kernel(keep_ref, other_ref, weight_ref, out_ref):
+def up_kernel(keep_ref, other_ref, weight_ref, out_hbm, out, sems):
     mixed = (keep_ref[...] + other_ref[...].astype(F32)).astype(BF16)
-    out_ref[...] = jnp.dot(mixed, weight_ref[...], preferred_element_type=F32).astype(BF16)
+    half = out.shape[1] // 2
+    copies = []
+    for i in range(2):
+        at = slice(i * half, (i + 1) * half)
+        out[:, at] = jnp.dot(mixed, weight_ref[:, at], preferred_element_type=F32).astype(BF16)
+        copies.append(pltpu.make_async_copy(out.at[:, at], out_hbm.at[:, at], sems.at[i]))
+        copies[i].start()
+    for copy in copies:
+        copy.wait()
 
 
 def on_device(tokens, lat_down, lat_up, expert_up, expert_down, routes, route_weights):
@@ -123,24 +133,32 @@
         whole = [(e, t) for e in range(exp_count) for t in range(tp_count)]
         return lax.ppermute(x, ("exp", "tp"), [(e * tp_count + t, peer(e, t)) for e, t in whole])
 
-    send, keep, terms = kernel_call(
+    send, keep, routes_here, scale_here = kernel_call(
         down_kernel,
         (
             jax.ShapeDtypeStruct((rows, latent_len), BF16),
             jax.ShapeDtypeStruct((rows, latent_len), F32),
-            jax.ShapeDtypeStruct((rows, terms_len), BF16),
+            jax.ShapeDtypeStruct(routes.shape[::-1], jnp.int32),
+            jax.ShapeDtypeStruct(routes.shape[::-1], F32),
         ),
         [in_space(x, pltpu.HBM) for x in (tokens, lat_down, routes.T, route_weights.T)],
         (pltpu.HBM,) * 4,
         [
             pltpu.VMEM((rows, width), BF16),
             pltpu.VMEM((latent_len, width), BF16),
-            pltpu.VMEM((routes.shape[1], rows), jnp.int32),
-            pltpu.VMEM((routes.shape[1], rows), F32),
             pltpu.SemaphoreType.DMA((3 + CHUNKS,)),
         ],
         2 * rows * width * latent_len,
         2 * width * latent_len,
+    )
+    terms = kernel_call(
+        terms_kernel,
+        jax.ShapeDtypeStruct((rows, terms_len), BF16),
+        (routes_here, scale_here),
+        (None,) * 2,
+        [],
+        rows * terms_len * 8,
+        2 * rows * terms_len,
     )
     latent_part = (keep + from_pair(send).astype(F32)).astype(BF16)
     message = jnp.concatenate([latent_part, terms], axis=1)
@@ -155,9 +173,9 @@
         4 * latent_len * local_count * units,
     )
     arrived = [
-        [sent(latent_part if over else message, step, over) for over in range(pairs)]
-        for step in range(exp_count // 2)
-    ]
+        [sent(message, step, over) for over in range(pairs)]
+        for step in reversed(range(exp_count // 2))
+    ][::-1]
     arrived, up_here, down_here = lax.optimization_barrier((arrived, up_here, down_here))
     own = []
     for blocks in arrived:
@@ -191,9 +209,10 @@
         jax.ShapeDtypeStruct((rows, lat_up.shape[1]), BF16),
         (keep, from_pair(keep.astype(BF16)), in_space(lat_up, pltpu.VMEM)),
         (None,) * 3,
-        [],
+        [pltpu.VMEM((rows, lat_up.shape[1]), BF16), pltpu.SemaphoreType.DMA((2,))],
         2 * rows * latent_len * lat_up.shape[1],
         2 * latent_len * lat_up.shape[1],
+        pltpu.HBM,
     )
 
 

time: 38.2 us -> 38.3 us (level)
    pallas_call x4 -> x5, Pallas kernels: 7.93 us -> 8.01 us  [kernel_call(): pl.pallas_call(body, out_shape=out_shape, in_specs=[vmem if s is None els...]
where the time goes in v6:
time: 38.3 us; the launch traced here: 38.2 us
  starting transfers between devices  19.6 us (51%)
  waiting for transfers between devices  10.2 us (27%)
  Pallas kernels  8.01 us (21%)
    ppermute x8, starting transfers between devices, sent(): lax.ppermute(x, ('exp', 'tp'), [(e * tp_count + t, peer(e, t)) for e, t i...  18.7 us
    pallas_call x5, Pallas kernels, kernel_call(): pl.pallas_call(body, out_shape=out_shape, in_specs=[vmem if s is None els...  8.01 us
    ppermute x8, waiting for transfers between devices, sent(): lax.ppermute(x, ('exp', 'tp'), [(e * tp_count + t, peer(e, t)) for e, t i...  5.62 us
    ppermute x4, waiting for transfers between devices, from_pair(): return lax.ppermute(x, 'tp', [(t, t ^ 1) for t in range(tp_count)])  4.62 us
    ppermute x4, starting transfers between devices, from_pair(): return lax.ppermute(x, 'tp', [(t, t ^ 1) for t in range(tp_count)])  0.87 us
  transfers between devices with their start and end apart: 12, of which 8 were waited for; matrix products, arithmetic and copies ran while one was open for 0% of the time, Pallas kernels for 7%

profile of v6, /device:TPU:0, one launch (start us, length us, event | category | flops | bytes accessed | tf_op | source)
XLA Modules:
  0.0 38.2 jit_solution(3945393509586328374)
XLA Ops:
  0.0 2.7 %shard_map.73 = (bf16[32,1024]{1,0:T(8,128)(2,1)S(1)}, f32[32,1024]{1,0:T(8,128)S(1)}, s32[4,32]{1,0:T(4,128)S(1)}, f32[4,32]{1,0:T(4,128)S(1)}) custom-call(bf16[32,1024]{1,0:T(8,128)(2,1)} %tokens_hbm.1, bf16[1024,1024]{1,0:T(8,128)(2,1)} %weight_hbm.1, s32[4,32]{1,0:T(4,128)} %bitcast.4, f32[4,32]{1,0:T(4,128)} %bitcast.5), custom_call_target="tpu_custom_call" | custom-call | flops 67108864 | bytes 2097152 | tf_op jit(solution)/shard_map/pallas_call | solution.py:22
  2.7 0.5 %collective-permute-start = (bf16[32,1024]{1,0:T(8,128)(2,1)S(1)}, bf16[32,1024]{1,0:T(8,128)(2,1)S(1)}, u32[]{:S(2)}, u32[]{:S(2)}) collective-permute-start(bf16[32,1024]{1,0:T(8,128)(2,1)S(1)} %get-tuple-element.20), channel_id=1, source_target_pairs={{0,1},{1,0},{2,3},{3,2},{4,5},{5,4},{6,7},{7,6},{8,9},{9,8},{10,11... | collective-permute-start | bytes 196616 | tf_op jit(solution)/shard_map/ppermute | solution.py:127
  3.2 0.1 shard_map.74
  3.3 0.8 %collective-permute-done = bf16[32,1024]{1,0:T(8,128)(2,1)S(1)} collective-permute-done((bf16[32,1024]{1,0:T(8,128)(2,1)S(1)}, bf16[32,1024]{1,0:T(8,128)(2,1)S(1)}, u32[]{:S(2)}, u32[]{:S(2)}) %collective-permute-start) | collective-permute-done | bytes 65568 | tf_op jit(solution)/shard_map/ppermute | solution.py:127
  4.2 3.9 %collective-permute-start.4 = (bf16[32,1152]{1,0:T(8,128)(2,1)S(1)}, bf16[32,1152]{1,0:T(8,128)(2,1)S(1)}, u32[]{:S(2)}, u32[]{:S(2)}) collective-permute-start(bf16[32,1152]{1,0:T(8,128)(2,1)S(1)} %pad_maximum_fusion.after_ref), channel_id=1, source_target_pairs={{0,6},{1,3},{2,4},{3,1},{4,2},{5,7},{6,0},{7,5},{8,14},{9,11},{10,... | collective-permute-start | bytes 221192 | tf_op jit(solution)/shard_map/ppermute | solution.py:134
  8.1 2.3 %collective-permute-start.3 = (bf16[32,1152]{1,0:T(8,128)(2,1)S(1)}, bf16[32,1152]{1,0:T(8,128)(2,1)S(1)}, u32[]{:S(2)}, u32[]{:S(2)}) collective-permute-start(bf16[32,1152]{1,0:T(8,128)(2,1)S(1)} %pad_maximum_fusion.after_ref), channel_id=1, source_target_pairs={{0,4},{1,1},{2,6},{3,3},{4,0},{5,5},{6,2},{7,7},{8,12},{9,9},{10,1... | collective-permute-start | bytes 221192 | tf_op jit(solution)/shard_map/ppermute | solution.py:134
  10.5 3.6 %collective-permute-start.2 = (bf16[32,1152]{1,0:T(8,128)(2,1)S(1)}, bf16[32,1152]{1,0:T(8,128)(2,1)S(1)}, u32[]{:S(2)}, u32[]{:S(2)}) collective-permute-start(bf16[32,1152]{1,0:T(8,128)(2,1)S(1)} %pad_maximum_fusion.after_ref), channel_id=1, source_target_pairs={{0,14},{1,11},{2,12},{3,9},{4,10},{5,15},{6,8},{7,13},{8,6},{9,3},... | collective-permute-start | bytes 221192 | tf_op jit(solution)/shard_map/ppermute | solution.py:134
  14.1 0.1 collective-permute-start.1
  14.2 2.6 %shard_map.75 = (bf16[2,672,1024]{2,1,0:T(8,128)(2,1)S(1)}, bf16[1344,1024]{1,0:T(8,128)(2,1)S(1)}) custom-call(bf16[32,1152]{1,0:T(8,128)(2,1)S(1)} %pad_maximum_fusion.after_ref, bf16[2,672,1024]{2,1,0:T(8,128)(2,1)} %up_hbm.1, bf16[1344,1024]{1,0:T(8,128)(2,1)} %bitcast.3), custom_call_target="tpu_custom_call" | custom-call | bytes 5505024 | tf_op jit(solution)/shard_map/pallas_call | solution.py:22
  16.8 0.0 collective-permute-done.4
  16.8 0.0 collective-permute-done.3
  16.9 1.0 %collective-permute-done.2 = bf16[32,1152]{1,0:T(8,128)(2,1)S(1)} collective-permute-done((bf16[32,1152]{1,0:T(8,128)(2,1)S(1)}, bf16[32,1152]{1,0:T(8,128)(2,1)S(1)}, u32[]{:S(2)}, u32[]{:S(2)}) %collective-permute-start.2) | collective-permute-done | bytes 73760 | tf_op jit(solution)/shard_map/ppermute | solution.py:134
  17.9 2.4 %collective-permute-done.1 = bf16[32,1152]{1,0:T(8,128)(2,1)S(1)} collective-permute-done((bf16[32,1152]{1,0:T(8,128)(2,1)S(1)}, bf16[32,1152]{1,0:T(8,128)(2,1)S(1)}, u32[]{:S(2)}, u32[]{:S(2)}) %collective-permute-start.1) | collective-permute-done | bytes 73760 | tf_op jit(solution)/shard_map/ppermute | solution.py:134
  20.3 0.0 copy-start
  20.3 0.1 collective-permute-start.5
  20.4 1.4 %collective-permute-done.5.other_ref = bf16[64,1152]{1,0:T(8,128)(2,1)S(1)} collective-permute-done((bf16[64,1152]{1,0:T(8,128)(2,1)S(1)}, bf16[64,1152]{1,0:T(8,128)(2,1)S(1)}, u32[]{:S(2)}, u32[]{:S(2)}) %collective-permute-start.5) | collective-permute-done | bytes 147488 | tf_op jit(solution)/shard_map/ppermute | solution.py:127
  21.8 1.5 %shard_map.76 = (bf16[64,1024]{1,0:T(8,128)(2,1)S(1)}, f32[64,1024]{1,0:T(8,128)S(1)}) custom-call(bf16[64,1152]{1,0:T(8,128)(2,1)S(1)} %maximum_maximum_fusion.own_ref, bf16[64,1152]{1,0:T(8,128)(2,1)S(1)} %collective-permute-done.5.other_ref, bf16[2,672,1024]{2,1,0:T(8,128)(2,1)S(1)} %get-tuple-element.29.up_ref, ...), custom_call_target="tpu_custom_call" | custom-call | flops 704643072 | bytes 5505024 | tf_op jit(solution)/shard_map/pallas_call | solution.py:22
  23.2 0.2 collective-permute-start.6
  23.5 1.2 %collective-permute-done.6 = bf16[64,1024]{1,0:T(8,128)(2,1)S(1)} collective-permute-done((bf16[64,1024]{1,0:T(8,128)(2,1)S(1)}, bf16[64,1024]{1,0:T(8,128)(2,1)S(1)}, u32[]{:S(2)}, u32[]{:S(2)}) %collective-permute-start.6) | collective-permute-done | bytes 131104 | tf_op jit(solution)/shard_map/ppermute | solution.py:127
  24.7 1.8 %collective-permute-start.8 = (bf16[32,1024]{1,0:T(8,128)(2,1)S(1)}, bf16[32,1024]{1,0:T(8,128)(2,1)S(1)}, u32[]{:S(2)}, u32[]{:S(2)}) collective-permute-start(bf16[32,1024]{1,0:T(8,128)(2,1)S(1)} %get-tuple-element.35), channel_id=1, source_target_pairs={{0,14},{1,11},{2,12},{3,9},{4,10},{5,15},{6,8},{7,13},{8,6},{9,3},... | collective-permute-start | bytes 196616 | tf_op jit(solution)/shard_map/ppermute | solution.py:134
  26.5 3.0 %collective-permute-start.7 = (bf16[32,1024]{1,0:T(8,128)(2,1)S(1)}, bf16[32,1024]{1,0:T(8,128)(2,1)S(1)}, u32[]{:S(2)}, u32[]{:S(2)}) collective-permute-start(bf16[32,1024]{1,0:T(8,128)(2,1)S(1)} %get-tuple-element.35), channel_id=1, source_target_pairs={{0,12},{1,9},{2,14},{3,11},{4,8},{5,13},{6,10},{7,15},{8,4},{9,1},... | collective-permute-start | bytes 196616 | tf_op jit(solution)/shard_map/ppermute | solution.py:134
  29.5 0.0 collective-permute-start.10
  29.5 3.9 %collective-permute-start.9 = (bf16[32,1024]{1,0:T(8,128)(2,1)S(1)}, bf16[32,1024]{1,0:T(8,128)(2,1)S(1)}, u32[]{:S(2)}, u32[]{:S(2)}) collective-permute-start(bf16[32,1024]{1,0:T(8,128)(2,1)S(1)} %get-tuple-element.36), channel_id=1, source_target_pairs={{0,4},{1,1},{2,6},{3,3},{4,0},{5,5},{6,2},{7,7},{8,12},{9,9},{10,1... | collective-permute-start | bytes 196616 | tf_op jit(solution)/shard_map/ppermute | solution.py:134
  33.4 0.0 collective-permute-done.8
  33.4 0.0 collective-permute-done.7
  33.5 1.2 %collective-permute-done.10 = bf16[32,1024]{1,0:T(8,128)(2,1)S(1)} collective-permute-done((bf16[32,1024]{1,0:T(8,128)(2,1)S(1)}, bf16[32,1024]{1,0:T(8,128)(2,1)S(1)}, u32[]{:S(2)}, u32[]{:S(2)}) %collective-permute-start.10) | collective-permute-done | bytes 65568 | tf_op jit(solution)/shard_map/ppermute | solution.py:134
  34.7 1.0 %collective-permute-done.9 = bf16[32,1024]{1,0:T(8,128)(2,1)S(1)} collective-permute-done((bf16[32,1024]{1,0:T(8,128)(2,1)S(1)}, bf16[32,1024]{1,0:T(8,128)(2,1)S(1)}, u32[]{:S(2)}, u32[]{:S(2)}) %collective-permute-start.9) | collective-permute-done | bytes 65568 | tf_op jit(solution)/shard_map/ppermute | solution.py:134
  35.7 0.1 collective-permute-start.11
  35.8 1.2 %collective-permute-done.11.other_ref = bf16[32,1024]{1,0:T(8,128)(2,1)S(1)} collective-permute-done((bf16[32,1024]{1,0:T(8,128)(2,1)S(1)}, bf16[32,1024]{1,0:T(8,128)(2,1)S(1)}, u32[]{:S(2)}, u32[]{:S(2)}) %collective-permute-start.11) | collective-permute-done | bytes 65568 | tf_op jit(solution)/shard_map/ppermute | solution.py:127
  37.0 0.0 copy-done
  37.0 1.1 %shard_map.77 = bf16[32,1024]{1,0:T(8,128)(2,1)} custom-call(f32[32,1024]{1,0:T(8,128)S(1)} %get-tuple-element.34.keep_ref, bf16[32,1024]{1,0:T(8,128)(2,1)S(1)} %collective-permute-done.11.other_ref, bf16[1024,1024]{1,0:T(8,128)(2,1)S(1)} %copy-done), custom_call_target="tpu_custom_call" | custom-call | flops 67108864 | bytes 2097152 | tf_op jit(solution)/shard_map/pallas_call | solution.py:22
  (9 shorter events, 0.2 us)
Async XLA Ops:
  2.7 1.4 %collective-permute-start = (bf16[32,1024]{1,0:T(8,128)(2,1)S(1)}, bf16[32,1024]{1,0:T(8,128)(2,1)S(1)}, u32[]{:S(2)}, u32[]{:S(2)}) collective-permute-start(bf16[32,1024]{1,0:T(8,128)(2,1)S(1)} %get-tuple-element.20), channel_id=1, source_target_pairs={{0,1},{1,0},{2,3},{3,2},{4,5},{5,4},{6,7},{7,6},{8,9},{9,8},{10,11... | collective-permute-start | bytes 196616 | tf_op jit(solution)/shard_map/ppermute | solution.py:127
  4.2 12.7 %collective-permute-start.4 = (bf16[32,1152]{1,0:T(8,128)(2,1)S(1)}, bf16[32,1152]{1,0:T(8,128)(2,1)S(1)}, u32[]{:S(2)}, u32[]{:S(2)}) collective-permute-start(bf16[32,1152]{1,0:T(8,128)(2,1)S(1)} %pad_maximum_fusion.after_ref), channel_id=1, source_target_pairs={{0,6},{1,3},{2,4},{3,1},{4,2},{5,7},{6,0},{7,5},{8,14},{9,11},{10,... | collective-permute-start | bytes 221192 | tf_op jit(solution)/shard_map/ppermute | solution.py:134
  8.1 8.7 %collective-permute-start.3 = (bf16[32,1152]{1,0:T(8,128)(2,1)S(1)}, bf16[32,1152]{1,0:T(8,128)(2,1)S(1)}, u32[]{:S(2)}, u32[]{:S(2)}) collective-permute-start(bf16[32,1152]{1,0:T(8,128)(2,1)S(1)} %pad_maximum_fusion.after_ref), channel_id=1, source_target_pairs={{0,4},{1,1},{2,6},{3,3},{4,0},{5,5},{6,2},{7,7},{8,12},{9,9},{10,1... | collective-permute-start | bytes 221192 | tf_op jit(solution)/shard_map/ppermute | solution.py:134
  10.5 7.4 %collective-permute-start.2 = (bf16[32,1152]{1,0:T(8,128)(2,1)S(1)}, bf16[32,1152]{1,0:T(8,128)(2,1)S(1)}, u32[]{:S(2)}, u32[]{:S(2)}) collective-permute-start(bf16[32,1152]{1,0:T(8,128)(2,1)S(1)} %pad_maximum_fusion.after_ref), channel_id=1, source_target_pairs={{0,14},{1,11},{2,12},{3,9},{4,10},{5,15},{6,8},{7,13},{8,6},{9,3},... | collective-permute-start | bytes 221192 | tf_op jit(solution)/shard_map/ppermute | solution.py:134
  14.1 6.2 %collective-permute-start.1 = (bf16[32,1152]{1,0:T(8,128)(2,1)S(1)}, bf16[32,1152]{1,0:T(8,128)(2,1)S(1)}, u32[]{:S(2)}, u32[]{:S(2)}) collective-permute-start(bf16[32,1152]{1,0:T(8,128)(2,1)S(1)} %pad_maximum_fusion.after_ref), channel_id=1, source_target_pairs={{0,12},{1,9},{2,14},{3,11},{4,8},{5,13},{6,10},{7,15},{8,4},{9,1},... | collective-permute-start | bytes 221192 | tf_op jit(solution)/shard_map/ppermute | solution.py:134
  20.3 16.7 %copy-start = (bf16[1024,1024]{1,0:T(8,128)(2,1)S(1)}, bf16[1024,1024]{1,0:T(8,128)(2,1)}, u32[]{:S(2)}) copy-start(bf16[1024,1024]{1,0:T(8,128)(2,1)} %weight_ref.1) | copy-start | bytes 6291460
  20.3 1.4 %collective-permute-start.5 = (bf16[64,1152]{1,0:T(8,128)(2,1)S(1)}, bf16[64,1152]{1,0:T(8,128)(2,1)S(1)}, u32[]{:S(2)}, u32[]{:S(2)}) collective-permute-start(bf16[64,1152]{1,0:T(8,128)(2,1)S(1)} %maximum_maximum_fusion.own_ref), channel_id=1, source_target_pairs={{0,1},{1,0},{2,3},{3,2},{4,5},{5,4},{6,7},{7,6},{8,9},{9,8},{10,11... | collective-permute-start | bytes 442376 | tf_op jit(solution)/shard_map/ppermute | solution.py:127
  23.2 1.4 %collective-permute-start.6 = (bf16[64,1024]{1,0:T(8,128)(2,1)S(1)}, bf16[64,1024]{1,0:T(8,128)(2,1)S(1)}, u32[]{:S(2)}, u32[]{:S(2)}) collective-permute-start(bf16[64,1024]{1,0:T(8,128)(2,1)S(1)} %get-tuple-element.32), channel_id=1, source_target_pairs={{0,1},{1,0},{2,3},{3,2},{4,5},{5,4},{6,7},{7,6},{8,9},{9,8},{10,11... | collective-permute-start | bytes 393224 | tf_op jit(solution)/shard_map/ppermute | solution.py:127
  24.7 8.7 %collective-permute-start.8 = (bf16[32,1024]{1,0:T(8,128)(2,1)S(1)}, bf16[32,1024]{1,0:T(8,128)(2,1)S(1)}, u32[]{:S(2)}, u32[]{:S(2)}) collective-permute-start(bf16[32,1024]{1,0:T(8,128)(2,1)S(1)} %get-tuple-element.35), channel_id=1, source_target_pairs={{0,14},{1,11},{2,12},{3,9},{4,10},{5,15},{6,8},{7,13},{8,6},{9,3},... | collective-permute-start | bytes 196616 | tf_op jit(solution)/shard_map/ppermute | solution.py:134
  26.5 6.9 %collective-permute-start.7 = (bf16[32,1024]{1,0:T(8,128)(2,1)S(1)}, bf16[32,1024]{1,0:T(8,128)(2,1)S(1)}, u32[]{:S(2)}, u32[]{:S(2)}) collective-permute-start(bf16[32,1024]{1,0:T(8,128)(2,1)S(1)} %get-tuple-element.35), channel_id=1, source_target_pairs={{0,12},{1,9},{2,14},{3,11},{4,8},{5,13},{6,10},{7,15},{8,4},{9,1},... | collective-permute-start | bytes 196616 | tf_op jit(solution)/shard_map/ppermute | solution.py:134
  29.5 5.2 %collective-permute-start.10 = (bf16[32,1024]{1,0:T(8,128)(2,1)S(1)}, bf16[32,1024]{1,0:T(8,128)(2,1)S(1)}, u32[]{:S(2)}, u32[]{:S(2)}) collective-permute-start(bf16[32,1024]{1,0:T(8,128)(2,1)S(1)} %get-tuple-element.36), channel_id=1, source_target_pairs={{0,6},{1,3},{2,4},{3,1},{4,2},{5,7},{6,0},{7,5},{8,14},{9,11},{10,... | collective-permute-start | bytes 196616 | tf_op jit(solution)/shard_map/ppermute | solution.py:134
  29.5 6.1 %collective-permute-start.9 = (bf16[32,1024]{1,0:T(8,128)(2,1)S(1)}, bf16[32,1024]{1,0:T(8,128)(2,1)S(1)}, u32[]{:S(2)}, u32[]{:S(2)}) collective-permute-start(bf16[32,1024]{1,0:T(8,128)(2,1)S(1)} %get-tuple-element.36), channel_id=1, source_target_pairs={{0,4},{1,1},{2,6},{3,3},{4,0},{5,5},{6,2},{7,7},{8,12},{9,9},{10,1... | collective-permute-start | bytes 196616 | tf_op jit(solution)/shard_map/ppermute | solution.py:134
  35.7 1.3 %collective-permute-start.11 = (bf16[32,1024]{1,0:T(8,128)(2,1)S(1)}, bf16[32,1024]{1,0:T(8,128)(2,1)S(1)}, u32[]{:S(2)}, u32[]{:S(2)}) collective-permute-start(bf16[32,1024]{1,0:T(8,128)(2,1)S(1)} %get-tuple-element.33), channel_id=1, source_target_pairs={{0,1},{1,0},{2,3},{3,2},{4,5},{5,4},{6,7},{7,6},{8,9},{9,8},{10,11... | collective-permute-start | bytes 196616 | tf_op jit(solution)/shard_map/ppermute | solution.py:127

commit v7 on v2

v7 whole, which is shorter than its diff:
```python
import jax
import jax.numpy as jnp
from jax import lax
from jax.experimental import pallas as pl
from jax.experimental.pallas import tpu as pltpu
from jax.sharding import PartitionSpec as P

BF16, F32 = jnp.bfloat16, jnp.float32
NT = (((1,), (1,)), ((), ()))
NN = (((1,), (0,)), ((), ()))
VMEM_LIMIT = 24 << 20
LANES = 128
CHUNKS = 2


def hbm(x):
    return pltpu.with_memory_space_constraint(x, pltpu.HBM)


def vmem(x):
    return pltpu.with_memory_space_constraint(x, pltpu.VMEM)


def shaped(dtype, *shape):
    return jax.ShapeDtypeStruct(shape, dtype)


def kernel_call(body, out_shape, args, in_hbm, scratch, flops, moved, out_space=pltpu.VMEM):
    def spec(space):
        return pl.BlockSpec(memory_space=space)

    return pl.pallas_call(
        body,
        out_shape=out_shape,
        in_specs=[spec(pltpu.HBM if i in in_hbm else pltpu.VMEM) for i in range(len(args))],
        out_specs=jax.tree.map(lambda _: spec(out_space), out_shape),
        scratch_shapes=scratch,
        compiler_params=pltpu.CompilerParams(vmem_limit_bytes=VMEM_LIMIT),
        cost_estimate=pl.CostEstimate(flops=flops, bytes_accessed=moved, transcendentals=0),
    )(*args)


def dot(a, b, dims):
    return lax.dot_general(a, b, dims, preferred_element_type=F32)


def half_at(own, half):
    odd = lax.axis_index("tp") % 2
    return pl.multiple_of((odd if own else 1 - odd) * half, half)


def down_kernel(own, tokens_hbm, weight_hbm, out_ref, tokens, weight, sems):
    half = out_ref.shape[1]
    size = half // CHUNKS
    load = pltpu.make_async_copy(tokens_hbm, tokens, sems.at[CHUNKS])
    load.start()
    chunks = []
    for i in range(CHUNKS):
        start = pl.multiple_of(half_at(own, half) + i * size, size)
        chunks.append(
            pltpu.make_async_copy(
                weight_hbm.at[pl.ds(start, size), :],
                weight.at[pl.ds(i * size, size), :],
                sems.at[i],
            )
        )
        chunks[i].start()
    load.wait()
    x = tokens[...]
    for i in range(CHUNKS):
        chunks[i].wait()
        at = slice(i * size, (i + 1) * size)
        out_ref[:, at] = dot(x, weight[at, :], NT).astype(out_ref.dtype)


def load_kernel(
    after_ref, routes_hbm, scale_hbm, up_hbm, down_hbm, terms_ref, up_ref, down_ref,
    routes, scale, sems,
):
    pairs = [(routes_hbm, routes), (scale_hbm, scale), (up_hbm, up_ref), (down_hbm, down_ref)]
    copies = [pltpu.make_async_copy(a, b, sems.at[i]) for i, (a, b) in enumerate(pairs)]
    for copy in copies:
        copy.start()
    copies[0].wait()
    copies[1].wait()
    rows, width = terms_ref.shape
    row = lax.broadcasted_iota(jnp.int32, (width, rows), 0)
    experts_all = width // 2
    expert = jnp.where(row < experts_all, row, row - experts_all)
    combine = jnp.zeros((width, rows), F32)
    for r in range(routes.shape[0]):
        combine += jnp.where(expert == routes[r : r + 1, :], scale[r : r + 1, :], 0.0)
    high = combine.astype(BF16).astype(F32)
    combine = jnp.where(row < experts_all, high, combine - high)
    combine = jnp.concatenate([combine, jnp.zeros((width, LANES - rows), F32)], axis=1)
    terms_ref[...] = combine.T[:rows, :].astype(BF16)
    copies[2].wait()
    copies[3].wait()


def first_kernel(messages_ref, up_ref, pre_ref):
    local_count, units, latent_len = up_ref.shape
    half = latent_len // 2
    rows = messages_ref[:, :half]
    for k in range(local_count):
        weight = up_ref[k, :, pl.ds(half_at(True, half), half)]
        pre_ref[:, k * units : (k + 1) * units] = dot(rows, weight, NT)


def second_kernel(messages_ref, other_ref, pre_ref, up_ref, down_ref, hidden_ref, theirs_ref):
    local_count, units, latent_len = up_ref.shape
    half = latent_len // 2
    terms = messages_ref[:, half:].astype(F32)
    lane = lax.broadcasted_iota(jnp.int32, terms.shape, 1)
    first = lax.axis_index("exp") * local_count
    rows = other_ref[...]
    for k in range(local_count):
        named = (lane == first + k) | (lane == first + k + terms.shape[1] // 2)
        weight = jnp.sum(jnp.where(named, terms, 0.0), axis=1, keepdims=True)
        at = slice(k * units, (k + 1) * units)
        pre_act = pre_ref[:, at] + dot(rows, up_ref[k, :, pl.ds(half_at(False, half), half)], NT)
        active = jnp.maximum(pre_act, 0.0)
        hidden_ref[:, at] = (active * active * weight).astype(BF16)
    theirs = dot(hidden_ref[...], down_ref[:, pl.ds(half_at(False, half), half)], NN)
    theirs_ref[...] = theirs.astype(BF16)


def third_kernel(hidden_ref, down_ref, mine_ref):
    half = mine_ref.shape[1]
    mine_ref[...] = dot(hidden_ref[...], down_ref[:, pl.ds(half_at(True, half), half)], NN)


def up_own_kernel(own_ref, weight_ref, out_ref):
    half = own_ref.shape[1]
    out_ref[...] = dot(own_ref[...], weight_ref[pl.ds(half_at(True, half), half), :], NN)


def up_kernel(part_ref, other_ref, weight_ref, out_hbm, out, sems):
    other = other_ref[...]
    at_rows = pl.ds(half_at(False, other.shape[1]), other.shape[1])
    half = out.shape[1] // 2
    copies = []
    for i in range(2):
        at = slice(i * half, (i + 1) * half)
        out[:, at] = (part_ref[:, at] + dot(other, weight_ref[at_rows, at], NN)).astype(BF16)
        copies.append(pltpu.make_async_copy(out.at[:, at], out_hbm.at[:, at], sems.at[i]))
        copies[i].start()
    for copy in copies:
        copy.wait()


def on_device(tokens, lat_down, lat_up, expert_up, expert_down, routes, route_weights):
    exp_count, tp_count = lax.axis_size("exp"), lax.axis_size("tp")
    local_count, units, latent_len = expert_up.shape
    rows, width = tokens.shape
    half = latent_len // 2
    all_rows = exp_count * rows
    all_units = local_count * units
    out_len = lat_up.shape[1]
    terms_len = -(-2 * local_count * exp_count // LANES) * LANES
    pair_masks = [1 << b for b in range(1, tp_count.bit_length() - 1)]

    def traded(x, axis, mask):
        return lax.ppermute(x, axis, [(i, i ^ mask) for i in range(lax.axis_size(axis))])

    def across(x):
        for mask in pair_masks:
            x = x + traded(x.astype(BF16), "tp", mask).astype(F32)
        return x

    def down_half(own, dtype):
        return kernel_call(
            lambda *refs: down_kernel(own, *refs),
            shaped(dtype, rows, half),
            (hbm(tokens), hbm(lat_down)),
            (0, 1),
            [
                pltpu.VMEM((rows, width), BF16),
                pltpu.VMEM((half, width), BF16),
                pltpu.SemaphoreType.DMA((CHUNKS + 1,)),
            ],
            2 * rows * width * half,
            2 * width * half,
        )

    theirs = down_half(False, BF16)
    mine = down_half(True, F32)
    mine = mine + traded(theirs, "tp", 1).astype(F32)
    down_rows = expert_down.reshape(all_units, latent_len)
    terms, up_here, down_here = kernel_call(
        load_kernel,
        (
            shaped(BF16, rows, terms_len),
            pltpu.VMEM(expert_up.shape, BF16),
            pltpu.VMEM(down_rows.shape, BF16),
        ),
        (mine.astype(BF16), *(hbm(x) for x in (routes.T, route_weights.T, expert_up, down_rows))),
        (1, 2, 3, 4),
        [
            pltpu.VMEM(routes.shape[::-1], jnp.int32),
            pltpu.VMEM(routes.shape[::-1], F32),
            pltpu.SemaphoreType.DMA((4,)),
        ],
        0,
        4 * latent_len * all_units,
    )
    up_here, down_here = vmem(up_here), vmem(down_here)
    message = jnp.concatenate([across(mine).astype(BF16), terms], axis=1)
    messages = [message] + [traded(message, "exp", s) for s in range(1, exp_count)]
    messages = jnp.concatenate(messages, axis=0)
    other = traded(messages[:, :half], "tp", 1)
    pre = kernel_call(
        first_kernel,
        shaped(F32, all_rows, all_units),
        (messages, up_here),
        (),
        [],
        all_rows * latent_len * all_units,
        latent_len * all_units,
    )
    hidden, theirs = kernel_call(
        second_kernel,
        (shaped(BF16, all_rows, all_units), shaped(BF16, all_rows, half)),
        (messages, other, pre, up_here, down_here),
        (),
        [],
        2 * all_rows * latent_len * all_units,
        2 * latent_len * all_units,
    )
    mine = kernel_call(
        third_kernel,
        shaped(F32, all_rows, half),
        (hidden, down_here),
        (),
        [],
        all_rows * latent_len * all_units,
        latent_len * all_units,
    )
    part = (mine + traded(theirs, "tp", 1).astype(F32)).astype(BF16)
    blocks = part.reshape(exp_count, rows, half)
    mixed = blocks[0].astype(F32)
    for s in range(1, exp_count):
        mixed = mixed + traded(blocks[s], "exp", s).astype(F32)
    mixed = across(mixed).astype(BF16)
    lat_up = vmem(lat_up)
    own_part = kernel_call(
        up_own_kernel,
        shaped(F32, rows, out_len),
        (mixed, lat_up),
        (),
        [],
        rows * latent_len * out_len,
        latent_len * out_len,
    )
    return kernel_call(
        up_kernel,
        shaped(BF16, rows, out_len),
        (own_part, traded(mixed, "tp", 1), lat_up),
        (),
        [pltpu.VMEM((rows, out_len), BF16), pltpu.SemaphoreType.DMA((2,))],
        rows * latent_len * out_len,
        latent_len * out_len,
        pltpu.HBM,
    )


def solution(mesh):
    return jax.shard_map(
        on_device,
        mesh=mesh,
        in_specs=(
            P(("grp", "exp"), "tp"),
            P(None, "tp"),
            P(None, "tp"),
            P("exp", "tp", None),
            P("exp", "tp", None),
            P(("grp", "exp"), None),
            P(("grp", "exp"), None),
        ),
        out_specs=P(("grp", "exp"), "tp"),
        check_vma=False,
    )
```

time: 63.7 us -> 36.8 us (0.58)
  blocking collectives: 19.3 us -> 0 us
  Pallas kernels: 0 us -> 9.6 us
  matrix products: 8.92 us -> 0 us
  waiting for transfers between devices: 18.3 us -> 14 us
  local copies, waits for them, and re-layouts: 2.06 us -> 0.03 us
  other arithmetic: 1.36 us -> 0.12 us
    all_to_all x2 -> x0, blocking collectives: 19.3 us -> none  [swap(): return lax.all_to_all(blocks, axes, split_axis=0, concat_axis=0, tiled=True)]
    all_to_all x3 -> x0, waiting for transfers between devices: 18.3 us -> none  [swap(): return lax.all_to_all(blocks, axes, split_axis=0, concat_axis=0, tiled=True)]
    ppermute x0 -> x12, waiting for transfers between devices: none -> 14 us  [traded(): lax.ppermute(x, axis, [(i, i ^ mask) for i in range(lax.axis_size(axis))])]
    all_to_all x3 -> x0, starting transfers between devices: 13.1 us -> none  [swap(): return lax.all_to_all(blocks, axes, split_axis=0, concat_axis=0, tiled=True)]
    ppermute x0 -> x12, starting transfers between devices: none -> 12.7 us  [traded(): lax.ppermute(x, axis, [(i, i ^ mask) for i in range(lax.axis_size(axis))])]
    pallas_call x0 -> x8, Pallas kernels: none -> 9.6 us  [kernel_call(): pl.pallas_call(body, out_shape=out_shape, in_specs=[spec(pltpu.HBM if i i...]
    dot_general x3 -> x0, matrix products: 8.92 us -> none  [the longest x1 3.74 us: on_device(): jnp.einsum('kth,khl->tl', hidden.astype(jnp.bfloat16), expert_down, prefe...]
    reduce_sum x3 -> x0, other arithmetic: 1.36 us -> none  [the longest x1 1.3 us: on_device(): combine = jnp.sum(jnp.where(named, route_weights[:, :, None], 0.0), axis=1)]
  transfers between devices with their start and end apart: 3 -> 12, of which waited for: 3 -> 9; matrix products, arithmetic and copies ran while one was open for 2% -> 0% of each run, Pallas kernels for 0% -> 16%
where the time goes in v7:
time: 36.8 us; the launch traced here: 36.6 us
  waiting for transfers between devices  14 us (38%)
  starting transfers between devices  12.7 us (35%)
  Pallas kernels  9.6 us (26%)
    ppermute x12, waiting for transfers between devices, traded(): lax.ppermute(x, axis, [(i, i ^ mask) for i in range(lax.axis_size(axis))])  14 us
    ppermute x12, starting transfers between devices, traded(): lax.ppermute(x, axis, [(i, i ^ mask) for i in range(lax.axis_size(axis))])  12.7 us
    pallas_call x8, Pallas kernels, kernel_call(): pl.pallas_call(body, out_shape=out_shape, in_specs=[spec(pltpu.HBM if i i...  9.6 us
  transfers between devices with their start and end apart: 12, of which 9 were waited for; matrix products, arithmetic and copies ran while one was open for 0% of the time, Pallas kernels for 16%

profile of v7, /device:TPU:0, one launch (start us, length us, event | category | flops | bytes accessed | tf_op | source)
XLA Modules:
  0.0 36.6 jit_solution(14472244512480357410)
XLA Ops:
  0.0 1.9 %shard_map.74 = bf16[32,512]{1,0:T(8,128)(2,1)S(1)} custom-call(bf16[32,1024]{1,0:T(8,128)(2,1)} %refs_0_.3, bf16[1024,1024]{1,0:T(8,128)(2,1)} %refs_1_.3), custom_call_target="tpu_custom_call" | custom-call | flops 33554432 | bytes 1048576 | tf_op jit(solution)/shard_map/pallas_call | solution.py:32
  1.9 0.5 %collective-permute-start = (bf16[32,512]{1,0:T(8,128)(2,1)S(1)}, bf16[32,512]{1,0:T(8,128)(2,1)S(1)}, u32[]{:S(2)}, u32[]{:S(2)}) collective-permute-start(bf16[32,512]{1,0:T(8,128)(2,1)S(1)} %shard_map.74), channel_id=1, source_target_pairs={{0,1},{1,0},{2,3},{3,2},{4,5},{5,4},{6,7},{7,6},{8,9},{9,8},{10,11... | collective-permute-start | bytes 98312 | tf_op jit(solution)/shard_map/ppermute | solution.py:164
  2.4 1.9 %shard_map.73 = f32[32,512]{1,0:T(8,128)S(1)} custom-call(bf16[32,1024]{1,0:T(8,128)(2,1)} %refs_0_.3, bf16[1024,1024]{1,0:T(8,128)(2,1)} %refs_1_.3), custom_call_target="tpu_custom_call" | custom-call | flops 33554432 | bytes 1048576 | tf_op jit(solution)/shard_map/pallas_call | solution.py:32
  4.3 0.0 collective-permute-done
  4.3 2.6 %collective-permute-start.1 = (bf16[32,512]{1,0:T(8,128)(2,1)S(1)}, bf16[32,512]{1,0:T(8,128)(2,1)S(1)}, u32[]{:S(2)}, u32[]{:S(2)}) collective-permute-start(bf16[32,512]{1,0:T(8,128)(2,1)S(1)} %fusion.after_ref), channel_id=1, source_target_pairs={{0,2},{1,3},{2,0},{3,1},{4,6},{5,7},{6,4},{7,5},{8,10},{9,11},{10,... | collective-permute-start | bytes 98312 | tf_op jit(solution)/shard_map/ppermute | solution.py:164
  6.9 2.7 %shard_map.75 = (bf16[32,128]{1,0:T(8,128)(2,1)S(1)}, bf16[2,672,1024]{2,1,0:T(8,128)(2,1)S(1)}, bf16[1344,1024]{1,0:T(8,128)(2,1)S(1)}) custom-call(bf16[32,512]{1,0:T(8,128)(2,1)S(1)} %fusion.after_ref, s32[4,32]{1,0:T(4,128)} %bitcast.4, f32[4,32]{1,0:T(4,128)} %bitcast.5, bf16[2,672,1024]{2,1,0:T(8,128)(2,1)} %up_hbm.1, bf16[1344,1024]{1,0:T(8,128)(2,1)} %bitcast.3), custom_call_target="tpu_custom_call" | custom-call | bytes 5505024 | tf_op jit(solution)/shard_map/pallas_call | solution.py:32
  9.6 0.0 collective-permute-done.1
  9.6 3.7 %collective-permute-start.4 = (bf16[32,640]{1,0:T(8,128)(2,1)S(1)}, bf16[32,640]{1,0:T(8,128)(2,1)S(1)}, u32[]{:S(2)}, u32[]{:S(2)}) collective-permute-start(bf16[32,640]{1,0:T(8,128)(2,1)S(1)} %pad_maximum_fusion.1), channel_id=1, source_target_pairs={{0,12},{4,8},{8,4},{12,0},{1,13},{5,9},{9,5},{13,1},{2,14},{6,10},... | collective-permute-start | bytes 122888 | tf_op jit(solution)/shard_map/ppermute | solution.py:164
  13.3 0.0 collective-permute-start.3
  13.3 0.8 %collective-permute-start.2 = (bf16[32,640]{1,0:T(8,128)(2,1)S(1)}, bf16[32,640]{1,0:T(8,128)(2,1)S(1)}, u32[]{:S(2)}, u32[]{:S(2)}) collective-permute-start(bf16[32,640]{1,0:T(8,128)(2,1)S(1)} %pad_maximum_fusion.1), channel_id=1, source_target_pairs={{0,4},{4,0},{8,12},{12,8},{1,5},{5,1},{9,13},{13,9},{2,6},{6,2},{1... | collective-permute-start | bytes 122888 | tf_op jit(solution)/shard_map/ppermute | solution.py:164
  14.1 1.5 %collective-permute-done.4 = bf16[32,640]{1,0:T(8,128)(2,1)S(1)} collective-permute-done((bf16[32,640]{1,0:T(8,128)(2,1)S(1)}, bf16[32,640]{1,0:T(8,128)(2,1)S(1)}, u32[]{:S(2)}, u32[]{:S(2)}) %collective-permute-start.4) | collective-permute-done | bytes 40992 | tf_op jit(solution)/shard_map/ppermute | solution.py:164
  15.6 2.7 %collective-permute-done.3 = bf16[32,640]{1,0:T(8,128)(2,1)S(1)} collective-permute-done((bf16[32,640]{1,0:T(8,128)(2,1)S(1)}, bf16[32,640]{1,0:T(8,128)(2,1)S(1)}, u32[]{:S(2)}, u32[]{:S(2)}) %collective-permute-start.3) | collective-permute-done | bytes 40992 | tf_op jit(solution)/shard_map/ppermute | solution.py:164
  18.2 0.1 collective-permute-start.5
  18.3 0.7 %shard_map.76.pre_ref = f32[128,1344]{1,0:T(8,128)S(1)} custom-call(bf16[128,640]{1,0:T(8,128)(2,1)S(1)} %pad_maximum_fusion.messages_ref, bf16[2,672,1024]{2,1,0:T(8,128)(2,1)S(1)} %get-tuple-element.11.up_ref), custom_call_target="tpu_custom_call" | custom-call | flops 176160768 | bytes 1376256 | tf_op jit(solution)/shard_map/pallas_call | solution.py:32
  19.0 0.7 %collective-permute-done.5.other_ref = bf16[128,512]{1,0:T(8,128)(2,1)S(1)} collective-permute-done((bf16[128,512]{1,0:T(8,128)(2,1)S(1)}, bf16[128,512]{1,0:T(8,128)(2,1)S(1)}, u32[]{:S(2)}, u32[]{:S(2)}) %collective-permute-start.5) | collective-permute-done | bytes 131104 | tf_op jit(solution)/shard_map/ppermute | solution.py:164
  19.7 0.9 %shard_map.77 = (bf16[128,1344]{1,0:T(8,128)(2,1)S(1)}, bf16[128,512]{1,0:T(8,128)(2,1)S(1)}) custom-call(bf16[128,640]{1,0:T(8,128)(2,1)S(1)} %pad_maximum_fusion.messages_ref, bf16[128,512]{1,0:T(8,128)(2,1)S(1)} %collective-permute-done.5.other_ref, f32[128,1344]{1,0:T(8,128)S(1)} %shard_map.76.pre_ref, ...), custom_call_target="tpu_custom_call" | custom-call | flops 352321536 | bytes 2752512 | tf_op jit(solution)/shard_map/pallas_call | solution.py:32
  20.6 0.0 copy-start
  20.6 0.2 collective-permute-start.6
  20.8 0.4 %shard_map.78 = f32[128,512]{1,0:T(8,128)S(1)} custom-call(bf16[128,1344]{1,0:T(8,128)(2,1)S(1)} %get-tuple-element.13.hidden_ref, bf16[1344,1024]{1,0:T(8,128)(2,1)S(1)} %get-tuple-element.12.down_ref), custom_call_target="tpu_custom_call" | custom-call | flops 176160768 | bytes 1376256 | tf_op jit(solution)/shard_map/pallas_call | solution.py:32
  21.2 0.8 %collective-permute-done.6 = bf16[128,512]{1,0:T(8,128)(2,1)S(1)} collective-permute-done((bf16[128,512]{1,0:T(8,128)(2,1)S(1)}, bf16[128,512]{1,0:T(8,128)(2,1)S(1)}, u32[]{:S(2)}, u32[]{:S(2)}) %collective-permute-start.6) | collective-permute-done | bytes 131104 | tf_op jit(solution)/shard_map/ppermute | solution.py:164
  22.0 0.6 %collective-permute-start.7 = (bf16[32,512]{1,0:T(8,128)(2,1)S(1)}, bf16[32,512]{1,0:T(8,128)(2,1)S(1)}, u32[]{:S(2)}, u32[]{:S(2)}) collective-permute-start(bf16[32,512]{1,0:T(8,128)(2,1)S(1)} %get-tuple-element.15), channel_id=1, source_target_pairs={{0,4},{4,0},{8,12},{12,8},{1,5},{5,1},{9,13},{13,9},{2,6},{6,2},{1... | collective-permute-start | bytes 98312 | tf_op jit(solution)/shard_map/ppermute | solution.py:164
  22.6 2.9 %collective-permute-start.9 = (bf16[32,512]{1,0:T(8,128)(2,1)S(1)}, bf16[32,512]{1,0:T(8,128)(2,1)S(1)}, u32[]{:S(2)}, u32[]{:S(2)}) collective-permute-start(bf16[32,512]{1,0:T(8,128)(2,1)S(1)} %get-tuple-element.16), channel_id=1, source_target_pairs={{0,12},{4,8},{8,4},{12,0},{1,13},{5,9},{9,5},{13,1},{2,14},{6,10},... | collective-permute-start | bytes 98312 | tf_op jit(solution)/shard_map/ppermute | solution.py:164
  25.6 0.0 collective-permute-start.8
  25.6 0.4 %collective-permute-done.7 = bf16[32,512]{1,0:T(8,128)(2,1)S(1)} collective-permute-done((bf16[32,512]{1,0:T(8,128)(2,1)S(1)}, bf16[32,512]{1,0:T(8,128)(2,1)S(1)}, u32[]{:S(2)}, u32[]{:S(2)}) %collective-permute-start.7) | collective-permute-done | bytes 32800 | tf_op jit(solution)/shard_map/ppermute | solution.py:164
  26.0 2.3 %collective-permute-done.9 = bf16[32,512]{1,0:T(8,128)(2,1)S(1)} collective-permute-done((bf16[32,512]{1,0:T(8,128)(2,1)S(1)}, bf16[32,512]{1,0:T(8,128)(2,1)S(1)}, u32[]{:S(2)}, u32[]{:S(2)}) %collective-permute-start.9) | collective-permute-done | bytes 32800 | tf_op jit(solution)/shard_map/ppermute | solution.py:164
  28.3 2.0 %collective-permute-done.8 = bf16[32,512]{1,0:T(8,128)(2,1)S(1)} collective-permute-done((bf16[32,512]{1,0:T(8,128)(2,1)S(1)}, bf16[32,512]{1,0:T(8,128)(2,1)S(1)}, u32[]{:S(2)}, u32[]{:S(2)}) %collective-permute-start.8) | collective-permute-done | bytes 32800 | tf_op jit(solution)/shard_map/ppermute | solution.py:164
  30.4 1.3 %collective-permute-start.10 = (bf16[32,512]{1,0:T(8,128)(2,1)S(1)}, bf16[32,512]{1,0:T(8,128)(2,1)S(1)}, u32[]{:S(2)}, u32[]{:S(2)}) collective-permute-start(bf16[32,512]{1,0:T(8,128)(2,1)S(1)} %fusion.1), channel_id=1, source_target_pairs={{0,2},{1,3},{2,0},{3,1},{4,6},{5,7},{6,4},{7,5},{8,10},{9,11},{10,... | collective-permute-start | bytes 98312 | tf_op jit(solution)/shard_map/ppermute | solution.py:164
  31.7 2.7 %collective-permute-done.10 = bf16[32,512]{1,0:T(8,128)(2,1)S(1)} collective-permute-done((bf16[32,512]{1,0:T(8,128)(2,1)S(1)}, bf16[32,512]{1,0:T(8,128)(2,1)S(1)}, u32[]{:S(2)}, u32[]{:S(2)}) %collective-permute-start.10) | collective-permute-done | bytes 32800 | tf_op jit(solution)/shard_map/ppermute | solution.py:164
  34.4 0.1 collective-permute-start.11
  34.5 0.3 shard_map.79.part_ref
  34.8 0.9 %collective-permute-done.11.other_ref = bf16[32,512]{1,0:T(8,128)(2,1)S(1)} collective-permute-done((bf16[32,512]{1,0:T(8,128)(2,1)S(1)}, bf16[32,512]{1,0:T(8,128)(2,1)S(1)}, u32[]{:S(2)}, u32[]{:S(2)}) %collective-permute-start.11) | collective-permute-done | bytes 32800 | tf_op jit(solution)/shard_map/ppermute | solution.py:164
  35.7 0.9 %shard_map.80 = bf16[32,1024]{1,0:T(8,128)(2,1)} custom-call(f32[32,1024]{1,0:T(8,128)S(1)} %shard_map.79.part_ref, bf16[32,512]{1,0:T(8,128)(2,1)S(1)} %collective-permute-done.11.other_ref, bf16[1024,1024]{1,0:T(8,128)(2,1)S(1)} %copy-done), custom_call_target="tpu_custom_call" | custom-call | flops 33554432 | bytes 1048576 | tf_op jit(solution)/shard_map/pallas_call | solution.py:32
  (11 shorter events, 0.1 us)
Async XLA Ops:
  1.9 2.4 %collective-permute-start = (bf16[32,512]{1,0:T(8,128)(2,1)S(1)}, bf16[32,512]{1,0:T(8,128)(2,1)S(1)}, u32[]{:S(2)}, u32[]{:S(2)}) collective-permute-start(bf16[32,512]{1,0:T(8,128)(2,1)S(1)} %shard_map.74), channel_id=1, source_target_pairs={{0,1},{1,0},{2,3},{3,2},{4,5},{5,4},{6,7},{7,6},{8,9},{9,8},{10,11... | collective-permute-start | bytes 98312 | tf_op jit(solution)/shard_map/ppermute | solution.py:164
  4.3 5.2 %collective-permute-start.1 = (bf16[32,512]{1,0:T(8,128)(2,1)S(1)}, bf16[32,512]{1,0:T(8,128)(2,1)S(1)}, u32[]{:S(2)}, u32[]{:S(2)}) collective-permute-start(bf16[32,512]{1,0:T(8,128)(2,1)S(1)} %fusion.after_ref), channel_id=1, source_target_pairs={{0,2},{1,3},{2,0},{3,1},{4,6},{5,7},{6,4},{7,5},{8,10},{9,11},{10,... | collective-permute-start | bytes 98312 | tf_op jit(solution)/shard_map/ppermute | solution.py:164
  9.6 5.9 %collective-permute-start.4 = (bf16[32,640]{1,0:T(8,128)(2,1)S(1)}, bf16[32,640]{1,0:T(8,128)(2,1)S(1)}, u32[]{:S(2)}, u32[]{:S(2)}) collective-permute-start(bf16[32,640]{1,0:T(8,128)(2,1)S(1)} %pad_maximum_fusion.1), channel_id=1, source_target_pairs={{0,12},{4,8},{8,4},{12,0},{1,13},{5,9},{9,5},{13,1},{2,14},{6,10},... | collective-permute-start | bytes 122888 | tf_op jit(solution)/shard_map/ppermute | solution.py:164
  13.3 4.9 %collective-permute-start.3 = (bf16[32,640]{1,0:T(8,128)(2,1)S(1)}, bf16[32,640]{1,0:T(8,128)(2,1)S(1)}, u32[]{:S(2)}, u32[]{:S(2)}) collective-permute-start(bf16[32,640]{1,0:T(8,128)(2,1)S(1)} %pad_maximum_fusion.1), channel_id=1, source_target_pairs={{0,8},{4,12},{8,0},{12,4},{1,9},{5,13},{9,1},{13,5},{2,10},{6,14},... | collective-permute-start | bytes 122888 | tf_op jit(solution)/shard_map/ppermute | solution.py:164
  13.3 4.9 %collective-permute-start.2 = (bf16[32,640]{1,0:T(8,128)(2,1)S(1)}, bf16[32,640]{1,0:T(8,128)(2,1)S(1)}, u32[]{:S(2)}, u32[]{:S(2)}) collective-permute-start(bf16[32,640]{1,0:T(8,128)(2,1)S(1)} %pad_maximum_fusion.1), channel_id=1, source_target_pairs={{0,4},{4,0},{8,12},{12,8},{1,5},{5,1},{9,13},{13,9},{2,6},{6,2},{1... | collective-permute-start | bytes 122888 | tf_op jit(solution)/shard_map/ppermute | solution.py:164
  18.2 1.4 %collective-permute-start.5 = (bf16[128,512]{1,0:T(8,128)(2,1)S(1)}, bf16[128,512]{1,0:T(8,128)(2,1)S(1)}, u32[]{:S(2)}, u32[]{:S(2)}) collective-permute-start(bf16[128,512]{1,0:T(8,128)(2,1)S(1)} %slice.24), channel_id=1, source_target_pairs={{0,1},{1,0},{2,3},{3,2},{4,5},{5,4},{6,7},{7,6},{8,9},{9,8},{10,11... | collective-permute-start | bytes 393224 | tf_op jit(solution)/shard_map/ppermute | solution.py:164
  20.6 13.9 %copy-start = (bf16[1024,1024]{1,0:T(8,128)(2,1)S(1)}, bf16[1024,1024]{1,0:T(8,128)(2,1)}, u32[]{:S(2)}) copy-start(bf16[1024,1024]{1,0:T(8,128)(2,1)} %weight_ref.3) | copy-start | bytes 6291460
  20.6 1.4 %collective-permute-start.6 = (bf16[128,512]{1,0:T(8,128)(2,1)S(1)}, bf16[128,512]{1,0:T(8,128)(2,1)S(1)}, u32[]{:S(2)}, u32[]{:S(2)}) collective-permute-start(bf16[128,512]{1,0:T(8,128)(2,1)S(1)} %get-tuple-element.14), channel_id=1, source_target_pairs={{0,1},{1,0},{2,3},{3,2},{4,5},{5,4},{6,7},{7,6},{8,9},{9,8},{10,11... | collective-permute-start | bytes 393224 | tf_op jit(solution)/shard_map/ppermute | solution.py:164
  22.0 4.0 %collective-permute-start.7 = (bf16[32,512]{1,0:T(8,128)(2,1)S(1)}, bf16[32,512]{1,0:T(8,128)(2,1)S(1)}, u32[]{:S(2)}, u32[]{:S(2)}) collective-permute-start(bf16[32,512]{1,0:T(8,128)(2,1)S(1)} %get-tuple-element.15), channel_id=1, source_target_pairs={{0,4},{4,0},{8,12},{12,8},{1,5},{5,1},{9,13},{13,9},{2,6},{6,2},{1... | collective-permute-start | bytes 98312 | tf_op jit(solution)/shard_map/ppermute | solution.py:164
  22.6 5.7 %collective-permute-start.9 = (bf16[32,512]{1,0:T(8,128)(2,1)S(1)}, bf16[32,512]{1,0:T(8,128)(2,1)S(1)}, u32[]{:S(2)}, u32[]{:S(2)}) collective-permute-start(bf16[32,512]{1,0:T(8,128)(2,1)S(1)} %get-tuple-element.16), channel_id=1, source_target_pairs={{0,12},{4,8},{8,4},{12,0},{1,13},{5,9},{9,5},{13,1},{2,14},{6,10},... | collective-permute-start | bytes 98312 | tf_op jit(solution)/shard_map/ppermute | solution.py:164
  25.6 4.8 %collective-permute-start.8 = (bf16[32,512]{1,0:T(8,128)(2,1)S(1)}, bf16[32,512]{1,0:T(8,128)(2,1)S(1)}, u32[]{:S(2)}, u32[]{:S(2)}) collective-permute-start(bf16[32,512]{1,0:T(8,128)(2,1)S(1)} %get-tuple-element.17), channel_id=1, source_target_pairs={{0,8},{4,12},{8,0},{12,4},{1,9},{5,13},{9,1},{13,5},{2,10},{6,14},... | collective-permute-start | bytes 98312 | tf_op jit(solution)/shard_map/ppermute | solution.py:164
  30.4 4.0 %collective-permute-start.10 = (bf16[32,512]{1,0:T(8,128)(2,1)S(1)}, bf16[32,512]{1,0:T(8,128)(2,1)S(1)}, u32[]{:S(2)}, u32[]{:S(2)}) collective-permute-start(bf16[32,512]{1,0:T(8,128)(2,1)S(1)} %fusion.1), channel_id=1, source_target_pairs={{0,2},{1,3},{2,0},{3,1},{4,6},{5,7},{6,4},{7,5},{8,10},{9,11},{10,... | collective-permute-start | bytes 98312 | tf_op jit(solution)/shard_map/ppermute | solution.py:164
  34.4 1.3 %collective-permute-start.11 = (bf16[32,512]{1,0:T(8,128)(2,1)S(1)}, bf16[32,512]{1,0:T(8,128)(2,1)S(1)}, u32[]{:S(2)}, u32[]{:S(2)}) collective-permute-start(bf16[32,512]{1,0:T(8,128)(2,1)S(1)} %add_convert_fusion.1.own_ref), channel_id=1, source_target_pairs={{0,1},{1,0},{2,3},{3,2},{4,5},{5,4},{6,7},{7,6},{8,9},{9,8},{10,11... | collective-permute-start | bytes 98312 | tf_op jit(solution)/shard_map/ppermute | solution.py:164

commit v8 on v7

--- a/solution.py
+++ b/solution.py
@@ -49,28 +49,37 @@
     return pl.multiple_of((odd if own else 1 - odd) * half, half)
 
 
-def down_kernel(own, tokens_hbm, weight_hbm, out_ref, tokens, weight, sems):
-    half = out_ref.shape[1]
+def down_kernel(tokens_hbm, weight_hbm, theirs_ref, tokens, mine_weight, weight, sems):
+    half = theirs_ref.shape[1]
     size = half // CHUNKS
-    load = pltpu.make_async_copy(tokens_hbm, tokens, sems.at[CHUNKS])
+    load = pltpu.make_async_copy(tokens_hbm, tokens, sems.at[0])
     load.start()
     chunks = []
     for i in range(CHUNKS):
-        start = pl.multiple_of(half_at(own, half) + i * size, size)
+        start = pl.multiple_of(half_at(False, half) + i * size, size)
         chunks.append(
             pltpu.make_async_copy(
                 weight_hbm.at[pl.ds(start, size), :],
                 weight.at[pl.ds(i * size, size), :],
-                sems.at[i],
+                sems.at[2 + i],
             )
         )
         chunks[i].start()
+    later = pltpu.make_async_copy(
+        weight_hbm.at[pl.ds(half_at(True, half), half), :], mine_weight, sems.at[1]
+    )
+    later.start()
     load.wait()
     x = tokens[...]
     for i in range(CHUNKS):
         chunks[i].wait()
         at = slice(i * size, (i + 1) * size)
-        out_ref[:, at] = dot(x, weight[at, :], NT).astype(out_ref.dtype)
+        theirs_ref[:, at] = dot(x, weight[at, :], NT).astype(BF16)
+    later.wait()
+
+
+def down_own_kernel(tokens_ref, weight_ref, mine_ref):
+    mine_ref[...] = dot(tokens_ref[...], weight_ref[...], NT)
 
 
 def load_kernel(
@@ -168,23 +177,28 @@
             x = x + traded(x.astype(BF16), "tp", mask).astype(F32)
         return x
 
-    def down_half(own, dtype):
-        return kernel_call(
-            lambda *refs: down_kernel(own, *refs),
-            shaped(dtype, rows, half),
-            (hbm(tokens), hbm(lat_down)),
-            (0, 1),
-            [
-                pltpu.VMEM((rows, width), BF16),
-                pltpu.VMEM((half, width), BF16),
-                pltpu.SemaphoreType.DMA((CHUNKS + 1,)),
-            ],
-            2 * rows * width * half,
-            2 * width * half,
-        )
-
-    theirs = down_half(False, BF16)
-    mine = down_half(True, F32)
+    theirs, tokens_here, weight_here = kernel_call(
+        down_kernel,
+        (
+            shaped(BF16, rows, half),
+            pltpu.VMEM((rows, width), BF16),
+            pltpu.VMEM((half, width), BF16),
+        ),
+        (hbm(tokens), hbm(lat_down)),
+        (0, 1),
+        [pltpu.VMEM((half, width), BF16), pltpu.SemaphoreType.DMA((CHUNKS + 2,))],
+        2 * rows * width * half,
+        4 * width * half,
+    )
+    mine = kernel_call(
+        down_own_kernel,
+        shaped(F32, rows, half),
+        (vmem(tokens_here), vmem(weight_here)),
+        (),
+        [],
+        2 * rows * width * half,
+        2 * width * half,
+    )
     mine = mine + traded(theirs, "tp", 1).astype(F32)
     down_rows = expert_down.reshape(all_units, latent_len)
     terms, up_here, down_here = kernel_call(
@@ -239,7 +253,7 @@
     part = (mine + traded(theirs, "tp", 1).astype(F32)).astype(BF16)
     blocks = part.reshape(exp_count, rows, half)
     mixed = blocks[0].astype(F32)
-    for s in range(1, exp_count):
+    for s in (exp_count - 1, *range(1, exp_count - 1)):
         mixed = mixed + traded(blocks[s], "exp", s).astype(F32)
     mixed = across(mixed).astype(BF16)
     lat_up = vmem(lat_up)

time: 36.8 us -> 34.5 us (0.938)
  waiting for transfers between devices: 14 us -> 12 us
  Pallas kernels: 9.6 us -> 8.12 us
  starting transfers between devices: 12.7 us -> 14 us
    ppermute x12, waiting for transfers between devices: 14 us -> 12 us  [traded(): lax.ppermute(x, axis, [(i, i ^ mask) for i in range(lax.axis_size(axis))])]
    pallas_call x8, Pallas kernels: 9.6 us -> 8.12 us  [kernel_call(): pl.pallas_call(body, out_shape=out_shape, in_specs=[spec(pltpu.HBM if i i...]
    ppermute x12, starting transfers between devices: 12.7 us -> 14 us  [traded(): lax.ppermute(x, axis, [(i, i ^ mask) for i in range(lax.axis_size(axis))])]
  transfers between devices with their start and end apart: 12 -> 12, of which waited for: 9 -> 10; matrix products, arithmetic and copies ran while one was open for 0% -> 0% of each run, Pallas kernels for 16% -> 13%
where the time goes in v8:
time: 34.5 us; the launch traced here: 34.3 us
  starting transfers between devices  14 us (41%)
  waiting for transfers between devices  12 us (35%)
  Pallas kernels  8.12 us (24%)
    ppermute x12, starting transfers between devices, traded(): lax.ppermute(x, axis, [(i, i ^ mask) for i in range(lax.axis_size(axis))])  14 us
    ppermute x12, waiting for transfers between devices, traded(): lax.ppermute(x, axis, [(i, i ^ mask) for i in range(lax.axis_size(axis))])  12 us
    pallas_call x8, Pallas kernels, kernel_call(): pl.pallas_call(body, out_shape=out_shape, in_specs=[spec(pltpu.HBM if i i...  8.12 us
  transfers between devices with their start and end apart: 12, of which 10 were waited for; matrix products, arithmetic and copies ran while one was open for 0% of the time, Pallas kernels for 13%

profile of v8, /device:TPU:0, one launch (start us, length us, event | category | flops | bytes accessed | tf_op | source)
XLA Modules:
  0.0 34.3 jit_solution(6946585666381464423)
XLA Ops:
  0.0 1.9 %shard_map.73 = (bf16[32,512]{1,0:T(8,128)(2,1)S(1)}, bf16[32,1024]{1,0:T(8,128)(2,1)S(1)}, bf16[512,1024]{1,0:T(8,128)(2,1)S(1)}) custom-call(bf16[32,1024]{1,0:T(8,128)(2,1)} %tokens_hbm.1, bf16[1024,1024]{1,0:T(8,128)(2,1)} %weight_hbm.1), custom_call_target="tpu_custom_call" | custom-call | flops 33554432 | bytes 2097152 | tf_op jit(solution)/shard_map/pallas_call | solution.py:32
  1.9 0.5 %collective-permute-start = (bf16[32,512]{1,0:T(8,128)(2,1)S(1)}, bf16[32,512]{1,0:T(8,128)(2,1)S(1)}, u32[]{:S(2)}, u32[]{:S(2)}) collective-permute-start(bf16[32,512]{1,0:T(8,128)(2,1)S(1)} %get-tuple-element.15), channel_id=1, source_target_pairs={{0,1},{1,0},{2,3},{3,2},{4,5},{5,4},{6,7},{7,6},{8,9},{9,8},{10,11... | collective-permute-start | bytes 98312 | tf_op jit(solution)/shard_map/ppermute | solution.py:173
  2.4 0.4 %shard_map.74 = f32[32,512]{1,0:T(8,128)S(1)} custom-call(bf16[32,1024]{1,0:T(8,128)(2,1)S(1)} %get-tuple-element.13.tokens_ref, bf16[512,1024]{1,0:T(8,128)(2,1)S(1)} %get-tuple-element.14.weight_ref), custom_call_target="tpu_custom_call" | custom-call | flops 33554432 | bytes 1048576 | tf_op jit(solution)/shard_map/pallas_call | solution.py:32
  2.8 0.5 %collective-permute-done = bf16[32,512]{1,0:T(8,128)(2,1)S(1)} collective-permute-done((bf16[32,512]{1,0:T(8,128)(2,1)S(1)}, bf16[32,512]{1,0:T(8,128)(2,1)S(1)}, u32[]{:S(2)}, u32[]{:S(2)}) %collective-permute-start) | collective-permute-done | bytes 32800 | tf_op jit(solution)/shard_map/ppermute | solution.py:173
  3.3 2.9 %collective-permute-start.1 = (bf16[32,512]{1,0:T(8,128)(2,1)S(1)}, bf16[32,512]{1,0:T(8,128)(2,1)S(1)}, u32[]{:S(2)}, u32[]{:S(2)}) collective-permute-start(bf16[32,512]{1,0:T(8,128)(2,1)S(1)} %fusion.after_ref), channel_id=1, source_target_pairs={{0,2},{1,3},{2,0},{3,1},{4,6},{5,7},{6,4},{7,5},{8,10},{9,11},{10,... | collective-permute-start | bytes 98312 | tf_op jit(solution)/shard_map/ppermute | solution.py:173
  6.2 2.7 %shard_map.75 = (bf16[32,128]{1,0:T(8,128)(2,1)S(1)}, bf16[2,672,1024]{2,1,0:T(8,128)(2,1)S(1)}, bf16[1344,1024]{1,0:T(8,128)(2,1)S(1)}) custom-call(bf16[32,512]{1,0:T(8,128)(2,1)S(1)} %fusion.after_ref, s32[4,32]{1,0:T(4,128)} %bitcast.4, f32[4,32]{1,0:T(4,128)} %bitcast.5, bf16[2,672,1024]{2,1,0:T(8,128)(2,1)} %up_hbm.1, bf16[1344,1024]{1,0:T(8,128)(2,1)} %bitcast.3), custom_call_target="tpu_custom_call" | custom-call | bytes 5505024 | tf_op jit(solution)/shard_map/pallas_call | solution.py:32
  8.9 0.0 collective-permute-done.1
  8.9 3.7 %collective-permute-start.4 = (bf16[32,640]{1,0:T(8,128)(2,1)S(1)}, bf16[32,640]{1,0:T(8,128)(2,1)S(1)}, u32[]{:S(2)}, u32[]{:S(2)}) collective-permute-start(bf16[32,640]{1,0:T(8,128)(2,1)S(1)} %pad_maximum_fusion.1), channel_id=1, source_target_pairs={{0,12},{4,8},{8,4},{12,0},{1,13},{5,9},{9,5},{13,1},{2,14},{6,10},... | collective-permute-start | bytes 122888 | tf_op jit(solution)/shard_map/ppermute | solution.py:173
  12.6 0.0 collective-permute-start.3
  12.6 0.8 %collective-permute-start.2 = (bf16[32,640]{1,0:T(8,128)(2,1)S(1)}, bf16[32,640]{1,0:T(8,128)(2,1)S(1)}, u32[]{:S(2)}, u32[]{:S(2)}) collective-permute-start(bf16[32,640]{1,0:T(8,128)(2,1)S(1)} %pad_maximum_fusion.1), channel_id=1, source_target_pairs={{0,4},{4,0},{8,12},{12,8},{1,5},{5,1},{9,13},{13,9},{2,6},{6,2},{1... | collective-permute-start | bytes 122888 | tf_op jit(solution)/shard_map/ppermute | solution.py:173
  13.4 1.5 %collective-permute-done.4 = bf16[32,640]{1,0:T(8,128)(2,1)S(1)} collective-permute-done((bf16[32,640]{1,0:T(8,128)(2,1)S(1)}, bf16[32,640]{1,0:T(8,128)(2,1)S(1)}, u32[]{:S(2)}, u32[]{:S(2)}) %collective-permute-start.4) | collective-permute-done | bytes 40992 | tf_op jit(solution)/shard_map/ppermute | solution.py:173
  14.9 2.6 %collective-permute-done.3 = bf16[32,640]{1,0:T(8,128)(2,1)S(1)} collective-permute-done((bf16[32,640]{1,0:T(8,128)(2,1)S(1)}, bf16[32,640]{1,0:T(8,128)(2,1)S(1)}, u32[]{:S(2)}, u32[]{:S(2)}) %collective-permute-start.3) | collective-permute-done | bytes 40992 | tf_op jit(solution)/shard_map/ppermute | solution.py:173
  17.5 0.1 collective-permute-start.5
  17.6 0.7 %shard_map.76.pre_ref = f32[128,1344]{1,0:T(8,128)S(1)} custom-call(bf16[128,640]{1,0:T(8,128)(2,1)S(1)} %pad_maximum_fusion.messages_ref, bf16[2,672,1024]{2,1,0:T(8,128)(2,1)S(1)} %get-tuple-element.17.up_ref), custom_call_target="tpu_custom_call" | custom-call | flops 176160768 | bytes 1376256 | tf_op jit(solution)/shard_map/pallas_call | solution.py:32
  18.3 0.7 %collective-permute-done.5.other_ref = bf16[128,512]{1,0:T(8,128)(2,1)S(1)} collective-permute-done((bf16[128,512]{1,0:T(8,128)(2,1)S(1)}, bf16[128,512]{1,0:T(8,128)(2,1)S(1)}, u32[]{:S(2)}, u32[]{:S(2)}) %collective-permute-start.5) | collective-permute-done | bytes 131104 | tf_op jit(solution)/shard_map/ppermute | solution.py:173
  18.9 0.9 %shard_map.77 = (bf16[128,1344]{1,0:T(8,128)(2,1)S(1)}, bf16[128,512]{1,0:T(8,128)(2,1)S(1)}) custom-call(bf16[128,640]{1,0:T(8,128)(2,1)S(1)} %pad_maximum_fusion.messages_ref, bf16[128,512]{1,0:T(8,128)(2,1)S(1)} %collective-permute-done.5.other_ref, f32[128,1344]{1,0:T(8,128)S(1)} %shard_map.76.pre_ref, ...), custom_call_target="tpu_custom_call" | custom-call | flops 352321536 | bytes 2752512 | tf_op jit(solution)/shard_map/pallas_call | solution.py:32
  19.9 0.0 copy-start
  19.9 0.2 collective-permute-start.6
  20.1 0.4 %shard_map.78 = f32[128,512]{1,0:T(8,128)S(1)} custom-call(bf16[128,1344]{1,0:T(8,128)(2,1)S(1)} %get-tuple-element.19.hidden_ref, bf16[1344,1024]{1,0:T(8,128)(2,1)S(1)} %get-tuple-element.18.down_ref), custom_call_target="tpu_custom_call" | custom-call | flops 176160768 | bytes 1376256 | tf_op jit(solution)/shard_map/pallas_call | solution.py:32
  20.5 0.8 %collective-permute-done.6 = bf16[128,512]{1,0:T(8,128)(2,1)S(1)} collective-permute-done((bf16[128,512]{1,0:T(8,128)(2,1)S(1)}, bf16[128,512]{1,0:T(8,128)(2,1)S(1)}, u32[]{:S(2)}, u32[]{:S(2)}) %collective-permute-start.6) | collective-permute-done | bytes 131104 | tf_op jit(solution)/shard_map/ppermute | solution.py:173
  21.3 1.7 %collective-permute-start.7 = (bf16[32,512]{1,0:T(8,128)(2,1)S(1)}, bf16[32,512]{1,0:T(8,128)(2,1)S(1)}, u32[]{:S(2)}, u32[]{:S(2)}) collective-permute-start(bf16[32,512]{1,0:T(8,128)(2,1)S(1)} %get-tuple-element.21), channel_id=1, source_target_pairs={{0,12},{4,8},{8,4},{12,0},{1,13},{5,9},{9,5},{13,1},{2,14},{6,10},... | collective-permute-start | bytes 98312 | tf_op jit(solution)/shard_map/ppermute | solution.py:173
  23.0 0.5 %collective-permute-start.9 = (bf16[32,512]{1,0:T(8,128)(2,1)S(1)}, bf16[32,512]{1,0:T(8,128)(2,1)S(1)}, u32[]{:S(2)}, u32[]{:S(2)}) collective-permute-start(bf16[32,512]{1,0:T(8,128)(2,1)S(1)} %get-tuple-element.22), channel_id=1, source_target_pairs={{0,8},{4,12},{8,0},{12,4},{1,9},{5,13},{9,1},{13,5},{2,10},{6,14},... | collective-permute-start | bytes 98312 | tf_op jit(solution)/shard_map/ppermute | solution.py:173
  23.5 2.3 %collective-permute-start.8 = (bf16[32,512]{1,0:T(8,128)(2,1)S(1)}, bf16[32,512]{1,0:T(8,128)(2,1)S(1)}, u32[]{:S(2)}, u32[]{:S(2)}) collective-permute-start(bf16[32,512]{1,0:T(8,128)(2,1)S(1)} %get-tuple-element.23), channel_id=1, source_target_pairs={{0,4},{4,0},{8,12},{12,8},{1,5},{5,1},{9,13},{13,9},{2,6},{6,2},{1... | collective-permute-start | bytes 98312 | tf_op jit(solution)/shard_map/ppermute | solution.py:173
  25.8 1.7 %collective-permute-done.7 = bf16[32,512]{1,0:T(8,128)(2,1)S(1)} collective-permute-done((bf16[32,512]{1,0:T(8,128)(2,1)S(1)}, bf16[32,512]{1,0:T(8,128)(2,1)S(1)}, u32[]{:S(2)}, u32[]{:S(2)}) %collective-permute-start.7) | collective-permute-done | bytes 32800 | tf_op jit(solution)/shard_map/ppermute | solution.py:173
  27.4 0.4 %collective-permute-done.9 = bf16[32,512]{1,0:T(8,128)(2,1)S(1)} collective-permute-done((bf16[32,512]{1,0:T(8,128)(2,1)S(1)}, bf16[32,512]{1,0:T(8,128)(2,1)S(1)}, u32[]{:S(2)}, u32[]{:S(2)}) %collective-permute-start.9) | collective-permute-done | bytes 32800 | tf_op jit(solution)/shard_map/ppermute | solution.py:173
  27.9 0.2 collective-permute-done.8
  28.1 1.3 %collective-permute-start.10 = (bf16[32,512]{1,0:T(8,128)(2,1)S(1)}, bf16[32,512]{1,0:T(8,128)(2,1)S(1)}, u32[]{:S(2)}, u32[]{:S(2)}) collective-permute-start(bf16[32,512]{1,0:T(8,128)(2,1)S(1)} %fusion.1), channel_id=1, source_target_pairs={{0,2},{1,3},{2,0},{3,1},{4,6},{5,7},{6,4},{7,5},{8,10},{9,11},{10,... | collective-permute-start | bytes 98312 | tf_op jit(solution)/shard_map/ppermute | solution.py:173
  29.4 2.7 %collective-permute-done.10 = bf16[32,512]{1,0:T(8,128)(2,1)S(1)} collective-permute-done((bf16[32,512]{1,0:T(8,128)(2,1)S(1)}, bf16[32,512]{1,0:T(8,128)(2,1)S(1)}, u32[]{:S(2)}, u32[]{:S(2)}) %collective-permute-start.10) | collective-permute-done | bytes 32800 | tf_op jit(solution)/shard_map/ppermute | solution.py:173
  32.1 0.1 collective-permute-start.11
  32.2 0.3 shard_map.79.part_ref
  32.5 0.9 %collective-permute-done.11.other_ref = bf16[32,512]{1,0:T(8,128)(2,1)S(1)} collective-permute-done((bf16[32,512]{1,0:T(8,128)(2,1)S(1)}, bf16[32,512]{1,0:T(8,128)(2,1)S(1)}, u32[]{:S(2)}, u32[]{:S(2)}) %collective-permute-start.11) | collective-permute-done | bytes 32800 | tf_op jit(solution)/shard_map/ppermute | solution.py:173
  33.4 0.9 %shard_map.80 = bf16[32,1024]{1,0:T(8,128)(2,1)} custom-call(f32[32,1024]{1,0:T(8,128)S(1)} %shard_map.79.part_ref, bf16[32,512]{1,0:T(8,128)(2,1)S(1)} %collective-permute-done.11.other_ref, bf16[1024,1024]{1,0:T(8,128)(2,1)S(1)} %copy-done), custom_call_target="tpu_custom_call" | custom-call | flops 33554432 | bytes 1048576 | tf_op jit(solution)/shard_map/pallas_call | solution.py:32
  (11 shorter events, 0.1 us)
Async XLA Ops:
  1.9 1.4 %collective-permute-start = (bf16[32,512]{1,0:T(8,128)(2,1)S(1)}, bf16[32,512]{1,0:T(8,128)(2,1)S(1)}, u32[]{:S(2)}, u32[]{:S(2)}) collective-permute-start(bf16[32,512]{1,0:T(8,128)(2,1)S(1)} %get-tuple-element.15), channel_id=1, source_target_pairs={{0,1},{1,0},{2,3},{3,2},{4,5},{5,4},{6,7},{7,6},{8,9},{9,8},{10,11... | collective-permute-start | bytes 98312 | tf_op jit(solution)/shard_map/ppermute | solution.py:173
  3.3 5.6 %collective-permute-start.1 = (bf16[32,512]{1,0:T(8,128)(2,1)S(1)}, bf16[32,512]{1,0:T(8,128)(2,1)S(1)}, u32[]{:S(2)}, u32[]{:S(2)}) collective-permute-start(bf16[32,512]{1,0:T(8,128)(2,1)S(1)} %fusion.after_ref), channel_id=1, source_target_pairs={{0,2},{1,3},{2,0},{3,1},{4,6},{5,7},{6,4},{7,5},{8,10},{9,11},{10,... | collective-permute-start | bytes 98312 | tf_op jit(solution)/shard_map/ppermute | solution.py:173
  8.9 6.0 %collective-permute-start.4 = (bf16[32,640]{1,0:T(8,128)(2,1)S(1)}, bf16[32,640]{1,0:T(8,128)(2,1)S(1)}, u32[]{:S(2)}, u32[]{:S(2)}) collective-permute-start(bf16[32,640]{1,0:T(8,128)(2,1)S(1)} %pad_maximum_fusion.1), channel_id=1, source_target_pairs={{0,12},{4,8},{8,4},{12,0},{1,13},{5,9},{9,5},{13,1},{2,14},{6,10},... | collective-permute-start | bytes 122888 | tf_op jit(solution)/shard_map/ppermute | solution.py:173
  12.6 4.9 %collective-permute-start.3 = (bf16[32,640]{1,0:T(8,128)(2,1)S(1)}, bf16[32,640]{1,0:T(8,128)(2,1)S(1)}, u32[]{:S(2)}, u32[]{:S(2)}) collective-permute-start(bf16[32,640]{1,0:T(8,128)(2,1)S(1)} %pad_maximum_fusion.1), channel_id=1, source_target_pairs={{0,8},{4,12},{8,0},{12,4},{1,9},{5,13},{9,1},{13,5},{2,10},{6,14},... | collective-permute-start | bytes 122888 | tf_op jit(solution)/shard_map/ppermute | solution.py:173
  12.6 4.9 %collective-permute-start.2 = (bf16[32,640]{1,0:T(8,128)(2,1)S(1)}, bf16[32,640]{1,0:T(8,128)(2,1)S(1)}, u32[]{:S(2)}, u32[]{:S(2)}) collective-permute-start(bf16[32,640]{1,0:T(8,128)(2,1)S(1)} %pad_maximum_fusion.1), channel_id=1, source_target_pairs={{0,4},{4,0},{8,12},{12,8},{1,5},{5,1},{9,13},{13,9},{2,6},{6,2},{1... | collective-permute-start | bytes 122888 | tf_op jit(solution)/shard_map/ppermute | solution.py:173
  17.5 1.4 %collective-permute-start.5 = (bf16[128,512]{1,0:T(8,128)(2,1)S(1)}, bf16[128,512]{1,0:T(8,128)(2,1)S(1)}, u32[]{:S(2)}, u32[]{:S(2)}) collective-permute-start(bf16[128,512]{1,0:T(8,128)(2,1)S(1)} %slice.24), channel_id=1, source_target_pairs={{0,1},{1,0},{2,3},{3,2},{4,5},{5,4},{6,7},{7,6},{8,9},{9,8},{10,11... | collective-permute-start | bytes 393224 | tf_op jit(solution)/shard_map/ppermute | solution.py:173
  19.9 12.3 %copy-start = (bf16[1024,1024]{1,0:T(8,128)(2,1)S(1)}, bf16[1024,1024]{1,0:T(8,128)(2,1)}, u32[]{:S(2)}) copy-start(bf16[1024,1024]{1,0:T(8,128)(2,1)} %weight_ref.3) | copy-start | bytes 6291460
  19.9 1.4 %collective-permute-start.6 = (bf16[128,512]{1,0:T(8,128)(2,1)S(1)}, bf16[128,512]{1,0:T(8,128)(2,1)S(1)}, u32[]{:S(2)}, u32[]{:S(2)}) collective-permute-start(bf16[128,512]{1,0:T(8,128)(2,1)S(1)} %get-tuple-element.20), channel_id=1, source_target_pairs={{0,1},{1,0},{2,3},{3,2},{4,5},{5,4},{6,7},{7,6},{8,9},{9,8},{10,11... | collective-permute-start | bytes 393224 | tf_op jit(solution)/shard_map/ppermute | solution.py:173
  21.3 6.1 %collective-permute-start.7 = (bf16[32,512]{1,0:T(8,128)(2,1)S(1)}, bf16[32,512]{1,0:T(8,128)(2,1)S(1)}, u32[]{:S(2)}, u32[]{:S(2)}) collective-permute-start(bf16[32,512]{1,0:T(8,128)(2,1)S(1)} %get-tuple-element.21), channel_id=1, source_target_pairs={{0,12},{4,8},{8,4},{12,0},{1,13},{5,9},{9,5},{13,1},{2,14},{6,10},... | collective-permute-start | bytes 98312 | tf_op jit(solution)/shard_map/ppermute | solution.py:173
  23.0 4.9 %collective-permute-start.9 = (bf16[32,512]{1,0:T(8,128)(2,1)S(1)}, bf16[32,512]{1,0:T(8,128)(2,1)S(1)}, u32[]{:S(2)}, u32[]{:S(2)}) collective-permute-start(bf16[32,512]{1,0:T(8,128)(2,1)S(1)} %get-tuple-element.22), channel_id=1, source_target_pairs={{0,8},{4,12},{8,0},{12,4},{1,9},{5,13},{9,1},{13,5},{2,10},{6,14},... | collective-permute-start | bytes 98312 | tf_op jit(solution)/shard_map/ppermute | solution.py:173
  23.5 4.6 %collective-permute-start.8 = (bf16[32,512]{1,0:T(8,128)(2,1)S(1)}, bf16[32,512]{1,0:T(8,128)(2,1)S(1)}, u32[]{:S(2)}, u32[]{:S(2)}) collective-permute-start(bf16[32,512]{1,0:T(8,128)(2,1)S(1)} %get-tuple-element.23), channel_id=1, source_target_pairs={{0,4},{4,0},{8,12},{12,8},{1,5},{5,1},{9,13},{13,9},{2,6},{6,2},{1... | collective-permute-start | bytes 98312 | tf_op jit(solution)/shard_map/ppermute | solution.py:173
  28.1 4.0 %collective-permute-start.10 = (bf16[32,512]{1,0:T(8,128)(2,1)S(1)}, bf16[32,512]{1,0:T(8,128)(2,1)S(1)}, u32[]{:S(2)}, u32[]{:S(2)}) collective-permute-start(bf16[32,512]{1,0:T(8,128)(2,1)S(1)} %fusion.1), channel_id=1, source_target_pairs={{0,2},{1,3},{2,0},{3,1},{4,6},{5,7},{6,4},{7,5},{8,10},{9,11},{10,... | collective-permute-start | bytes 98312 | tf_op jit(solution)/shard_map/ppermute | solution.py:173
  32.1 1.3 %collective-permute-start.11 = (bf16[32,512]{1,0:T(8,128)(2,1)S(1)}, bf16[32,512]{1,0:T(8,128)(2,1)S(1)}, u32[]{:S(2)}, u32[]{:S(2)}) collective-permute-start(bf16[32,512]{1,0:T(8,128)(2,1)S(1)} %add_convert_fusion.1.own_ref), channel_id=1, source_target_pairs={{0,1},{1,0},{2,3},{3,2},{4,5},{5,4},{6,7},{7,6},{8,9},{9,8},{10,11... | collective-permute-start | bytes 98312 | tf_op jit(solution)/shard_map/ppermute | solution.py:173

commit v9 on v8

--- a/solution.py
+++ b/solution.py
@@ -172,6 +172,9 @@
     def traded(x, axis, mask):
         return lax.ppermute(x, axis, [(i, i ^ mask) for i in range(lax.axis_size(axis))])
 
+    def turned(x, shift):
+        return lax.ppermute(x, "exp", [(i, (i + shift) % exp_count) for i in range(exp_count)])
+
     def across(x):
         for mask in pair_masks:
             x = x + traded(x.astype(BF16), "tp", mask).astype(F32)
@@ -220,8 +223,9 @@
     )
     up_here, down_here = vmem(up_here), vmem(down_here)
     message = jnp.concatenate([across(mine).astype(BF16), terms], axis=1)
-    messages = [message] + [traded(message, "exp", s) for s in range(1, exp_count)]
-    messages = jnp.concatenate(messages, axis=0)
+    order = (*range(2, exp_count), 1)
+    found = {s: turned(message, s) for s in order}
+    messages = jnp.concatenate([message] + [found[s] for s in range(1, exp_count)], axis=0)
     other = traded(messages[:, :half], "tp", 1)
     pre = kernel_call(
         first_kernel,
@@ -253,8 +257,8 @@
     part = (mine + traded(theirs, "tp", 1).astype(F32)).astype(BF16)
     blocks = part.reshape(exp_count, rows, half)
     mixed = blocks[0].astype(F32)
-    for s in (exp_count - 1, *range(1, exp_count - 1)):
-        mixed = mixed + traded(blocks[s], "exp", s).astype(F32)
+    for s in range(1, exp_count):
+        mixed = mixed + turned(blocks[s], exp_count - s).astype(F32)
     mixed = across(mixed).astype(BF16)
     lat_up = vmem(lat_up)
     own_part = kernel_call(

time: 34.5 us -> 35.8 us (1.038)
  waiting for transfers between devices: 12 us -> 14.3 us
  starting transfers between devices: 14 us -> 12.9 us
    ppermute x12 -> x6, starting transfers between devices: 14 us -> 5.05 us  [traded(): lax.ppermute(x, axis, [(i, i ^ mask) for i in range(lax.axis_size(axis))])]
    ppermute x0 -> x6, waiting for transfers between devices: none -> 8.78 us  [turned(): lax.ppermute(x, 'exp', [(i, (i + shift) % exp_count) for i in range(exp_c...]
    ppermute x0 -> x6, starting transfers between devices: none -> 7.86 us  [turned(): lax.ppermute(x, 'exp', [(i, (i + shift) % exp_count) for i in range(exp_c...]
    ppermute x12 -> x6, waiting for transfers between devices: 12 us -> 5.54 us  [traded(): lax.ppermute(x, axis, [(i, i ^ mask) for i in range(lax.axis_size(axis))])]
  transfers between devices with their start and end apart: 12 -> 12, of which waited for: 10 -> 11; matrix products, arithmetic and copies ran while one was open for 0% -> 0% of each run, Pallas kernels for 13% -> 12%
where the time goes in v9:
time: 35.8 us; the launch traced here: 35.6 us
  waiting for transfers between devices  14.3 us (40%)
  starting transfers between devices  12.9 us (36%)
  Pallas kernels  8.12 us (23%)
    ppermute x6, waiting for transfers between devices, turned(): lax.ppermute(x, 'exp', [(i, (i + shift) % exp_count) for i in range(exp_c...  8.78 us
    pallas_call x8, Pallas kernels, kernel_call(): pl.pallas_call(body, out_shape=out_shape, in_specs=[spec(pltpu.HBM if i i...  8.12 us
    ppermute x6, starting transfers between devices, turned(): lax.ppermute(x, 'exp', [(i, (i + shift) % exp_count) for i in range(exp_c...  7.86 us
    ppermute x6, waiting for transfers between devices, traded(): lax.ppermute(x, axis, [(i, i ^ mask) for i in range(lax.axis_size(axis))])  5.54 us
    ppermute x6, starting transfers between devices, traded(): lax.ppermute(x, axis, [(i, i ^ mask) for i in range(lax.axis_size(axis))])  5.05 us
  transfers between devices with their start and end apart: 12, of which 11 were waited for; matrix products, arithmetic and copies ran while one was open for 0% of the time, Pallas kernels for 12%

profile of v9, /device:TPU:0, one launch (start us, length us, event | category | flops | bytes accessed | tf_op | source)
XLA Modules:
  0.0 35.6 jit_solution(17145740238930846664)
XLA Ops:
  0.0 1.9 %shard_map.73 = (bf16[32,512]{1,0:T(8,128)(2,1)S(1)}, bf16[32,1024]{1,0:T(8,128)(2,1)S(1)}, bf16[512,1024]{1,0:T(8,128)(2,1)S(1)}) custom-call(bf16[32,1024]{1,0:T(8,128)(2,1)} %tokens_hbm.1, bf16[1024,1024]{1,0:T(8,128)(2,1)} %weight_hbm.1), custom_call_target="tpu_custom_call" | custom-call | flops 33554432 | bytes 2097152 | tf_op jit(solution)/shard_map/pallas_call | solution.py:32
  1.9 0.5 %collective-permute-start = (bf16[32,512]{1,0:T(8,128)(2,1)S(1)}, bf16[32,512]{1,0:T(8,128)(2,1)S(1)}, u32[]{:S(2)}, u32[]{:S(2)}) collective-permute-start(bf16[32,512]{1,0:T(8,128)(2,1)S(1)} %get-tuple-element.15), channel_id=1, source_target_pairs={{0,1},{1,0},{2,3},{3,2},{4,5},{5,4},{6,7},{7,6},{8,9},{9,8},{10,11... | collective-permute-start | bytes 98312 | tf_op jit(solution)/shard_map/ppermute | solution.py:173
  2.4 0.4 %shard_map.74 = f32[32,512]{1,0:T(8,128)S(1)} custom-call(bf16[32,1024]{1,0:T(8,128)(2,1)S(1)} %get-tuple-element.13.tokens_ref, bf16[512,1024]{1,0:T(8,128)(2,1)S(1)} %get-tuple-element.14.weight_ref), custom_call_target="tpu_custom_call" | custom-call | flops 33554432 | bytes 1048576 | tf_op jit(solution)/shard_map/pallas_call | solution.py:32
  2.8 0.5 %collective-permute-done = bf16[32,512]{1,0:T(8,128)(2,1)S(1)} collective-permute-done((bf16[32,512]{1,0:T(8,128)(2,1)S(1)}, bf16[32,512]{1,0:T(8,128)(2,1)S(1)}, u32[]{:S(2)}, u32[]{:S(2)}) %collective-permute-start) | collective-permute-done | bytes 32800 | tf_op jit(solution)/shard_map/ppermute | solution.py:173
  3.3 2.9 %collective-permute-start.1 = (bf16[32,512]{1,0:T(8,128)(2,1)S(1)}, bf16[32,512]{1,0:T(8,128)(2,1)S(1)}, u32[]{:S(2)}, u32[]{:S(2)}) collective-permute-start(bf16[32,512]{1,0:T(8,128)(2,1)S(1)} %fusion.after_ref), channel_id=1, source_target_pairs={{0,2},{1,3},{2,0},{3,1},{4,6},{5,7},{6,4},{7,5},{8,10},{9,11},{10,... | collective-permute-start | bytes 98312 | tf_op jit(solution)/shard_map/ppermute | solution.py:173
  6.2 2.7 %shard_map.75 = (bf16[32,128]{1,0:T(8,128)(2,1)S(1)}, bf16[2,672,1024]{2,1,0:T(8,128)(2,1)S(1)}, bf16[1344,1024]{1,0:T(8,128)(2,1)S(1)}) custom-call(bf16[32,512]{1,0:T(8,128)(2,1)S(1)} %fusion.after_ref, s32[4,32]{1,0:T(4,128)} %bitcast.4, f32[4,32]{1,0:T(4,128)} %bitcast.5, bf16[2,672,1024]{2,1,0:T(8,128)(2,1)} %up_hbm.1, bf16[1344,1024]{1,0:T(8,128)(2,1)} %bitcast.3), custom_call_target="tpu_custom_call" | custom-call | bytes 5505024 | tf_op jit(solution)/shard_map/pallas_call | solution.py:32
  8.9 3.7 %collective-permute-start.4 = (bf16[32,640]{1,0:T(8,128)(2,1)S(1)}, bf16[32,640]{1,0:T(8,128)(2,1)S(1)}, u32[]{:S(2)}, u32[]{:S(2)}) collective-permute-start(bf16[32,640]{1,0:T(8,128)(2,1)S(1)} %pad_maximum_fusion.1), channel_id=1, source_target_pairs={{0,12},{4,0},{8,4},{12,8},{1,13},{5,1},{9,5},{13,9},{2,14},{6,2},{... | collective-permute-start | bytes 122888 | tf_op jit(solution)/shard_map/ppermute | solution.py:176
  12.6 0.0 collective-permute-start.3
  12.6 1.0 %collective-permute-start.2 = (bf16[32,640]{1,0:T(8,128)(2,1)S(1)}, bf16[32,640]{1,0:T(8,128)(2,1)S(1)}, u32[]{:S(2)}, u32[]{:S(2)}) collective-permute-start(bf16[32,640]{1,0:T(8,128)(2,1)S(1)} %pad_maximum_fusion.1), channel_id=1, source_target_pairs={{0,4},{4,8},{8,12},{12,0},{1,5},{5,9},{9,13},{13,1},{2,6},{6,10},{... | collective-permute-start | bytes 122888 | tf_op jit(solution)/shard_map/ppermute | solution.py:176
  13.6 0.7 %collective-permute-done.4 = bf16[32,640]{1,0:T(8,128)(2,1)S(1)} collective-permute-done((bf16[32,640]{1,0:T(8,128)(2,1)S(1)}, bf16[32,640]{1,0:T(8,128)(2,1)S(1)}, u32[]{:S(2)}, u32[]{:S(2)}) %collective-permute-start.4) | collective-permute-done | bytes 40992 | tf_op jit(solution)/shard_map/ppermute | solution.py:176
  14.3 3.2 %collective-permute-done.3 = bf16[32,640]{1,0:T(8,128)(2,1)S(1)} collective-permute-done((bf16[32,640]{1,0:T(8,128)(2,1)S(1)}, bf16[32,640]{1,0:T(8,128)(2,1)S(1)}, u32[]{:S(2)}, u32[]{:S(2)}) %collective-permute-start.3) | collective-permute-done | bytes 40992 | tf_op jit(solution)/shard_map/ppermute | solution.py:176
  17.5 0.9 %collective-permute-done.2 = bf16[32,640]{1,0:T(8,128)(2,1)S(1)} collective-permute-done((bf16[32,640]{1,0:T(8,128)(2,1)S(1)}, bf16[32,640]{1,0:T(8,128)(2,1)S(1)}, u32[]{:S(2)}, u32[]{:S(2)}) %collective-permute-start.2) | collective-permute-done | bytes 40992 | tf_op jit(solution)/shard_map/ppermute | solution.py:176
  18.4 0.1 collective-permute-start.5
  18.5 0.7 %shard_map.76.pre_ref = f32[128,1344]{1,0:T(8,128)S(1)} custom-call(bf16[128,640]{1,0:T(8,128)(2,1)S(1)} %pad_maximum_fusion.messages_ref, bf16[2,672,1024]{2,1,0:T(8,128)(2,1)S(1)} %get-tuple-element.17.up_ref), custom_call_target="tpu_custom_call" | custom-call | flops 176160768 | bytes 1376256 | tf_op jit(solution)/shard_map/pallas_call | solution.py:32
  19.2 0.7 %collective-permute-done.5.other_ref = bf16[128,512]{1,0:T(8,128)(2,1)S(1)} collective-permute-done((bf16[128,512]{1,0:T(8,128)(2,1)S(1)}, bf16[128,512]{1,0:T(8,128)(2,1)S(1)}, u32[]{:S(2)}, u32[]{:S(2)}) %collective-permute-start.5) | collective-permute-done | bytes 131104 | tf_op jit(solution)/shard_map/ppermute | solution.py:173
  19.8 0.9 %shard_map.77 = (bf16[128,1344]{1,0:T(8,128)(2,1)S(1)}, bf16[128,512]{1,0:T(8,128)(2,1)S(1)}) custom-call(bf16[128,640]{1,0:T(8,128)(2,1)S(1)} %pad_maximum_fusion.messages_ref, bf16[128,512]{1,0:T(8,128)(2,1)S(1)} %collective-permute-done.5.other_ref, f32[128,1344]{1,0:T(8,128)S(1)} %shard_map.76.pre_ref, ...), custom_call_target="tpu_custom_call" | custom-call | flops 352321536 | bytes 2752512 | tf_op jit(solution)/shard_map/pallas_call | solution.py:32
  20.7 0.0 copy-start
  20.7 0.2 collective-permute-start.6
  20.9 0.4 %shard_map.78 = f32[128,512]{1,0:T(8,128)S(1)} custom-call(bf16[128,1344]{1,0:T(8,128)(2,1)S(1)} %get-tuple-element.19.hidden_ref, bf16[1344,1024]{1,0:T(8,128)(2,1)S(1)} %get-tuple-element.18.down_ref), custom_call_target="tpu_custom_call" | custom-call | flops 176160768 | bytes 1376256 | tf_op jit(solution)/shard_map/pallas_call | solution.py:32
  21.3 0.8 %collective-permute-done.6 = bf16[128,512]{1,0:T(8,128)(2,1)S(1)} collective-permute-done((bf16[128,512]{1,0:T(8,128)(2,1)S(1)}, bf16[128,512]{1,0:T(8,128)(2,1)S(1)}, u32[]{:S(2)}, u32[]{:S(2)}) %collective-permute-start.6) | collective-permute-done | bytes 131104 | tf_op jit(solution)/shard_map/ppermute | solution.py:173
  22.2 0.8 %collective-permute-start.7 = (bf16[32,512]{1,0:T(8,128)(2,1)S(1)}, bf16[32,512]{1,0:T(8,128)(2,1)S(1)}, u32[]{:S(2)}, u32[]{:S(2)}) collective-permute-start(bf16[32,512]{1,0:T(8,128)(2,1)S(1)} %get-tuple-element.21), channel_id=1, source_target_pairs={{0,12},{4,0},{8,4},{12,8},{1,13},{5,1},{9,5},{13,9},{2,14},{6,2},{... | collective-permute-start | bytes 98312 | tf_op jit(solution)/shard_map/ppermute | solution.py:176
  23.0 1.3 %collective-permute-start.9 = (bf16[32,512]{1,0:T(8,128)(2,1)S(1)}, bf16[32,512]{1,0:T(8,128)(2,1)S(1)}, u32[]{:S(2)}, u32[]{:S(2)}) collective-permute-start(bf16[32,512]{1,0:T(8,128)(2,1)S(1)} %get-tuple-element.22), channel_id=1, source_target_pairs={{0,4},{4,8},{8,12},{12,0},{1,5},{5,9},{9,13},{13,1},{2,6},{6,10},{... | collective-permute-start | bytes 98312 | tf_op jit(solution)/shard_map/ppermute | solution.py:176
  24.3 1.1 %collective-permute-start.8 = (bf16[32,512]{1,0:T(8,128)(2,1)S(1)}, bf16[32,512]{1,0:T(8,128)(2,1)S(1)}, u32[]{:S(2)}, u32[]{:S(2)}) collective-permute-start(bf16[32,512]{1,0:T(8,128)(2,1)S(1)} %get-tuple-element.23), channel_id=1, source_target_pairs={{0,8},{4,12},{8,0},{12,4},{1,9},{5,13},{9,1},{13,5},{2,10},{6,14},... | collective-permute-start | bytes 98312 | tf_op jit(solution)/shard_map/ppermute | solution.py:176
  25.4 0.8 %collective-permute-done.7 = bf16[32,512]{1,0:T(8,128)(2,1)S(1)} collective-permute-done((bf16[32,512]{1,0:T(8,128)(2,1)S(1)}, bf16[32,512]{1,0:T(8,128)(2,1)S(1)}, u32[]{:S(2)}, u32[]{:S(2)}) %collective-permute-start.7) | collective-permute-done | bytes 32800 | tf_op jit(solution)/shard_map/ppermute | solution.py:176
  26.2 2.5 %collective-permute-done.9 = bf16[32,512]{1,0:T(8,128)(2,1)S(1)} collective-permute-done((bf16[32,512]{1,0:T(8,128)(2,1)S(1)}, bf16[32,512]{1,0:T(8,128)(2,1)S(1)}, u32[]{:S(2)}, u32[]{:S(2)}) %collective-permute-start.9) | collective-permute-done | bytes 32800 | tf_op jit(solution)/shard_map/ppermute | solution.py:176
  28.7 0.7 %collective-permute-done.8 = bf16[32,512]{1,0:T(8,128)(2,1)S(1)} collective-permute-done((bf16[32,512]{1,0:T(8,128)(2,1)S(1)}, bf16[32,512]{1,0:T(8,128)(2,1)S(1)}, u32[]{:S(2)}, u32[]{:S(2)}) %collective-permute-start.8) | collective-permute-done | bytes 32800 | tf_op jit(solution)/shard_map/ppermute | solution.py:176
  29.4 1.3 %collective-permute-start.10 = (bf16[32,512]{1,0:T(8,128)(2,1)S(1)}, bf16[32,512]{1,0:T(8,128)(2,1)S(1)}, u32[]{:S(2)}, u32[]{:S(2)}) collective-permute-start(bf16[32,512]{1,0:T(8,128)(2,1)S(1)} %fusion.1), channel_id=1, source_target_pairs={{0,2},{1,3},{2,0},{3,1},{4,6},{5,7},{6,4},{7,5},{8,10},{9,11},{10,... | collective-permute-start | bytes 98312 | tf_op jit(solution)/shard_map/ppermute | solution.py:173
  30.7 2.7 %collective-permute-done.10 = bf16[32,512]{1,0:T(8,128)(2,1)S(1)} collective-permute-done((bf16[32,512]{1,0:T(8,128)(2,1)S(1)}, bf16[32,512]{1,0:T(8,128)(2,1)S(1)}, u32[]{:S(2)}, u32[]{:S(2)}) %collective-permute-start.10) | collective-permute-done | bytes 32800 | tf_op jit(solution)/shard_map/ppermute | solution.py:173
  33.4 0.1 collective-permute-start.11
  33.5 0.3 shard_map.79.part_ref
  33.8 0.9 %collective-permute-done.11.other_ref = bf16[32,512]{1,0:T(8,128)(2,1)S(1)} collective-permute-done((bf16[32,512]{1,0:T(8,128)(2,1)S(1)}, bf16[32,512]{1,0:T(8,128)(2,1)S(1)}, u32[]{:S(2)}, u32[]{:S(2)}) %collective-permute-start.11) | collective-permute-done | bytes 32800 | tf_op jit(solution)/shard_map/ppermute | solution.py:173
  34.7 0.9 %shard_map.80 = bf16[32,1024]{1,0:T(8,128)(2,1)} custom-call(f32[32,1024]{1,0:T(8,128)S(1)} %shard_map.79.part_ref, bf16[32,512]{1,0:T(8,128)(2,1)S(1)} %collective-permute-done.11.other_ref, bf16[1024,1024]{1,0:T(8,128)(2,1)S(1)} %copy-done), custom_call_target="tpu_custom_call" | custom-call | flops 33554432 | bytes 1048576 | tf_op jit(solution)/shard_map/pallas_call | solution.py:32
  (11 shorter events, 0.1 us)
Async XLA Ops:
  1.9 1.4 %collective-permute-start = (bf16[32,512]{1,0:T(8,128)(2,1)S(1)}, bf16[32,512]{1,0:T(8,128)(2,1)S(1)}, u32[]{:S(2)}, u32[]{:S(2)}) collective-permute-start(bf16[32,512]{1,0:T(8,128)(2,1)S(1)} %get-tuple-element.15), channel_id=1, source_target_pairs={{0,1},{1,0},{2,3},{3,2},{4,5},{5,4},{6,7},{7,6},{8,9},{9,8},{10,11... | collective-permute-start | bytes 98312 | tf_op jit(solution)/shard_map/ppermute | solution.py:173
  3.3 5.6 %collective-permute-start.1 = (bf16[32,512]{1,0:T(8,128)(2,1)S(1)}, bf16[32,512]{1,0:T(8,128)(2,1)S(1)}, u32[]{:S(2)}, u32[]{:S(2)}) collective-permute-start(bf16[32,512]{1,0:T(8,128)(2,1)S(1)} %fusion.after_ref), channel_id=1, source_target_pairs={{0,2},{1,3},{2,0},{3,1},{4,6},{5,7},{6,4},{7,5},{8,10},{9,11},{10,... | collective-permute-start | bytes 98312 | tf_op jit(solution)/shard_map/ppermute | solution.py:173
  8.9 5.4 %collective-permute-start.4 = (bf16[32,640]{1,0:T(8,128)(2,1)S(1)}, bf16[32,640]{1,0:T(8,128)(2,1)S(1)}, u32[]{:S(2)}, u32[]{:S(2)}) collective-permute-start(bf16[32,640]{1,0:T(8,128)(2,1)S(1)} %pad_maximum_fusion.1), channel_id=1, source_target_pairs={{0,12},{4,0},{8,4},{12,8},{1,13},{5,1},{9,5},{13,9},{2,14},{6,2},{... | collective-permute-start | bytes 122888 | tf_op jit(solution)/shard_map/ppermute | solution.py:176
  12.6 4.9 %collective-permute-start.3 = (bf16[32,640]{1,0:T(8,128)(2,1)S(1)}, bf16[32,640]{1,0:T(8,128)(2,1)S(1)}, u32[]{:S(2)}, u32[]{:S(2)}) collective-permute-start(bf16[32,640]{1,0:T(8,128)(2,1)S(1)} %pad_maximum_fusion.1), channel_id=1, source_target_pairs={{0,8},{4,12},{8,0},{12,4},{1,9},{5,13},{9,1},{13,5},{2,10},{6,14},... | collective-permute-start | bytes 122888 | tf_op jit(solution)/shard_map/ppermute | solution.py:176
  12.6 5.8 %collective-permute-start.2 = (bf16[32,640]{1,0:T(8,128)(2,1)S(1)}, bf16[32,640]{1,0:T(8,128)(2,1)S(1)}, u32[]{:S(2)}, u32[]{:S(2)}) collective-permute-start(bf16[32,640]{1,0:T(8,128)(2,1)S(1)} %pad_maximum_fusion.1), channel_id=1, source_target_pairs={{0,4},{4,8},{8,12},{12,0},{1,5},{5,9},{9,13},{13,1},{2,6},{6,10},{... | collective-permute-start | bytes 122888 | tf_op jit(solution)/shard_map/ppermute | solution.py:176
  18.4 1.4 %collective-permute-start.5 = (bf16[128,512]{1,0:T(8,128)(2,1)S(1)}, bf16[128,512]{1,0:T(8,128)(2,1)S(1)}, u32[]{:S(2)}, u32[]{:S(2)}) collective-permute-start(bf16[128,512]{1,0:T(8,128)(2,1)S(1)} %slice.24), channel_id=1, source_target_pairs={{0,1},{1,0},{2,3},{3,2},{4,5},{5,4},{6,7},{7,6},{8,9},{9,8},{10,11... | collective-permute-start | bytes 393224 | tf_op jit(solution)/shard_map/ppermute | solution.py:173
  20.7 12.8 %copy-start = (bf16[1024,1024]{1,0:T(8,128)(2,1)S(1)}, bf16[1024,1024]{1,0:T(8,128)(2,1)}, u32[]{:S(2)}) copy-start(bf16[1024,1024]{1,0:T(8,128)(2,1)} %weight_ref.3) | copy-start | bytes 6291460
  20.7 1.4 %collective-permute-start.6 = (bf16[128,512]{1,0:T(8,128)(2,1)S(1)}, bf16[128,512]{1,0:T(8,128)(2,1)S(1)}, u32[]{:S(2)}, u32[]{:S(2)}) collective-permute-start(bf16[128,512]{1,0:T(8,128)(2,1)S(1)} %get-tuple-element.20), channel_id=1, source_target_pairs={{0,1},{1,0},{2,3},{3,2},{4,5},{5,4},{6,7},{7,6},{8,9},{9,8},{10,11... | collective-permute-start | bytes 393224 | tf_op jit(solution)/shard_map/ppermute | solution.py:173
  22.2 4.0 %collective-permute-start.7 = (bf16[32,512]{1,0:T(8,128)(2,1)S(1)}, bf16[32,512]{1,0:T(8,128)(2,1)S(1)}, u32[]{:S(2)}, u32[]{:S(2)}) collective-permute-start(bf16[32,512]{1,0:T(8,128)(2,1)S(1)} %get-tuple-element.21), channel_id=1, source_target_pairs={{0,12},{4,0},{8,4},{12,8},{1,13},{5,1},{9,5},{13,9},{2,14},{6,2},{... | collective-permute-start | bytes 98312 | tf_op jit(solution)/shard_map/ppermute | solution.py:176
  23.0 5.7 %collective-permute-start.9 = (bf16[32,512]{1,0:T(8,128)(2,1)S(1)}, bf16[32,512]{1,0:T(8,128)(2,1)S(1)}, u32[]{:S(2)}, u32[]{:S(2)}) collective-permute-start(bf16[32,512]{1,0:T(8,128)(2,1)S(1)} %get-tuple-element.22), channel_id=1, source_target_pairs={{0,4},{4,8},{8,12},{12,0},{1,5},{5,9},{9,13},{13,1},{2,6},{6,10},{... | collective-permute-start | bytes 98312 | tf_op jit(solution)/shard_map/ppermute | solution.py:176
  24.3 5.1 %collective-permute-start.8 = (bf16[32,512]{1,0:T(8,128)(2,1)S(1)}, bf16[32,512]{1,0:T(8,128)(2,1)S(1)}, u32[]{:S(2)}, u32[]{:S(2)}) collective-permute-start(bf16[32,512]{1,0:T(8,128)(2,1)S(1)} %get-tuple-element.23), channel_id=1, source_target_pairs={{0,8},{4,12},{8,0},{12,4},{1,9},{5,13},{9,1},{13,5},{2,10},{6,14},... | collective-permute-start | bytes 98312 | tf_op jit(solution)/shard_map/ppermute | solution.py:176
  29.4 4.0 %collective-permute-start.10 = (bf16[32,512]{1,0:T(8,128)(2,1)S(1)}, bf16[32,512]{1,0:T(8,128)(2,1)S(1)}, u32[]{:S(2)}, u32[]{:S(2)}) collective-permute-start(bf16[32,512]{1,0:T(8,128)(2,1)S(1)} %fusion.1), channel_id=1, source_target_pairs={{0,2},{1,3},{2,0},{3,1},{4,6},{5,7},{6,4},{7,5},{8,10},{9,11},{10,... | collective-permute-start | bytes 98312 | tf_op jit(solution)/shard_map/ppermute | solution.py:173
  33.4 1.3 %collective-permute-start.11 = (bf16[32,512]{1,0:T(8,128)(2,1)S(1)}, bf16[32,512]{1,0:T(8,128)(2,1)S(1)}, u32[]{:S(2)}, u32[]{:S(2)}) collective-permute-start(bf16[32,512]{1,0:T(8,128)(2,1)S(1)} %add_convert_fusion.1.own_ref), channel_id=1, source_target_pairs={{0,1},{1,0},{2,3},{3,2},{4,5},{5,4},{6,7},{7,6},{8,9},{9,8},{10,11... | collective-permute-start | bytes 98312 | tf_op jit(solution)/shard_map/ppermute | solution.py:173

commit v10 on v8

--- a/solution.py
+++ b/solution.py
@@ -10,7 +10,8 @@
 NN = (((1,), (0,)), ((), ()))
 VMEM_LIMIT = 24 << 20
 LANES = 128
-CHUNKS = 2
+CHUNKS = 4
+STORES = 4
 
 
 def hbm(x):
@@ -147,10 +148,10 @@
 def up_kernel(part_ref, other_ref, weight_ref, out_hbm, out, sems):
     other = other_ref[...]
     at_rows = pl.ds(half_at(False, other.shape[1]), other.shape[1])
-    half = out.shape[1] // 2
+    size = out.shape[1] // STORES
     copies = []
-    for i in range(2):
-        at = slice(i * half, (i + 1) * half)
+    for i in range(STORES):
+        at = slice(i * size, (i + 1) * size)
         out[:, at] = (part_ref[:, at] + dot(other, weight_ref[at_rows, at], NN)).astype(BF16)
         copies.append(pltpu.make_async_copy(out.at[:, at], out_hbm.at[:, at], sems.at[i]))
         copies[i].start()
@@ -167,6 +168,7 @@
     all_units = local_count * units
     out_len = lat_up.shape[1]
     terms_len = -(-2 * local_count * exp_count // LANES) * LANES
+    order = (*range(exp_count // 2, exp_count), *range(exp_count // 2 - 1, 0, -1))
     pair_masks = [1 << b for b in range(1, tp_count.bit_length() - 1)]
 
     def traded(x, axis, mask):
@@ -220,8 +222,8 @@
     )
     up_here, down_here = vmem(up_here), vmem(down_here)
     message = jnp.concatenate([across(mine).astype(BF16), terms], axis=1)
-    messages = [message] + [traded(message, "exp", s) for s in range(1, exp_count)]
-    messages = jnp.concatenate(messages, axis=0)
+    found = {s: traded(message, "exp", s) for s in order[::-1]}
+    messages = jnp.concatenate([message] + [found[s] for s in range(1, exp_count)], axis=0)
     other = traded(messages[:, :half], "tp", 1)
     pre = kernel_call(
         first_kernel,
@@ -253,7 +255,7 @@
     part = (mine + traded(theirs, "tp", 1).astype(F32)).astype(BF16)
     blocks = part.reshape(exp_count, rows, half)
     mixed = blocks[0].astype(F32)
-    for s in (exp_count - 1, *range(1, exp_count - 1)):
+    for s in (order[0], *order[:0:-1]):
         mixed = mixed + traded(blocks[s], "exp", s).astype(F32)
     mixed = across(mixed).astype(BF16)
     lat_up = vmem(lat_up)
@@ -271,7 +273,7 @@
         shaped(BF16, rows, out_len),
         (own_part, traded(mixed, "tp", 1), lat_up),
         (),
-        [pltpu.VMEM((rows, out_len), BF16), pltpu.SemaphoreType.DMA((2,))],
+        [pltpu.VMEM((rows, out_len), BF16), pltpu.SemaphoreType.DMA((STORES,))],
         rows * latent_len * out_len,
         latent_len * out_len,
         pltpu.HBM,

time: 34.5 us -> 35.7 us (1.035)
  waiting for transfers between devices: 12 us -> 13.9 us
  starting transfers between devices: 14 us -> 13.1 us
    ppermute x12, waiting for transfers between devices: 12 us -> 13.9 us  [traded(): lax.ppermute(x, axis, [(i, i ^ mask) for i in range(lax.axis_size(axis))])]
    ppermute x12, starting transfers between devices: 14 us -> 13.1 us  [traded(): lax.ppermute(x, axis, [(i, i ^ mask) for i in range(lax.axis_size(axis))])]
  transfers between devices with their start and end apart: 12 -> 12, of which waited for: 10 -> 9; matrix products, arithmetic and copies ran while one was open for 0% -> 0% of each run, Pallas kernels for 13% -> 12%
where the time goes in v10:
time: 35.7 us; the launch traced here: 35.5 us
  waiting for transfers between devices  13.9 us (39%)
  starting transfers between devices  13.1 us (37%)
  Pallas kernels  8.31 us (23%)
    ppermute x12, waiting for transfers between devices, traded(): lax.ppermute(x, axis, [(i, i ^ mask) for i in range(lax.axis_size(axis))])  13.9 us
    ppermute x12, starting transfers between devices, traded(): lax.ppermute(x, axis, [(i, i ^ mask) for i in range(lax.axis_size(axis))])  13.1 us
    pallas_call x8, Pallas kernels, kernel_call(): pl.pallas_call(body, out_shape=out_shape, in_specs=[spec(pltpu.HBM if i i...  8.31 us
  transfers between devices with their start and end apart: 12, of which 9 were waited for; matrix products, arithmetic and copies ran while one was open for 0% of the time, Pallas kernels for 12%

profile of v10, /device:TPU:0, one launch (start us, length us, event | category | flops | bytes accessed | tf_op | source)
XLA Modules:
  0.0 35.5 jit_solution(1803885298526415916)
XLA Ops:
  0.0 2.1 %shard_map.73 = (bf16[32,512]{1,0:T(8,128)(2,1)S(1)}, bf16[32,1024]{1,0:T(8,128)(2,1)S(1)}, bf16[512,1024]{1,0:T(8,128)(2,1)S(1)}) custom-call(bf16[32,1024]{1,0:T(8,128)(2,1)} %tokens_hbm.1, bf16[1024,1024]{1,0:T(8,128)(2,1)} %weight_hbm.1), custom_call_target="tpu_custom_call" | custom-call | flops 33554432 | bytes 2097152 | tf_op jit(solution)/shard_map/pallas_call | solution.py:33
  2.1 0.5 %collective-permute-start = (bf16[32,512]{1,0:T(8,128)(2,1)S(1)}, bf16[32,512]{1,0:T(8,128)(2,1)S(1)}, u32[]{:S(2)}, u32[]{:S(2)}) collective-permute-start(bf16[32,512]{1,0:T(8,128)(2,1)S(1)} %get-tuple-element.15), channel_id=1, source_target_pairs={{0,1},{1,0},{2,3},{3,2},{4,5},{5,4},{6,7},{7,6},{8,9},{9,8},{10,11... | collective-permute-start | bytes 98312 | tf_op jit(solution)/shard_map/ppermute | solution.py:175
  2.6 0.4 %shard_map.74 = f32[32,512]{1,0:T(8,128)S(1)} custom-call(bf16[32,1024]{1,0:T(8,128)(2,1)S(1)} %get-tuple-element.13.tokens_ref, bf16[512,1024]{1,0:T(8,128)(2,1)S(1)} %get-tuple-element.14.weight_ref), custom_call_target="tpu_custom_call" | custom-call | flops 33554432 | bytes 1048576 | tf_op jit(solution)/shard_map/pallas_call | solution.py:33
  3.0 0.5 %collective-permute-done = bf16[32,512]{1,0:T(8,128)(2,1)S(1)} collective-permute-done((bf16[32,512]{1,0:T(8,128)(2,1)S(1)}, bf16[32,512]{1,0:T(8,128)(2,1)S(1)}, u32[]{:S(2)}, u32[]{:S(2)}) %collective-permute-start) | collective-permute-done | bytes 32800 | tf_op jit(solution)/shard_map/ppermute | solution.py:175
  3.5 2.9 %collective-permute-start.1 = (bf16[32,512]{1,0:T(8,128)(2,1)S(1)}, bf16[32,512]{1,0:T(8,128)(2,1)S(1)}, u32[]{:S(2)}, u32[]{:S(2)}) collective-permute-start(bf16[32,512]{1,0:T(8,128)(2,1)S(1)} %fusion.after_ref), channel_id=1, source_target_pairs={{0,2},{1,3},{2,0},{3,1},{4,6},{5,7},{6,4},{7,5},{8,10},{9,11},{10,... | collective-permute-start | bytes 98312 | tf_op jit(solution)/shard_map/ppermute | solution.py:175
  6.4 2.7 %shard_map.75 = (bf16[32,128]{1,0:T(8,128)(2,1)S(1)}, bf16[2,672,1024]{2,1,0:T(8,128)(2,1)S(1)}, bf16[1344,1024]{1,0:T(8,128)(2,1)S(1)}) custom-call(bf16[32,512]{1,0:T(8,128)(2,1)S(1)} %fusion.after_ref, s32[4,32]{1,0:T(4,128)} %bitcast.4, f32[4,32]{1,0:T(4,128)} %bitcast.5, bf16[2,672,1024]{2,1,0:T(8,128)(2,1)} %up_hbm.1, bf16[1344,1024]{1,0:T(8,128)(2,1)} %bitcast.3), custom_call_target="tpu_custom_call" | custom-call | bytes 5505024 | tf_op jit(solution)/shard_map/pallas_call | solution.py:33
  9.1 3.7 %collective-permute-start.4 = (bf16[32,640]{1,0:T(8,128)(2,1)S(1)}, bf16[32,640]{1,0:T(8,128)(2,1)S(1)}, u32[]{:S(2)}, u32[]{:S(2)}) collective-permute-start(bf16[32,640]{1,0:T(8,128)(2,1)S(1)} %pad_maximum_fusion.1), channel_id=1, source_target_pairs={{0,12},{4,8},{8,4},{12,0},{1,13},{5,9},{9,5},{13,1},{2,14},{6,10},... | collective-permute-start | bytes 122888 | tf_op jit(solution)/shard_map/ppermute | solution.py:175
  12.8 0.0 collective-permute-start.3
  12.8 0.8 %collective-permute-start.2 = (bf16[32,640]{1,0:T(8,128)(2,1)S(1)}, bf16[32,640]{1,0:T(8,128)(2,1)S(1)}, u32[]{:S(2)}, u32[]{:S(2)}) collective-permute-start(bf16[32,640]{1,0:T(8,128)(2,1)S(1)} %pad_maximum_fusion.1), channel_id=1, source_target_pairs={{0,4},{4,0},{8,12},{12,8},{1,5},{5,1},{9,13},{13,9},{2,6},{6,2},{1... | collective-permute-start | bytes 122888 | tf_op jit(solution)/shard_map/ppermute | solution.py:175
  13.6 1.5 %collective-permute-done.4 = bf16[32,640]{1,0:T(8,128)(2,1)S(1)} collective-permute-done((bf16[32,640]{1,0:T(8,128)(2,1)S(1)}, bf16[32,640]{1,0:T(8,128)(2,1)S(1)}, u32[]{:S(2)}, u32[]{:S(2)}) %collective-permute-start.4) | collective-permute-done | bytes 40992 | tf_op jit(solution)/shard_map/ppermute | solution.py:175
  15.1 2.6 %collective-permute-done.3 = bf16[32,640]{1,0:T(8,128)(2,1)S(1)} collective-permute-done((bf16[32,640]{1,0:T(8,128)(2,1)S(1)}, bf16[32,640]{1,0:T(8,128)(2,1)S(1)}, u32[]{:S(2)}, u32[]{:S(2)}) %collective-permute-start.3) | collective-permute-done | bytes 40992 | tf_op jit(solution)/shard_map/ppermute | solution.py:175
  17.7 0.0 collective-permute-done.2
  17.7 0.1 collective-permute-start.5
  17.8 0.7 %shard_map.76.pre_ref = f32[128,1344]{1,0:T(8,128)S(1)} custom-call(bf16[128,640]{1,0:T(8,128)(2,1)S(1)} %pad_maximum_fusion.messages_ref, bf16[2,672,1024]{2,1,0:T(8,128)(2,1)S(1)} %get-tuple-element.17.up_ref), custom_call_target="tpu_custom_call" | custom-call | flops 176160768 | bytes 1376256 | tf_op jit(solution)/shard_map/pallas_call | solution.py:33
  18.5 0.7 %collective-permute-done.5.other_ref = bf16[128,512]{1,0:T(8,128)(2,1)S(1)} collective-permute-done((bf16[128,512]{1,0:T(8,128)(2,1)S(1)}, bf16[128,512]{1,0:T(8,128)(2,1)S(1)}, u32[]{:S(2)}, u32[]{:S(2)}) %collective-permute-start.5) | collective-permute-done | bytes 131104 | tf_op jit(solution)/shard_map/ppermute | solution.py:175
  19.1 0.9 %shard_map.77 = (bf16[128,1344]{1,0:T(8,128)(2,1)S(1)}, bf16[128,512]{1,0:T(8,128)(2,1)S(1)}) custom-call(bf16[128,640]{1,0:T(8,128)(2,1)S(1)} %pad_maximum_fusion.messages_ref, bf16[128,512]{1,0:T(8,128)(2,1)S(1)} %collective-permute-done.5.other_ref, f32[128,1344]{1,0:T(8,128)S(1)} %shard_map.76.pre_ref, ...), custom_call_target="tpu_custom_call" | custom-call | flops 352321536 | bytes 2752512 | tf_op jit(solution)/shard_map/pallas_call | solution.py:33
  20.0 0.0 copy-start
  20.0 0.2 collective-permute-start.6
  20.2 0.4 %shard_map.78 = f32[128,512]{1,0:T(8,128)S(1)} custom-call(bf16[128,1344]{1,0:T(8,128)(2,1)S(1)} %get-tuple-element.19.hidden_ref, bf16[1344,1024]{1,0:T(8,128)(2,1)S(1)} %get-tuple-element.18.down_ref), custom_call_target="tpu_custom_call" | custom-call | flops 176160768 | bytes 1376256 | tf_op jit(solution)/shard_map/pallas_call | solution.py:33
  20.6 0.8 %collective-permute-done.6 = bf16[128,512]{1,0:T(8,128)(2,1)S(1)} collective-permute-done((bf16[128,512]{1,0:T(8,128)(2,1)S(1)}, bf16[128,512]{1,0:T(8,128)(2,1)S(1)}, u32[]{:S(2)}, u32[]{:S(2)}) %collective-permute-start.6) | collective-permute-done | bytes 131104 | tf_op jit(solution)/shard_map/ppermute | solution.py:175
  21.5 2.1 %collective-permute-start.7 = (bf16[32,512]{1,0:T(8,128)(2,1)S(1)}, bf16[32,512]{1,0:T(8,128)(2,1)S(1)}, u32[]{:S(2)}, u32[]{:S(2)}) collective-permute-start(bf16[32,512]{1,0:T(8,128)(2,1)S(1)} %get-tuple-element.21), channel_id=1, source_target_pairs={{0,8},{4,12},{8,0},{12,4},{1,9},{5,13},{9,1},{13,5},{2,10},{6,14},... | collective-permute-start | bytes 98312 | tf_op jit(solution)/shard_map/ppermute | solution.py:175
  23.6 0.5 %collective-permute-start.9 = (bf16[32,512]{1,0:T(8,128)(2,1)S(1)}, bf16[32,512]{1,0:T(8,128)(2,1)S(1)}, u32[]{:S(2)}, u32[]{:S(2)}) collective-permute-start(bf16[32,512]{1,0:T(8,128)(2,1)S(1)} %get-tuple-element.22), channel_id=1, source_target_pairs={{0,12},{4,8},{8,4},{12,0},{1,13},{5,9},{9,5},{13,1},{2,14},{6,10},... | collective-permute-start | bytes 98312 | tf_op jit(solution)/shard_map/ppermute | solution.py:175
  24.1 0.9 %collective-permute-start.8 = (bf16[32,512]{1,0:T(8,128)(2,1)S(1)}, bf16[32,512]{1,0:T(8,128)(2,1)S(1)}, u32[]{:S(2)}, u32[]{:S(2)}) collective-permute-start(bf16[32,512]{1,0:T(8,128)(2,1)S(1)} %get-tuple-element.23), channel_id=1, source_target_pairs={{0,4},{4,0},{8,12},{12,8},{1,5},{5,1},{9,13},{13,9},{2,6},{6,2},{1... | collective-permute-start | bytes 98312 | tf_op jit(solution)/shard_map/ppermute | solution.py:175
  25.0 1.7 %collective-permute-done.7 = bf16[32,512]{1,0:T(8,128)(2,1)S(1)} collective-permute-done((bf16[32,512]{1,0:T(8,128)(2,1)S(1)}, bf16[32,512]{1,0:T(8,128)(2,1)S(1)}, u32[]{:S(2)}, u32[]{:S(2)}) %collective-permute-start.7) | collective-permute-done | bytes 32800 | tf_op jit(solution)/shard_map/ppermute | solution.py:175
  26.8 2.5 %collective-permute-done.9 = bf16[32,512]{1,0:T(8,128)(2,1)S(1)} collective-permute-done((bf16[32,512]{1,0:T(8,128)(2,1)S(1)}, bf16[32,512]{1,0:T(8,128)(2,1)S(1)}, u32[]{:S(2)}, u32[]{:S(2)}) %collective-permute-start.9) | collective-permute-done | bytes 32800 | tf_op jit(solution)/shard_map/ppermute | solution.py:175
  29.3 0.0 collective-permute-done.8
  29.3 1.3 %collective-permute-start.10 = (bf16[32,512]{1,0:T(8,128)(2,1)S(1)}, bf16[32,512]{1,0:T(8,128)(2,1)S(1)}, u32[]{:S(2)}, u32[]{:S(2)}) collective-permute-start(bf16[32,512]{1,0:T(8,128)(2,1)S(1)} %fusion.1), channel_id=1, source_target_pairs={{0,2},{1,3},{2,0},{3,1},{4,6},{5,7},{6,4},{7,5},{8,10},{9,11},{10,... | collective-permute-start | bytes 98312 | tf_op jit(solution)/shard_map/ppermute | solution.py:175
  30.6 2.7 %collective-permute-done.10 = bf16[32,512]{1,0:T(8,128)(2,1)S(1)} collective-permute-done((bf16[32,512]{1,0:T(8,128)(2,1)S(1)}, bf16[32,512]{1,0:T(8,128)(2,1)S(1)}, u32[]{:S(2)}, u32[]{:S(2)}) %collective-permute-start.10) | collective-permute-done | bytes 32800 | tf_op jit(solution)/shard_map/ppermute | solution.py:175
  33.3 0.1 collective-permute-start.11
  33.4 0.3 shard_map.79.part_ref
  33.7 0.9 %collective-permute-done.11.other_ref = bf16[32,512]{1,0:T(8,128)(2,1)S(1)} collective-permute-done((bf16[32,512]{1,0:T(8,128)(2,1)S(1)}, bf16[32,512]{1,0:T(8,128)(2,1)S(1)}, u32[]{:S(2)}, u32[]{:S(2)}) %collective-permute-start.11) | collective-permute-done | bytes 32800 | tf_op jit(solution)/shard_map/ppermute | solution.py:175
  34.6 0.9 %shard_map.80 = bf16[32,1024]{1,0:T(8,128)(2,1)} custom-call(f32[32,1024]{1,0:T(8,128)S(1)} %shard_map.79.part_ref, bf16[32,512]{1,0:T(8,128)(2,1)S(1)} %collective-permute-done.11.other_ref, bf16[1024,1024]{1,0:T(8,128)(2,1)S(1)} %copy-done), custom_call_target="tpu_custom_call" | custom-call | flops 33554432 | bytes 1048576 | tf_op jit(solution)/shard_map/pallas_call | solution.py:33
  (11 shorter events, 0.1 us)
Async XLA Ops:
  2.1 1.4 %collective-permute-start = (bf16[32,512]{1,0:T(8,128)(2,1)S(1)}, bf16[32,512]{1,0:T(8,128)(2,1)S(1)}, u32[]{:S(2)}, u32[]{:S(2)}) collective-permute-start(bf16[32,512]{1,0:T(8,128)(2,1)S(1)} %get-tuple-element.15), channel_id=1, source_target_pairs={{0,1},{1,0},{2,3},{3,2},{4,5},{5,4},{6,7},{7,6},{8,9},{9,8},{10,11... | collective-permute-start | bytes 98312 | tf_op jit(solution)/shard_map/ppermute | solution.py:175
  3.5 5.6 %collective-permute-start.1 = (bf16[32,512]{1,0:T(8,128)(2,1)S(1)}, bf16[32,512]{1,0:T(8,128)(2,1)S(1)}, u32[]{:S(2)}, u32[]{:S(2)}) collective-permute-start(bf16[32,512]{1,0:T(8,128)(2,1)S(1)} %fusion.after_ref), channel_id=1, source_target_pairs={{0,2},{1,3},{2,0},{3,1},{4,6},{5,7},{6,4},{7,5},{8,10},{9,11},{10,... | collective-permute-start | bytes 98312 | tf_op jit(solution)/shard_map/ppermute | solution.py:175
  9.1 6.0 %collective-permute-start.4 = (bf16[32,640]{1,0:T(8,128)(2,1)S(1)}, bf16[32,640]{1,0:T(8,128)(2,1)S(1)}, u32[]{:S(2)}, u32[]{:S(2)}) collective-permute-start(bf16[32,640]{1,0:T(8,128)(2,1)S(1)} %pad_maximum_fusion.1), channel_id=1, source_target_pairs={{0,12},{4,8},{8,4},{12,0},{1,13},{5,9},{9,5},{13,1},{2,14},{6,10},... | collective-permute-start | bytes 122888 | tf_op jit(solution)/shard_map/ppermute | solution.py:175
  12.8 4.9 %collective-permute-start.3 = (bf16[32,640]{1,0:T(8,128)(2,1)S(1)}, bf16[32,640]{1,0:T(8,128)(2,1)S(1)}, u32[]{:S(2)}, u32[]{:S(2)}) collective-permute-start(bf16[32,640]{1,0:T(8,128)(2,1)S(1)} %pad_maximum_fusion.1), channel_id=1, source_target_pairs={{0,8},{4,12},{8,0},{12,4},{1,9},{5,13},{9,1},{13,5},{2,10},{6,14},... | collective-permute-start | bytes 122888 | tf_op jit(solution)/shard_map/ppermute | solution.py:175
  12.8 4.9 %collective-permute-start.2 = (bf16[32,640]{1,0:T(8,128)(2,1)S(1)}, bf16[32,640]{1,0:T(8,128)(2,1)S(1)}, u32[]{:S(2)}, u32[]{:S(2)}) collective-permute-start(bf16[32,640]{1,0:T(8,128)(2,1)S(1)} %pad_maximum_fusion.1), channel_id=1, source_target_pairs={{0,4},{4,0},{8,12},{12,8},{1,5},{5,1},{9,13},{13,9},{2,6},{6,2},{1... | collective-permute-start | bytes 122888 | tf_op jit(solution)/shard_map/ppermute | solution.py:175
  17.7 1.4 %collective-permute-start.5 = (bf16[128,512]{1,0:T(8,128)(2,1)S(1)}, bf16[128,512]{1,0:T(8,128)(2,1)S(1)}, u32[]{:S(2)}, u32[]{:S(2)}) collective-permute-start(bf16[128,512]{1,0:T(8,128)(2,1)S(1)} %slice.24), channel_id=1, source_target_pairs={{0,1},{1,0},{2,3},{3,2},{4,5},{5,4},{6,7},{7,6},{8,9},{9,8},{10,11... | collective-permute-start | bytes 393224 | tf_op jit(solution)/shard_map/ppermute | solution.py:175
  20.0 13.4 %copy-start = (bf16[1024,1024]{1,0:T(8,128)(2,1)S(1)}, bf16[1024,1024]{1,0:T(8,128)(2,1)}, u32[]{:S(2)}) copy-start(bf16[1024,1024]{1,0:T(8,128)(2,1)} %weight_ref.3) | copy-start | bytes 6291460
  20.0 1.4 %collective-permute-start.6 = (bf16[128,512]{1,0:T(8,128)(2,1)S(1)}, bf16[128,512]{1,0:T(8,128)(2,1)S(1)}, u32[]{:S(2)}, u32[]{:S(2)}) collective-permute-start(bf16[128,512]{1,0:T(8,128)(2,1)S(1)} %get-tuple-element.20), channel_id=1, source_target_pairs={{0,1},{1,0},{2,3},{3,2},{4,5},{5,4},{6,7},{7,6},{8,9},{9,8},{10,11... | collective-permute-start | bytes 393224 | tf_op jit(solution)/shard_map/ppermute | solution.py:175
  21.5 5.3 %collective-permute-start.7 = (bf16[32,512]{1,0:T(8,128)(2,1)S(1)}, bf16[32,512]{1,0:T(8,128)(2,1)S(1)}, u32[]{:S(2)}, u32[]{:S(2)}) collective-permute-start(bf16[32,512]{1,0:T(8,128)(2,1)S(1)} %get-tuple-element.21), channel_id=1, source_target_pairs={{0,8},{4,12},{8,0},{12,4},{1,9},{5,13},{9,1},{13,5},{2,10},{6,14},... | collective-permute-start | bytes 98312 | tf_op jit(solution)/shard_map/ppermute | solution.py:175
  23.6 5.7 %collective-permute-start.9 = (bf16[32,512]{1,0:T(8,128)(2,1)S(1)}, bf16[32,512]{1,0:T(8,128)(2,1)S(1)}, u32[]{:S(2)}, u32[]{:S(2)}) collective-permute-start(bf16[32,512]{1,0:T(8,128)(2,1)S(1)} %get-tuple-element.22), channel_id=1, source_target_pairs={{0,12},{4,8},{8,4},{12,0},{1,13},{5,9},{9,5},{13,1},{2,14},{6,10},... | collective-permute-start | bytes 98312 | tf_op jit(solution)/shard_map/ppermute | solution.py:175
  24.1 5.2 %collective-permute-start.8 = (bf16[32,512]{1,0:T(8,128)(2,1)S(1)}, bf16[32,512]{1,0:T(8,128)(2,1)S(1)}, u32[]{:S(2)}, u32[]{:S(2)}) collective-permute-start(bf16[32,512]{1,0:T(8,128)(2,1)S(1)} %get-tuple-element.23), channel_id=1, source_target_pairs={{0,4},{4,0},{8,12},{12,8},{1,5},{5,1},{9,13},{13,9},{2,6},{6,2},{1... | collective-permute-start | bytes 98312 | tf_op jit(solution)/shard_map/ppermute | solution.py:175
  29.3 4.0 %collective-permute-start.10 = (bf16[32,512]{1,0:T(8,128)(2,1)S(1)}, bf16[32,512]{1,0:T(8,128)(2,1)S(1)}, u32[]{:S(2)}, u32[]{:S(2)}) collective-permute-start(bf16[32,512]{1,0:T(8,128)(2,1)S(1)} %fusion.1), channel_id=1, source_target_pairs={{0,2},{1,3},{2,0},{3,1},{4,6},{5,7},{6,4},{7,5},{8,10},{9,11},{10,... | collective-permute-start | bytes 98312 | tf_op jit(solution)/shard_map/ppermute | solution.py:175
  33.3 1.3 %collective-permute-start.11 = (bf16[32,512]{1,0:T(8,128)(2,1)S(1)}, bf16[32,512]{1,0:T(8,128)(2,1)S(1)}, u32[]{:S(2)}, u32[]{:S(2)}) collective-permute-start(bf16[32,512]{1,0:T(8,128)(2,1)S(1)} %add_convert_fusion.1.own_ref), channel_id=1, source_target_pairs={{0,1},{1,0},{2,3},{3,2},{4,5},{5,4},{6,7},{7,6},{8,9},{9,8},{10,11... | collective-permute-start | bytes 98312 | tf_op jit(solution)/shard_map/ppermute | solution.py:175

commit v11 on v7

v11 whole, which is shorter than its diff:
```python
import jax
import jax.numpy as jnp
from jax import lax
from jax.experimental import pallas as pl
from jax.experimental.pallas import tpu as pltpu
from jax.sharding import PartitionSpec as P

BF16, F32 = jnp.bfloat16, jnp.float32
NT = (((1,), (1,)), ((), ()))
NN = (((1,), (0,)), ((), ()))
VMEM_LIMIT = 24 << 20
LANES = 128


def hbm(x):
    return pltpu.with_memory_space_constraint(x, pltpu.HBM)


def vmem(x):
    return pltpu.with_memory_space_constraint(x, pltpu.VMEM)


def shaped(dtype, *shape):
    return jax.ShapeDtypeStruct(shape, dtype)


def kernel_call(body, out_shape, args, in_hbm, scratch, flops, moved, out_space=pltpu.VMEM):
    def spec(space):
        return pl.BlockSpec(memory_space=space)

    return pl.pallas_call(
        body,
        out_shape=out_shape,
        in_specs=[spec(pltpu.HBM if i in in_hbm else pltpu.VMEM) for i in range(len(args))],
        out_specs=jax.tree.map(lambda _: spec(out_space), out_shape),
        scratch_shapes=scratch,
        compiler_params=pltpu.CompilerParams(vmem_limit_bytes=VMEM_LIMIT),
        cost_estimate=pl.CostEstimate(flops=flops, bytes_accessed=moved, transcendentals=0),
    )(*args)


def dot(a, b, dims):
    return lax.dot_general(a, b, dims, preferred_element_type=F32)


def speaks():
    return lax.axis_index("tp") % 2 == 1


def down_kernel(tokens_hbm, weight_hbm, out_ref, tokens, weight, sems):
    length = out_ref.shape[1]
    load = pltpu.make_async_copy(tokens_hbm, tokens, sems.at[0])
    load.start()
    pieces = [slice(0, length // 4), slice(length // 4, length // 2), slice(length // 2, length)]
    copies = []
    for i, at in enumerate(pieces):
        copies.append(pltpu.make_async_copy(weight_hbm.at[at, :], weight.at[at, :], sems.at[1 + i]))
        copies[i].start()
    load.wait()
    x = tokens[...]
    for copy, at in zip(copies, pieces):
        copy.wait()
        out_ref[:, at] = dot(x, weight[at, :], NT).astype(BF16)


def load_kernel(
    after_ref, routes_hbm, scale_hbm, up_hbm, down_hbm, terms_ref, up_ref, down_ref,
    routes, scale, sems,
):
    pairs = [(routes_hbm, routes), (scale_hbm, scale), (up_hbm, up_ref), (down_hbm, down_ref)]
    copies = [pltpu.make_async_copy(a, b, sems.at[i]) for i, (a, b) in enumerate(pairs)]
    for copy in copies:
        copy.start()
    copies[0].wait()
    copies[1].wait()
    rows, width = terms_ref.shape
    row = lax.broadcasted_iota(jnp.int32, (width, rows), 0)
    experts_all = width // 2
    expert = jnp.where(row < experts_all, row, row - experts_all)
    combine = jnp.zeros((width, rows), F32)
    for r in range(routes.shape[0]):
        combine += jnp.where(expert == routes[r : r + 1, :], scale[r : r + 1, :], 0.0)
    high = combine.astype(BF16).astype(F32)
    combine = jnp.where(row < experts_all, high, combine - high)
    combine = jnp.concatenate([combine, jnp.zeros((width, LANES - rows), F32)], axis=1)
    terms_ref[...] = combine.T[:rows, :].astype(BF16)
    copies[2].wait()
    copies[3].wait()


def first_kernel(own_ref, other_ref, up_ref, pre_ref):
    local_count, units, latent_len = up_ref.shape
    half = latent_len // 2
    rows = jnp.where(speaks(), own_ref[:, :half], other_ref[:, :half])
    for k in range(local_count):
        pre_ref[:, k * units : (k + 1) * units] = dot(rows, up_ref[k, :, :half], NT)


def second_kernel(
    own_ref, other_ref, late_own_ref, late_other_ref, pre_ref, up_ref, down_ref, out_ref, hidden
):
    local_count, units, latent_len = up_ref.shape
    half = latent_len // 2
    speaking = speaks()
    terms = jnp.where(speaking, own_ref[:, half:], other_ref[:, half:]).astype(F32)
    rows = jnp.where(speaking, late_own_ref[...], late_other_ref[...])
    lane = lax.broadcasted_iota(jnp.int32, terms.shape, 1)
    first = lax.axis_index("exp") * local_count
    for k in range(local_count):
        named = (lane == first + k) | (lane == first + k + terms.shape[1] // 2)
        weight = jnp.sum(jnp.where(named, terms, 0.0), axis=1, keepdims=True)
        at = slice(k * units, (k + 1) * units)
        active = jnp.maximum(pre_ref[:, at] + dot(rows, up_ref[k, :, half:], NT), 0.0)
        hidden[:, at] = (active * active * weight).astype(BF16)
    acts = hidden[...]
    for at in (slice(0, half), slice(half, latent_len)):
        out_ref[:, at] = dot(acts, down_ref[:, at], NN).astype(BF16)


def up_kernel(own_ref, other_ref, weight_ref, out_hbm, out, sems):
    mixed = jnp.where(speaks(), own_ref[...], other_ref[...])
    half = out.shape[1] // 2
    copies = []
    for i in range(2):
        at = slice(i * half, (i + 1) * half)
        out[:, at] = dot(mixed, weight_ref[:, at], NN).astype(BF16)
        copies.append(pltpu.make_async_copy(out.at[:, at], out_hbm.at[:, at], sems.at[i]))
        copies[i].start()
    for copy in copies:
        copy.wait()


def on_device(tokens, lat_down, lat_up, expert_up, expert_down, routes, route_weights):
    exp_count, tp_count = lax.axis_size("exp"), lax.axis_size("tp")
    local_count, units, latent_len = expert_up.shape
    rows, width = tokens.shape
    half = latent_len // 2
    all_rows = exp_count * rows
    all_units = local_count * units
    out_len = lat_up.shape[1]
    terms_len = -(-2 * local_count * exp_count // LANES) * LANES
    pair_masks = [1 << b for b in range(1, tp_count.bit_length() - 1)]
    odd = range(1, tp_count, 2)

    def to_speaker(x):
        return lax.ppermute(x, "tp", [(t - 1, t) for t in odd])

    def from_speaker(x):
        return lax.ppermute(x, "tp", [(t, t - 1) for t in odd])

    def traded(x, mask):
        places = [(e, t) for e in range(exp_count) for t in odd]
        hops = [(e * tp_count + t, (e ^ mask) * tp_count + t) for e, t in places]
        return lax.ppermute(x, ("exp", "tp"), hops)

    def total(*parts):
        return sum(p.astype(F32) for p in parts).astype(BF16)

    def across(x):
        for mask in pair_masks:
            x = total(x, lax.ppermute(x, "tp", [(t, t ^ mask) for t in odd]))
        return x

    partial = kernel_call(
        down_kernel,
        shaped(BF16, rows, latent_len),
        (hbm(tokens), hbm(lat_down)),
        (0, 1),
        [
            pltpu.VMEM((rows, width), BF16),
            pltpu.VMEM((latent_len, width), BF16),
            pltpu.SemaphoreType.DMA((4,)),
        ],
        2 * rows * width * latent_len,
        2 * width * latent_len,
    )
    partial = total(partial, to_speaker(partial))
    down_rows = expert_down.reshape(all_units, latent_len)
    terms, up_here, down_here = kernel_call(
        load_kernel,
        (
            shaped(BF16, rows, terms_len),
            pltpu.VMEM(expert_up.shape, BF16),
            pltpu.VMEM(down_rows.shape, BF16),
        ),
        (partial, *(hbm(x) for x in (routes.T, route_weights.T, expert_up, down_rows))),
        (1, 2, 3, 4),
        [
            pltpu.VMEM(routes.shape[::-1], jnp.int32),
            pltpu.VMEM(routes.shape[::-1], F32),
            pltpu.SemaphoreType.DMA((4,)),
        ],
        0,
        4 * latent_len * all_units,
    )
    up_here, down_here = vmem(up_here), vmem(down_here)
    latent = across(partial)
    message = jnp.concatenate([latent[:, :half], terms, latent[:, half:]], axis=1)
    messages = [message] + [traded(message, s) for s in range(1, exp_count)]
    messages = jnp.concatenate(messages, axis=0)
    early, late = messages[:, : half + terms_len], messages[:, half + terms_len :]
    early_other, late_other = from_speaker(early), from_speaker(late)
    pre = kernel_call(
        first_kernel,
        shaped(F32, all_rows, all_units),
        (early, early_other, up_here),
        (),
        [],
        all_rows * latent_len * all_units,
        latent_len * all_units,
    )
    part = kernel_call(
        second_kernel,
        shaped(BF16, all_rows, latent_len),
        (early, early_other, late, late_other, pre, up_here, down_here),
        (),
        [pltpu.VMEM((all_rows, all_units), BF16)],
        3 * all_rows * latent_len * all_units,
        3 * latent_len * all_units,
    )
    part = total(part, to_speaker(part))
    blocks = part.reshape(exp_count, rows, latent_len)
    mixed = blocks[0].astype(F32)
    for s in (exp_count - 1, *range(1, exp_count - 1)):
        mixed = mixed + traded(blocks[s], s).astype(F32)
    mixed = across(mixed.astype(BF16))
    return kernel_call(
        up_kernel,
        shaped(BF16, rows, out_len),
        (mixed, from_speaker(mixed), vmem(lat_up)),
        (),
        [pltpu.VMEM((rows, out_len), BF16), pltpu.SemaphoreType.DMA((2,))],
        2 * rows * latent_len * out_len,
        2 * latent_len * out_len,
        pltpu.HBM,
    )


def solution(mesh):
    return jax.shard_map(
        on_device,
        mesh=mesh,
        in_specs=(
            P(("grp", "exp"), "tp"),
            P(None, "tp"),
            P(None, "tp"),
            P("exp", "tp", None),
            P("exp", "tp", None),
            P(("grp", "exp"), None),
            P(("grp", "exp"), None),
        ),
        out_specs=P(("grp", "exp"), "tp"),
        check_vma=False,
    )
```

time: 36.8 us -> 53.1 us (1.44)
  waiting for transfers between devices: 14 us -> 30.7 us
  Pallas kernels: 9.6 us -> 7.84 us
  starting transfers between devices: 12.7 us -> 13.6 us
    ppermute x12 -> x13, waiting for transfers between devices: 14 us -> 30.7 us  [the longest x3 28.7 us: from_speaker(): return lax.ppermute(x, 'tp', [(t, t - 1) for t in odd])]
    pallas_call x8 -> x5, Pallas kernels: 9.6 us -> 7.84 us  [kernel_call(): pl.pallas_call(body, out_shape=out_shape, in_specs=[spec(pltpu.HBM if i i...]
    ppermute x12 -> x13, starting transfers between devices: 12.7 us -> 13.6 us  [the longest x2 4.43 us: to_speaker(): return lax.ppermute(x, 'tp', [(t - 1, t) for t in odd])]
  transfers between devices with their start and end apart: 12 -> 13, of which waited for: 9 -> 5; matrix products, arithmetic and copies ran while one was open for 0% -> 0% of each run, Pallas kernels for 16% -> 6%
where the time goes in v11:
time: 53.1 us; the launch traced here: 52.7 us
  waiting for transfers between devices  30.7 us (58%)
  starting transfers between devices  13.6 us (26%)
  Pallas kernels  7.84 us (15%)
    ppermute x3, waiting for transfers between devices, from_speaker(): return lax.ppermute(x, 'tp', [(t, t - 1) for t in odd])  28.7 us
    pallas_call x5, Pallas kernels, kernel_call(): pl.pallas_call(body, out_shape=out_shape, in_specs=[spec(pltpu.HBM if i i...  7.84 us
    ppermute x2, starting transfers between devices, to_speaker(): return lax.ppermute(x, 'tp', [(t - 1, t) for t in odd])  4.43 us
    ppermute x6, starting transfers between devices, traded(): return lax.ppermute(x, ('exp', 'tp'), hops)  3.99 us
    ppermute x3, starting transfers between devices, from_speaker(): return lax.ppermute(x, 'tp', [(t, t - 1) for t in odd])  3.88 us
    ppermute x2, waiting for transfers between devices, to_speaker(): return lax.ppermute(x, 'tp', [(t - 1, t) for t in odd])  2.01 us
    ppermute x2, starting transfers between devices, across(): x = total(x, lax.ppermute(x, 'tp', [(t, t ^ mask) for t in odd]))  1.33 us
  transfers between devices with their start and end apart: 13, of which 5 were waited for; matrix products, arithmetic and copies ran while one was open for 0% of the time, Pallas kernels for 6%

profile of v11, /device:TPU:0, one launch (start us, length us, event | category | flops | bytes accessed | tf_op | source)
XLA Modules:
  0.0 52.7 jit_solution(17875385346188731767)
XLA Ops:
  0.0 2.3 %shard_map.73 = bf16[32,1024]{1,0:T(8,128)(2,1)S(1)} custom-call(bf16[32,1024]{1,0:T(8,128)(2,1)} %tokens_hbm.1, bf16[1024,1024]{1,0:T(8,128)(2,1)} %weight_hbm.1), custom_call_target="tpu_custom_call" | custom-call | flops 67108864 | bytes 2097152 | tf_op jit(solution)/shard_map/pallas_call | solution.py:31
  2.3 2.4 %collective-permute-start = (bf16[32,1024]{1,0:T(8,128)(2,1)S(1)}, bf16[32,1024]{1,0:T(8,128)(2,1)S(1)}, u32[]{:S(2)}, u32[]{:S(2)}) collective-permute-start(bf16[32,1024]{1,0:T(8,128)(2,1)S(1)} %shard_map.73), channel_id=1, source_target_pairs={{0,1},{2,3},{4,5},{6,7},{8,9},{10,11},{12,13},{14,15},{16,17},{18,... | collective-permute-start | bytes 196616 | tf_op jit(solution)/shard_map/ppermute | solution.py:146
  4.7 0.9 %collective-permute-done = bf16[32,1024]{1,0:T(8,128)(2,1)S(1)} collective-permute-done((bf16[32,1024]{1,0:T(8,128)(2,1)S(1)}, bf16[32,1024]{1,0:T(8,128)(2,1)S(1)}, u32[]{:S(2)}, u32[]{:S(2)}) %collective-permute-start) | collective-permute-done | bytes 65568 | tf_op jit(solution)/shard_map/ppermute | solution.py:146
  5.6 0.7 %collective-permute-start.1 = (bf16[32,1024]{1,0:T(8,128)(2,1)S(1)}, bf16[32,1024]{1,0:T(8,128)(2,1)S(1)}, u32[]{:S(2)}, u32[]{:S(2)}) collective-permute-start(bf16[32,1024]{1,0:T(8,128)(2,1)S(1)} %add_convert_fusion.4.after_ref), channel_id=1, source_target_pairs={{1,3},{3,1},{5,7},{7,5},{9,11},{11,9},{13,15},{15,13},{17,19},{19,... | collective-permute-start | bytes 196616 | tf_op jit(solution)/shard_map/ppermute | solution.py:161
  6.3 2.7 %shard_map.74 = (bf16[32,128]{1,0:T(8,128)(2,1)S(1)}, bf16[2,672,1024]{2,1,0:T(8,128)(2,1)S(1)}, bf16[1344,1024]{1,0:T(8,128)(2,1)S(1)}) custom-call(bf16[32,1024]{1,0:T(8,128)(2,1)S(1)} %add_convert_fusion.4.after_ref, s32[4,32]{1,0:T(4,128)} %bitcast.4, f32[4,32]{1,0:T(4,128)} %bitcast.5, bf16[2,672,1024]{2,1,0:T(8,128)(2,1)} %up_hbm.1, ...), custom_call_target="tpu_custom_call" | custom-call | bytes 5505024 | tf_op jit(solution)/shard_map/pallas_call | solution.py:31
  9.0 0.0 collective-permute-done.1
  9.0 0.7 %collective-permute-start.4 = (bf16[32,1152]{1,0:T(8,128)(2,1)S(1)}, bf16[32,1152]{1,0:T(8,128)(2,1)S(1)}, u32[]{:S(2)}, u32[]{:S(2)}) collective-permute-start(bf16[32,1152]{1,0:T(8,128)(2,1)S(1)} %pad_maximum_fusion.2), channel_id=1, source_target_pairs={{1,13},{3,15},{5,9},{7,11},{9,5},{11,7},{13,1},{15,3},{17,29},{19,... | collective-permute-start | bytes 221192 | tf_op jit(solution)/shard_map/ppermute | solution.py:154
  9.7 0.7 %collective-permute-start.3 = (bf16[32,1152]{1,0:T(8,128)(2,1)S(1)}, bf16[32,1152]{1,0:T(8,128)(2,1)S(1)}, u32[]{:S(2)}, u32[]{:S(2)}) collective-permute-start(bf16[32,1152]{1,0:T(8,128)(2,1)S(1)} %pad_maximum_fusion.2), channel_id=1, source_target_pairs={{1,9},{3,11},{5,13},{7,15},{9,1},{11,3},{13,5},{15,7},{17,25},{19,... | collective-permute-start | bytes 221192 | tf_op jit(solution)/shard_map/ppermute | solution.py:154
  10.4 0.7 %collective-permute-start.2 = (bf16[32,1152]{1,0:T(8,128)(2,1)S(1)}, bf16[32,1152]{1,0:T(8,128)(2,1)S(1)}, u32[]{:S(2)}, u32[]{:S(2)}) collective-permute-start(bf16[32,1152]{1,0:T(8,128)(2,1)S(1)} %pad_maximum_fusion.2), channel_id=1, source_target_pairs={{1,5},{3,7},{5,1},{7,3},{9,13},{11,15},{13,9},{15,11},{17,21},{19,... | collective-permute-start | bytes 221192 | tf_op jit(solution)/shard_map/ppermute | solution.py:154
  11.0 0.0 collective-permute-done.4
  11.1 0.0 collective-permute-done.3
  11.1 0.0 collective-permute-done.2
  11.1 1.3 %collective-permute-start.5 = (bf16[128,640]{1,0:T(8,128)(2,1)S(1)}, bf16[128,640]{1,0:T(8,128)(2,1)S(1)}, u32[]{:S(2)}, u32[]{:S(2)}) collective-permute-start(bf16[128,640]{1,0:T(8,128)(2,1)S(1)} %slice.38.own_ref), channel_id=1, source_target_pairs={{1,0},{3,2},{5,4},{7,6},{9,8},{11,10},{13,12},{15,14},{17,16},{19,... | collective-permute-start | bytes 491528 | tf_op jit(solution)/shard_map/ppermute | solution.py:149
  12.5 1.3 %collective-permute-start.6 = (bf16[128,512]{1,0:T(8,128)(2,1)S(1)}, bf16[128,512]{1,0:T(8,128)(2,1)S(1)}, u32[]{:S(2)}, u32[]{:S(2)}) collective-permute-start(bf16[128,512]{1,0:T(8,128)(2,1)S(1)} %pad_maximum_fusion.1.late_own_ref), channel_id=1, source_target_pairs={{1,0},{3,2},{5,4},{7,6},{9,8},{11,10},{13,12},{15,14},{17,16},{19,... | collective-permute-start | bytes 393224 | tf_op jit(solution)/shard_map/ppermute | solution.py:149
  13.8 13.4 %collective-permute-done.5.other_ref = bf16[128,640]{1,0:T(8,128)(2,1)S(1)} collective-permute-done((bf16[128,640]{1,0:T(8,128)(2,1)S(1)}, bf16[128,640]{1,0:T(8,128)(2,1)S(1)}, u32[]{:S(2)}, u32[]{:S(2)}) %collective-permute-start.5) | collective-permute-done | bytes 163872 | tf_op jit(solution)/shard_map/ppermute | solution.py:149
  27.1 0.7 %shard_map.75.pre_ref = f32[128,1344]{1,0:T(8,128)S(1)} custom-call(bf16[128,640]{1,0:T(8,128)(2,1)S(1)} %slice.38.own_ref, bf16[128,640]{1,0:T(8,128)(2,1)S(1)} %collective-permute-done.5.other_ref, bf16[2,672,1024]{2,1,0:T(8,128)(2,1)S(1)} %get-tuple-element.9.up_ref), custom_call_target="tpu_custom_call" | custom-call | flops 176160768 | bytes 1376256 | tf_op jit(solution)/shard_map/pallas_call | solution.py:31
  27.8 0.6 %collective-permute-done.6.late_other_ref = bf16[128,512]{1,0:T(8,128)(2,1)S(1)} collective-permute-done((bf16[128,512]{1,0:T(8,128)(2,1)S(1)}, bf16[128,512]{1,0:T(8,128)(2,1)S(1)}, u32[]{:S(2)}, u32[]{:S(2)}) %collective-permute-start.6) | collective-permute-done | bytes 131104 | tf_op jit(solution)/shard_map/ppermute | solution.py:149
  28.4 1.1 %shard_map.76 = bf16[128,1024]{1,0:T(8,128)(2,1)S(1)} custom-call(bf16[128,640]{1,0:T(8,128)(2,1)S(1)} %slice.38.own_ref, bf16[128,640]{1,0:T(8,128)(2,1)S(1)} %collective-permute-done.5.other_ref, bf16[128,512]{1,0:T(8,128)(2,1)S(1)} %pad_maximum_fusion.1.late_own_ref, bf16[128,512]{1,0:T(8,128)(2,1)S(1)} %collective-permute-done.6.late_other_ref, ...), custom_call_target="tpu_custom_call" | custom-call | flops 528482304 | bytes 4128768 | tf_op jit(solution)/shard_map/pallas_call | solution.py:31
  29.5 2.1 %collective-permute-start.7 = (bf16[128,1024]{1,0:T(8,128)(2,1)S(1)}, bf16[128,1024]{1,0:T(8,128)(2,1)S(1)}, u32[]{:S(2)}, u32[]{:S(2)}) collective-permute-start(bf16[128,1024]{1,0:T(8,128)(2,1)S(1)} %shard_map.76), channel_id=1, source_target_pairs={{0,1},{2,3},{4,5},{6,7},{8,9},{10,11},{12,13},{14,15},{16,17},{18,... | collective-permute-start | bytes 786440 | tf_op jit(solution)/shard_map/ppermute | solution.py:146
  31.6 1.1 %collective-permute-done.7 = bf16[128,1024]{1,0:T(8,128)(2,1)S(1)} collective-permute-done((bf16[128,1024]{1,0:T(8,128)(2,1)S(1)}, bf16[128,1024]{1,0:T(8,128)(2,1)S(1)}, u32[]{:S(2)}, u32[]{:S(2)}) %collective-permute-start.7) | collective-permute-done | bytes 262176 | tf_op jit(solution)/shard_map/ppermute | solution.py:146
  32.7 0.1 add_convert_fusion
  32.8 0.7 %collective-permute-start.8 = (bf16[32,1024]{1,0:T(8,128)(2,1)S(1)}, bf16[32,1024]{1,0:T(8,128)(2,1)S(1)}, u32[]{:S(2)}, u32[]{:S(2)}) collective-permute-start(bf16[32,1024]{1,0:T(8,128)(2,1)S(1)} %get-tuple-element.11), channel_id=1, source_target_pairs={{1,13},{3,15},{5,9},{7,11},{9,5},{11,7},{13,1},{15,3},{17,29},{19,... | collective-permute-start | bytes 196616 | tf_op jit(solution)/shard_map/ppermute | solution.py:154
  33.5 0.7 %collective-permute-start.10 = (bf16[32,1024]{1,0:T(8,128)(2,1)S(1)}, bf16[32,1024]{1,0:T(8,128)(2,1)S(1)}, u32[]{:S(2)}, u32[]{:S(2)}) collective-permute-start(bf16[32,1024]{1,0:T(8,128)(2,1)S(1)} %get-tuple-element.12), channel_id=1, source_target_pairs={{1,9},{3,11},{5,13},{7,15},{9,1},{11,3},{13,5},{15,7},{17,25},{19,... | collective-permute-start | bytes 196616 | tf_op jit(solution)/shard_map/ppermute | solution.py:154
  34.2 0.7 %collective-permute-start.9 = (bf16[32,1024]{1,0:T(8,128)(2,1)S(1)}, bf16[32,1024]{1,0:T(8,128)(2,1)S(1)}, u32[]{:S(2)}, u32[]{:S(2)}) collective-permute-start(bf16[32,1024]{1,0:T(8,128)(2,1)S(1)} %get-tuple-element.13), channel_id=1, source_target_pairs={{1,5},{3,7},{5,1},{7,3},{9,13},{11,15},{13,9},{15,11},{17,21},{19,... | collective-permute-start | bytes 196616 | tf_op jit(solution)/shard_map/ppermute | solution.py:154
  34.8 0.0 collective-permute-done.8
  34.8 0.0 collective-permute-done.10
  34.9 0.0 collective-permute-done.9
  34.9 0.7 %collective-permute-start.11 = (bf16[32,1024]{1,0:T(8,128)(2,1)S(1)}, bf16[32,1024]{1,0:T(8,128)(2,1)S(1)}, u32[]{:S(2)}, u32[]{:S(2)}) collective-permute-start(bf16[32,1024]{1,0:T(8,128)(2,1)S(1)} %add_convert_fusion.2), channel_id=1, source_target_pairs={{1,3},{3,1},{5,7},{7,5},{9,11},{11,9},{13,15},{15,13},{17,19},{19,... | collective-permute-start | bytes 196616 | tf_op jit(solution)/shard_map/ppermute | solution.py:161
  35.6 0.0 collective-permute-done.11
  35.6 1.3 %collective-permute-start.12 = (bf16[32,1024]{1,0:T(8,128)(2,1)S(1)}, bf16[32,1024]{1,0:T(8,128)(2,1)S(1)}, u32[]{:S(2)}, u32[]{:S(2)}) collective-permute-start(bf16[32,1024]{1,0:T(8,128)(2,1)S(1)} %add_convert_fusion.1.own_ref), channel_id=1, source_target_pairs={{1,0},{3,2},{5,4},{7,6},{9,8},{11,10},{13,12},{15,14},{17,16},{19,... | collective-permute-start | bytes 196616 | tf_op jit(solution)/shard_map/ppermute | solution.py:149
  36.9 14.7 %collective-permute-done.12.other_ref = bf16[32,1024]{1,0:T(8,128)(2,1)S(1)} collective-permute-done((bf16[32,1024]{1,0:T(8,128)(2,1)S(1)}, bf16[32,1024]{1,0:T(8,128)(2,1)S(1)}, u32[]{:S(2)}, u32[]{:S(2)}) %collective-permute-start.12) | collective-permute-done | bytes 65568 | tf_op jit(solution)/shard_map/ppermute | solution.py:149
  51.6 1.1 %shard_map.77 = bf16[32,1024]{1,0:T(8,128)(2,1)} custom-call(bf16[32,1024]{1,0:T(8,128)(2,1)S(1)} %add_convert_fusion.1.own_ref, bf16[32,1024]{1,0:T(8,128)(2,1)S(1)} %collective-permute-done.12.other_ref, bf16[1024,1024]{1,0:T(8,128)(2,1)S(1)} %copy-done), custom_call_target="tpu_custom_call" | custom-call | flops 67108864 | bytes 2097152 | tf_op jit(solution)/shard_map/pallas_call | solution.py:31
  (12 shorter events, 0.2 us)
Async XLA Ops:
  2.3 3.2 %collective-permute-start = (bf16[32,1024]{1,0:T(8,128)(2,1)S(1)}, bf16[32,1024]{1,0:T(8,128)(2,1)S(1)}, u32[]{:S(2)}, u32[]{:S(2)}) collective-permute-start(bf16[32,1024]{1,0:T(8,128)(2,1)S(1)} %shard_map.73), channel_id=1, source_target_pairs={{0,1},{2,3},{4,5},{6,7},{8,9},{10,11},{12,13},{14,15},{16,17},{18,... | collective-permute-start | bytes 196616 | tf_op jit(solution)/shard_map/ppermute | solution.py:146
  5.6 3.4 %collective-permute-start.1 = (bf16[32,1024]{1,0:T(8,128)(2,1)S(1)}, bf16[32,1024]{1,0:T(8,128)(2,1)S(1)}, u32[]{:S(2)}, u32[]{:S(2)}) collective-permute-start(bf16[32,1024]{1,0:T(8,128)(2,1)S(1)} %add_convert_fusion.4.after_ref), channel_id=1, source_target_pairs={{1,3},{3,1},{5,7},{7,5},{9,11},{11,9},{13,15},{15,13},{17,19},{19,... | collective-permute-start | bytes 196616 | tf_op jit(solution)/shard_map/ppermute | solution.py:161
  9.0 2.0 %collective-permute-start.4 = (bf16[32,1152]{1,0:T(8,128)(2,1)S(1)}, bf16[32,1152]{1,0:T(8,128)(2,1)S(1)}, u32[]{:S(2)}, u32[]{:S(2)}) collective-permute-start(bf16[32,1152]{1,0:T(8,128)(2,1)S(1)} %pad_maximum_fusion.2), channel_id=1, source_target_pairs={{1,13},{3,15},{5,9},{7,11},{9,5},{11,7},{13,1},{15,3},{17,29},{19,... | collective-permute-start | bytes 221192 | tf_op jit(solution)/shard_map/ppermute | solution.py:154
  9.7 1.4 %collective-permute-start.3 = (bf16[32,1152]{1,0:T(8,128)(2,1)S(1)}, bf16[32,1152]{1,0:T(8,128)(2,1)S(1)}, u32[]{:S(2)}, u32[]{:S(2)}) collective-permute-start(bf16[32,1152]{1,0:T(8,128)(2,1)S(1)} %pad_maximum_fusion.2), channel_id=1, source_target_pairs={{1,9},{3,11},{5,13},{7,15},{9,1},{11,3},{13,5},{15,7},{17,25},{19,... | collective-permute-start | bytes 221192 | tf_op jit(solution)/shard_map/ppermute | solution.py:154
  10.4 0.7 %collective-permute-start.2 = (bf16[32,1152]{1,0:T(8,128)(2,1)S(1)}, bf16[32,1152]{1,0:T(8,128)(2,1)S(1)}, u32[]{:S(2)}, u32[]{:S(2)}) collective-permute-start(bf16[32,1152]{1,0:T(8,128)(2,1)S(1)} %pad_maximum_fusion.2), channel_id=1, source_target_pairs={{1,5},{3,7},{5,1},{7,3},{9,13},{11,15},{13,9},{15,11},{17,21},{19,... | collective-permute-start | bytes 221192 | tf_op jit(solution)/shard_map/ppermute | solution.py:154
  11.1 16.0 %collective-permute-start.5 = (bf16[128,640]{1,0:T(8,128)(2,1)S(1)}, bf16[128,640]{1,0:T(8,128)(2,1)S(1)}, u32[]{:S(2)}, u32[]{:S(2)}) collective-permute-start(bf16[128,640]{1,0:T(8,128)(2,1)S(1)} %slice.38.own_ref), channel_id=1, source_target_pairs={{1,0},{3,2},{5,4},{7,6},{9,8},{11,10},{13,12},{15,14},{17,16},{19,... | collective-permute-start | bytes 491528 | tf_op jit(solution)/shard_map/ppermute | solution.py:149
  12.5 16.0 %collective-permute-start.6 = (bf16[128,512]{1,0:T(8,128)(2,1)S(1)}, bf16[128,512]{1,0:T(8,128)(2,1)S(1)}, u32[]{:S(2)}, u32[]{:S(2)}) collective-permute-start(bf16[128,512]{1,0:T(8,128)(2,1)S(1)} %pad_maximum_fusion.1.late_own_ref), channel_id=1, source_target_pairs={{1,0},{3,2},{5,4},{7,6},{9,8},{11,10},{13,12},{15,14},{17,16},{19,... | collective-permute-start | bytes 393224 | tf_op jit(solution)/shard_map/ppermute | solution.py:149
  28.4 23.2 %copy-start = (bf16[1024,1024]{1,0:T(8,128)(2,1)S(1)}, bf16[1024,1024]{1,0:T(8,128)(2,1)}, u32[]{:S(2)}) copy-start(bf16[1024,1024]{1,0:T(8,128)(2,1)} %weight_ref.1) | copy-start | bytes 6291460
  29.5 3.2 %collective-permute-start.7 = (bf16[128,1024]{1,0:T(8,128)(2,1)S(1)}, bf16[128,1024]{1,0:T(8,128)(2,1)S(1)}, u32[]{:S(2)}, u32[]{:S(2)}) collective-permute-start(bf16[128,1024]{1,0:T(8,128)(2,1)S(1)} %shard_map.76), channel_id=1, source_target_pairs={{0,1},{2,3},{4,5},{6,7},{8,9},{10,11},{12,13},{14,15},{16,17},{18,... | collective-permute-start | bytes 786440 | tf_op jit(solution)/shard_map/ppermute | solution.py:146
  32.8 2.0 %collective-permute-start.8 = (bf16[32,1024]{1,0:T(8,128)(2,1)S(1)}, bf16[32,1024]{1,0:T(8,128)(2,1)S(1)}, u32[]{:S(2)}, u32[]{:S(2)}) collective-permute-start(bf16[32,1024]{1,0:T(8,128)(2,1)S(1)} %get-tuple-element.11), channel_id=1, source_target_pairs={{1,13},{3,15},{5,9},{7,11},{9,5},{11,7},{13,1},{15,3},{17,29},{19,... | collective-permute-start | bytes 196616 | tf_op jit(solution)/shard_map/ppermute | solution.py:154
  33.5 1.4 %collective-permute-start.10 = (bf16[32,1024]{1,0:T(8,128)(2,1)S(1)}, bf16[32,1024]{1,0:T(8,128)(2,1)S(1)}, u32[]{:S(2)}, u32[]{:S(2)}) collective-permute-start(bf16[32,1024]{1,0:T(8,128)(2,1)S(1)} %get-tuple-element.12), channel_id=1, source_target_pairs={{1,9},{3,11},{5,13},{7,15},{9,1},{11,3},{13,5},{15,7},{17,25},{19,... | collective-permute-start | bytes 196616 | tf_op jit(solution)/shard_map/ppermute | solution.py:154
  34.2 0.7 %collective-permute-start.9 = (bf16[32,1024]{1,0:T(8,128)(2,1)S(1)}, bf16[32,1024]{1,0:T(8,128)(2,1)S(1)}, u32[]{:S(2)}, u32[]{:S(2)}) collective-permute-start(bf16[32,1024]{1,0:T(8,128)(2,1)S(1)} %get-tuple-element.13), channel_id=1, source_target_pairs={{1,5},{3,7},{5,1},{7,3},{9,13},{11,15},{13,9},{15,11},{17,21},{19,... | collective-permute-start | bytes 196616 | tf_op jit(solution)/shard_map/ppermute | solution.py:154
  34.9 0.7 %collective-permute-start.11 = (bf16[32,1024]{1,0:T(8,128)(2,1)S(1)}, bf16[32,1024]{1,0:T(8,128)(2,1)S(1)}, u32[]{:S(2)}, u32[]{:S(2)}) collective-permute-start(bf16[32,1024]{1,0:T(8,128)(2,1)S(1)} %add_convert_fusion.2), channel_id=1, source_target_pairs={{1,3},{3,1},{5,7},{7,5},{9,11},{11,9},{13,15},{15,13},{17,19},{19,... | collective-permute-start | bytes 196616 | tf_op jit(solution)/shard_map/ppermute | solution.py:161
  35.6 16.0 %collective-permute-start.12 = (bf16[32,1024]{1,0:T(8,128)(2,1)S(1)}, bf16[32,1024]{1,0:T(8,128)(2,1)S(1)}, u32[]{:S(2)}, u32[]{:S(2)}) collective-permute-start(bf16[32,1024]{1,0:T(8,128)(2,1)S(1)} %add_convert_fusion.1.own_ref), channel_id=1, source_target_pairs={{1,0},{3,2},{5,4},{7,6},{9,8},{11,10},{13,12},{15,14},{17,16},{19,... | collective-permute-start | bytes 196616 | tf_op jit(solution)/shard_map/ppermute | solution.py:149

commit v12 on v8

--- a/solution.py
+++ b/solution.py
@@ -45,7 +45,10 @@
 
 
 def half_at(own, half):
-    odd = lax.axis_index("tp") % 2
+    bits = lax.axis_index("exp") // (lax.axis_size("exp") // 2)
+    for b in range(lax.axis_size("tp").bit_length() - 1):
+        bits = bits + lax.axis_index("tp") // (1 << b)
+    odd = bits % 2
     return pl.multiple_of((odd if own else 1 - odd) * half, half)
 
 
@@ -167,14 +170,20 @@
     all_units = local_count * units
     out_len = lat_up.shape[1]
     terms_len = -(-2 * local_count * exp_count // LANES) * LANES
-    pair_masks = [1 << b for b in range(1, tp_count.bit_length() - 1)]
-
-    def traded(x, axis, mask):
-        return lax.ppermute(x, axis, [(i, i ^ mask) for i in range(lax.axis_size(axis))])
+    pair_masks = [(1 << b) + 1 for b in range(1, tp_count.bit_length() - 1)]
+
+    def over_tp(x, mask):
+        return lax.ppermute(x, "tp", [(t, t ^ mask) for t in range(tp_count)])
+
+    def over_exp(x, mask):
+        turn = mask // (exp_count // 2)
+        places = [(e, t) for e in range(exp_count) for t in range(tp_count)]
+        hops = [(e * tp_count + t, (e ^ mask) * tp_count + (t ^ turn)) for e, t in places]
+        return lax.ppermute(x, ("exp", "tp"), hops)
 
     def across(x):
         for mask in pair_masks:
-            x = x + traded(x.astype(BF16), "tp", mask).astype(F32)
+            x = x + over_tp(x.astype(BF16), mask).astype(F32)
         return x
 
     theirs, tokens_here, weight_here = kernel_call(
@@ -199,7 +208,7 @@
         2 * rows * width * half,
         2 * width * half,
     )
-    mine = mine + traded(theirs, "tp", 1).astype(F32)
+    mine = mine + over_tp(theirs, 1).astype(F32)
     down_rows = expert_down.reshape(all_units, latent_len)
     terms, up_here, down_here = kernel_call(
         load_kernel,
@@ -220,9 +229,9 @@
     )
     up_here, down_here = vmem(up_here), vmem(down_here)
     message = jnp.concatenate([across(mine).astype(BF16), terms], axis=1)
-    messages = [message] + [traded(message, "exp", s) for s in range(1, exp_count)]
+    messages = [message] + [over_exp(message, s) for s in range(1, exp_count)]
     messages = jnp.concatenate(messages, axis=0)
-    other = traded(messages[:, :half], "tp", 1)
+    other = over_tp(messages[:, :half], 1)
     pre = kernel_call(
         first_kernel,
         shaped(F32, all_rows, all_units),
@@ -250,11 +259,11 @@
         all_rows * latent_len * all_units,
         latent_len * all_units,
     )
-    part = (mine + traded(theirs, "tp", 1).astype(F32)).astype(BF16)
+    part = (mine + over_tp(theirs, 1).astype(F32)).astype(BF16)
     blocks = part.reshape(exp_count, rows, half)
     mixed = blocks[0].astype(F32)
     for s in (exp_count - 1, *range(1, exp_count - 1)):
-        mixed = mixed + traded(blocks[s], "exp", s).astype(F32)
+        mixed = mixed + over_exp(blocks[s], s).astype(F32)
     mixed = across(mixed).astype(BF16)
     lat_up = vmem(lat_up)
     own_part = kernel_call(
@@ -269,7 +278,7 @@
     return kernel_call(
         up_kernel,
         shaped(BF16, rows, out_len),
-        (own_part, traded(mixed, "tp", 1), lat_up),
+        (own_part, over_tp(mixed, 1), lat_up),
         (),
         [pltpu.VMEM((rows, out_len), BF16), pltpu.SemaphoreType.DMA((2,))],
         rows * latent_len * out_len,

time: 34.5 us -> 33.7 us (0.977)
  starting transfers between devices: 14 us -> 12.6 us
  waiting for transfers between devices: 12 us -> 12.5 us
    ppermute x12, starting transfers between devices: 14 us -> 12.6 us  [the longest x6 8.43 us: over_exp(): return lax.ppermute(x, ('exp', 'tp'), hops)]
    ppermute x12, waiting for transfers between devices: 12 us -> 12.5 us  [the longest x6 6.88 us: over_exp(): return lax.ppermute(x, ('exp', 'tp'), hops)]
where the time goes in v12:
time: 33.7 us; the launch traced here: 33.6 us
  starting transfers between devices  12.6 us (37%)
  waiting for transfers between devices  12.5 us (37%)
  Pallas kernels  8.12 us (24%)
    ppermute x6, starting transfers between devices, over_exp(): return lax.ppermute(x, ('exp', 'tp'), hops)  8.43 us
    pallas_call x8, Pallas kernels, kernel_call(): pl.pallas_call(body, out_shape=out_shape, in_specs=[spec(pltpu.HBM if i i...  8.12 us
    ppermute x6, waiting for transfers between devices, over_exp(): return lax.ppermute(x, ('exp', 'tp'), hops)  6.88 us
    ppermute x6, waiting for transfers between devices, over_tp(): return lax.ppermute(x, 'tp', [(t, t ^ mask) for t in range(tp_count)])  5.65 us
    ppermute x6, starting transfers between devices, over_tp(): return lax.ppermute(x, 'tp', [(t, t ^ mask) for t in range(tp_count)])  4.19 us
  transfers between devices with their start and end apart: 12, of which 10 were waited for; matrix products, arithmetic and copies ran while one was open for 0% of the time, Pallas kernels for 13%

profile of v12, /device:TPU:0, one launch (start us, length us, event | category | flops | bytes accessed | tf_op | source)
XLA Modules:
  0.0 33.6 jit_solution(11737060496630757747)
XLA Ops:
  0.0 1.9 %shard_map.73 = (bf16[32,512]{1,0:T(8,128)(2,1)S(1)}, bf16[32,1024]{1,0:T(8,128)(2,1)S(1)}, bf16[512,1024]{1,0:T(8,128)(2,1)S(1)}) custom-call(bf16[32,1024]{1,0:T(8,128)(2,1)} %tokens_hbm.1, bf16[1024,1024]{1,0:T(8,128)(2,1)} %weight_hbm.1), custom_call_target="tpu_custom_call" | custom-call | flops 33554432 | bytes 2097152 | tf_op jit(solution)/shard_map/pallas_call | solution.py:32
  1.9 0.5 %collective-permute-start = (bf16[32,512]{1,0:T(8,128)(2,1)S(1)}, bf16[32,512]{1,0:T(8,128)(2,1)S(1)}, u32[]{:S(2)}, u32[]{:S(2)}) collective-permute-start(bf16[32,512]{1,0:T(8,128)(2,1)S(1)} %get-tuple-element.15), channel_id=1, source_target_pairs={{0,1},{1,0},{2,3},{3,2},{4,5},{5,4},{6,7},{7,6},{8,9},{9,8},{10,11... | collective-permute-start | bytes 98312 | tf_op jit(solution)/shard_map/ppermute | solution.py:176
  2.4 0.4 %shard_map.74 = f32[32,512]{1,0:T(8,128)S(1)} custom-call(bf16[32,1024]{1,0:T(8,128)(2,1)S(1)} %get-tuple-element.13.tokens_ref, bf16[512,1024]{1,0:T(8,128)(2,1)S(1)} %get-tuple-element.14.weight_ref), custom_call_target="tpu_custom_call" | custom-call | flops 33554432 | bytes 1048576 | tf_op jit(solution)/shard_map/pallas_call | solution.py:32
  2.8 0.5 %collective-permute-done = bf16[32,512]{1,0:T(8,128)(2,1)S(1)} collective-permute-done((bf16[32,512]{1,0:T(8,128)(2,1)S(1)}, bf16[32,512]{1,0:T(8,128)(2,1)S(1)}, u32[]{:S(2)}, u32[]{:S(2)}) %collective-permute-start) | collective-permute-done | bytes 32800 | tf_op jit(solution)/shard_map/ppermute | solution.py:176
  3.3 2.7 %collective-permute-start.1 = (bf16[32,512]{1,0:T(8,128)(2,1)S(1)}, bf16[32,512]{1,0:T(8,128)(2,1)S(1)}, u32[]{:S(2)}, u32[]{:S(2)}) collective-permute-start(bf16[32,512]{1,0:T(8,128)(2,1)S(1)} %fusion.after_ref), channel_id=1, source_target_pairs={{0,3},{1,2},{2,1},{3,0},{4,7},{5,6},{6,5},{7,4},{8,11},{9,10},{10,... | collective-permute-start | bytes 98312 | tf_op jit(solution)/shard_map/ppermute | solution.py:176
  6.0 2.7 %shard_map.75 = (bf16[32,128]{1,0:T(8,128)(2,1)S(1)}, bf16[2,672,1024]{2,1,0:T(8,128)(2,1)S(1)}, bf16[1344,1024]{1,0:T(8,128)(2,1)S(1)}) custom-call(bf16[32,512]{1,0:T(8,128)(2,1)S(1)} %fusion.after_ref, s32[4,32]{1,0:T(4,128)} %bitcast.4, f32[4,32]{1,0:T(4,128)} %bitcast.5, bf16[2,672,1024]{2,1,0:T(8,128)(2,1)} %up_hbm.1, bf16[1344,1024]{1,0:T(8,128)(2,1)} %bitcast.3), custom_call_target="tpu_custom_call" | custom-call | bytes 5505024 | tf_op jit(solution)/shard_map/pallas_call | solution.py:32
  8.6 0.0 collective-permute-done.1
  8.7 3.6 %collective-permute-start.4 = (bf16[32,640]{1,0:T(8,128)(2,1)S(1)}, bf16[32,640]{1,0:T(8,128)(2,1)S(1)}, u32[]{:S(2)}, u32[]{:S(2)}) collective-permute-start(bf16[32,640]{1,0:T(8,128)(2,1)S(1)} %pad_maximum_fusion.1), channel_id=1, source_target_pairs={{0,13},{1,12},{2,15},{3,14},{4,9},{5,8},{6,11},{7,10},{8,5},{9,4},... | collective-permute-start | bytes 122888 | tf_op jit(solution)/shard_map/ppermute | solution.py:182
  12.3 0.0 collective-permute-start.3
  12.3 0.6 %collective-permute-start.2 = (bf16[32,640]{1,0:T(8,128)(2,1)S(1)}, bf16[32,640]{1,0:T(8,128)(2,1)S(1)}, u32[]{:S(2)}, u32[]{:S(2)}) collective-permute-start(bf16[32,640]{1,0:T(8,128)(2,1)S(1)} %pad_maximum_fusion.1), channel_id=1, source_target_pairs={{0,4},{1,5},{2,6},{3,7},{4,0},{5,1},{6,2},{7,3},{8,12},{9,13},{10,... | collective-permute-start | bytes 122888 | tf_op jit(solution)/shard_map/ppermute | solution.py:182
  13.0 1.3 %collective-permute-done.4 = bf16[32,640]{1,0:T(8,128)(2,1)S(1)} collective-permute-done((bf16[32,640]{1,0:T(8,128)(2,1)S(1)}, bf16[32,640]{1,0:T(8,128)(2,1)S(1)}, u32[]{:S(2)}, u32[]{:S(2)}) %collective-permute-start.4) | collective-permute-done | bytes 40992 | tf_op jit(solution)/shard_map/ppermute | solution.py:182
  14.2 2.6 %collective-permute-done.3 = bf16[32,640]{1,0:T(8,128)(2,1)S(1)} collective-permute-done((bf16[32,640]{1,0:T(8,128)(2,1)S(1)}, bf16[32,640]{1,0:T(8,128)(2,1)S(1)}, u32[]{:S(2)}, u32[]{:S(2)}) %collective-permute-start.3) | collective-permute-done | bytes 40992 | tf_op jit(solution)/shard_map/ppermute | solution.py:182
  16.8 0.4 %collective-permute-done.2 = bf16[32,640]{1,0:T(8,128)(2,1)S(1)} collective-permute-done((bf16[32,640]{1,0:T(8,128)(2,1)S(1)}, bf16[32,640]{1,0:T(8,128)(2,1)S(1)}, u32[]{:S(2)}, u32[]{:S(2)}) %collective-permute-start.2) | collective-permute-done | bytes 40992 | tf_op jit(solution)/shard_map/ppermute | solution.py:182
  17.2 0.1 collective-permute-start.5
  17.3 0.7 %shard_map.76.pre_ref = f32[128,1344]{1,0:T(8,128)S(1)} custom-call(bf16[128,640]{1,0:T(8,128)(2,1)S(1)} %pad_maximum_fusion.messages_ref, bf16[2,672,1024]{2,1,0:T(8,128)(2,1)S(1)} %get-tuple-element.17.up_ref), custom_call_target="tpu_custom_call" | custom-call | flops 176160768 | bytes 1376256 | tf_op jit(solution)/shard_map/pallas_call | solution.py:32
  18.0 0.7 %collective-permute-done.5.other_ref = bf16[128,512]{1,0:T(8,128)(2,1)S(1)} collective-permute-done((bf16[128,512]{1,0:T(8,128)(2,1)S(1)}, bf16[128,512]{1,0:T(8,128)(2,1)S(1)}, u32[]{:S(2)}, u32[]{:S(2)}) %collective-permute-start.5) | collective-permute-done | bytes 131104 | tf_op jit(solution)/shard_map/ppermute | solution.py:176
  18.6 0.9 %shard_map.77 = (bf16[128,1344]{1,0:T(8,128)(2,1)S(1)}, bf16[128,512]{1,0:T(8,128)(2,1)S(1)}) custom-call(bf16[128,640]{1,0:T(8,128)(2,1)S(1)} %pad_maximum_fusion.messages_ref, bf16[128,512]{1,0:T(8,128)(2,1)S(1)} %collective-permute-done.5.other_ref, f32[128,1344]{1,0:T(8,128)S(1)} %shard_map.76.pre_ref, ...), custom_call_target="tpu_custom_call" | custom-call | flops 352321536 | bytes 2752512 | tf_op jit(solution)/shard_map/pallas_call | solution.py:32
  19.5 0.0 copy-start
  19.6 0.2 collective-permute-start.6
  19.8 0.4 %shard_map.78 = f32[128,512]{1,0:T(8,128)S(1)} custom-call(bf16[128,1344]{1,0:T(8,128)(2,1)S(1)} %get-tuple-element.19.hidden_ref, bf16[1344,1024]{1,0:T(8,128)(2,1)S(1)} %get-tuple-element.18.down_ref), custom_call_target="tpu_custom_call" | custom-call | flops 176160768 | bytes 1376256 | tf_op jit(solution)/shard_map/pallas_call | solution.py:32
  20.1 0.8 %collective-permute-done.6 = bf16[128,512]{1,0:T(8,128)(2,1)S(1)} collective-permute-done((bf16[128,512]{1,0:T(8,128)(2,1)S(1)}, bf16[128,512]{1,0:T(8,128)(2,1)S(1)}, u32[]{:S(2)}, u32[]{:S(2)}) %collective-permute-start.6) | collective-permute-done | bytes 131104 | tf_op jit(solution)/shard_map/ppermute | solution.py:176
  21.0 1.7 %collective-permute-start.7 = (bf16[32,512]{1,0:T(8,128)(2,1)S(1)}, bf16[32,512]{1,0:T(8,128)(2,1)S(1)}, u32[]{:S(2)}, u32[]{:S(2)}) collective-permute-start(bf16[32,512]{1,0:T(8,128)(2,1)S(1)} %get-tuple-element.21), channel_id=1, source_target_pairs={{0,13},{1,12},{2,15},{3,14},{4,9},{5,8},{6,11},{7,10},{8,5},{9,4},... | collective-permute-start | bytes 98312 | tf_op jit(solution)/shard_map/ppermute | solution.py:182
  22.7 0.4 %collective-permute-start.9 = (bf16[32,512]{1,0:T(8,128)(2,1)S(1)}, bf16[32,512]{1,0:T(8,128)(2,1)S(1)}, u32[]{:S(2)}, u32[]{:S(2)}) collective-permute-start(bf16[32,512]{1,0:T(8,128)(2,1)S(1)} %get-tuple-element.22), channel_id=1, source_target_pairs={{0,9},{1,8},{2,11},{3,10},{4,13},{5,12},{6,15},{7,14},{8,1},{9,0},... | collective-permute-start | bytes 98312 | tf_op jit(solution)/shard_map/ppermute | solution.py:182
  23.1 2.1 %collective-permute-start.8 = (bf16[32,512]{1,0:T(8,128)(2,1)S(1)}, bf16[32,512]{1,0:T(8,128)(2,1)S(1)}, u32[]{:S(2)}, u32[]{:S(2)}) collective-permute-start(bf16[32,512]{1,0:T(8,128)(2,1)S(1)} %get-tuple-element.23), channel_id=1, source_target_pairs={{0,4},{1,5},{2,6},{3,7},{4,0},{5,1},{6,2},{7,3},{8,12},{9,13},{10,... | collective-permute-start | bytes 98312 | tf_op jit(solution)/shard_map/ppermute | solution.py:182
  25.2 1.1 %collective-permute-done.7 = bf16[32,512]{1,0:T(8,128)(2,1)S(1)} collective-permute-done((bf16[32,512]{1,0:T(8,128)(2,1)S(1)}, bf16[32,512]{1,0:T(8,128)(2,1)S(1)}, u32[]{:S(2)}, u32[]{:S(2)}) %collective-permute-start.7) | collective-permute-done | bytes 32800 | tf_op jit(solution)/shard_map/ppermute | solution.py:182
  26.2 1.6 %collective-permute-done.9 = bf16[32,512]{1,0:T(8,128)(2,1)S(1)} collective-permute-done((bf16[32,512]{1,0:T(8,128)(2,1)S(1)}, bf16[32,512]{1,0:T(8,128)(2,1)S(1)}, u32[]{:S(2)}, u32[]{:S(2)}) %collective-permute-start.9) | collective-permute-done | bytes 32800 | tf_op jit(solution)/shard_map/ppermute | solution.py:182
  27.9 0.6 %collective-permute-start.10 = (bf16[32,512]{1,0:T(8,128)(2,1)S(1)}, bf16[32,512]{1,0:T(8,128)(2,1)S(1)}, u32[]{:S(2)}, u32[]{:S(2)}) collective-permute-start(bf16[32,512]{1,0:T(8,128)(2,1)S(1)} %fusion.1), channel_id=1, source_target_pairs={{0,3},{1,2},{2,1},{3,0},{4,7},{5,6},{6,5},{7,4},{8,11},{9,10},{10,... | collective-permute-start | bytes 98312 | tf_op jit(solution)/shard_map/ppermute | solution.py:176
  28.4 2.9 %collective-permute-done.10 = bf16[32,512]{1,0:T(8,128)(2,1)S(1)} collective-permute-done((bf16[32,512]{1,0:T(8,128)(2,1)S(1)}, bf16[32,512]{1,0:T(8,128)(2,1)S(1)}, u32[]{:S(2)}, u32[]{:S(2)}) %collective-permute-start.10) | collective-permute-done | bytes 32800 | tf_op jit(solution)/shard_map/ppermute | solution.py:176
  31.4 0.2 collective-permute-start.11
  31.5 0.3 shard_map.79.part_ref
  31.8 0.8 %collective-permute-done.11.other_ref = bf16[32,512]{1,0:T(8,128)(2,1)S(1)} collective-permute-done((bf16[32,512]{1,0:T(8,128)(2,1)S(1)}, bf16[32,512]{1,0:T(8,128)(2,1)S(1)}, u32[]{:S(2)}, u32[]{:S(2)}) %collective-permute-start.11) | collective-permute-done | bytes 32800 | tf_op jit(solution)/shard_map/ppermute | solution.py:176
  32.6 0.9 %shard_map.80 = bf16[32,1024]{1,0:T(8,128)(2,1)} custom-call(f32[32,1024]{1,0:T(8,128)S(1)} %shard_map.79.part_ref, bf16[32,512]{1,0:T(8,128)(2,1)S(1)} %collective-permute-done.11.other_ref, bf16[1024,1024]{1,0:T(8,128)(2,1)S(1)} %copy-done), custom_call_target="tpu_custom_call" | custom-call | flops 33554432 | bytes 1048576 | tf_op jit(solution)/shard_map/pallas_call | solution.py:32
  (11 shorter events, 0.1 us)
Async XLA Ops:
  1.9 1.4 %collective-permute-start = (bf16[32,512]{1,0:T(8,128)(2,1)S(1)}, bf16[32,512]{1,0:T(8,128)(2,1)S(1)}, u32[]{:S(2)}, u32[]{:S(2)}) collective-permute-start(bf16[32,512]{1,0:T(8,128)(2,1)S(1)} %get-tuple-element.15), channel_id=1, source_target_pairs={{0,1},{1,0},{2,3},{3,2},{4,5},{5,4},{6,7},{7,6},{8,9},{9,8},{10,11... | collective-permute-start | bytes 98312 | tf_op jit(solution)/shard_map/ppermute | solution.py:176
  3.3 5.3 %collective-permute-start.1 = (bf16[32,512]{1,0:T(8,128)(2,1)S(1)}, bf16[32,512]{1,0:T(8,128)(2,1)S(1)}, u32[]{:S(2)}, u32[]{:S(2)}) collective-permute-start(bf16[32,512]{1,0:T(8,128)(2,1)S(1)} %fusion.after_ref), channel_id=1, source_target_pairs={{0,3},{1,2},{2,1},{3,0},{4,7},{5,6},{6,5},{7,4},{8,11},{9,10},{10,... | collective-permute-start | bytes 98312 | tf_op jit(solution)/shard_map/ppermute | solution.py:176
  8.7 5.6 %collective-permute-start.4 = (bf16[32,640]{1,0:T(8,128)(2,1)S(1)}, bf16[32,640]{1,0:T(8,128)(2,1)S(1)}, u32[]{:S(2)}, u32[]{:S(2)}) collective-permute-start(bf16[32,640]{1,0:T(8,128)(2,1)S(1)} %pad_maximum_fusion.1), channel_id=1, source_target_pairs={{0,13},{1,12},{2,15},{3,14},{4,9},{5,8},{6,11},{7,10},{8,5},{9,4},... | collective-permute-start | bytes 122888 | tf_op jit(solution)/shard_map/ppermute | solution.py:182
  12.3 4.5 %collective-permute-start.3 = (bf16[32,640]{1,0:T(8,128)(2,1)S(1)}, bf16[32,640]{1,0:T(8,128)(2,1)S(1)}, u32[]{:S(2)}, u32[]{:S(2)}) collective-permute-start(bf16[32,640]{1,0:T(8,128)(2,1)S(1)} %pad_maximum_fusion.1), channel_id=1, source_target_pairs={{0,9},{1,8},{2,11},{3,10},{4,13},{5,12},{6,15},{7,14},{8,1},{9,0},... | collective-permute-start | bytes 122888 | tf_op jit(solution)/shard_map/ppermute | solution.py:182
  12.3 4.9 %collective-permute-start.2 = (bf16[32,640]{1,0:T(8,128)(2,1)S(1)}, bf16[32,640]{1,0:T(8,128)(2,1)S(1)}, u32[]{:S(2)}, u32[]{:S(2)}) collective-permute-start(bf16[32,640]{1,0:T(8,128)(2,1)S(1)} %pad_maximum_fusion.1), channel_id=1, source_target_pairs={{0,4},{1,5},{2,6},{3,7},{4,0},{5,1},{6,2},{7,3},{8,12},{9,13},{10,... | collective-permute-start | bytes 122888 | tf_op jit(solution)/shard_map/ppermute | solution.py:182
  17.2 1.4 %collective-permute-start.5 = (bf16[128,512]{1,0:T(8,128)(2,1)S(1)}, bf16[128,512]{1,0:T(8,128)(2,1)S(1)}, u32[]{:S(2)}, u32[]{:S(2)}) collective-permute-start(bf16[128,512]{1,0:T(8,128)(2,1)S(1)} %slice.24), channel_id=1, source_target_pairs={{0,1},{1,0},{2,3},{3,2},{4,5},{5,4},{6,7},{7,6},{8,9},{9,8},{10,11... | collective-permute-start | bytes 393224 | tf_op jit(solution)/shard_map/ppermute | solution.py:176
  19.5 12.0 %copy-start = (bf16[1024,1024]{1,0:T(8,128)(2,1)S(1)}, bf16[1024,1024]{1,0:T(8,128)(2,1)}, u32[]{:S(2)}) copy-start(bf16[1024,1024]{1,0:T(8,128)(2,1)} %weight_ref.3) | copy-start | bytes 6291460
  19.6 1.4 %collective-permute-start.6 = (bf16[128,512]{1,0:T(8,128)(2,1)S(1)}, bf16[128,512]{1,0:T(8,128)(2,1)S(1)}, u32[]{:S(2)}, u32[]{:S(2)}) collective-permute-start(bf16[128,512]{1,0:T(8,128)(2,1)S(1)} %get-tuple-element.20), channel_id=1, source_target_pairs={{0,1},{1,0},{2,3},{3,2},{4,5},{5,4},{6,7},{7,6},{8,9},{9,8},{10,11... | collective-permute-start | bytes 393224 | tf_op jit(solution)/shard_map/ppermute | solution.py:176
  21.0 5.2 %collective-permute-start.7 = (bf16[32,512]{1,0:T(8,128)(2,1)S(1)}, bf16[32,512]{1,0:T(8,128)(2,1)S(1)}, u32[]{:S(2)}, u32[]{:S(2)}) collective-permute-start(bf16[32,512]{1,0:T(8,128)(2,1)S(1)} %get-tuple-element.21), channel_id=1, source_target_pairs={{0,13},{1,12},{2,15},{3,14},{4,9},{5,8},{6,11},{7,10},{8,5},{9,4},... | collective-permute-start | bytes 98312 | tf_op jit(solution)/shard_map/ppermute | solution.py:182
  22.7 5.1 %collective-permute-start.9 = (bf16[32,512]{1,0:T(8,128)(2,1)S(1)}, bf16[32,512]{1,0:T(8,128)(2,1)S(1)}, u32[]{:S(2)}, u32[]{:S(2)}) collective-permute-start(bf16[32,512]{1,0:T(8,128)(2,1)S(1)} %get-tuple-element.22), channel_id=1, source_target_pairs={{0,9},{1,8},{2,11},{3,10},{4,13},{5,12},{6,15},{7,14},{8,1},{9,0},... | collective-permute-start | bytes 98312 | tf_op jit(solution)/shard_map/ppermute | solution.py:182
  23.1 4.7 %collective-permute-start.8 = (bf16[32,512]{1,0:T(8,128)(2,1)S(1)}, bf16[32,512]{1,0:T(8,128)(2,1)S(1)}, u32[]{:S(2)}, u32[]{:S(2)}) collective-permute-start(bf16[32,512]{1,0:T(8,128)(2,1)S(1)} %get-tuple-element.23), channel_id=1, source_target_pairs={{0,4},{1,5},{2,6},{3,7},{4,0},{5,1},{6,2},{7,3},{8,12},{9,13},{10,... | collective-permute-start | bytes 98312 | tf_op jit(solution)/shard_map/ppermute | solution.py:182
  27.9 3.5 %collective-permute-start.10 = (bf16[32,512]{1,0:T(8,128)(2,1)S(1)}, bf16[32,512]{1,0:T(8,128)(2,1)S(1)}, u32[]{:S(2)}, u32[]{:S(2)}) collective-permute-start(bf16[32,512]{1,0:T(8,128)(2,1)S(1)} %fusion.1), channel_id=1, source_target_pairs={{0,3},{1,2},{2,1},{3,0},{4,7},{5,6},{6,5},{7,4},{8,11},{9,10},{10,... | collective-permute-start | bytes 98312 | tf_op jit(solution)/shard_map/ppermute | solution.py:176
  31.4 1.3 %collective-permute-start.11 = (bf16[32,512]{1,0:T(8,128)(2,1)S(1)}, bf16[32,512]{1,0:T(8,128)(2,1)S(1)}, u32[]{:S(2)}, u32[]{:S(2)}) collective-permute-start(bf16[32,512]{1,0:T(8,128)(2,1)S(1)} %add_convert_fusion.1.own_ref), channel_id=1, source_target_pairs={{0,1},{1,0},{2,3},{3,2},{4,5},{5,4},{6,7},{7,6},{8,9},{9,8},{10,11... | collective-permute-start | bytes 98312 | tf_op jit(solution)/shard_map/ppermute | solution.py:176

commit v13 on v12

--- a/solution.py
+++ b/solution.py
@@ -45,9 +45,10 @@
 
 
 def half_at(own, half):
-    bits = lax.axis_index("exp") // (lax.axis_size("exp") // 2)
-    for b in range(lax.axis_size("tp").bit_length() - 1):
-        bits = bits + lax.axis_index("tp") // (1 << b)
+    bits = 0
+    for axis in ("exp", "tp"):
+        for b in range(lax.axis_size(axis).bit_length() - 1):
+            bits = bits + lax.axis_index(axis) // (1 << b)
     odd = bits % 2
     return pl.multiple_of((odd if own else 1 - odd) * half, half)
 
@@ -176,7 +177,7 @@
         return lax.ppermute(x, "tp", [(t, t ^ mask) for t in range(tp_count)])
 
     def over_exp(x, mask):
-        turn = mask // (exp_count // 2)
+        turn = mask.bit_count() % 2
         places = [(e, t) for e in range(exp_count) for t in range(tp_count)]
         hops = [(e * tp_count + t, (e ^ mask) * tp_count + (t ^ turn)) for e, t in places]
         return lax.ppermute(x, ("exp", "tp"), hops)

time: 33.7 us -> 33.8 us (level)
  transfers between devices with their start and end apart: 12 -> 12, of which waited for: 10 -> 9; matrix products, arithmetic and copies ran while one was open for 0% -> 0% of each run, Pallas kernels for 13% -> 13%
where the time goes in v13:
time: 33.8 us; the launch traced here: 33.6 us
  starting transfers between devices  12.9 us (38%)
  waiting for transfers between devices  12.4 us (37%)
  Pallas kernels  8.1 us (24%)
    ppermute x6, starting transfers between devices, over_exp(): return lax.ppermute(x, ('exp', 'tp'), hops)  8.35 us
    pallas_call x8, Pallas kernels, kernel_call(): pl.pallas_call(body, out_shape=out_shape, in_specs=[spec(pltpu.HBM if i i...  8.1 us
    ppermute x6, waiting for transfers between devices, over_exp(): return lax.ppermute(x, ('exp', 'tp'), hops)  7.02 us
    ppermute x6, waiting for transfers between devices, over_tp(): return lax.ppermute(x, 'tp', [(t, t ^ mask) for t in range(tp_count)])  5.36 us
    ppermute x6, starting transfers between devices, over_tp(): return lax.ppermute(x, 'tp', [(t, t ^ mask) for t in range(tp_count)])  4.53 us
  transfers between devices with their start and end apart: 12, of which 9 were waited for; matrix products, arithmetic and copies ran while one was open for 0% of the time, Pallas kernels for 13%

profile of v13, /device:TPU:0, one launch (start us, length us, event | category | flops | bytes accessed | tf_op | source)
XLA Modules:
  0.0 33.6 jit_solution(1466180775130459242)
XLA Ops:
  0.0 1.9 %shard_map.73 = (bf16[32,512]{1,0:T(8,128)(2,1)S(1)}, bf16[32,1024]{1,0:T(8,128)(2,1)S(1)}, bf16[512,1024]{1,0:T(8,128)(2,1)S(1)}) custom-call(bf16[32,1024]{1,0:T(8,128)(2,1)} %tokens_hbm.1, bf16[1024,1024]{1,0:T(8,128)(2,1)} %weight_hbm.1), custom_call_target="tpu_custom_call" | custom-call | flops 33554432 | bytes 2097152 | tf_op jit(solution)/shard_map/pallas_call | solution.py:32
  1.9 0.5 %collective-permute-start = (bf16[32,512]{1,0:T(8,128)(2,1)S(1)}, bf16[32,512]{1,0:T(8,128)(2,1)S(1)}, u32[]{:S(2)}, u32[]{:S(2)}) collective-permute-start(bf16[32,512]{1,0:T(8,128)(2,1)S(1)} %get-tuple-element.15), channel_id=1, source_target_pairs={{0,1},{1,0},{2,3},{3,2},{4,5},{5,4},{6,7},{7,6},{8,9},{9,8},{10,11... | collective-permute-start | bytes 98312 | tf_op jit(solution)/shard_map/ppermute | solution.py:177
  2.4 0.4 %shard_map.74 = f32[32,512]{1,0:T(8,128)S(1)} custom-call(bf16[32,1024]{1,0:T(8,128)(2,1)S(1)} %get-tuple-element.13.tokens_ref, bf16[512,1024]{1,0:T(8,128)(2,1)S(1)} %get-tuple-element.14.weight_ref), custom_call_target="tpu_custom_call" | custom-call | flops 33554432 | bytes 1048576 | tf_op jit(solution)/shard_map/pallas_call | solution.py:32
  2.8 0.5 %collective-permute-done = bf16[32,512]{1,0:T(8,128)(2,1)S(1)} collective-permute-done((bf16[32,512]{1,0:T(8,128)(2,1)S(1)}, bf16[32,512]{1,0:T(8,128)(2,1)S(1)}, u32[]{:S(2)}, u32[]{:S(2)}) %collective-permute-start) | collective-permute-done | bytes 32800 | tf_op jit(solution)/shard_map/ppermute | solution.py:177
  3.3 2.7 %collective-permute-start.1 = (bf16[32,512]{1,0:T(8,128)(2,1)S(1)}, bf16[32,512]{1,0:T(8,128)(2,1)S(1)}, u32[]{:S(2)}, u32[]{:S(2)}) collective-permute-start(bf16[32,512]{1,0:T(8,128)(2,1)S(1)} %fusion.after_ref), channel_id=1, source_target_pairs={{0,3},{1,2},{2,1},{3,0},{4,7},{5,6},{6,5},{7,4},{8,11},{9,10},{10,... | collective-permute-start | bytes 98312 | tf_op jit(solution)/shard_map/ppermute | solution.py:177
  6.0 2.7 %shard_map.75 = (bf16[32,128]{1,0:T(8,128)(2,1)S(1)}, bf16[2,672,1024]{2,1,0:T(8,128)(2,1)S(1)}, bf16[1344,1024]{1,0:T(8,128)(2,1)S(1)}) custom-call(bf16[32,512]{1,0:T(8,128)(2,1)S(1)} %fusion.after_ref, s32[4,32]{1,0:T(4,128)} %bitcast.4, f32[4,32]{1,0:T(4,128)} %bitcast.5, bf16[2,672,1024]{2,1,0:T(8,128)(2,1)} %up_hbm.1, bf16[1344,1024]{1,0:T(8,128)(2,1)} %bitcast.3), custom_call_target="tpu_custom_call" | custom-call | bytes 5505024 | tf_op jit(solution)/shard_map/pallas_call | solution.py:32
  8.6 0.0 collective-permute-done.1
  8.7 3.7 %collective-permute-start.4 = (bf16[32,640]{1,0:T(8,128)(2,1)S(1)}, bf16[32,640]{1,0:T(8,128)(2,1)S(1)}, u32[]{:S(2)}, u32[]{:S(2)}) collective-permute-start(bf16[32,640]{1,0:T(8,128)(2,1)S(1)} %pad_maximum_fusion.1), channel_id=1, source_target_pairs={{0,12},{1,13},{2,14},{3,15},{4,8},{5,9},{6,10},{7,11},{8,4},{9,5},... | collective-permute-start | bytes 122888 | tf_op jit(solution)/shard_map/ppermute | solution.py:183
  12.4 0.0 collective-permute-start.3
  12.4 0.5 %collective-permute-start.2 = (bf16[32,640]{1,0:T(8,128)(2,1)S(1)}, bf16[32,640]{1,0:T(8,128)(2,1)S(1)}, u32[]{:S(2)}, u32[]{:S(2)}) collective-permute-start(bf16[32,640]{1,0:T(8,128)(2,1)S(1)} %pad_maximum_fusion.1), channel_id=1, source_target_pairs={{0,5},{1,4},{2,7},{3,6},{4,1},{5,0},{6,3},{7,2},{8,13},{9,12},{10,... | collective-permute-start | bytes 122888 | tf_op jit(solution)/shard_map/ppermute | solution.py:183
  12.9 1.7 %collective-permute-done.4 = bf16[32,640]{1,0:T(8,128)(2,1)S(1)} collective-permute-done((bf16[32,640]{1,0:T(8,128)(2,1)S(1)}, bf16[32,640]{1,0:T(8,128)(2,1)S(1)}, u32[]{:S(2)}, u32[]{:S(2)}) %collective-permute-start.4) | collective-permute-done | bytes 40992 | tf_op jit(solution)/shard_map/ppermute | solution.py:183
  14.6 2.3 %collective-permute-done.3 = bf16[32,640]{1,0:T(8,128)(2,1)S(1)} collective-permute-done((bf16[32,640]{1,0:T(8,128)(2,1)S(1)}, bf16[32,640]{1,0:T(8,128)(2,1)S(1)}, u32[]{:S(2)}, u32[]{:S(2)}) %collective-permute-start.3) | collective-permute-done | bytes 40992 | tf_op jit(solution)/shard_map/ppermute | solution.py:183
  16.9 0.0 collective-permute-done.2
  16.9 0.2 collective-permute-start.5
  17.1 0.6 %shard_map.76.pre_ref = f32[128,1344]{1,0:T(8,128)S(1)} custom-call(bf16[128,640]{1,0:T(8,128)(2,1)S(1)} %pad_maximum_fusion.messages_ref, bf16[2,672,1024]{2,1,0:T(8,128)(2,1)S(1)} %get-tuple-element.17.up_ref), custom_call_target="tpu_custom_call" | custom-call | flops 176160768 | bytes 1376256 | tf_op jit(solution)/shard_map/pallas_call | solution.py:32
  17.8 0.6 %collective-permute-done.5.other_ref = bf16[128,512]{1,0:T(8,128)(2,1)S(1)} collective-permute-done((bf16[128,512]{1,0:T(8,128)(2,1)S(1)}, bf16[128,512]{1,0:T(8,128)(2,1)S(1)}, u32[]{:S(2)}, u32[]{:S(2)}) %collective-permute-start.5) | collective-permute-done | bytes 131104 | tf_op jit(solution)/shard_map/ppermute | solution.py:177
  18.3 0.9 %shard_map.77 = (bf16[128,1344]{1,0:T(8,128)(2,1)S(1)}, bf16[128,512]{1,0:T(8,128)(2,1)S(1)}) custom-call(bf16[128,640]{1,0:T(8,128)(2,1)S(1)} %pad_maximum_fusion.messages_ref, bf16[128,512]{1,0:T(8,128)(2,1)S(1)} %collective-permute-done.5.other_ref, f32[128,1344]{1,0:T(8,128)S(1)} %shard_map.76.pre_ref, ...), custom_call_target="tpu_custom_call" | custom-call | flops 352321536 | bytes 2752512 | tf_op jit(solution)/shard_map/pallas_call | solution.py:32
  19.2 0.0 copy-start
  19.2 0.2 collective-permute-start.6
  19.4 0.4 %shard_map.78 = f32[128,512]{1,0:T(8,128)S(1)} custom-call(bf16[128,1344]{1,0:T(8,128)(2,1)S(1)} %get-tuple-element.19.hidden_ref, bf16[1344,1024]{1,0:T(8,128)(2,1)S(1)} %get-tuple-element.18.down_ref), custom_call_target="tpu_custom_call" | custom-call | flops 176160768 | bytes 1376256 | tf_op jit(solution)/shard_map/pallas_call | solution.py:32
  19.8 0.8 %collective-permute-done.6 = bf16[128,512]{1,0:T(8,128)(2,1)S(1)} collective-permute-done((bf16[128,512]{1,0:T(8,128)(2,1)S(1)}, bf16[128,512]{1,0:T(8,128)(2,1)S(1)}, u32[]{:S(2)}, u32[]{:S(2)}) %collective-permute-start.6) | collective-permute-done | bytes 131104 | tf_op jit(solution)/shard_map/ppermute | solution.py:177
  20.7 2.1 %collective-permute-start.7 = (bf16[32,512]{1,0:T(8,128)(2,1)S(1)}, bf16[32,512]{1,0:T(8,128)(2,1)S(1)}, u32[]{:S(2)}, u32[]{:S(2)}) collective-permute-start(bf16[32,512]{1,0:T(8,128)(2,1)S(1)} %get-tuple-element.21), channel_id=1, source_target_pairs={{0,12},{1,13},{2,14},{3,15},{4,8},{5,9},{6,10},{7,11},{8,4},{9,5},... | collective-permute-start | bytes 98312 | tf_op jit(solution)/shard_map/ppermute | solution.py:183
  22.8 0.0 collective-permute-start.9
  22.9 2.0 %collective-permute-start.8 = (bf16[32,512]{1,0:T(8,128)(2,1)S(1)}, bf16[32,512]{1,0:T(8,128)(2,1)S(1)}, u32[]{:S(2)}, u32[]{:S(2)}) collective-permute-start(bf16[32,512]{1,0:T(8,128)(2,1)S(1)} %get-tuple-element.23), channel_id=1, source_target_pairs={{0,5},{1,4},{2,7},{3,6},{4,1},{5,0},{6,3},{7,2},{8,13},{9,12},{10,... | collective-permute-start | bytes 98312 | tf_op jit(solution)/shard_map/ppermute | solution.py:183
  24.9 1.8 %collective-permute-done.7 = bf16[32,512]{1,0:T(8,128)(2,1)S(1)} collective-permute-done((bf16[32,512]{1,0:T(8,128)(2,1)S(1)}, bf16[32,512]{1,0:T(8,128)(2,1)S(1)}, u32[]{:S(2)}, u32[]{:S(2)}) %collective-permute-start.7) | collective-permute-done | bytes 32800 | tf_op jit(solution)/shard_map/ppermute | solution.py:183
  26.7 1.2 %collective-permute-done.9 = bf16[32,512]{1,0:T(8,128)(2,1)S(1)} collective-permute-done((bf16[32,512]{1,0:T(8,128)(2,1)S(1)}, bf16[32,512]{1,0:T(8,128)(2,1)S(1)}, u32[]{:S(2)}, u32[]{:S(2)}) %collective-permute-start.9) | collective-permute-done | bytes 32800 | tf_op jit(solution)/shard_map/ppermute | solution.py:183
  27.9 0.8 %collective-permute-start.10 = (bf16[32,512]{1,0:T(8,128)(2,1)S(1)}, bf16[32,512]{1,0:T(8,128)(2,1)S(1)}, u32[]{:S(2)}, u32[]{:S(2)}) collective-permute-start(bf16[32,512]{1,0:T(8,128)(2,1)S(1)} %fusion.1), channel_id=1, source_target_pairs={{0,3},{1,2},{2,1},{3,0},{4,7},{5,6},{6,5},{7,4},{8,11},{9,10},{10,... | collective-permute-start | bytes 98312 | tf_op jit(solution)/shard_map/ppermute | solution.py:177
  28.7 2.7 %collective-permute-done.10 = bf16[32,512]{1,0:T(8,128)(2,1)S(1)} collective-permute-done((bf16[32,512]{1,0:T(8,128)(2,1)S(1)}, bf16[32,512]{1,0:T(8,128)(2,1)S(1)}, u32[]{:S(2)}, u32[]{:S(2)}) %collective-permute-start.10) | collective-permute-done | bytes 32800 | tf_op jit(solution)/shard_map/ppermute | solution.py:177
  31.4 0.2 collective-permute-start.11
  31.6 0.3 shard_map.79.part_ref
  31.9 0.8 %collective-permute-done.11.other_ref = bf16[32,512]{1,0:T(8,128)(2,1)S(1)} collective-permute-done((bf16[32,512]{1,0:T(8,128)(2,1)S(1)}, bf16[32,512]{1,0:T(8,128)(2,1)S(1)}, u32[]{:S(2)}, u32[]{:S(2)}) %collective-permute-start.11) | collective-permute-done | bytes 32800 | tf_op jit(solution)/shard_map/ppermute | solution.py:177
  32.7 0.9 %shard_map.80 = bf16[32,1024]{1,0:T(8,128)(2,1)} custom-call(f32[32,1024]{1,0:T(8,128)S(1)} %shard_map.79.part_ref, bf16[32,512]{1,0:T(8,128)(2,1)S(1)} %collective-permute-done.11.other_ref, bf16[1024,1024]{1,0:T(8,128)(2,1)S(1)} %copy-done), custom_call_target="tpu_custom_call" | custom-call | flops 33554432 | bytes 1048576 | tf_op jit(solution)/shard_map/pallas_call | solution.py:32
  (11 shorter events, 0.1 us)
Async XLA Ops:
  1.9 1.4 %collective-permute-start = (bf16[32,512]{1,0:T(8,128)(2,1)S(1)}, bf16[32,512]{1,0:T(8,128)(2,1)S(1)}, u32[]{:S(2)}, u32[]{:S(2)}) collective-permute-start(bf16[32,512]{1,0:T(8,128)(2,1)S(1)} %get-tuple-element.15), channel_id=1, source_target_pairs={{0,1},{1,0},{2,3},{3,2},{4,5},{5,4},{6,7},{7,6},{8,9},{9,8},{10,11... | collective-permute-start | bytes 98312 | tf_op jit(solution)/shard_map/ppermute | solution.py:177
  3.3 5.3 %collective-permute-start.1 = (bf16[32,512]{1,0:T(8,128)(2,1)S(1)}, bf16[32,512]{1,0:T(8,128)(2,1)S(1)}, u32[]{:S(2)}, u32[]{:S(2)}) collective-permute-start(bf16[32,512]{1,0:T(8,128)(2,1)S(1)} %fusion.after_ref), channel_id=1, source_target_pairs={{0,3},{1,2},{2,1},{3,0},{4,7},{5,6},{6,5},{7,4},{8,11},{9,10},{10,... | collective-permute-start | bytes 98312 | tf_op jit(solution)/shard_map/ppermute | solution.py:177
  8.7 5.9 %collective-permute-start.4 = (bf16[32,640]{1,0:T(8,128)(2,1)S(1)}, bf16[32,640]{1,0:T(8,128)(2,1)S(1)}, u32[]{:S(2)}, u32[]{:S(2)}) collective-permute-start(bf16[32,640]{1,0:T(8,128)(2,1)S(1)} %pad_maximum_fusion.1), channel_id=1, source_target_pairs={{0,12},{1,13},{2,14},{3,15},{4,8},{5,9},{6,10},{7,11},{8,4},{9,5},... | collective-permute-start | bytes 122888 | tf_op jit(solution)/shard_map/ppermute | solution.py:183
  12.4 4.5 %collective-permute-start.3 = (bf16[32,640]{1,0:T(8,128)(2,1)S(1)}, bf16[32,640]{1,0:T(8,128)(2,1)S(1)}, u32[]{:S(2)}, u32[]{:S(2)}) collective-permute-start(bf16[32,640]{1,0:T(8,128)(2,1)S(1)} %pad_maximum_fusion.1), channel_id=1, source_target_pairs={{0,9},{1,8},{2,11},{3,10},{4,13},{5,12},{6,15},{7,14},{8,1},{9,0},... | collective-permute-start | bytes 122888 | tf_op jit(solution)/shard_map/ppermute | solution.py:183
  12.4 4.5 %collective-permute-start.2 = (bf16[32,640]{1,0:T(8,128)(2,1)S(1)}, bf16[32,640]{1,0:T(8,128)(2,1)S(1)}, u32[]{:S(2)}, u32[]{:S(2)}) collective-permute-start(bf16[32,640]{1,0:T(8,128)(2,1)S(1)} %pad_maximum_fusion.1), channel_id=1, source_target_pairs={{0,5},{1,4},{2,7},{3,6},{4,1},{5,0},{6,3},{7,2},{8,13},{9,12},{10,... | collective-permute-start | bytes 122888 | tf_op jit(solution)/shard_map/ppermute | solution.py:183
  16.9 1.4 %collective-permute-start.5 = (bf16[128,512]{1,0:T(8,128)(2,1)S(1)}, bf16[128,512]{1,0:T(8,128)(2,1)S(1)}, u32[]{:S(2)}, u32[]{:S(2)}) collective-permute-start(bf16[128,512]{1,0:T(8,128)(2,1)S(1)} %slice.24), channel_id=1, source_target_pairs={{0,1},{1,0},{2,3},{3,2},{4,5},{5,4},{6,7},{7,6},{8,9},{9,8},{10,11... | collective-permute-start | bytes 393224 | tf_op jit(solution)/shard_map/ppermute | solution.py:177
  19.2 12.4 %copy-start = (bf16[1024,1024]{1,0:T(8,128)(2,1)S(1)}, bf16[1024,1024]{1,0:T(8,128)(2,1)}, u32[]{:S(2)}) copy-start(bf16[1024,1024]{1,0:T(8,128)(2,1)} %weight_ref.3) | copy-start | bytes 6291460
  19.2 1.4 %collective-permute-start.6 = (bf16[128,512]{1,0:T(8,128)(2,1)S(1)}, bf16[128,512]{1,0:T(8,128)(2,1)S(1)}, u32[]{:S(2)}, u32[]{:S(2)}) collective-permute-start(bf16[128,512]{1,0:T(8,128)(2,1)S(1)} %get-tuple-element.20), channel_id=1, source_target_pairs={{0,1},{1,0},{2,3},{3,2},{4,5},{5,4},{6,7},{7,6},{8,9},{9,8},{10,11... | collective-permute-start | bytes 393224 | tf_op jit(solution)/shard_map/ppermute | solution.py:177
  20.7 6.0 %collective-permute-start.7 = (bf16[32,512]{1,0:T(8,128)(2,1)S(1)}, bf16[32,512]{1,0:T(8,128)(2,1)S(1)}, u32[]{:S(2)}, u32[]{:S(2)}) collective-permute-start(bf16[32,512]{1,0:T(8,128)(2,1)S(1)} %get-tuple-element.21), channel_id=1, source_target_pairs={{0,12},{1,13},{2,14},{3,15},{4,8},{5,9},{6,10},{7,11},{8,4},{9,5},... | collective-permute-start | bytes 98312 | tf_op jit(solution)/shard_map/ppermute | solution.py:183
  22.8 5.0 %collective-permute-start.9 = (bf16[32,512]{1,0:T(8,128)(2,1)S(1)}, bf16[32,512]{1,0:T(8,128)(2,1)S(1)}, u32[]{:S(2)}, u32[]{:S(2)}) collective-permute-start(bf16[32,512]{1,0:T(8,128)(2,1)S(1)} %get-tuple-element.22), channel_id=1, source_target_pairs={{0,9},{1,8},{2,11},{3,10},{4,13},{5,12},{6,15},{7,14},{8,1},{9,0},... | collective-permute-start | bytes 98312 | tf_op jit(solution)/shard_map/ppermute | solution.py:183
  22.9 5.0 %collective-permute-start.8 = (bf16[32,512]{1,0:T(8,128)(2,1)S(1)}, bf16[32,512]{1,0:T(8,128)(2,1)S(1)}, u32[]{:S(2)}, u32[]{:S(2)}) collective-permute-start(bf16[32,512]{1,0:T(8,128)(2,1)S(1)} %get-tuple-element.23), channel_id=1, source_target_pairs={{0,5},{1,4},{2,7},{3,6},{4,1},{5,0},{6,3},{7,2},{8,13},{9,12},{10,... | collective-permute-start | bytes 98312 | tf_op jit(solution)/shard_map/ppermute | solution.py:183
  27.9 3.5 %collective-permute-start.10 = (bf16[32,512]{1,0:T(8,128)(2,1)S(1)}, bf16[32,512]{1,0:T(8,128)(2,1)S(1)}, u32[]{:S(2)}, u32[]{:S(2)}) collective-permute-start(bf16[32,512]{1,0:T(8,128)(2,1)S(1)} %fusion.1), channel_id=1, source_target_pairs={{0,3},{1,2},{2,1},{3,0},{4,7},{5,6},{6,5},{7,4},{8,11},{9,10},{10,... | collective-permute-start | bytes 98312 | tf_op jit(solution)/shard_map/ppermute | solution.py:177
  31.4 1.3 %collective-permute-start.11 = (bf16[32,512]{1,0:T(8,128)(2,1)S(1)}, bf16[32,512]{1,0:T(8,128)(2,1)S(1)}, u32[]{:S(2)}, u32[]{:S(2)}) collective-permute-start(bf16[32,512]{1,0:T(8,128)(2,1)S(1)} %add_convert_fusion.1.own_ref), channel_id=1, source_target_pairs={{0,1},{1,0},{2,3},{3,2},{4,5},{5,4},{6,7},{7,6},{8,9},{9,8},{10,11... | collective-permute-start | bytes 98312 | tf_op jit(solution)/shard_map/ppermute | solution.py:177

commit v14 on v13

--- a/solution.py
+++ b/solution.py
@@ -86,11 +86,16 @@
     mine_ref[...] = dot(tokens_ref[...], weight_ref[...], NT)
 
 
-def load_kernel(
-    after_ref, routes_hbm, scale_hbm, up_hbm, down_hbm, terms_ref, up_ref, down_ref,
-    routes, scale, sems,
+def load_kernel(after_ref, hbm_ref, here_ref, sem):
+    copy = pltpu.make_async_copy(hbm_ref, here_ref, sem)
+    copy.start()
+    copy.wait()
+
+
+def terms_kernel(
+    after_ref, routes_hbm, scale_hbm, up_hbm, terms_ref, up_ref, routes, scale, sems
 ):
-    pairs = [(routes_hbm, routes), (scale_hbm, scale), (up_hbm, up_ref), (down_hbm, down_ref)]
+    pairs = [(routes_hbm, routes), (scale_hbm, scale), (up_hbm, up_ref)]
     copies = [pltpu.make_async_copy(a, b, sems.at[i]) for i, (a, b) in enumerate(pairs)]
     for copy in copies:
         copy.start()
@@ -108,7 +113,6 @@
     combine = jnp.concatenate([combine, jnp.zeros((width, LANES - rows), F32)], axis=1)
     terms_ref[...] = combine.T[:rows, :].astype(BF16)
     copies[2].wait()
-    copies[3].wait()
 
 
 def first_kernel(messages_ref, up_ref, pre_ref):
@@ -210,28 +214,34 @@
         2 * width * half,
     )
     mine = mine + over_tp(theirs, 1).astype(F32)
-    down_rows = expert_down.reshape(all_units, latent_len)
-    terms, up_here, down_here = kernel_call(
-        load_kernel,
-        (
-            shaped(BF16, rows, terms_len),
-            pltpu.VMEM(expert_up.shape, BF16),
-            pltpu.VMEM(down_rows.shape, BF16),
-        ),
-        (mine.astype(BF16), *(hbm(x) for x in (routes.T, route_weights.T, expert_up, down_rows))),
-        (1, 2, 3, 4),
+    terms, up_here = kernel_call(
+        terms_kernel,
+        (shaped(BF16, rows, terms_len), pltpu.VMEM(expert_up.shape, BF16)),
+        (mine.astype(BF16), *(hbm(x) for x in (routes.T, route_weights.T, expert_up))),
+        (1, 2, 3),
         [
             pltpu.VMEM(routes.shape[::-1], jnp.int32),
             pltpu.VMEM(routes.shape[::-1], F32),
-            pltpu.SemaphoreType.DMA((4,)),
+            pltpu.SemaphoreType.DMA((3,)),
         ],
         0,
-        4 * latent_len * all_units,
-    )
-    up_here, down_here = vmem(up_here), vmem(down_here)
+        2 * latent_len * all_units,
+    )
+    up_here = vmem(up_here)
     message = jnp.concatenate([across(mine).astype(BF16), terms], axis=1)
+    down_rows = expert_down.reshape(all_units, latent_len)
+    down_here = kernel_call(
+        load_kernel,
+        pltpu.VMEM(down_rows.shape, BF16),
+        (message, hbm(down_rows)),
+        (1,),
+        [pltpu.SemaphoreType.DMA],
+        0,
+        2 * latent_len * all_units,
+    )
     messages = [message] + [over_exp(message, s) for s in range(1, exp_count)]
-    messages = jnp.concatenate(messages, axis=0)
+    messages[-1], down_here = lax.optimization_barrier((messages[-1], down_here))
+    messages, down_here = jnp.concatenate(messages, axis=0), vmem(down_here)
     other = over_tp(messages[:, :half], 1)
     pre = kernel_call(
         first_kernel,

time: 33.8 us -> 33.4 us (0.988)
  waiting for transfers between devices: 12.4 us -> 10.5 us
  Pallas kernels: 8.1 us -> 9.05 us
  starting transfers between devices: 12.9 us -> 13.4 us
    ppermute x6, waiting for transfers between devices: 7.02 us -> 5.54 us  [over_exp(): return lax.ppermute(x, ('exp', 'tp'), hops)]
    pallas_call x8 -> x9, Pallas kernels: 8.1 us -> 9.05 us  [kernel_call(): pl.pallas_call(body, out_shape=out_shape, in_specs=[spec(pltpu.HBM if i i...]
    ppermute x6, starting transfers between devices: 4.53 us -> 4.95 us  [over_tp(): return lax.ppermute(x, 'tp', [(t, t ^ mask) for t in range(tp_count)])]
    ppermute x6, waiting for transfers between devices: 5.36 us -> 4.98 us  [over_tp(): return lax.ppermute(x, 'tp', [(t, t ^ mask) for t in range(tp_count)])]
  transfers between devices with their start and end apart: 12 -> 12, of which waited for: 9 -> 8; matrix products, arithmetic and copies ran while one was open for 0% -> 0% of each run, Pallas kernels for 13% -> 16%
where the time goes in v14:
time: 33.4 us; the launch traced here: 33.2 us
  starting transfers between devices  13.4 us (40%)
  waiting for transfers between devices  10.5 us (31%)
  Pallas kernels  9.05 us (27%)
    pallas_call x9, Pallas kernels, kernel_call(): pl.pallas_call(body, out_shape=out_shape, in_specs=[spec(pltpu.HBM if i i...  9.05 us
    ppermute x6, starting transfers between devices, over_exp(): return lax.ppermute(x, ('exp', 'tp'), hops)  8.43 us
    ppermute x6, waiting for transfers between devices, over_exp(): return lax.ppermute(x, ('exp', 'tp'), hops)  5.54 us
    ppermute x6, waiting for transfers between devices, over_tp(): return lax.ppermute(x, 'tp', [(t, t ^ mask) for t in range(tp_count)])  4.98 us
    ppermute x6, starting transfers between devices, over_tp(): return lax.ppermute(x, 'tp', [(t, t ^ mask) for t in range(tp_count)])  4.95 us
  transfers between devices with their start and end apart: 12, of which 8 were waited for; matrix products, arithmetic and copies ran while one was open for 0% of the time, Pallas kernels for 16%

profile of v14, /device:TPU:0, one launch (start us, length us, event | category | flops | bytes accessed | tf_op | source)
XLA Modules:
  0.0 33.2 jit_solution(5634305269208935183)
XLA Ops:
  0.0 1.9 %shard_map.73 = (bf16[32,512]{1,0:T(8,128)(2,1)S(1)}, bf16[32,1024]{1,0:T(8,128)(2,1)S(1)}, bf16[512,1024]{1,0:T(8,128)(2,1)S(1)}) custom-call(bf16[32,1024]{1,0:T(8,128)(2,1)} %tokens_hbm.1, bf16[1024,1024]{1,0:T(8,128)(2,1)} %weight_hbm.1), custom_call_target="tpu_custom_call" | custom-call | flops 33554432 | bytes 2097152 | tf_op jit(solution)/shard_map/pallas_call | solution.py:32
  1.9 0.5 %collective-permute-start = (bf16[32,512]{1,0:T(8,128)(2,1)S(1)}, bf16[32,512]{1,0:T(8,128)(2,1)S(1)}, u32[]{:S(2)}, u32[]{:S(2)}) collective-permute-start(bf16[32,512]{1,0:T(8,128)(2,1)S(1)} %get-tuple-element.16), channel_id=1, source_target_pairs={{0,1},{1,0},{2,3},{3,2},{4,5},{5,4},{6,7},{7,6},{8,9},{9,8},{10,11... | collective-permute-start | bytes 98312 | tf_op jit(solution)/shard_map/ppermute | solution.py:181
  2.4 0.4 %shard_map.74 = f32[32,512]{1,0:T(8,128)S(1)} custom-call(bf16[32,1024]{1,0:T(8,128)(2,1)S(1)} %get-tuple-element.14.tokens_ref, bf16[512,1024]{1,0:T(8,128)(2,1)S(1)} %get-tuple-element.15.weight_ref), custom_call_target="tpu_custom_call" | custom-call | flops 33554432 | bytes 1048576 | tf_op jit(solution)/shard_map/pallas_call | solution.py:32
  2.8 0.5 %collective-permute-done = bf16[32,512]{1,0:T(8,128)(2,1)S(1)} collective-permute-done((bf16[32,512]{1,0:T(8,128)(2,1)S(1)}, bf16[32,512]{1,0:T(8,128)(2,1)S(1)}, u32[]{:S(2)}, u32[]{:S(2)}) %collective-permute-start) | collective-permute-done | bytes 32800 | tf_op jit(solution)/shard_map/ppermute | solution.py:181
  3.3 2.7 %collective-permute-start.1 = (bf16[32,512]{1,0:T(8,128)(2,1)S(1)}, bf16[32,512]{1,0:T(8,128)(2,1)S(1)}, u32[]{:S(2)}, u32[]{:S(2)}) collective-permute-start(bf16[32,512]{1,0:T(8,128)(2,1)S(1)} %fusion.after_ref), channel_id=1, source_target_pairs={{0,3},{1,2},{2,1},{3,0},{4,7},{5,6},{6,5},{7,4},{8,11},{9,10},{10,... | collective-permute-start | bytes 98312 | tf_op jit(solution)/shard_map/ppermute | solution.py:181
  6.0 1.8 %shard_map.75 = (bf16[32,128]{1,0:T(8,128)(2,1)S(1)}, bf16[2,672,1024]{2,1,0:T(8,128)(2,1)S(1)}) custom-call(bf16[32,512]{1,0:T(8,128)(2,1)S(1)} %fusion.after_ref, s32[4,32]{1,0:T(4,128)} %bitcast.4, f32[4,32]{1,0:T(4,128)} %bitcast.5, bf16[2,672,1024]{2,1,0:T(8,128)(2,1)} %up_hbm.1), custom_call_target="tpu_custom_call" | custom-call | bytes 2752512 | tf_op jit(solution)/shard_map/pallas_call | solution.py:32
  7.8 0.0 collective-permute-done.1
  7.9 3.9 %collective-permute-start.4 = (bf16[32,640]{1,0:T(8,128)(2,1)S(1)}, bf16[32,640]{1,0:T(8,128)(2,1)S(1)}, u32[]{:S(2)}, u32[]{:S(2)}) collective-permute-start(bf16[32,640]{1,0:T(8,128)(2,1)S(1)} %pad_maximum_fusion.1.after_ref), channel_id=1, source_target_pairs={{0,12},{1,13},{2,14},{3,15},{4,8},{5,9},{6,10},{7,11},{8,4},{9,5},... | collective-permute-start | bytes 122888 | tf_op jit(solution)/shard_map/ppermute | solution.py:187
  11.8 0.0 collective-permute-start.3
  11.8 0.4 %collective-permute-start.2 = (bf16[32,640]{1,0:T(8,128)(2,1)S(1)}, bf16[32,640]{1,0:T(8,128)(2,1)S(1)}, u32[]{:S(2)}, u32[]{:S(2)}) collective-permute-start(bf16[32,640]{1,0:T(8,128)(2,1)S(1)} %pad_maximum_fusion.1.after_ref), channel_id=1, source_target_pairs={{0,5},{1,4},{2,7},{3,6},{4,1},{5,0},{6,3},{7,2},{8,13},{9,12},{10,... | collective-permute-start | bytes 122888 | tf_op jit(solution)/shard_map/ppermute | solution.py:187
  12.1 1.8 %shard_map.76.down_ref = bf16[1344,1024]{1,0:T(8,128)(2,1)S(1)} custom-call(bf16[32,640]{1,0:T(8,128)(2,1)S(1)} %pad_maximum_fusion.1.after_ref, bf16[1344,1024]{1,0:T(8,128)(2,1)} %bitcast.3), custom_call_target="tpu_custom_call" | custom-call | bytes 2752512 | tf_op jit(solution)/shard_map/pallas_call | solution.py:32
  13.9 2.5 %collective-permute-done.3 = bf16[32,640]{1,0:T(8,128)(2,1)S(1)} collective-permute-done((bf16[32,640]{1,0:T(8,128)(2,1)S(1)}, bf16[32,640]{1,0:T(8,128)(2,1)S(1)}, u32[]{:S(2)}, u32[]{:S(2)}) %collective-permute-start.3) | collective-permute-done | bytes 40992 | tf_op jit(solution)/shard_map/ppermute | solution.py:187
  16.5 0.0 collective-permute-done.2
  16.5 0.2 collective-permute-start.5
  16.7 0.6 %shard_map.77.pre_ref = f32[128,1344]{1,0:T(8,128)S(1)} custom-call(bf16[128,640]{1,0:T(8,128)(2,1)S(1)} %pad_maximum_fusion.messages_ref, bf16[2,672,1024]{2,1,0:T(8,128)(2,1)S(1)} %get-tuple-element.19.up_ref), custom_call_target="tpu_custom_call" | custom-call | flops 176160768 | bytes 1376256 | tf_op jit(solution)/shard_map/pallas_call | solution.py:32
  17.3 0.6 %collective-permute-done.5.other_ref = bf16[128,512]{1,0:T(8,128)(2,1)S(1)} collective-permute-done((bf16[128,512]{1,0:T(8,128)(2,1)S(1)}, bf16[128,512]{1,0:T(8,128)(2,1)S(1)}, u32[]{:S(2)}, u32[]{:S(2)}) %collective-permute-start.5) | collective-permute-done | bytes 131104 | tf_op jit(solution)/shard_map/ppermute | solution.py:181
  17.9 0.9 %shard_map.78 = (bf16[128,1344]{1,0:T(8,128)(2,1)S(1)}, bf16[128,512]{1,0:T(8,128)(2,1)S(1)}) custom-call(bf16[128,640]{1,0:T(8,128)(2,1)S(1)} %pad_maximum_fusion.messages_ref, bf16[128,512]{1,0:T(8,128)(2,1)S(1)} %collective-permute-done.5.other_ref, f32[128,1344]{1,0:T(8,128)S(1)} %shard_map.77.pre_ref, ...), custom_call_target="tpu_custom_call" | custom-call | flops 352321536 | bytes 2752512 | tf_op jit(solution)/shard_map/pallas_call | solution.py:32
  18.8 0.0 copy-start
  18.8 0.2 collective-permute-start.6
  19.0 0.4 %shard_map.79 = f32[128,512]{1,0:T(8,128)S(1)} custom-call(bf16[128,1344]{1,0:T(8,128)(2,1)S(1)} %get-tuple-element.21.hidden_ref, bf16[1344,1024]{1,0:T(8,128)(2,1)S(1)} %shard_map.76.down_ref), custom_call_target="tpu_custom_call" | custom-call | flops 176160768 | bytes 1376256 | tf_op jit(solution)/shard_map/pallas_call | solution.py:32
  19.4 0.8 %collective-permute-done.6 = bf16[128,512]{1,0:T(8,128)(2,1)S(1)} collective-permute-done((bf16[128,512]{1,0:T(8,128)(2,1)S(1)}, bf16[128,512]{1,0:T(8,128)(2,1)S(1)}, u32[]{:S(2)}, u32[]{:S(2)}) %collective-permute-start.6) | collective-permute-done | bytes 131104 | tf_op jit(solution)/shard_map/ppermute | solution.py:181
  20.3 2.1 %collective-permute-start.7 = (bf16[32,512]{1,0:T(8,128)(2,1)S(1)}, bf16[32,512]{1,0:T(8,128)(2,1)S(1)}, u32[]{:S(2)}, u32[]{:S(2)}) collective-permute-start(bf16[32,512]{1,0:T(8,128)(2,1)S(1)} %get-tuple-element.23), channel_id=1, source_target_pairs={{0,12},{1,13},{2,14},{3,15},{4,8},{5,9},{6,10},{7,11},{8,4},{9,5},... | collective-permute-start | bytes 98312 | tf_op jit(solution)/shard_map/ppermute | solution.py:187
  22.4 0.0 collective-permute-start.9
  22.4 2.0 %collective-permute-start.8 = (bf16[32,512]{1,0:T(8,128)(2,1)S(1)}, bf16[32,512]{1,0:T(8,128)(2,1)S(1)}, u32[]{:S(2)}, u32[]{:S(2)}) collective-permute-start(bf16[32,512]{1,0:T(8,128)(2,1)S(1)} %get-tuple-element.25), channel_id=1, source_target_pairs={{0,5},{1,4},{2,7},{3,6},{4,1},{5,0},{6,3},{7,2},{8,13},{9,12},{10,... | collective-permute-start | bytes 98312 | tf_op jit(solution)/shard_map/ppermute | solution.py:187
  24.5 2.0 %collective-permute-done.7 = bf16[32,512]{1,0:T(8,128)(2,1)S(1)} collective-permute-done((bf16[32,512]{1,0:T(8,128)(2,1)S(1)}, bf16[32,512]{1,0:T(8,128)(2,1)S(1)}, u32[]{:S(2)}, u32[]{:S(2)}) %collective-permute-start.7) | collective-permute-done | bytes 32800 | tf_op jit(solution)/shard_map/ppermute | solution.py:187
  26.5 1.0 %collective-permute-done.9 = bf16[32,512]{1,0:T(8,128)(2,1)S(1)} collective-permute-done((bf16[32,512]{1,0:T(8,128)(2,1)S(1)}, bf16[32,512]{1,0:T(8,128)(2,1)S(1)}, u32[]{:S(2)}, u32[]{:S(2)}) %collective-permute-start.9) | collective-permute-done | bytes 32800 | tf_op jit(solution)/shard_map/ppermute | solution.py:187
  27.5 1.2 %collective-permute-start.10 = (bf16[32,512]{1,0:T(8,128)(2,1)S(1)}, bf16[32,512]{1,0:T(8,128)(2,1)S(1)}, u32[]{:S(2)}, u32[]{:S(2)}) collective-permute-start(bf16[32,512]{1,0:T(8,128)(2,1)S(1)} %fusion.1), channel_id=1, source_target_pairs={{0,3},{1,2},{2,1},{3,0},{4,7},{5,6},{6,5},{7,4},{8,11},{9,10},{10,... | collective-permute-start | bytes 98312 | tf_op jit(solution)/shard_map/ppermute | solution.py:181
  28.7 2.3 %collective-permute-done.10 = bf16[32,512]{1,0:T(8,128)(2,1)S(1)} collective-permute-done((bf16[32,512]{1,0:T(8,128)(2,1)S(1)}, bf16[32,512]{1,0:T(8,128)(2,1)S(1)}, u32[]{:S(2)}, u32[]{:S(2)}) %collective-permute-start.10) | collective-permute-done | bytes 32800 | tf_op jit(solution)/shard_map/ppermute | solution.py:181
  31.0 0.2 collective-permute-start.11
  31.2 0.3 shard_map.80.part_ref
  31.5 0.8 %collective-permute-done.11.other_ref = bf16[32,512]{1,0:T(8,128)(2,1)S(1)} collective-permute-done((bf16[32,512]{1,0:T(8,128)(2,1)S(1)}, bf16[32,512]{1,0:T(8,128)(2,1)S(1)}, u32[]{:S(2)}, u32[]{:S(2)}) %collective-permute-start.11) | collective-permute-done | bytes 32800 | tf_op jit(solution)/shard_map/ppermute | solution.py:181
  32.3 0.9 %shard_map.81 = bf16[32,1024]{1,0:T(8,128)(2,1)} custom-call(f32[32,1024]{1,0:T(8,128)S(1)} %shard_map.80.part_ref, bf16[32,512]{1,0:T(8,128)(2,1)S(1)} %collective-permute-done.11.other_ref, bf16[1024,1024]{1,0:T(8,128)(2,1)S(1)} %copy-done), custom_call_target="tpu_custom_call" | custom-call | flops 33554432 | bytes 1048576 | tf_op jit(solution)/shard_map/pallas_call | solution.py:32
  (12 shorter events, 0.1 us)
Async XLA Ops:
  1.9 1.4 %collective-permute-start = (bf16[32,512]{1,0:T(8,128)(2,1)S(1)}, bf16[32,512]{1,0:T(8,128)(2,1)S(1)}, u32[]{:S(2)}, u32[]{:S(2)}) collective-permute-start(bf16[32,512]{1,0:T(8,128)(2,1)S(1)} %get-tuple-element.16), channel_id=1, source_target_pairs={{0,1},{1,0},{2,3},{3,2},{4,5},{5,4},{6,7},{7,6},{8,9},{9,8},{10,11... | collective-permute-start | bytes 98312 | tf_op jit(solution)/shard_map/ppermute | solution.py:181
  3.3 4.5 %collective-permute-start.1 = (bf16[32,512]{1,0:T(8,128)(2,1)S(1)}, bf16[32,512]{1,0:T(8,128)(2,1)S(1)}, u32[]{:S(2)}, u32[]{:S(2)}) collective-permute-start(bf16[32,512]{1,0:T(8,128)(2,1)S(1)} %fusion.after_ref), channel_id=1, source_target_pairs={{0,3},{1,2},{2,1},{3,0},{4,7},{5,6},{6,5},{7,4},{8,11},{9,10},{10,... | collective-permute-start | bytes 98312 | tf_op jit(solution)/shard_map/ppermute | solution.py:181
  7.9 6.1 %collective-permute-start.4 = (bf16[32,640]{1,0:T(8,128)(2,1)S(1)}, bf16[32,640]{1,0:T(8,128)(2,1)S(1)}, u32[]{:S(2)}, u32[]{:S(2)}) collective-permute-start(bf16[32,640]{1,0:T(8,128)(2,1)S(1)} %pad_maximum_fusion.1.after_ref), channel_id=1, source_target_pairs={{0,12},{1,13},{2,14},{3,15},{4,8},{5,9},{6,10},{7,11},{8,4},{9,5},... | collective-permute-start | bytes 122888 | tf_op jit(solution)/shard_map/ppermute | solution.py:187
  11.8 4.7 %collective-permute-start.3 = (bf16[32,640]{1,0:T(8,128)(2,1)S(1)}, bf16[32,640]{1,0:T(8,128)(2,1)S(1)}, u32[]{:S(2)}, u32[]{:S(2)}) collective-permute-start(bf16[32,640]{1,0:T(8,128)(2,1)S(1)} %pad_maximum_fusion.1.after_ref), channel_id=1, source_target_pairs={{0,9},{1,8},{2,11},{3,10},{4,13},{5,12},{6,15},{7,14},{8,1},{9,0},... | collective-permute-start | bytes 122888 | tf_op jit(solution)/shard_map/ppermute | solution.py:187
  11.8 4.7 %collective-permute-start.2 = (bf16[32,640]{1,0:T(8,128)(2,1)S(1)}, bf16[32,640]{1,0:T(8,128)(2,1)S(1)}, u32[]{:S(2)}, u32[]{:S(2)}) collective-permute-start(bf16[32,640]{1,0:T(8,128)(2,1)S(1)} %pad_maximum_fusion.1.after_ref), channel_id=1, source_target_pairs={{0,5},{1,4},{2,7},{3,6},{4,1},{5,0},{6,3},{7,2},{8,13},{9,12},{10,... | collective-permute-start | bytes 122888 | tf_op jit(solution)/shard_map/ppermute | solution.py:187
  16.5 1.4 %collective-permute-start.5 = (bf16[128,512]{1,0:T(8,128)(2,1)S(1)}, bf16[128,512]{1,0:T(8,128)(2,1)S(1)}, u32[]{:S(2)}, u32[]{:S(2)}) collective-permute-start(bf16[128,512]{1,0:T(8,128)(2,1)S(1)} %slice.24), channel_id=1, source_target_pairs={{0,1},{1,0},{2,3},{3,2},{4,5},{5,4},{6,7},{7,6},{8,9},{9,8},{10,11... | collective-permute-start | bytes 393224 | tf_op jit(solution)/shard_map/ppermute | solution.py:181
  18.8 12.4 %copy-start = (bf16[1024,1024]{1,0:T(8,128)(2,1)S(1)}, bf16[1024,1024]{1,0:T(8,128)(2,1)}, u32[]{:S(2)}) copy-start(bf16[1024,1024]{1,0:T(8,128)(2,1)} %weight_ref.3) | copy-start | bytes 6291460
  18.8 1.4 %collective-permute-start.6 = (bf16[128,512]{1,0:T(8,128)(2,1)S(1)}, bf16[128,512]{1,0:T(8,128)(2,1)S(1)}, u32[]{:S(2)}, u32[]{:S(2)}) collective-permute-start(bf16[128,512]{1,0:T(8,128)(2,1)S(1)} %get-tuple-element.22), channel_id=1, source_target_pairs={{0,1},{1,0},{2,3},{3,2},{4,5},{5,4},{6,7},{7,6},{8,9},{9,8},{10,11... | collective-permute-start | bytes 393224 | tf_op jit(solution)/shard_map/ppermute | solution.py:181
  20.3 6.2 %collective-permute-start.7 = (bf16[32,512]{1,0:T(8,128)(2,1)S(1)}, bf16[32,512]{1,0:T(8,128)(2,1)S(1)}, u32[]{:S(2)}, u32[]{:S(2)}) collective-permute-start(bf16[32,512]{1,0:T(8,128)(2,1)S(1)} %get-tuple-element.23), channel_id=1, source_target_pairs={{0,12},{1,13},{2,14},{3,15},{4,8},{5,9},{6,10},{7,11},{8,4},{9,5},... | collective-permute-start | bytes 98312 | tf_op jit(solution)/shard_map/ppermute | solution.py:187
  22.4 5.0 %collective-permute-start.9 = (bf16[32,512]{1,0:T(8,128)(2,1)S(1)}, bf16[32,512]{1,0:T(8,128)(2,1)S(1)}, u32[]{:S(2)}, u32[]{:S(2)}) collective-permute-start(bf16[32,512]{1,0:T(8,128)(2,1)S(1)} %get-tuple-element.24), channel_id=1, source_target_pairs={{0,9},{1,8},{2,11},{3,10},{4,13},{5,12},{6,15},{7,14},{8,1},{9,0},... | collective-permute-start | bytes 98312 | tf_op jit(solution)/shard_map/ppermute | solution.py:187
  22.4 5.0 %collective-permute-start.8 = (bf16[32,512]{1,0:T(8,128)(2,1)S(1)}, bf16[32,512]{1,0:T(8,128)(2,1)S(1)}, u32[]{:S(2)}, u32[]{:S(2)}) collective-permute-start(bf16[32,512]{1,0:T(8,128)(2,1)S(1)} %get-tuple-element.25), channel_id=1, source_target_pairs={{0,5},{1,4},{2,7},{3,6},{4,1},{5,0},{6,3},{7,2},{8,13},{9,12},{10,... | collective-permute-start | bytes 98312 | tf_op jit(solution)/shard_map/ppermute | solution.py:187
  27.5 3.5 %collective-permute-start.10 = (bf16[32,512]{1,0:T(8,128)(2,1)S(1)}, bf16[32,512]{1,0:T(8,128)(2,1)S(1)}, u32[]{:S(2)}, u32[]{:S(2)}) collective-permute-start(bf16[32,512]{1,0:T(8,128)(2,1)S(1)} %fusion.1), channel_id=1, source_target_pairs={{0,3},{1,2},{2,1},{3,0},{4,7},{5,6},{6,5},{7,4},{8,11},{9,10},{10,... | collective-permute-start | bytes 98312 | tf_op jit(solution)/shard_map/ppermute | solution.py:181
  31.0 1.3 %collective-permute-start.11 = (bf16[32,512]{1,0:T(8,128)(2,1)S(1)}, bf16[32,512]{1,0:T(8,128)(2,1)S(1)}, u32[]{:S(2)}, u32[]{:S(2)}) collective-permute-start(bf16[32,512]{1,0:T(8,128)(2,1)S(1)} %add_convert_fusion.1.own_ref), channel_id=1, source_target_pairs={{0,1},{1,0},{2,3},{3,2},{4,5},{5,4},{6,7},{7,6},{8,9},{9,8},{10,11... | collective-permute-start | bytes 98312 | tf_op jit(solution)/shard_map/ppermute | solution.py:181

commit v15 on v14

--- a/solution.py
+++ b/solution.py
@@ -10,7 +10,8 @@
 NN = (((1,), (0,)), ((), ()))
 VMEM_LIMIT = 24 << 20
 LANES = 128
-CHUNKS = 2
+CHUNKS = 1
+TILE = 16
 
 
 def hbm(x):
@@ -92,8 +93,13 @@
     copy.wait()
 
 
+def group_at(group, experts_all):
+    side_by_side = LANES // (2 * experts_all)
+    return group // side_by_side, group % side_by_side * 2 * experts_all
+
+
 def terms_kernel(
-    after_ref, routes_hbm, scale_hbm, up_hbm, terms_ref, up_ref, routes, scale, sems
+    experts_all, after_ref, routes_hbm, scale_hbm, up_hbm, terms_ref, up_ref, routes, scale, sems
 ):
     pairs = [(routes_hbm, routes), (scale_hbm, scale), (up_hbm, up_ref)]
     copies = [pltpu.make_async_copy(a, b, sems.at[i]) for i, (a, b) in enumerate(pairs)]
@@ -101,39 +107,76 @@
         copy.start()
     copies[0].wait()
     copies[1].wait()
-    rows, width = terms_ref.shape
-    row = lax.broadcasted_iota(jnp.int32, (width, rows), 0)
-    experts_all = width // 2
+    rows = routes.shape[1]
+    row = lax.broadcasted_iota(jnp.int32, (LANES, rows), 0)
     expert = jnp.where(row < experts_all, row, row - experts_all)
-    combine = jnp.zeros((width, rows), F32)
+    combine = jnp.zeros((LANES, rows), F32)
     for r in range(routes.shape[0]):
         combine += jnp.where(expert == routes[r : r + 1, :], scale[r : r + 1, :], 0.0)
+    combine = jnp.where(row < 2 * experts_all, combine, 0.0)
     high = combine.astype(BF16).astype(F32)
     combine = jnp.where(row < experts_all, high, combine - high)
-    combine = jnp.concatenate([combine, jnp.zeros((width, LANES - rows), F32)], axis=1)
-    terms_ref[...] = combine.T[:rows, :].astype(BF16)
+    combine = jnp.concatenate([combine, jnp.zeros((LANES, LANES - rows), F32)], axis=1)
+    turned = combine.T
+    packed = [jnp.zeros((TILE, LANES), F32)] * (terms_ref.shape[0] // TILE)
+    for g in range(rows // TILE):
+        tile, at = group_at(g, experts_all)
+        part = turned[g * TILE : (g + 1) * TILE, :]
+        packed[tile] += pltpu.roll(part, at, 1) if at else part
+    for tile, part in enumerate(packed):
+        terms_ref[tile * TILE : (tile + 1) * TILE, :] = part.astype(BF16)
     copies[2].wait()
 
 
-def first_kernel(messages_ref, up_ref, pre_ref):
+def fold_kernel(latent_ref, terms_ref, message_ref):
+    rows, half = latent_ref.shape
+    for c in range(half // LANES):
+        columns = latent_ref[:, c * LANES : (c + 1) * LANES]
+        message_ref[c * rows : (c + 1) * rows, :] = columns.astype(BF16)
+    message_ref[half // LANES * rows :, :] = terms_ref[...]
+
+
+def unfold_kernel(*refs):
+    *messages, latent_ref, terms_ref = refs
+    rows = latent_ref.shape[0] // len(messages)
+    tiles = terms_ref.shape[0] // len(messages)
+    parts = latent_ref.shape[1] // LANES
+    for b, message in enumerate(messages):
+        for c in range(parts):
+            columns = message[c * rows : (c + 1) * rows, :]
+            latent_ref[b * rows : (b + 1) * rows, c * LANES : (c + 1) * LANES] = columns
+        terms_ref[b * tiles : (b + 1) * tiles, :] = message[parts * rows :, :]
+
+
+def first_kernel(own_ref, up_ref, pre_ref):
     local_count, units, latent_len = up_ref.shape
     half = latent_len // 2
-    rows = messages_ref[:, :half]
+    rows = own_ref[...]
     for k in range(local_count):
         weight = up_ref[k, :, pl.ds(half_at(True, half), half)]
         pre_ref[:, k * units : (k + 1) * units] = dot(rows, weight, NT)
 
 
-def second_kernel(messages_ref, other_ref, pre_ref, up_ref, down_ref, hidden_ref, theirs_ref):
+def second_kernel(terms_ref, other_ref, pre_ref, up_ref, down_ref, hidden_ref, theirs_ref):
     local_count, units, latent_len = up_ref.shape
     half = latent_len // 2
-    terms = messages_ref[:, half:].astype(F32)
-    lane = lax.broadcasted_iota(jnp.int32, terms.shape, 1)
+    blocks = lax.axis_size("exp")
+    experts_all = local_count * blocks
+    groups = other_ref.shape[0] // blocks // TILE
+    tiles = terms_ref.shape[0] // blocks // TILE
     first = lax.axis_index("exp") * local_count
+    lane = lax.broadcasted_iota(jnp.int32, (TILE, LANES), 1)
     rows = other_ref[...]
     for k in range(local_count):
-        named = (lane == first + k) | (lane == first + k + terms.shape[1] // 2)
-        weight = jnp.sum(jnp.where(named, terms, 0.0), axis=1, keepdims=True)
+        weight = []
+        for b in range(blocks):
+            for g in range(groups):
+                tile, at = group_at(g, experts_all)
+                tile = (b * tiles + tile) * TILE
+                terms = terms_ref[tile : tile + TILE, :].astype(F32)
+                named = (lane == at + first + k) | (lane == at + first + k + experts_all)
+                weight.append(jnp.sum(jnp.where(named, terms, 0.0), axis=1, keepdims=True))
+        weight = jnp.concatenate(weight, axis=0)
         at = slice(k * units, (k + 1) * units)
         pre_act = pre_ref[:, at] + dot(rows, up_ref[k, :, pl.ds(half_at(False, half), half)], NT)
         active = jnp.maximum(pre_act, 0.0)
@@ -174,7 +217,9 @@
     all_rows = exp_count * rows
     all_units = local_count * units
     out_len = lat_up.shape[1]
-    terms_len = -(-2 * local_count * exp_count // LANES) * LANES
+    experts_all = local_count * exp_count
+    parts = half // LANES
+    terms_rows = -(-rows // TILE // (LANES // (2 * experts_all))) * TILE
     pair_masks = [(1 << b) + 1 for b in range(1, tp_count.bit_length() - 1)]
 
     def over_tp(x, mask):
@@ -215,8 +260,8 @@
     )
     mine = mine + over_tp(theirs, 1).astype(F32)
     terms, up_here = kernel_call(
-        terms_kernel,
-        (shaped(BF16, rows, terms_len), pltpu.VMEM(expert_up.shape, BF16)),
+        lambda *refs: terms_kernel(experts_all, *refs),
+        (shaped(BF16, terms_rows, LANES), pltpu.VMEM(expert_up.shape, BF16)),
         (mine.astype(BF16), *(hbm(x) for x in (routes.T, route_weights.T, expert_up))),
         (1, 2, 3),
         [
@@ -228,7 +273,15 @@
         2 * latent_len * all_units,
     )
     up_here = vmem(up_here)
-    message = jnp.concatenate([across(mine).astype(BF16), terms], axis=1)
+    message = kernel_call(
+        fold_kernel,
+        shaped(BF16, parts * rows + terms_rows, LANES),
+        (across(mine), terms),
+        (),
+        [],
+        0,
+        6 * rows * half,
+    )
     down_rows = expert_down.reshape(all_units, latent_len)
     down_here = kernel_call(
         load_kernel,
@@ -241,12 +294,21 @@
     )
     messages = [message] + [over_exp(message, s) for s in range(1, exp_count)]
     messages[-1], down_here = lax.optimization_barrier((messages[-1], down_here))
-    messages, down_here = jnp.concatenate(messages, axis=0), vmem(down_here)
-    other = over_tp(messages[:, :half], 1)
+    down_here = vmem(down_here)
+    latent, terms = kernel_call(
+        unfold_kernel,
+        (shaped(BF16, all_rows, half), shaped(BF16, exp_count * terms_rows, LANES)),
+        messages,
+        (),
+        [],
+        0,
+        4 * all_rows * half,
+    )
+    other = over_tp(latent, 1)
     pre = kernel_call(
         first_kernel,
         shaped(F32, all_rows, all_units),
-        (messages, up_here),
+        (latent, up_here),
         (),
         [],
         all_rows * latent_len * all_units,
@@ -255,7 +317,7 @@
     hidden, theirs = kernel_call(
         second_kernel,
         (shaped(BF16, all_rows, all_units), shaped(BF16, all_rows, half)),
-        (messages, other, pre, up_here, down_here),
+        (terms, other, pre, up_here, down_here),
         (),
         [],
         2 * all_rows * latent_len * all_units,

time: 33.4 us -> 33.1 us (level)
    pallas_call x9 -> x11, Pallas kernels: 9.05 us -> 8.91 us  [kernel_call(): pl.pallas_call(body, out_shape=out_shape, in_specs=[spec(pltpu.HBM if i i...]
where the time goes in v15:
time: 33.1 us; the launch traced here: 32.9 us
  starting transfers between devices  13.4 us (40%)
  waiting for transfers between devices  10.3 us (31%)
  Pallas kernels  8.91 us (27%)
    pallas_call x11, Pallas kernels, kernel_call(): pl.pallas_call(body, out_shape=out_shape, in_specs=[spec(pltpu.HBM if i i...  8.91 us
    ppermute x6, starting transfers between devices, over_exp(): return lax.ppermute(x, ('exp', 'tp'), hops)  8.43 us
    ppermute x6, waiting for transfers between devices, over_exp(): return lax.ppermute(x, ('exp', 'tp'), hops)  5.45 us
    ppermute x6, starting transfers between devices, over_tp(): return lax.ppermute(x, 'tp', [(t, t ^ mask) for t in range(tp_count)])  5.01 us
    ppermute x6, waiting for transfers between devices, over_tp(): return lax.ppermute(x, 'tp', [(t, t ^ mask) for t in range(tp_count)])  4.87 us
  transfers between devices with their start and end apart: 12, of which 8 were waited for; matrix products, arithmetic and copies ran while one was open for 0% of the time, Pallas kernels for 16%

profile of v15, /device:TPU:0, one launch (start us, length us, event | category | flops | bytes accessed | tf_op | source)
XLA Modules:
  0.0 32.9 jit_solution(16295518278780481390)
XLA Ops:
  0.0 1.7 %shard_map.73 = (bf16[32,512]{1,0:T(8,128)(2,1)S(1)}, bf16[32,1024]{1,0:T(8,128)(2,1)S(1)}, bf16[512,1024]{1,0:T(8,128)(2,1)S(1)}) custom-call(bf16[32,1024]{1,0:T(8,128)(2,1)} %tokens_hbm.1, bf16[1024,1024]{1,0:T(8,128)(2,1)} %weight_hbm.1), custom_call_target="tpu_custom_call" | custom-call | flops 33554432 | bytes 2097152 | tf_op jit(solution)/shard_map/pallas_call | solution.py:33
  1.7 0.5 %collective-permute-start = (bf16[32,512]{1,0:T(8,128)(2,1)S(1)}, bf16[32,512]{1,0:T(8,128)(2,1)S(1)}, u32[]{:S(2)}, u32[]{:S(2)}) collective-permute-start(bf16[32,512]{1,0:T(8,128)(2,1)S(1)} %get-tuple-element.18), channel_id=1, source_target_pairs={{0,1},{1,0},{2,3},{3,2},{4,5},{5,4},{6,7},{7,6},{8,9},{9,8},{10,11... | collective-permute-start | bytes 98312 | tf_op jit(solution)/shard_map/ppermute | solution.py:226
  2.2 0.4 %shard_map.74 = f32[32,512]{1,0:T(8,128)S(1)} custom-call(bf16[32,1024]{1,0:T(8,128)(2,1)S(1)} %get-tuple-element.16.tokens_ref, bf16[512,1024]{1,0:T(8,128)(2,1)S(1)} %get-tuple-element.17.weight_ref), custom_call_target="tpu_custom_call" | custom-call | flops 33554432 | bytes 1048576 | tf_op jit(solution)/shard_map/pallas_call | solution.py:33
  2.6 0.5 %collective-permute-done = bf16[32,512]{1,0:T(8,128)(2,1)S(1)} collective-permute-done((bf16[32,512]{1,0:T(8,128)(2,1)S(1)}, bf16[32,512]{1,0:T(8,128)(2,1)S(1)}, u32[]{:S(2)}, u32[]{:S(2)}) %collective-permute-start) | collective-permute-done | bytes 32800 | tf_op jit(solution)/shard_map/ppermute | solution.py:226
  3.1 2.7 %collective-permute-start.1 = (bf16[32,512]{1,0:T(8,128)(2,1)S(1)}, bf16[32,512]{1,0:T(8,128)(2,1)S(1)}, u32[]{:S(2)}, u32[]{:S(2)}) collective-permute-start(bf16[32,512]{1,0:T(8,128)(2,1)S(1)} %fusion.refs_0_), channel_id=1, source_target_pairs={{0,3},{1,2},{2,1},{3,0},{4,7},{5,6},{6,5},{7,4},{8,11},{9,10},{10,... | collective-permute-start | bytes 98312 | tf_op jit(solution)/shard_map/ppermute | solution.py:226
  5.8 1.8 %shard_map.75 = (bf16[16,128]{1,0:T(8,128)(2,1)S(1)}, bf16[2,672,1024]{2,1,0:T(8,128)(2,1)S(1)}) custom-call(bf16[32,512]{1,0:T(8,128)(2,1)S(1)} %fusion.refs_0_, s32[4,32]{1,0:T(4,128)} %bitcast.4, f32[4,32]{1,0:T(4,128)} %bitcast.5, bf16[2,672,1024]{2,1,0:T(8,128)(2,1)} %refs_3_.1), custom_call_target="tpu_custom_call" | custom-call | bytes 2752512 | tf_op jit(solution)/shard_map/pallas_call | solution.py:33
  7.6 0.0 collective-permute-done.1
  7.7 3.9 %collective-permute-start.4 = (bf16[144,128]{1,0:T(8,128)(2,1)S(1)}, bf16[144,128]{1,0:T(8,128)(2,1)S(1)}, u32[]{:S(2)}, u32[]{:S(2)}) collective-permute-start(bf16[144,128]{1,0:T(8,128)(2,1)S(1)} %shard_map.76.after_ref.refs_0_), channel_id=1, source_target_pairs={{0,12},{1,13},{2,14},{3,15},{4,8},{5,9},{6,10},{7,11},{8,4},{9,5},... | collective-permute-start | bytes 110600 | tf_op jit(solution)/shard_map/ppermute | solution.py:232
  11.6 0.0 collective-permute-start.3
  11.6 0.4 %collective-permute-start.2 = (bf16[144,128]{1,0:T(8,128)(2,1)S(1)}, bf16[144,128]{1,0:T(8,128)(2,1)S(1)}, u32[]{:S(2)}, u32[]{:S(2)}) collective-permute-start(bf16[144,128]{1,0:T(8,128)(2,1)S(1)} %shard_map.76.after_ref.refs_0_), channel_id=1, source_target_pairs={{0,5},{1,4},{2,7},{3,6},{4,1},{5,0},{6,3},{7,2},{8,13},{9,12},{10,... | collective-permute-start | bytes 110600 | tf_op jit(solution)/shard_map/ppermute | solution.py:232
  11.9 1.8 %shard_map.77.down_ref = bf16[1344,1024]{1,0:T(8,128)(2,1)S(1)} custom-call(bf16[144,128]{1,0:T(8,128)(2,1)S(1)} %shard_map.76.after_ref.refs_0_, bf16[1344,1024]{1,0:T(8,128)(2,1)} %bitcast.3), custom_call_target="tpu_custom_call" | custom-call | bytes 2752512 | tf_op jit(solution)/shard_map/pallas_call | solution.py:33
  13.7 2.4 %collective-permute-done.3.refs_2_ = bf16[144,128]{1,0:T(8,128)(2,1)S(1)} collective-permute-done((bf16[144,128]{1,0:T(8,128)(2,1)S(1)}, bf16[144,128]{1,0:T(8,128)(2,1)S(1)}, u32[]{:S(2)}, u32[]{:S(2)}) %collective-permute-start.3) | collective-permute-done | bytes 36896 | tf_op jit(solution)/shard_map/ppermute | solution.py:232
  16.2 0.2 collective-permute-start.5
  16.4 0.6 %shard_map.79.pre_ref = f32[128,1344]{1,0:T(8,128)S(1)} custom-call(bf16[128,512]{1,0:T(8,128)(2,1)S(1)} %get-tuple-element.22.own_ref, bf16[2,672,1024]{2,1,0:T(8,128)(2,1)S(1)} %get-tuple-element.23.up_ref), custom_call_target="tpu_custom_call" | custom-call | flops 176160768 | bytes 1376256 | tf_op jit(solution)/shard_map/pallas_call | solution.py:33
  17.0 0.6 %collective-permute-done.5.other_ref = bf16[128,512]{1,0:T(8,128)(2,1)S(1)} collective-permute-done((bf16[128,512]{1,0:T(8,128)(2,1)S(1)}, bf16[128,512]{1,0:T(8,128)(2,1)S(1)}, u32[]{:S(2)}, u32[]{:S(2)}) %collective-permute-start.5) | collective-permute-done | bytes 131104 | tf_op jit(solution)/shard_map/ppermute | solution.py:226
  17.6 0.9 %shard_map.80 = (bf16[128,1344]{1,0:T(8,128)(2,1)S(1)}, bf16[128,512]{1,0:T(8,128)(2,1)S(1)}) custom-call(bf16[64,128]{1,0:T(8,128)(2,1)S(1)} %get-tuple-element.21.terms_ref, bf16[128,512]{1,0:T(8,128)(2,1)S(1)} %collective-permute-done.5.other_ref, f32[128,1344]{1,0:T(8,128)S(1)} %shard_map.79.pre_ref, bf16[2,672,1024]{2,1,0:T(8,128)(2,1)S(1)} %get-tuple-element.23.up_ref, ...), custom_call_target="tpu_custom_call" | custom-call | flops 352321536 | bytes 2752512 | tf_op jit(solution)/shard_map/pallas_call | solution.py:33
  18.5 0.0 copy-start
  18.6 0.2 collective-permute-start.6
  18.8 0.4 %shard_map.81 = f32[128,512]{1,0:T(8,128)S(1)} custom-call(bf16[128,1344]{1,0:T(8,128)(2,1)S(1)} %get-tuple-element.25.hidden_ref, bf16[1344,1024]{1,0:T(8,128)(2,1)S(1)} %shard_map.77.down_ref), custom_call_target="tpu_custom_call" | custom-call | flops 176160768 | bytes 1376256 | tf_op jit(solution)/shard_map/pallas_call | solution.py:33
  19.1 0.8 %collective-permute-done.6 = bf16[128,512]{1,0:T(8,128)(2,1)S(1)} collective-permute-done((bf16[128,512]{1,0:T(8,128)(2,1)S(1)}, bf16[128,512]{1,0:T(8,128)(2,1)S(1)}, u32[]{:S(2)}, u32[]{:S(2)}) %collective-permute-start.6) | collective-permute-done | bytes 131104 | tf_op jit(solution)/shard_map/ppermute | solution.py:226
  20.0 2.0 %collective-permute-start.7 = (bf16[32,512]{1,0:T(8,128)(2,1)S(1)}, bf16[32,512]{1,0:T(8,128)(2,1)S(1)}, u32[]{:S(2)}, u32[]{:S(2)}) collective-permute-start(bf16[32,512]{1,0:T(8,128)(2,1)S(1)} %get-tuple-element.27), channel_id=1, source_target_pairs={{0,12},{1,13},{2,14},{3,15},{4,8},{5,9},{6,10},{7,11},{8,4},{9,5},... | collective-permute-start | bytes 98312 | tf_op jit(solution)/shard_map/ppermute | solution.py:232
  22.0 0.0 collective-permute-start.9
  22.0 2.2 %collective-permute-start.8 = (bf16[32,512]{1,0:T(8,128)(2,1)S(1)}, bf16[32,512]{1,0:T(8,128)(2,1)S(1)}, u32[]{:S(2)}, u32[]{:S(2)}) collective-permute-start(bf16[32,512]{1,0:T(8,128)(2,1)S(1)} %get-tuple-element.29), channel_id=1, source_target_pairs={{0,5},{1,4},{2,7},{3,6},{4,1},{5,0},{6,3},{7,2},{8,13},{9,12},{10,... | collective-permute-start | bytes 98312 | tf_op jit(solution)/shard_map/ppermute | solution.py:232
  24.2 2.0 %collective-permute-done.7 = bf16[32,512]{1,0:T(8,128)(2,1)S(1)} collective-permute-done((bf16[32,512]{1,0:T(8,128)(2,1)S(1)}, bf16[32,512]{1,0:T(8,128)(2,1)S(1)}, u32[]{:S(2)}, u32[]{:S(2)}) %collective-permute-start.7) | collective-permute-done | bytes 32800 | tf_op jit(solution)/shard_map/ppermute | solution.py:232
  26.2 1.0 %collective-permute-done.9 = bf16[32,512]{1,0:T(8,128)(2,1)S(1)} collective-permute-done((bf16[32,512]{1,0:T(8,128)(2,1)S(1)}, bf16[32,512]{1,0:T(8,128)(2,1)S(1)}, u32[]{:S(2)}, u32[]{:S(2)}) %collective-permute-start.9) | collective-permute-done | bytes 32800 | tf_op jit(solution)/shard_map/ppermute | solution.py:232
  27.2 0.0 collective-permute-done.8
  27.2 1.3 %collective-permute-start.10 = (bf16[32,512]{1,0:T(8,128)(2,1)S(1)}, bf16[32,512]{1,0:T(8,128)(2,1)S(1)}, u32[]{:S(2)}, u32[]{:S(2)}) collective-permute-start(bf16[32,512]{1,0:T(8,128)(2,1)S(1)} %fusion.1), channel_id=1, source_target_pairs={{0,3},{1,2},{2,1},{3,0},{4,7},{5,6},{6,5},{7,4},{8,11},{9,10},{10,... | collective-permute-start | bytes 98312 | tf_op jit(solution)/shard_map/ppermute | solution.py:226
  28.5 2.2 %collective-permute-done.10 = bf16[32,512]{1,0:T(8,128)(2,1)S(1)} collective-permute-done((bf16[32,512]{1,0:T(8,128)(2,1)S(1)}, bf16[32,512]{1,0:T(8,128)(2,1)S(1)}, u32[]{:S(2)}, u32[]{:S(2)}) %collective-permute-start.10) | collective-permute-done | bytes 32800 | tf_op jit(solution)/shard_map/ppermute | solution.py:226
  30.7 0.2 collective-permute-start.11
  30.9 0.3 shard_map.82.part_ref
  31.2 0.8 %collective-permute-done.11.other_ref = bf16[32,512]{1,0:T(8,128)(2,1)S(1)} collective-permute-done((bf16[32,512]{1,0:T(8,128)(2,1)S(1)}, bf16[32,512]{1,0:T(8,128)(2,1)S(1)}, u32[]{:S(2)}, u32[]{:S(2)}) %collective-permute-start.11) | collective-permute-done | bytes 32800 | tf_op jit(solution)/shard_map/ppermute | solution.py:226
  32.0 0.9 %shard_map.83 = bf16[32,1024]{1,0:T(8,128)(2,1)} custom-call(f32[32,1024]{1,0:T(8,128)S(1)} %shard_map.82.part_ref, bf16[32,512]{1,0:T(8,128)(2,1)S(1)} %collective-permute-done.11.other_ref, bf16[1024,1024]{1,0:T(8,128)(2,1)S(1)} %copy-done), custom_call_target="tpu_custom_call" | custom-call | flops 33554432 | bytes 1048576 | tf_op jit(solution)/shard_map/pallas_call | solution.py:33
  (11 shorter events, 0.1 us)
Async XLA Ops:
  1.7 1.4 %collective-permute-start = (bf16[32,512]{1,0:T(8,128)(2,1)S(1)}, bf16[32,512]{1,0:T(8,128)(2,1)S(1)}, u32[]{:S(2)}, u32[]{:S(2)}) collective-permute-start(bf16[32,512]{1,0:T(8,128)(2,1)S(1)} %get-tuple-element.18), channel_id=1, source_target_pairs={{0,1},{1,0},{2,3},{3,2},{4,5},{5,4},{6,7},{7,6},{8,9},{9,8},{10,11... | collective-permute-start | bytes 98312 | tf_op jit(solution)/shard_map/ppermute | solution.py:226
  3.1 4.5 %collective-permute-start.1 = (bf16[32,512]{1,0:T(8,128)(2,1)S(1)}, bf16[32,512]{1,0:T(8,128)(2,1)S(1)}, u32[]{:S(2)}, u32[]{:S(2)}) collective-permute-start(bf16[32,512]{1,0:T(8,128)(2,1)S(1)} %fusion.refs_0_), channel_id=1, source_target_pairs={{0,3},{1,2},{2,1},{3,0},{4,7},{5,6},{6,5},{7,4},{8,11},{9,10},{10,... | collective-permute-start | bytes 98312 | tf_op jit(solution)/shard_map/ppermute | solution.py:226
  7.7 6.1 %collective-permute-start.4 = (bf16[144,128]{1,0:T(8,128)(2,1)S(1)}, bf16[144,128]{1,0:T(8,128)(2,1)S(1)}, u32[]{:S(2)}, u32[]{:S(2)}) collective-permute-start(bf16[144,128]{1,0:T(8,128)(2,1)S(1)} %shard_map.76.after_ref.refs_0_), channel_id=1, source_target_pairs={{0,12},{1,13},{2,14},{3,15},{4,8},{5,9},{6,10},{7,11},{8,4},{9,5},... | collective-permute-start | bytes 110600 | tf_op jit(solution)/shard_map/ppermute | solution.py:232
  11.6 4.6 %collective-permute-start.3 = (bf16[144,128]{1,0:T(8,128)(2,1)S(1)}, bf16[144,128]{1,0:T(8,128)(2,1)S(1)}, u32[]{:S(2)}, u32[]{:S(2)}) collective-permute-start(bf16[144,128]{1,0:T(8,128)(2,1)S(1)} %shard_map.76.after_ref.refs_0_), channel_id=1, source_target_pairs={{0,9},{1,8},{2,11},{3,10},{4,13},{5,12},{6,15},{7,14},{8,1},{9,0},... | collective-permute-start | bytes 110600 | tf_op jit(solution)/shard_map/ppermute | solution.py:232
  11.6 4.6 %collective-permute-start.2 = (bf16[144,128]{1,0:T(8,128)(2,1)S(1)}, bf16[144,128]{1,0:T(8,128)(2,1)S(1)}, u32[]{:S(2)}, u32[]{:S(2)}) collective-permute-start(bf16[144,128]{1,0:T(8,128)(2,1)S(1)} %shard_map.76.after_ref.refs_0_), channel_id=1, source_target_pairs={{0,5},{1,4},{2,7},{3,6},{4,1},{5,0},{6,3},{7,2},{8,13},{9,12},{10,... | collective-permute-start | bytes 110600 | tf_op jit(solution)/shard_map/ppermute | solution.py:232
  16.2 1.4 %collective-permute-start.5 = (bf16[128,512]{1,0:T(8,128)(2,1)S(1)}, bf16[128,512]{1,0:T(8,128)(2,1)S(1)}, u32[]{:S(2)}, u32[]{:S(2)}) collective-permute-start(bf16[128,512]{1,0:T(8,128)(2,1)S(1)} %get-tuple-element.22.own_ref), channel_id=1, source_target_pairs={{0,1},{1,0},{2,3},{3,2},{4,5},{5,4},{6,7},{7,6},{8,9},{9,8},{10,11... | collective-permute-start | bytes 393224 | tf_op jit(solution)/shard_map/ppermute | solution.py:226
  18.5 12.4 %copy-start = (bf16[1024,1024]{1,0:T(8,128)(2,1)S(1)}, bf16[1024,1024]{1,0:T(8,128)(2,1)}, u32[]{:S(2)}) copy-start(bf16[1024,1024]{1,0:T(8,128)(2,1)} %weight_ref.3) | copy-start | bytes 6291460
  18.6 1.4 %collective-permute-start.6 = (bf16[128,512]{1,0:T(8,128)(2,1)S(1)}, bf16[128,512]{1,0:T(8,128)(2,1)S(1)}, u32[]{:S(2)}, u32[]{:S(2)}) collective-permute-start(bf16[128,512]{1,0:T(8,128)(2,1)S(1)} %get-tuple-element.26), channel_id=1, source_target_pairs={{0,1},{1,0},{2,3},{3,2},{4,5},{5,4},{6,7},{7,6},{8,9},{9,8},{10,11... | collective-permute-start | bytes 393224 | tf_op jit(solution)/shard_map/ppermute | solution.py:226
  20.0 6.2 %collective-permute-start.7 = (bf16[32,512]{1,0:T(8,128)(2,1)S(1)}, bf16[32,512]{1,0:T(8,128)(2,1)S(1)}, u32[]{:S(2)}, u32[]{:S(2)}) collective-permute-start(bf16[32,512]{1,0:T(8,128)(2,1)S(1)} %get-tuple-element.27), channel_id=1, source_target_pairs={{0,12},{1,13},{2,14},{3,15},{4,8},{5,9},{6,10},{7,11},{8,4},{9,5},... | collective-permute-start | bytes 98312 | tf_op jit(solution)/shard_map/ppermute | solution.py:232
  22.0 5.2 %collective-permute-start.9 = (bf16[32,512]{1,0:T(8,128)(2,1)S(1)}, bf16[32,512]{1,0:T(8,128)(2,1)S(1)}, u32[]{:S(2)}, u32[]{:S(2)}) collective-permute-start(bf16[32,512]{1,0:T(8,128)(2,1)S(1)} %get-tuple-element.28), channel_id=1, source_target_pairs={{0,9},{1,8},{2,11},{3,10},{4,13},{5,12},{6,15},{7,14},{8,1},{9,0},... | collective-permute-start | bytes 98312 | tf_op jit(solution)/shard_map/ppermute | solution.py:232
  22.0 5.2 %collective-permute-start.8 = (bf16[32,512]{1,0:T(8,128)(2,1)S(1)}, bf16[32,512]{1,0:T(8,128)(2,1)S(1)}, u32[]{:S(2)}, u32[]{:S(2)}) collective-permute-start(bf16[32,512]{1,0:T(8,128)(2,1)S(1)} %get-tuple-element.29), channel_id=1, source_target_pairs={{0,5},{1,4},{2,7},{3,6},{4,1},{5,0},{6,3},{7,2},{8,13},{9,12},{10,... | collective-permute-start | bytes 98312 | tf_op jit(solution)/shard_map/ppermute | solution.py:232
  27.2 3.5 %collective-permute-start.10 = (bf16[32,512]{1,0:T(8,128)(2,1)S(1)}, bf16[32,512]{1,0:T(8,128)(2,1)S(1)}, u32[]{:S(2)}, u32[]{:S(2)}) collective-permute-start(bf16[32,512]{1,0:T(8,128)(2,1)S(1)} %fusion.1), channel_id=1, source_target_pairs={{0,3},{1,2},{2,1},{3,0},{4,7},{5,6},{6,5},{7,4},{8,11},{9,10},{10,... | collective-permute-start | bytes 98312 | tf_op jit(solution)/shard_map/ppermute | solution.py:226
  30.7 1.3 %collective-permute-start.11 = (bf16[32,512]{1,0:T(8,128)(2,1)S(1)}, bf16[32,512]{1,0:T(8,128)(2,1)S(1)}, u32[]{:S(2)}, u32[]{:S(2)}) collective-permute-start(bf16[32,512]{1,0:T(8,128)(2,1)S(1)} %add_convert_fusion.1.own_ref), channel_id=1, source_target_pairs={{0,1},{1,0},{2,3},{3,2},{4,5},{5,4},{6,7},{7,6},{8,9},{9,8},{10,11... | collective-permute-start | bytes 98312 | tf_op jit(solution)/shard_map/ppermute | solution.py:226

commit v16 on v15

--- a/solution.py
+++ b/solution.py
@@ -136,12 +136,13 @@
     message_ref[half // LANES * rows :, :] = terms_ref[...]
 
 
-def unfold_kernel(*refs):
+def unfold_kernel(spots, *refs):
     *messages, latent_ref, terms_ref = refs
     rows = latent_ref.shape[0] // len(messages)
     tiles = terms_ref.shape[0] // len(messages)
     parts = latent_ref.shape[1] // LANES
-    for b, message in enumerate(messages):
+    for s, message in enumerate(messages):
+        b = spots.index(s)
         for c in range(parts):
             columns = message[c * rows : (c + 1) * rows, :]
             latent_ref[b * rows : (b + 1) * rows, c * LANES : (c + 1) * LANES] = columns
@@ -157,7 +158,7 @@
         pre_ref[:, k * units : (k + 1) * units] = dot(rows, weight, NT)
 
 
-def second_kernel(terms_ref, other_ref, pre_ref, up_ref, down_ref, hidden_ref, theirs_ref):
+def second_kernel(late, terms_ref, other_ref, pre_ref, up_ref, down_ref, hidden_ref, theirs_ref):
     local_count, units, latent_len = up_ref.shape
     half = latent_len // 2
     blocks = lax.axis_size("exp")
@@ -166,28 +167,34 @@
     tiles = terms_ref.shape[0] // blocks // TILE
     first = lax.axis_index("exp") * local_count
     lane = lax.broadcasted_iota(jnp.int32, (TILE, LANES), 1)
-    rows = other_ref[...]
+    side = other_ref.shape[0] // 2
+    mine = slice(side, 2 * side) if late else slice(0, side)
+    rows = other_ref[mine, :]
     for k in range(local_count):
         weight = []
-        for b in range(blocks):
+        for b in range(blocks // 2):
             for g in range(groups):
                 tile, at = group_at(g, experts_all)
-                tile = (b * tiles + tile) * TILE
+                tile = ((b + late * (blocks // 2)) * tiles + tile) * TILE
                 terms = terms_ref[tile : tile + TILE, :].astype(F32)
                 named = (lane == at + first + k) | (lane == at + first + k + experts_all)
                 weight.append(jnp.sum(jnp.where(named, terms, 0.0), axis=1, keepdims=True))
         weight = jnp.concatenate(weight, axis=0)
         at = slice(k * units, (k + 1) * units)
-        pre_act = pre_ref[:, at] + dot(rows, up_ref[k, :, pl.ds(half_at(False, half), half)], NT)
-        active = jnp.maximum(pre_act, 0.0)
+        product = dot(rows, up_ref[k, :, pl.ds(half_at(False, half), half)], NT)
+        active = jnp.maximum(pre_ref[mine, at] + product, 0.0)
         hidden_ref[:, at] = (active * active * weight).astype(BF16)
     theirs = dot(hidden_ref[...], down_ref[:, pl.ds(half_at(False, half), half)], NN)
     theirs_ref[...] = theirs.astype(BF16)
 
 
-def third_kernel(hidden_ref, down_ref, mine_ref):
-    half = mine_ref.shape[1]
-    mine_ref[...] = dot(hidden_ref[...], down_ref[:, pl.ds(half_at(True, half), half)], NN)
+def third_kernel(late_ref, early_ref, down_ref, late_out_ref, early_out_ref):
+    half = early_out_ref.shape[1]
+    side = early_out_ref.shape[0]
+    rows = jnp.concatenate([early_ref[...], late_ref[...]], axis=0)
+    result = dot(rows, down_ref[:, pl.ds(half_at(True, half), half)], NN)
+    early_out_ref[...] = result[:side, :]
+    late_out_ref[...] = result[side:, :]
 
 
 def up_own_kernel(own_ref, weight_ref, out_ref):
@@ -219,6 +226,7 @@
     out_len = lat_up.shape[1]
     experts_all = local_count * exp_count
     parts = half // LANES
+    spots = (0, exp_count - 1, *range(1, exp_count - 1))
     terms_rows = -(-rows // TILE // (LANES // (2 * experts_all))) * TILE
     pair_masks = [(1 << b) + 1 for b in range(1, tp_count.bit_length() - 1)]
 
@@ -296,7 +304,7 @@
     messages[-1], down_here = lax.optimization_barrier((messages[-1], down_here))
     down_here = vmem(down_here)
     latent, terms = kernel_call(
-        unfold_kernel,
+        lambda *refs: unfold_kernel(spots, *refs),
         (shaped(BF16, all_rows, half), shaped(BF16, exp_count * terms_rows, LANES)),
         messages,
         (),
@@ -314,29 +322,39 @@
         all_rows * latent_len * all_units,
         latent_len * all_units,
     )
-    hidden, theirs = kernel_call(
-        second_kernel,
-        (shaped(BF16, all_rows, all_units), shaped(BF16, all_rows, half)),
-        (terms, other, pre, up_here, down_here),
-        (),
-        [],
-        2 * all_rows * latent_len * all_units,
-        2 * latent_len * all_units,
-    )
-    mine = kernel_call(
+    side_rows = all_rows // 2
+
+    def experts(late):
+        return kernel_call(
+            lambda *refs: second_kernel(late, *refs),
+            (shaped(BF16, side_rows, all_units), shaped(BF16, side_rows, half)),
+            (terms, other, pre, up_here, down_here),
+            (),
+            [],
+            2 * side_rows * latent_len * all_units,
+            2 * latent_len * all_units,
+        )
+
+    early_hidden, early_theirs = experts(False)
+    late_hidden, late_theirs = experts(True)
+    late_mine, early_mine = kernel_call(
         third_kernel,
-        shaped(F32, all_rows, half),
-        (hidden, down_here),
+        (shaped(F32, side_rows, half), shaped(F32, side_rows, half)),
+        (late_hidden, early_hidden, down_here),
         (),
         [],
         all_rows * latent_len * all_units,
         latent_len * all_units,
     )
-    part = (mine + over_tp(theirs, 1).astype(F32)).astype(BF16)
-    blocks = part.reshape(exp_count, rows, half)
+    early_part = (early_mine + over_tp(early_theirs, 1).astype(F32)).astype(BF16)
+    late_part = (late_mine + over_tp(late_theirs, 1).astype(F32)).astype(BF16)
+    blocks = (
+        *early_part.reshape(exp_count // 2, rows, half),
+        *late_part.reshape(exp_count // 2, rows, half),
+    )
     mixed = blocks[0].astype(F32)
-    for s in (exp_count - 1, *range(1, exp_count - 1)):
-        mixed = mixed + over_exp(blocks[s], s).astype(F32)
+    for s in range(exp_count - 1, 0, -1):
+        mixed = mixed + over_exp(blocks[spots.index(s)], s).astype(F32)
     mixed = across(mixed).astype(BF16)
     lat_up = vmem(lat_up)
     own_part = kernel_call(

time: 33.1 us -> 33.5 us (1.012)
  waiting for transfers between devices: 10.3 us -> 9.43 us
  Pallas kernels: 8.91 us -> 9.65 us
  starting transfers between devices: 13.4 us -> 13.9 us
    ppermute x6 -> x7, waiting for transfers between devices: 4.87 us -> 4.07 us  [over_tp(): return lax.ppermute(x, 'tp', [(t, t ^ mask) for t in range(tp_count)])]
    pallas_call x11 -> x12, Pallas kernels: 8.91 us -> 9.65 us  [kernel_call(): pl.pallas_call(body, out_shape=out_shape, in_specs=[spec(pltpu.HBM if i i...]
    ppermute x6 -> x7, starting transfers between devices: 5.01 us -> 5.44 us  [over_tp(): return lax.ppermute(x, 'tp', [(t, t ^ mask) for t in range(tp_count)])]
  transfers between devices with their start and end apart: 12 -> 13, of which waited for: 8 -> 7; matrix products, arithmetic and copies ran while one was open for 0% -> 0% of each run, Pallas kernels for 16% -> 18%
where the time goes in v16:
time: 33.5 us; the launch traced here: 33.3 us
  starting transfers between devices  13.9 us (41%)
  Pallas kernels  9.65 us (29%)
  waiting for transfers between devices  9.43 us (28%)
    pallas_call x12, Pallas kernels, kernel_call(): pl.pallas_call(body, out_shape=out_shape, in_specs=[spec(pltpu.HBM if i i...  9.65 us
    ppermute x6, starting transfers between devices, over_exp(): return lax.ppermute(x, ('exp', 'tp'), hops)  8.49 us
    ppermute x7, starting transfers between devices, over_tp(): return lax.ppermute(x, 'tp', [(t, t ^ mask) for t in range(tp_count)])  5.44 us
    ppermute x6, waiting for transfers between devices, over_exp(): return lax.ppermute(x, ('exp', 'tp'), hops)  5.36 us
    ppermute x7, waiting for transfers between devices, over_tp(): return lax.ppermute(x, 'tp', [(t, t ^ mask) for t in range(tp_count)])  4.07 us
  transfers between devices with their start and end apart: 13, of which 7 were waited for; matrix products, arithmetic and copies ran while one was open for 0% of the time, Pallas kernels for 18%

profile of v16, /device:TPU:0, one launch (start us, length us, event | category | flops | bytes accessed | tf_op | source)
XLA Modules:
  0.0 33.3 jit_solution(5198593209033667676)
XLA Ops:
  0.0 1.7 %shard_map.73 = (bf16[32,512]{1,0:T(8,128)(2,1)S(1)}, bf16[32,1024]{1,0:T(8,128)(2,1)S(1)}, bf16[512,1024]{1,0:T(8,128)(2,1)S(1)}) custom-call(bf16[32,1024]{1,0:T(8,128)(2,1)} %tokens_hbm.1, bf16[1024,1024]{1,0:T(8,128)(2,1)} %weight_hbm.1), custom_call_target="tpu_custom_call" | custom-call | flops 33554432 | bytes 2097152 | tf_op jit(solution)/shard_map/pallas_call | solution.py:33
  1.7 0.5 %collective-permute-start = (bf16[32,512]{1,0:T(8,128)(2,1)S(1)}, bf16[32,512]{1,0:T(8,128)(2,1)S(1)}, u32[]{:S(2)}, u32[]{:S(2)}) collective-permute-start(bf16[32,512]{1,0:T(8,128)(2,1)S(1)} %get-tuple-element.22), channel_id=1, source_target_pairs={{0,1},{1,0},{2,3},{3,2},{4,5},{5,4},{6,7},{7,6},{8,9},{9,8},{10,11... | collective-permute-start | bytes 98312 | tf_op jit(solution)/shard_map/ppermute | solution.py:234
  2.2 0.4 %shard_map.74 = f32[32,512]{1,0:T(8,128)S(1)} custom-call(bf16[32,1024]{1,0:T(8,128)(2,1)S(1)} %get-tuple-element.20.tokens_ref, bf16[512,1024]{1,0:T(8,128)(2,1)S(1)} %get-tuple-element.21.weight_ref), custom_call_target="tpu_custom_call" | custom-call | flops 33554432 | bytes 1048576 | tf_op jit(solution)/shard_map/pallas_call | solution.py:33
  2.6 0.5 %collective-permute-done = bf16[32,512]{1,0:T(8,128)(2,1)S(1)} collective-permute-done((bf16[32,512]{1,0:T(8,128)(2,1)S(1)}, bf16[32,512]{1,0:T(8,128)(2,1)S(1)}, u32[]{:S(2)}, u32[]{:S(2)}) %collective-permute-start) | collective-permute-done | bytes 32800 | tf_op jit(solution)/shard_map/ppermute | solution.py:234
  3.1 2.7 %collective-permute-start.1 = (bf16[32,512]{1,0:T(8,128)(2,1)S(1)}, bf16[32,512]{1,0:T(8,128)(2,1)S(1)}, u32[]{:S(2)}, u32[]{:S(2)}) collective-permute-start(bf16[32,512]{1,0:T(8,128)(2,1)S(1)} %fusion.refs_0_), channel_id=1, source_target_pairs={{0,3},{1,2},{2,1},{3,0},{4,7},{5,6},{6,5},{7,4},{8,11},{9,10},{10,... | collective-permute-start | bytes 98312 | tf_op jit(solution)/shard_map/ppermute | solution.py:234
  5.8 1.8 %shard_map.75 = (bf16[16,128]{1,0:T(8,128)(2,1)S(1)}, bf16[2,672,1024]{2,1,0:T(8,128)(2,1)S(1)}) custom-call(bf16[32,512]{1,0:T(8,128)(2,1)S(1)} %fusion.refs_0_, s32[4,32]{1,0:T(4,128)} %bitcast.4, f32[4,32]{1,0:T(4,128)} %bitcast.5, bf16[2,672,1024]{2,1,0:T(8,128)(2,1)} %refs_3_.1), custom_call_target="tpu_custom_call" | custom-call | bytes 2752512 | tf_op jit(solution)/shard_map/pallas_call | solution.py:33
  7.6 0.0 collective-permute-done.1
  7.7 3.9 %collective-permute-start.4 = (bf16[144,128]{1,0:T(8,128)(2,1)S(1)}, bf16[144,128]{1,0:T(8,128)(2,1)S(1)}, u32[]{:S(2)}, u32[]{:S(2)}) collective-permute-start(bf16[144,128]{1,0:T(8,128)(2,1)S(1)} %shard_map.76.after_ref.refs_0_), channel_id=1, source_target_pairs={{0,12},{1,13},{2,14},{3,15},{4,8},{5,9},{6,10},{7,11},{8,4},{9,5},... | collective-permute-start | bytes 110600 | tf_op jit(solution)/shard_map/ppermute | solution.py:240
  11.6 0.0 collective-permute-start.3
  11.6 0.4 %collective-permute-start.2 = (bf16[144,128]{1,0:T(8,128)(2,1)S(1)}, bf16[144,128]{1,0:T(8,128)(2,1)S(1)}, u32[]{:S(2)}, u32[]{:S(2)}) collective-permute-start(bf16[144,128]{1,0:T(8,128)(2,1)S(1)} %shard_map.76.after_ref.refs_0_), channel_id=1, source_target_pairs={{0,5},{1,4},{2,7},{3,6},{4,1},{5,0},{6,3},{7,2},{8,13},{9,12},{10,... | collective-permute-start | bytes 110600 | tf_op jit(solution)/shard_map/ppermute | solution.py:240
  11.9 1.8 %shard_map.77.refs_4_.down_ref = bf16[1344,1024]{1,0:T(8,128)(2,1)S(1)} custom-call(bf16[144,128]{1,0:T(8,128)(2,1)S(1)} %shard_map.76.after_ref.refs_0_, bf16[1344,1024]{1,0:T(8,128)(2,1)} %bitcast.3), custom_call_target="tpu_custom_call" | custom-call | bytes 2752512 | tf_op jit(solution)/shard_map/pallas_call | solution.py:33
  13.7 2.4 %collective-permute-done.3.refs_2_ = bf16[144,128]{1,0:T(8,128)(2,1)S(1)} collective-permute-done((bf16[144,128]{1,0:T(8,128)(2,1)S(1)}, bf16[144,128]{1,0:T(8,128)(2,1)S(1)}, u32[]{:S(2)}, u32[]{:S(2)}) %collective-permute-start.3) | collective-permute-done | bytes 36896 | tf_op jit(solution)/shard_map/ppermute | solution.py:240
  16.2 0.2 collective-permute-start.5
  16.4 0.6 %shard_map.79.refs_2_ = f32[128,1344]{1,0:T(8,128)S(1)} custom-call(bf16[128,512]{1,0:T(8,128)(2,1)S(1)} %get-tuple-element.26.own_ref, bf16[2,672,1024]{2,1,0:T(8,128)(2,1)S(1)} %get-tuple-element.27.up_ref.refs_3_), custom_call_target="tpu_custom_call" | custom-call | flops 176160768 | bytes 1376256 | tf_op jit(solution)/shard_map/pallas_call | solution.py:33
  17.0 0.6 %collective-permute-done.5.refs_1_ = bf16[128,512]{1,0:T(8,128)(2,1)S(1)} collective-permute-done((bf16[128,512]{1,0:T(8,128)(2,1)S(1)}, bf16[128,512]{1,0:T(8,128)(2,1)S(1)}, u32[]{:S(2)}, u32[]{:S(2)}) %collective-permute-start.5) | collective-permute-done | bytes 131104 | tf_op jit(solution)/shard_map/ppermute | solution.py:234
  17.6 0.8 %shard_map.81 = (bf16[64,1344]{1,0:T(8,128)(2,1)S(1)}, bf16[64,512]{1,0:T(8,128)(2,1)S(1)}) custom-call(bf16[64,128]{1,0:T(8,128)(2,1)S(1)} %get-tuple-element.25.refs_0_, bf16[128,512]{1,0:T(8,128)(2,1)S(1)} %collective-permute-done.5.refs_1_, f32[128,1344]{1,0:T(8,128)S(1)} %shard_map.79.refs_2_, ...), custom_call_target="tpu_custom_call" | custom-call | flops 176160768 | bytes 2752512 | tf_op jit(solution)/shard_map/pallas_call | solution.py:33
  18.5 0.2 collective-permute-start.6
  18.7 0.8 %shard_map.80 = (bf16[64,1344]{1,0:T(8,128)(2,1)S(1)}, bf16[64,512]{1,0:T(8,128)(2,1)S(1)}) custom-call(bf16[64,128]{1,0:T(8,128)(2,1)S(1)} %get-tuple-element.25.refs_0_, bf16[128,512]{1,0:T(8,128)(2,1)S(1)} %collective-permute-done.5.refs_1_, f32[128,1344]{1,0:T(8,128)S(1)} %shard_map.79.refs_2_, ...), custom_call_target="tpu_custom_call" | custom-call | flops 176160768 | bytes 2752512 | tf_op jit(solution)/shard_map/pallas_call | solution.py:33
  19.5 0.0 copy-start
  19.5 0.4 %collective-permute-start.8 = (bf16[64,512]{1,0:T(8,128)(2,1)S(1)}, bf16[64,512]{1,0:T(8,128)(2,1)S(1)}, u32[]{:S(2)}, u32[]{:S(2)}) collective-permute-start(bf16[64,512]{1,0:T(8,128)(2,1)S(1)} %get-tuple-element.34), channel_id=1, source_target_pairs={{0,1},{1,0},{2,3},{3,2},{4,5},{5,4},{6,7},{7,6},{8,9},{9,8},{10,11... | collective-permute-start | bytes 196616 | tf_op jit(solution)/shard_map/ppermute | solution.py:234
  19.9 0.4 %shard_map.82 = (f32[64,512]{1,0:T(8,128)S(1)}, f32[64,512]{1,0:T(8,128)S(1)}) custom-call(bf16[64,1344]{1,0:T(8,128)(2,1)S(1)} %get-tuple-element.29.late_ref, bf16[64,1344]{1,0:T(8,128)(2,1)S(1)} %get-tuple-element.30.early_ref, bf16[1344,1024]{1,0:T(8,128)(2,1)S(1)} %shard_map.77.refs_4_.down_ref), custom_call_target="tpu_custom_call" | custom-call | flops 176160768 | bytes 1376256 | tf_op jit(solution)/shard_map/pallas_call | solution.py:33
  20.4 2.0 %collective-permute-start.7 = (bf16[32,512]{1,0:T(8,128)(2,1)S(1)}, bf16[32,512]{1,0:T(8,128)(2,1)S(1)}, u32[]{:S(2)}, u32[]{:S(2)}) collective-permute-start(bf16[32,512]{1,0:T(8,128)(2,1)S(1)} %unstack.21), channel_id=1, source_target_pairs={{0,12},{1,13},{2,14},{3,15},{4,8},{5,9},{6,10},{7,11},{8,4},{9,5},... | collective-permute-start | bytes 98312 | tf_op jit(solution)/shard_map/ppermute | solution.py:240
  22.4 0.1 collective-permute-start.9
  22.5 2.1 %collective-permute-start.10 = (bf16[32,512]{1,0:T(8,128)(2,1)S(1)}, bf16[32,512]{1,0:T(8,128)(2,1)S(1)}, u32[]{:S(2)}, u32[]{:S(2)}) collective-permute-start(bf16[32,512]{1,0:T(8,128)(2,1)S(1)} %get-tuple-element.36), channel_id=1, source_target_pairs={{0,5},{1,4},{2,7},{3,6},{4,1},{5,0},{6,3},{7,2},{8,13},{9,12},{10,... | collective-permute-start | bytes 98312 | tf_op jit(solution)/shard_map/ppermute | solution.py:240
  24.7 1.8 %collective-permute-done.7 = bf16[32,512]{1,0:T(8,128)(2,1)S(1)} collective-permute-done((bf16[32,512]{1,0:T(8,128)(2,1)S(1)}, bf16[32,512]{1,0:T(8,128)(2,1)S(1)}, u32[]{:S(2)}, u32[]{:S(2)}) %collective-permute-start.7) | collective-permute-done | bytes 32800 | tf_op jit(solution)/shard_map/ppermute | solution.py:240
  26.4 1.1 %collective-permute-done.9 = bf16[32,512]{1,0:T(8,128)(2,1)S(1)} collective-permute-done((bf16[32,512]{1,0:T(8,128)(2,1)S(1)}, bf16[32,512]{1,0:T(8,128)(2,1)S(1)}, u32[]{:S(2)}, u32[]{:S(2)}) %collective-permute-start.9) | collective-permute-done | bytes 32800 | tf_op jit(solution)/shard_map/ppermute | solution.py:240
  27.6 1.3 %collective-permute-start.11 = (bf16[32,512]{1,0:T(8,128)(2,1)S(1)}, bf16[32,512]{1,0:T(8,128)(2,1)S(1)}, u32[]{:S(2)}, u32[]{:S(2)}) collective-permute-start(bf16[32,512]{1,0:T(8,128)(2,1)S(1)} %fusion.1), channel_id=1, source_target_pairs={{0,3},{1,2},{2,1},{3,0},{4,7},{5,6},{6,5},{7,4},{8,11},{9,10},{10,... | collective-permute-start | bytes 98312 | tf_op jit(solution)/shard_map/ppermute | solution.py:234
  28.9 2.2 %collective-permute-done.11 = bf16[32,512]{1,0:T(8,128)(2,1)S(1)} collective-permute-done((bf16[32,512]{1,0:T(8,128)(2,1)S(1)}, bf16[32,512]{1,0:T(8,128)(2,1)S(1)}, u32[]{:S(2)}, u32[]{:S(2)}) %collective-permute-start.11) | collective-permute-done | bytes 32800 | tf_op jit(solution)/shard_map/ppermute | solution.py:234
  31.1 0.2 collective-permute-start.12
  31.3 0.3 shard_map.83.part_ref
  31.5 0.8 %collective-permute-done.12.other_ref = bf16[32,512]{1,0:T(8,128)(2,1)S(1)} collective-permute-done((bf16[32,512]{1,0:T(8,128)(2,1)S(1)}, bf16[32,512]{1,0:T(8,128)(2,1)S(1)}, u32[]{:S(2)}, u32[]{:S(2)}) %collective-permute-start.12) | collective-permute-done | bytes 32800 | tf_op jit(solution)/shard_map/ppermute | solution.py:234
  32.4 0.9 %shard_map.84 = bf16[32,1024]{1,0:T(8,128)(2,1)} custom-call(f32[32,1024]{1,0:T(8,128)S(1)} %shard_map.83.part_ref, bf16[32,512]{1,0:T(8,128)(2,1)S(1)} %collective-permute-done.12.other_ref, bf16[1024,1024]{1,0:T(8,128)(2,1)S(1)} %copy-done), custom_call_target="tpu_custom_call" | custom-call | flops 33554432 | bytes 1048576 | tf_op jit(solution)/shard_map/pallas_call | solution.py:33
  (16 shorter events, 0.2 us)
Async XLA Ops:
  1.7 1.4 %collective-permute-start = (bf16[32,512]{1,0:T(8,128)(2,1)S(1)}, bf16[32,512]{1,0:T(8,128)(2,1)S(1)}, u32[]{:S(2)}, u32[]{:S(2)}) collective-permute-start(bf16[32,512]{1,0:T(8,128)(2,1)S(1)} %get-tuple-element.22), channel_id=1, source_target_pairs={{0,1},{1,0},{2,3},{3,2},{4,5},{5,4},{6,7},{7,6},{8,9},{9,8},{10,11... | collective-permute-start | bytes 98312 | tf_op jit(solution)/shard_map/ppermute | solution.py:234
  3.1 4.5 %collective-permute-start.1 = (bf16[32,512]{1,0:T(8,128)(2,1)S(1)}, bf16[32,512]{1,0:T(8,128)(2,1)S(1)}, u32[]{:S(2)}, u32[]{:S(2)}) collective-permute-start(bf16[32,512]{1,0:T(8,128)(2,1)S(1)} %fusion.refs_0_), channel_id=1, source_target_pairs={{0,3},{1,2},{2,1},{3,0},{4,7},{5,6},{6,5},{7,4},{8,11},{9,10},{10,... | collective-permute-start | bytes 98312 | tf_op jit(solution)/shard_map/ppermute | solution.py:234
  7.7 6.1 %collective-permute-start.4 = (bf16[144,128]{1,0:T(8,128)(2,1)S(1)}, bf16[144,128]{1,0:T(8,128)(2,1)S(1)}, u32[]{:S(2)}, u32[]{:S(2)}) collective-permute-start(bf16[144,128]{1,0:T(8,128)(2,1)S(1)} %shard_map.76.after_ref.refs_0_), channel_id=1, source_target_pairs={{0,12},{1,13},{2,14},{3,15},{4,8},{5,9},{6,10},{7,11},{8,4},{9,5},... | collective-permute-start | bytes 110600 | tf_op jit(solution)/shard_map/ppermute | solution.py:240
  11.6 4.6 %collective-permute-start.3 = (bf16[144,128]{1,0:T(8,128)(2,1)S(1)}, bf16[144,128]{1,0:T(8,128)(2,1)S(1)}, u32[]{:S(2)}, u32[]{:S(2)}) collective-permute-start(bf16[144,128]{1,0:T(8,128)(2,1)S(1)} %shard_map.76.after_ref.refs_0_), channel_id=1, source_target_pairs={{0,9},{1,8},{2,11},{3,10},{4,13},{5,12},{6,15},{7,14},{8,1},{9,0},... | collective-permute-start | bytes 110600 | tf_op jit(solution)/shard_map/ppermute | solution.py:240
  11.6 4.6 %collective-permute-start.2 = (bf16[144,128]{1,0:T(8,128)(2,1)S(1)}, bf16[144,128]{1,0:T(8,128)(2,1)S(1)}, u32[]{:S(2)}, u32[]{:S(2)}) collective-permute-start(bf16[144,128]{1,0:T(8,128)(2,1)S(1)} %shard_map.76.after_ref.refs_0_), channel_id=1, source_target_pairs={{0,5},{1,4},{2,7},{3,6},{4,1},{5,0},{6,3},{7,2},{8,13},{9,12},{10,... | collective-permute-start | bytes 110600 | tf_op jit(solution)/shard_map/ppermute | solution.py:240
  16.2 1.4 %collective-permute-start.5 = (bf16[128,512]{1,0:T(8,128)(2,1)S(1)}, bf16[128,512]{1,0:T(8,128)(2,1)S(1)}, u32[]{:S(2)}, u32[]{:S(2)}) collective-permute-start(bf16[128,512]{1,0:T(8,128)(2,1)S(1)} %get-tuple-element.26.own_ref), channel_id=1, source_target_pairs={{0,1},{1,0},{2,3},{3,2},{4,5},{5,4},{6,7},{7,6},{8,9},{9,8},{10,11... | collective-permute-start | bytes 393224 | tf_op jit(solution)/shard_map/ppermute | solution.py:234
  18.5 1.9 %collective-permute-start.6 = (bf16[64,512]{1,0:T(8,128)(2,1)S(1)}, bf16[64,512]{1,0:T(8,128)(2,1)S(1)}, u32[]{:S(2)}, u32[]{:S(2)}) collective-permute-start(bf16[64,512]{1,0:T(8,128)(2,1)S(1)} %get-tuple-element.32), channel_id=1, source_target_pairs={{0,1},{1,0},{2,3},{3,2},{4,5},{5,4},{6,7},{7,6},{8,9},{9,8},{10,11... | collective-permute-start | bytes 196616 | tf_op jit(solution)/shard_map/ppermute | solution.py:234
  19.5 11.8 %copy-start = (bf16[1024,1024]{1,0:T(8,128)(2,1)S(1)}, bf16[1024,1024]{1,0:T(8,128)(2,1)}, u32[]{:S(2)}) copy-start(bf16[1024,1024]{1,0:T(8,128)(2,1)} %weight_ref.3) | copy-start | bytes 6291460
  19.5 2.9 %collective-permute-start.8 = (bf16[64,512]{1,0:T(8,128)(2,1)S(1)}, bf16[64,512]{1,0:T(8,128)(2,1)S(1)}, u32[]{:S(2)}, u32[]{:S(2)}) collective-permute-start(bf16[64,512]{1,0:T(8,128)(2,1)S(1)} %get-tuple-element.34), channel_id=1, source_target_pairs={{0,1},{1,0},{2,3},{3,2},{4,5},{5,4},{6,7},{7,6},{8,9},{9,8},{10,11... | collective-permute-start | bytes 196616 | tf_op jit(solution)/shard_map/ppermute | solution.py:234
  20.4 6.0 %collective-permute-start.7 = (bf16[32,512]{1,0:T(8,128)(2,1)S(1)}, bf16[32,512]{1,0:T(8,128)(2,1)S(1)}, u32[]{:S(2)}, u32[]{:S(2)}) collective-permute-start(bf16[32,512]{1,0:T(8,128)(2,1)S(1)} %unstack.21), channel_id=1, source_target_pairs={{0,12},{1,13},{2,14},{3,15},{4,8},{5,9},{6,10},{7,11},{8,4},{9,5},... | collective-permute-start | bytes 98312 | tf_op jit(solution)/shard_map/ppermute | solution.py:240
  22.4 5.1 %collective-permute-start.9 = (bf16[32,512]{1,0:T(8,128)(2,1)S(1)}, bf16[32,512]{1,0:T(8,128)(2,1)S(1)}, u32[]{:S(2)}, u32[]{:S(2)}) collective-permute-start(bf16[32,512]{1,0:T(8,128)(2,1)S(1)} %get-tuple-element.35), channel_id=1, source_target_pairs={{0,9},{1,8},{2,11},{3,10},{4,13},{5,12},{6,15},{7,14},{8,1},{9,0},... | collective-permute-start | bytes 98312 | tf_op jit(solution)/shard_map/ppermute | solution.py:240
  22.5 5.1 %collective-permute-start.10 = (bf16[32,512]{1,0:T(8,128)(2,1)S(1)}, bf16[32,512]{1,0:T(8,128)(2,1)S(1)}, u32[]{:S(2)}, u32[]{:S(2)}) collective-permute-start(bf16[32,512]{1,0:T(8,128)(2,1)S(1)} %get-tuple-element.36), channel_id=1, source_target_pairs={{0,5},{1,4},{2,7},{3,6},{4,1},{5,0},{6,3},{7,2},{8,13},{9,12},{10,... | collective-permute-start | bytes 98312 | tf_op jit(solution)/shard_map/ppermute | solution.py:240
  27.6 3.5 %collective-permute-start.11 = (bf16[32,512]{1,0:T(8,128)(2,1)S(1)}, bf16[32,512]{1,0:T(8,128)(2,1)S(1)}, u32[]{:S(2)}, u32[]{:S(2)}) collective-permute-start(bf16[32,512]{1,0:T(8,128)(2,1)S(1)} %fusion.1), channel_id=1, source_target_pairs={{0,3},{1,2},{2,1},{3,0},{4,7},{5,6},{6,5},{7,4},{8,11},{9,10},{10,... | collective-permute-start | bytes 98312 | tf_op jit(solution)/shard_map/ppermute | solution.py:234
  31.1 1.3 %collective-permute-start.12 = (bf16[32,512]{1,0:T(8,128)(2,1)S(1)}, bf16[32,512]{1,0:T(8,128)(2,1)S(1)}, u32[]{:S(2)}, u32[]{:S(2)}) collective-permute-start(bf16[32,512]{1,0:T(8,128)(2,1)S(1)} %add_convert_fusion.2.own_ref), channel_id=1, source_target_pairs={{0,1},{1,0},{2,3},{3,2},{4,5},{5,4},{6,7},{7,6},{8,9},{9,8},{10,11... | collective-permute-start | bytes 98312 | tf_op jit(solution)/shard_map/ppermute | solution.py:234

commit v17 on v15

--- a/solution.py
+++ b/solution.py
@@ -46,10 +46,9 @@
 
 
 def half_at(own, half):
-    bits = 0
-    for axis in ("exp", "tp"):
-        for b in range(lax.axis_size(axis).bit_length() - 1):
-            bits = bits + lax.axis_index(axis) // (1 << b)
+    bits = lax.axis_index("exp")
+    for b in range(lax.axis_size("tp").bit_length() - 1):
+        bits = bits + lax.axis_index("tp") // (1 << b)
     odd = bits % 2
     return pl.multiple_of((odd if own else 1 - odd) * half, half)
 
@@ -226,7 +225,7 @@
         return lax.ppermute(x, "tp", [(t, t ^ mask) for t in range(tp_count)])
 
     def over_exp(x, mask):
-        turn = mask.bit_count() % 2
+        turn = mask % 2
         places = [(e, t) for e in range(exp_count) for t in range(tp_count)]
         hops = [(e * tp_count + t, (e ^ mask) * tp_count + (t ^ turn)) for e, t in places]
         return lax.ppermute(x, ("exp", "tp"), hops)

time: 33.1 us -> 33 us (level)
  starting transfers between devices: 13.4 us -> 12.8 us
  waiting for transfers between devices: 10.3 us -> 10.8 us
    ppermute x6, starting transfers between devices: 8.43 us -> 7.92 us  [over_exp(): return lax.ppermute(x, ('exp', 'tp'), hops)]
where the time goes in v17:
time: 33 us; the launch traced here: 32.8 us
  starting transfers between devices  12.8 us (39%)
  waiting for transfers between devices  10.8 us (33%)
  Pallas kernels  8.92 us (27%)
    pallas_call x11, Pallas kernels, kernel_call(): pl.pallas_call(body, out_shape=out_shape, in_specs=[spec(pltpu.HBM if i i...  8.92 us
    ppermute x6, starting transfers between devices, over_exp(): return lax.ppermute(x, ('exp', 'tp'), hops)  7.92 us
    ppermute x6, waiting for transfers between devices, over_exp(): return lax.ppermute(x, ('exp', 'tp'), hops)  5.76 us
    ppermute x6, waiting for transfers between devices, over_tp(): return lax.ppermute(x, 'tp', [(t, t ^ mask) for t in range(tp_count)])  5.06 us
    ppermute x6, starting transfers between devices, over_tp(): return lax.ppermute(x, 'tp', [(t, t ^ mask) for t in range(tp_count)])  4.86 us
  transfers between devices with their start and end apart: 12, of which 8 were waited for; matrix products, arithmetic and copies ran while one was open for 0% of the time, Pallas kernels for 16%

profile of v17, /device:TPU:0, one launch (start us, length us, event | category | flops | bytes accessed | tf_op | source)
XLA Modules:
  0.0 32.8 jit_solution(13172529910561203605)
XLA Ops:
  0.0 1.7 %shard_map.73 = (bf16[32,512]{1,0:T(8,128)(2,1)S(1)}, bf16[32,1024]{1,0:T(8,128)(2,1)S(1)}, bf16[512,1024]{1,0:T(8,128)(2,1)S(1)}) custom-call(bf16[32,1024]{1,0:T(8,128)(2,1)} %tokens_hbm.1, bf16[1024,1024]{1,0:T(8,128)(2,1)} %weight_hbm.1), custom_call_target="tpu_custom_call" | custom-call | flops 33554432 | bytes 2097152 | tf_op jit(solution)/shard_map/pallas_call | solution.py:33
  1.7 0.5 %collective-permute-start = (bf16[32,512]{1,0:T(8,128)(2,1)S(1)}, bf16[32,512]{1,0:T(8,128)(2,1)S(1)}, u32[]{:S(2)}, u32[]{:S(2)}) collective-permute-start(bf16[32,512]{1,0:T(8,128)(2,1)S(1)} %get-tuple-element.18), channel_id=1, source_target_pairs={{0,1},{1,0},{2,3},{3,2},{4,5},{5,4},{6,7},{7,6},{8,9},{9,8},{10,11... | collective-permute-start | bytes 98312 | tf_op jit(solution)/shard_map/ppermute | solution.py:225
  2.2 0.4 %shard_map.74 = f32[32,512]{1,0:T(8,128)S(1)} custom-call(bf16[32,1024]{1,0:T(8,128)(2,1)S(1)} %get-tuple-element.16.tokens_ref, bf16[512,1024]{1,0:T(8,128)(2,1)S(1)} %get-tuple-element.17.weight_ref), custom_call_target="tpu_custom_call" | custom-call | flops 33554432 | bytes 1048576 | tf_op jit(solution)/shard_map/pallas_call | solution.py:33
  2.6 0.5 %collective-permute-done = bf16[32,512]{1,0:T(8,128)(2,1)S(1)} collective-permute-done((bf16[32,512]{1,0:T(8,128)(2,1)S(1)}, bf16[32,512]{1,0:T(8,128)(2,1)S(1)}, u32[]{:S(2)}, u32[]{:S(2)}) %collective-permute-start) | collective-permute-done | bytes 32800 | tf_op jit(solution)/shard_map/ppermute | solution.py:225
  3.1 2.7 %collective-permute-start.1 = (bf16[32,512]{1,0:T(8,128)(2,1)S(1)}, bf16[32,512]{1,0:T(8,128)(2,1)S(1)}, u32[]{:S(2)}, u32[]{:S(2)}) collective-permute-start(bf16[32,512]{1,0:T(8,128)(2,1)S(1)} %fusion.refs_0_), channel_id=1, source_target_pairs={{0,3},{1,2},{2,1},{3,0},{4,7},{5,6},{6,5},{7,4},{8,11},{9,10},{10,... | collective-permute-start | bytes 98312 | tf_op jit(solution)/shard_map/ppermute | solution.py:225
  5.8 1.8 %shard_map.75 = (bf16[16,128]{1,0:T(8,128)(2,1)S(1)}, bf16[2,672,1024]{2,1,0:T(8,128)(2,1)S(1)}) custom-call(bf16[32,512]{1,0:T(8,128)(2,1)S(1)} %fusion.refs_0_, s32[4,32]{1,0:T(4,128)} %bitcast.4, f32[4,32]{1,0:T(4,128)} %bitcast.5, bf16[2,672,1024]{2,1,0:T(8,128)(2,1)} %refs_3_.1), custom_call_target="tpu_custom_call" | custom-call | bytes 2752512 | tf_op jit(solution)/shard_map/pallas_call | solution.py:33
  7.6 0.0 collective-permute-done.1
  7.7 3.7 %collective-permute-start.4 = (bf16[144,128]{1,0:T(8,128)(2,1)S(1)}, bf16[144,128]{1,0:T(8,128)(2,1)S(1)}, u32[]{:S(2)}, u32[]{:S(2)}) collective-permute-start(bf16[144,128]{1,0:T(8,128)(2,1)S(1)} %shard_map.76.after_ref.refs_0_), channel_id=1, source_target_pairs={{0,13},{1,12},{2,15},{3,14},{4,9},{5,8},{6,11},{7,10},{8,5},{9,4},... | collective-permute-start | bytes 110600 | tf_op jit(solution)/shard_map/ppermute | solution.py:231
  11.3 0.4 %collective-permute-start.2 = (bf16[144,128]{1,0:T(8,128)(2,1)S(1)}, bf16[144,128]{1,0:T(8,128)(2,1)S(1)}, u32[]{:S(2)}, u32[]{:S(2)}) collective-permute-start(bf16[144,128]{1,0:T(8,128)(2,1)S(1)} %shard_map.76.after_ref.refs_0_), channel_id=1, source_target_pairs={{0,5},{1,4},{2,7},{3,6},{4,1},{5,0},{6,3},{7,2},{8,13},{9,12},{10,... | collective-permute-start | bytes 110600 | tf_op jit(solution)/shard_map/ppermute | solution.py:231
  11.7 1.8 %shard_map.77.down_ref = bf16[1344,1024]{1,0:T(8,128)(2,1)S(1)} custom-call(bf16[144,128]{1,0:T(8,128)(2,1)S(1)} %shard_map.76.after_ref.refs_0_, bf16[1344,1024]{1,0:T(8,128)(2,1)} %bitcast.3), custom_call_target="tpu_custom_call" | custom-call | bytes 2752512 | tf_op jit(solution)/shard_map/pallas_call | solution.py:33
  13.5 0.0 collective-permute-done.4.refs_3_
  13.5 2.7 %collective-permute-done.3.refs_2_ = bf16[144,128]{1,0:T(8,128)(2,1)S(1)} collective-permute-done((bf16[144,128]{1,0:T(8,128)(2,1)S(1)}, bf16[144,128]{1,0:T(8,128)(2,1)S(1)}, u32[]{:S(2)}, u32[]{:S(2)}) %collective-permute-start.3) | collective-permute-done | bytes 36896 | tf_op jit(solution)/shard_map/ppermute | solution.py:231
  16.2 0.0 collective-permute-done.2.refs_1_
  16.2 0.1 collective-permute-start.5
  16.3 0.7 %shard_map.79.pre_ref = f32[128,1344]{1,0:T(8,128)S(1)} custom-call(bf16[128,512]{1,0:T(8,128)(2,1)S(1)} %get-tuple-element.22.own_ref, bf16[2,672,1024]{2,1,0:T(8,128)(2,1)S(1)} %get-tuple-element.23.up_ref), custom_call_target="tpu_custom_call" | custom-call | flops 176160768 | bytes 1376256 | tf_op jit(solution)/shard_map/pallas_call | solution.py:33
  17.0 0.7 %collective-permute-done.5.other_ref = bf16[128,512]{1,0:T(8,128)(2,1)S(1)} collective-permute-done((bf16[128,512]{1,0:T(8,128)(2,1)S(1)}, bf16[128,512]{1,0:T(8,128)(2,1)S(1)}, u32[]{:S(2)}, u32[]{:S(2)}) %collective-permute-start.5) | collective-permute-done | bytes 131104 | tf_op jit(solution)/shard_map/ppermute | solution.py:225
  17.6 0.9 %shard_map.80 = (bf16[128,1344]{1,0:T(8,128)(2,1)S(1)}, bf16[128,512]{1,0:T(8,128)(2,1)S(1)}) custom-call(bf16[64,128]{1,0:T(8,128)(2,1)S(1)} %get-tuple-element.21.terms_ref, bf16[128,512]{1,0:T(8,128)(2,1)S(1)} %collective-permute-done.5.other_ref, f32[128,1344]{1,0:T(8,128)S(1)} %shard_map.79.pre_ref, bf16[2,672,1024]{2,1,0:T(8,128)(2,1)S(1)} %get-tuple-element.23.up_ref, ...), custom_call_target="tpu_custom_call" | custom-call | flops 352321536 | bytes 2752512 | tf_op jit(solution)/shard_map/pallas_call | solution.py:33
  18.6 0.0 copy-start
  18.6 0.2 collective-permute-start.6
  18.8 0.4 %shard_map.81 = f32[128,512]{1,0:T(8,128)S(1)} custom-call(bf16[128,1344]{1,0:T(8,128)(2,1)S(1)} %get-tuple-element.25.hidden_ref, bf16[1344,1024]{1,0:T(8,128)(2,1)S(1)} %shard_map.77.down_ref), custom_call_target="tpu_custom_call" | custom-call | flops 176160768 | bytes 1376256 | tf_op jit(solution)/shard_map/pallas_call | solution.py:33
  19.2 0.8 %collective-permute-done.6 = bf16[128,512]{1,0:T(8,128)(2,1)S(1)} collective-permute-done((bf16[128,512]{1,0:T(8,128)(2,1)S(1)}, bf16[128,512]{1,0:T(8,128)(2,1)S(1)}, u32[]{:S(2)}, u32[]{:S(2)}) %collective-permute-start.6) | collective-permute-done | bytes 131104 | tf_op jit(solution)/shard_map/ppermute | solution.py:225
  20.0 1.6 %collective-permute-start.7 = (bf16[32,512]{1,0:T(8,128)(2,1)S(1)}, bf16[32,512]{1,0:T(8,128)(2,1)S(1)}, u32[]{:S(2)}, u32[]{:S(2)}) collective-permute-start(bf16[32,512]{1,0:T(8,128)(2,1)S(1)} %get-tuple-element.27), channel_id=1, source_target_pairs={{0,13},{1,12},{2,15},{3,14},{4,9},{5,8},{6,11},{7,10},{8,5},{9,4},... | collective-permute-start | bytes 98312 | tf_op jit(solution)/shard_map/ppermute | solution.py:231
  21.6 0.2 collective-permute-start.9
  21.8 2.1 %collective-permute-start.8 = (bf16[32,512]{1,0:T(8,128)(2,1)S(1)}, bf16[32,512]{1,0:T(8,128)(2,1)S(1)}, u32[]{:S(2)}, u32[]{:S(2)}) collective-permute-start(bf16[32,512]{1,0:T(8,128)(2,1)S(1)} %get-tuple-element.29), channel_id=1, source_target_pairs={{0,5},{1,4},{2,7},{3,6},{4,1},{5,0},{6,3},{7,2},{8,13},{9,12},{10,... | collective-permute-start | bytes 98312 | tf_op jit(solution)/shard_map/ppermute | solution.py:231
  23.9 1.3 %collective-permute-done.7 = bf16[32,512]{1,0:T(8,128)(2,1)S(1)} collective-permute-done((bf16[32,512]{1,0:T(8,128)(2,1)S(1)}, bf16[32,512]{1,0:T(8,128)(2,1)S(1)}, u32[]{:S(2)}, u32[]{:S(2)}) %collective-permute-start.7) | collective-permute-done | bytes 32800 | tf_op jit(solution)/shard_map/ppermute | solution.py:231
  25.3 1.7 %collective-permute-done.9 = bf16[32,512]{1,0:T(8,128)(2,1)S(1)} collective-permute-done((bf16[32,512]{1,0:T(8,128)(2,1)S(1)}, bf16[32,512]{1,0:T(8,128)(2,1)S(1)}, u32[]{:S(2)}, u32[]{:S(2)}) %collective-permute-start.9) | collective-permute-done | bytes 32800 | tf_op jit(solution)/shard_map/ppermute | solution.py:231
  27.0 1.2 %collective-permute-start.10 = (bf16[32,512]{1,0:T(8,128)(2,1)S(1)}, bf16[32,512]{1,0:T(8,128)(2,1)S(1)}, u32[]{:S(2)}, u32[]{:S(2)}) collective-permute-start(bf16[32,512]{1,0:T(8,128)(2,1)S(1)} %fusion.1), channel_id=1, source_target_pairs={{0,3},{1,2},{2,1},{3,0},{4,7},{5,6},{6,5},{7,4},{8,11},{9,10},{10,... | collective-permute-start | bytes 98312 | tf_op jit(solution)/shard_map/ppermute | solution.py:225
  28.2 2.3 %collective-permute-done.10 = bf16[32,512]{1,0:T(8,128)(2,1)S(1)} collective-permute-done((bf16[32,512]{1,0:T(8,128)(2,1)S(1)}, bf16[32,512]{1,0:T(8,128)(2,1)S(1)}, u32[]{:S(2)}, u32[]{:S(2)}) %collective-permute-start.10) | collective-permute-done | bytes 32800 | tf_op jit(solution)/shard_map/ppermute | solution.py:225
  30.6 0.2 collective-permute-start.11
  30.7 0.3 shard_map.82.part_ref
  31.0 0.8 %collective-permute-done.11.other_ref = bf16[32,512]{1,0:T(8,128)(2,1)S(1)} collective-permute-done((bf16[32,512]{1,0:T(8,128)(2,1)S(1)}, bf16[32,512]{1,0:T(8,128)(2,1)S(1)}, u32[]{:S(2)}, u32[]{:S(2)}) %collective-permute-start.11) | collective-permute-done | bytes 32800 | tf_op jit(solution)/shard_map/ppermute | solution.py:225
  31.8 0.9 %shard_map.83 = bf16[32,1024]{1,0:T(8,128)(2,1)} custom-call(f32[32,1024]{1,0:T(8,128)S(1)} %shard_map.82.part_ref, bf16[32,512]{1,0:T(8,128)(2,1)S(1)} %collective-permute-done.11.other_ref, bf16[1024,1024]{1,0:T(8,128)(2,1)S(1)} %copy-done), custom_call_target="tpu_custom_call" | custom-call | flops 33554432 | bytes 1048576 | tf_op jit(solution)/shard_map/pallas_call | solution.py:33
  (11 shorter events, 0.1 us)
Async XLA Ops:
  1.7 1.4 %collective-permute-start = (bf16[32,512]{1,0:T(8,128)(2,1)S(1)}, bf16[32,512]{1,0:T(8,128)(2,1)S(1)}, u32[]{:S(2)}, u32[]{:S(2)}) collective-permute-start(bf16[32,512]{1,0:T(8,128)(2,1)S(1)} %get-tuple-element.18), channel_id=1, source_target_pairs={{0,1},{1,0},{2,3},{3,2},{4,5},{5,4},{6,7},{7,6},{8,9},{9,8},{10,11... | collective-permute-start | bytes 98312 | tf_op jit(solution)/shard_map/ppermute | solution.py:225
  3.1 4.5 %collective-permute-start.1 = (bf16[32,512]{1,0:T(8,128)(2,1)S(1)}, bf16[32,512]{1,0:T(8,128)(2,1)S(1)}, u32[]{:S(2)}, u32[]{:S(2)}) collective-permute-start(bf16[32,512]{1,0:T(8,128)(2,1)S(1)} %fusion.refs_0_), channel_id=1, source_target_pairs={{0,3},{1,2},{2,1},{3,0},{4,7},{5,6},{6,5},{7,4},{8,11},{9,10},{10,... | collective-permute-start | bytes 98312 | tf_op jit(solution)/shard_map/ppermute | solution.py:225
  7.7 5.8 %collective-permute-start.4 = (bf16[144,128]{1,0:T(8,128)(2,1)S(1)}, bf16[144,128]{1,0:T(8,128)(2,1)S(1)}, u32[]{:S(2)}, u32[]{:S(2)}) collective-permute-start(bf16[144,128]{1,0:T(8,128)(2,1)S(1)} %shard_map.76.after_ref.refs_0_), channel_id=1, source_target_pairs={{0,13},{1,12},{2,15},{3,14},{4,9},{5,8},{6,11},{7,10},{8,5},{9,4},... | collective-permute-start | bytes 110600 | tf_op jit(solution)/shard_map/ppermute | solution.py:231
  11.3 4.9 %collective-permute-start.3 = (bf16[144,128]{1,0:T(8,128)(2,1)S(1)}, bf16[144,128]{1,0:T(8,128)(2,1)S(1)}, u32[]{:S(2)}, u32[]{:S(2)}) collective-permute-start(bf16[144,128]{1,0:T(8,128)(2,1)S(1)} %shard_map.76.after_ref.refs_0_), channel_id=1, source_target_pairs={{0,8},{1,9},{2,10},{3,11},{4,12},{5,13},{6,14},{7,15},{8,0},{9,1},... | collective-permute-start | bytes 110600 | tf_op jit(solution)/shard_map/ppermute | solution.py:231
  11.3 4.9 %collective-permute-start.2 = (bf16[144,128]{1,0:T(8,128)(2,1)S(1)}, bf16[144,128]{1,0:T(8,128)(2,1)S(1)}, u32[]{:S(2)}, u32[]{:S(2)}) collective-permute-start(bf16[144,128]{1,0:T(8,128)(2,1)S(1)} %shard_map.76.after_ref.refs_0_), channel_id=1, source_target_pairs={{0,5},{1,4},{2,7},{3,6},{4,1},{5,0},{6,3},{7,2},{8,13},{9,12},{10,... | collective-permute-start | bytes 110600 | tf_op jit(solution)/shard_map/ppermute | solution.py:231
  16.2 1.4 %collective-permute-start.5 = (bf16[128,512]{1,0:T(8,128)(2,1)S(1)}, bf16[128,512]{1,0:T(8,128)(2,1)S(1)}, u32[]{:S(2)}, u32[]{:S(2)}) collective-permute-start(bf16[128,512]{1,0:T(8,128)(2,1)S(1)} %get-tuple-element.22.own_ref), channel_id=1, source_target_pairs={{0,1},{1,0},{2,3},{3,2},{4,5},{5,4},{6,7},{7,6},{8,9},{9,8},{10,11... | collective-permute-start | bytes 393224 | tf_op jit(solution)/shard_map/ppermute | solution.py:225
  18.6 12.2 %copy-start = (bf16[1024,1024]{1,0:T(8,128)(2,1)S(1)}, bf16[1024,1024]{1,0:T(8,128)(2,1)}, u32[]{:S(2)}) copy-start(bf16[1024,1024]{1,0:T(8,128)(2,1)} %weight_ref.3) | copy-start | bytes 6291460
  18.6 1.4 %collective-permute-start.6 = (bf16[128,512]{1,0:T(8,128)(2,1)S(1)}, bf16[128,512]{1,0:T(8,128)(2,1)S(1)}, u32[]{:S(2)}, u32[]{:S(2)}) collective-permute-start(bf16[128,512]{1,0:T(8,128)(2,1)S(1)} %get-tuple-element.26), channel_id=1, source_target_pairs={{0,1},{1,0},{2,3},{3,2},{4,5},{5,4},{6,7},{7,6},{8,9},{9,8},{10,11... | collective-permute-start | bytes 393224 | tf_op jit(solution)/shard_map/ppermute | solution.py:225
  20.0 5.2 %collective-permute-start.7 = (bf16[32,512]{1,0:T(8,128)(2,1)S(1)}, bf16[32,512]{1,0:T(8,128)(2,1)S(1)}, u32[]{:S(2)}, u32[]{:S(2)}) collective-permute-start(bf16[32,512]{1,0:T(8,128)(2,1)S(1)} %get-tuple-element.27), channel_id=1, source_target_pairs={{0,13},{1,12},{2,15},{3,14},{4,9},{5,8},{6,11},{7,10},{8,5},{9,4},... | collective-permute-start | bytes 98312 | tf_op jit(solution)/shard_map/ppermute | solution.py:231
  21.6 5.4 %collective-permute-start.9 = (bf16[32,512]{1,0:T(8,128)(2,1)S(1)}, bf16[32,512]{1,0:T(8,128)(2,1)S(1)}, u32[]{:S(2)}, u32[]{:S(2)}) collective-permute-start(bf16[32,512]{1,0:T(8,128)(2,1)S(1)} %get-tuple-element.28), channel_id=1, source_target_pairs={{0,8},{1,9},{2,10},{3,11},{4,12},{5,13},{6,14},{7,15},{8,0},{9,1},... | collective-permute-start | bytes 98312 | tf_op jit(solution)/shard_map/ppermute | solution.py:231
  21.8 5.2 %collective-permute-start.8 = (bf16[32,512]{1,0:T(8,128)(2,1)S(1)}, bf16[32,512]{1,0:T(8,128)(2,1)S(1)}, u32[]{:S(2)}, u32[]{:S(2)}) collective-permute-start(bf16[32,512]{1,0:T(8,128)(2,1)S(1)} %get-tuple-element.29), channel_id=1, source_target_pairs={{0,5},{1,4},{2,7},{3,6},{4,1},{5,0},{6,3},{7,2},{8,13},{9,12},{10,... | collective-permute-start | bytes 98312 | tf_op jit(solution)/shard_map/ppermute | solution.py:231
  27.0 3.5 %collective-permute-start.10 = (bf16[32,512]{1,0:T(8,128)(2,1)S(1)}, bf16[32,512]{1,0:T(8,128)(2,1)S(1)}, u32[]{:S(2)}, u32[]{:S(2)}) collective-permute-start(bf16[32,512]{1,0:T(8,128)(2,1)S(1)} %fusion.1), channel_id=1, source_target_pairs={{0,3},{1,2},{2,1},{3,0},{4,7},{5,6},{6,5},{7,4},{8,11},{9,10},{10,... | collective-permute-start | bytes 98312 | tf_op jit(solution)/shard_map/ppermute | solution.py:225
  30.6 1.3 %collective-permute-start.11 = (bf16[32,512]{1,0:T(8,128)(2,1)S(1)}, bf16[32,512]{1,0:T(8,128)(2,1)S(1)}, u32[]{:S(2)}, u32[]{:S(2)}) collective-permute-start(bf16[32,512]{1,0:T(8,128)(2,1)S(1)} %add_convert_fusion.1.own_ref), channel_id=1, source_target_pairs={{0,1},{1,0},{2,3},{3,2},{4,5},{5,4},{6,7},{7,6},{8,9},{9,8},{10,11... | collective-permute-start | bytes 98312 | tf_op jit(solution)/shard_map/ppermute | solution.py:225

commit v18 on v17

--- a/solution.py
+++ b/solution.py
@@ -197,10 +197,9 @@
 def up_kernel(part_ref, other_ref, weight_ref, out_hbm, out, sems):
     other = other_ref[...]
     at_rows = pl.ds(half_at(False, other.shape[1]), other.shape[1])
-    half = out.shape[1] // 2
+    length = out.shape[1]
     copies = []
-    for i in range(2):
-        at = slice(i * half, (i + 1) * half)
+    for i, at in enumerate((slice(0, length // 4 * 3), slice(length // 4 * 3, length))):
         out[:, at] = (part_ref[:, at] + dot(other, weight_ref[at_rows, at], NN)).astype(BF16)
         copies.append(pltpu.make_async_copy(out.at[:, at], out_hbm.at[:, at], sems.at[i]))
         copies[i].start()
@@ -334,7 +333,7 @@
     part = (mine + over_tp(theirs, 1).astype(F32)).astype(BF16)
     blocks = part.reshape(exp_count, rows, half)
     mixed = blocks[0].astype(F32)
-    for s in (exp_count - 1, *range(1, exp_count - 1)):
+    for s in (exp_count - 1, *range(exp_count - 2, 0, -1)):
         mixed = mixed + over_exp(blocks[s], s).astype(F32)
     mixed = across(mixed).astype(BF16)
     lat_up = vmem(lat_up)

time: 33 us -> 33.3 us (level)
  waiting for transfers between devices: 10.8 us -> 11.9 us
  starting transfers between devices: 12.8 us -> 12 us
    ppermute x6, waiting for transfers between devices: 5.06 us -> 6.28 us  [over_tp(): return lax.ppermute(x, 'tp', [(t, t ^ mask) for t in range(tp_count)])]
    ppermute x6, starting transfers between devices: 4.86 us -> 3.83 us  [over_tp(): return lax.ppermute(x, 'tp', [(t, t ^ mask) for t in range(tp_count)])]
where the time goes in v18:
time: 33.3 us; the launch traced here: 33.1 us
  starting transfers between devices  12 us (36%)
  waiting for transfers between devices  11.9 us (36%)
  Pallas kernels  8.93 us (27%)
    pallas_call x11, Pallas kernels, kernel_call(): pl.pallas_call(body, out_shape=out_shape, in_specs=[spec(pltpu.HBM if i i...  8.93 us
    ppermute x6, starting transfers between devices, over_exp(): return lax.ppermute(x, ('exp', 'tp'), hops)  8.2 us
    ppermute x6, waiting for transfers between devices, over_tp(): return lax.ppermute(x, 'tp', [(t, t ^ mask) for t in range(tp_count)])  6.28 us
    ppermute x6, waiting for transfers between devices, over_exp(): return lax.ppermute(x, ('exp', 'tp'), hops)  5.64 us
    ppermute x6, starting transfers between devices, over_tp(): return lax.ppermute(x, 'tp', [(t, t ^ mask) for t in range(tp_count)])  3.83 us
  transfers between devices with their start and end apart: 12, of which 8 were waited for; matrix products, arithmetic and copies ran while one was open for 0% of the time, Pallas kernels for 16%

profile of v18, /device:TPU:0, one launch (start us, length us, event | category | flops | bytes accessed | tf_op | source)
XLA Modules:
  0.0 33.1 jit_solution(1450206424832463008)
XLA Ops:
  0.0 1.7 %shard_map.73 = (bf16[32,512]{1,0:T(8,128)(2,1)S(1)}, bf16[32,1024]{1,0:T(8,128)(2,1)S(1)}, bf16[512,1024]{1,0:T(8,128)(2,1)S(1)}) custom-call(bf16[32,1024]{1,0:T(8,128)(2,1)} %tokens_hbm.1, bf16[1024,1024]{1,0:T(8,128)(2,1)} %weight_hbm.1), custom_call_target="tpu_custom_call" | custom-call | flops 33554432 | bytes 2097152 | tf_op jit(solution)/shard_map/pallas_call | solution.py:33
  1.7 0.5 %collective-permute-start = (bf16[32,512]{1,0:T(8,128)(2,1)S(1)}, bf16[32,512]{1,0:T(8,128)(2,1)S(1)}, u32[]{:S(2)}, u32[]{:S(2)}) collective-permute-start(bf16[32,512]{1,0:T(8,128)(2,1)S(1)} %get-tuple-element.18), channel_id=1, source_target_pairs={{0,1},{1,0},{2,3},{3,2},{4,5},{5,4},{6,7},{7,6},{8,9},{9,8},{10,11... | collective-permute-start | bytes 98312 | tf_op jit(solution)/shard_map/ppermute | solution.py:224
  2.2 0.4 %shard_map.74 = f32[32,512]{1,0:T(8,128)S(1)} custom-call(bf16[32,1024]{1,0:T(8,128)(2,1)S(1)} %get-tuple-element.16.tokens_ref, bf16[512,1024]{1,0:T(8,128)(2,1)S(1)} %get-tuple-element.17.weight_ref), custom_call_target="tpu_custom_call" | custom-call | flops 33554432 | bytes 1048576 | tf_op jit(solution)/shard_map/pallas_call | solution.py:33
  2.6 0.5 %collective-permute-done = bf16[32,512]{1,0:T(8,128)(2,1)S(1)} collective-permute-done((bf16[32,512]{1,0:T(8,128)(2,1)S(1)}, bf16[32,512]{1,0:T(8,128)(2,1)S(1)}, u32[]{:S(2)}, u32[]{:S(2)}) %collective-permute-start) | collective-permute-done | bytes 32800 | tf_op jit(solution)/shard_map/ppermute | solution.py:224
  3.1 2.7 %collective-permute-start.1 = (bf16[32,512]{1,0:T(8,128)(2,1)S(1)}, bf16[32,512]{1,0:T(8,128)(2,1)S(1)}, u32[]{:S(2)}, u32[]{:S(2)}) collective-permute-start(bf16[32,512]{1,0:T(8,128)(2,1)S(1)} %fusion.refs_0_), channel_id=1, source_target_pairs={{0,3},{1,2},{2,1},{3,0},{4,7},{5,6},{6,5},{7,4},{8,11},{9,10},{10,... | collective-permute-start | bytes 98312 | tf_op jit(solution)/shard_map/ppermute | solution.py:224
  5.8 1.8 %shard_map.75 = (bf16[16,128]{1,0:T(8,128)(2,1)S(1)}, bf16[2,672,1024]{2,1,0:T(8,128)(2,1)S(1)}) custom-call(bf16[32,512]{1,0:T(8,128)(2,1)S(1)} %fusion.refs_0_, s32[4,32]{1,0:T(4,128)} %bitcast.4, f32[4,32]{1,0:T(4,128)} %bitcast.5, bf16[2,672,1024]{2,1,0:T(8,128)(2,1)} %refs_3_.1), custom_call_target="tpu_custom_call" | custom-call | bytes 2752512 | tf_op jit(solution)/shard_map/pallas_call | solution.py:33
  7.6 0.0 collective-permute-done.1
  7.7 3.7 %collective-permute-start.4 = (bf16[144,128]{1,0:T(8,128)(2,1)S(1)}, bf16[144,128]{1,0:T(8,128)(2,1)S(1)}, u32[]{:S(2)}, u32[]{:S(2)}) collective-permute-start(bf16[144,128]{1,0:T(8,128)(2,1)S(1)} %shard_map.76.after_ref.refs_0_), channel_id=1, source_target_pairs={{0,13},{1,12},{2,15},{3,14},{4,9},{5,8},{6,11},{7,10},{8,5},{9,4},... | collective-permute-start | bytes 110600 | tf_op jit(solution)/shard_map/ppermute | solution.py:230
  11.3 0.0 collective-permute-start.3
  11.3 0.4 %collective-permute-start.2 = (bf16[144,128]{1,0:T(8,128)(2,1)S(1)}, bf16[144,128]{1,0:T(8,128)(2,1)S(1)}, u32[]{:S(2)}, u32[]{:S(2)}) collective-permute-start(bf16[144,128]{1,0:T(8,128)(2,1)S(1)} %shard_map.76.after_ref.refs_0_), channel_id=1, source_target_pairs={{0,5},{1,4},{2,7},{3,6},{4,1},{5,0},{6,3},{7,2},{8,13},{9,12},{10,... | collective-permute-start | bytes 110600 | tf_op jit(solution)/shard_map/ppermute | solution.py:230
  11.7 1.8 %shard_map.77.down_ref = bf16[1344,1024]{1,0:T(8,128)(2,1)S(1)} custom-call(bf16[144,128]{1,0:T(8,128)(2,1)S(1)} %shard_map.76.after_ref.refs_0_, bf16[1344,1024]{1,0:T(8,128)(2,1)} %bitcast.3), custom_call_target="tpu_custom_call" | custom-call | bytes 2752512 | tf_op jit(solution)/shard_map/pallas_call | solution.py:33
  13.5 0.0 collective-permute-done.4.refs_3_
  13.5 2.7 %collective-permute-done.3.refs_2_ = bf16[144,128]{1,0:T(8,128)(2,1)S(1)} collective-permute-done((bf16[144,128]{1,0:T(8,128)(2,1)S(1)}, bf16[144,128]{1,0:T(8,128)(2,1)S(1)}, u32[]{:S(2)}, u32[]{:S(2)}) %collective-permute-start.3) | collective-permute-done | bytes 36896 | tf_op jit(solution)/shard_map/ppermute | solution.py:230
  16.2 0.1 collective-permute-start.5
  16.3 0.7 %shard_map.79.pre_ref = f32[128,1344]{1,0:T(8,128)S(1)} custom-call(bf16[128,512]{1,0:T(8,128)(2,1)S(1)} %get-tuple-element.22.own_ref, bf16[2,672,1024]{2,1,0:T(8,128)(2,1)S(1)} %get-tuple-element.23.up_ref), custom_call_target="tpu_custom_call" | custom-call | flops 176160768 | bytes 1376256 | tf_op jit(solution)/shard_map/pallas_call | solution.py:33
  17.0 0.7 %collective-permute-done.5.other_ref = bf16[128,512]{1,0:T(8,128)(2,1)S(1)} collective-permute-done((bf16[128,512]{1,0:T(8,128)(2,1)S(1)}, bf16[128,512]{1,0:T(8,128)(2,1)S(1)}, u32[]{:S(2)}, u32[]{:S(2)}) %collective-permute-start.5) | collective-permute-done | bytes 131104 | tf_op jit(solution)/shard_map/ppermute | solution.py:224
  17.6 0.9 %shard_map.80 = (bf16[128,1344]{1,0:T(8,128)(2,1)S(1)}, bf16[128,512]{1,0:T(8,128)(2,1)S(1)}) custom-call(bf16[64,128]{1,0:T(8,128)(2,1)S(1)} %get-tuple-element.21.terms_ref, bf16[128,512]{1,0:T(8,128)(2,1)S(1)} %collective-permute-done.5.other_ref, f32[128,1344]{1,0:T(8,128)S(1)} %shard_map.79.pre_ref, bf16[2,672,1024]{2,1,0:T(8,128)(2,1)S(1)} %get-tuple-element.23.up_ref, ...), custom_call_target="tpu_custom_call" | custom-call | flops 352321536 | bytes 2752512 | tf_op jit(solution)/shard_map/pallas_call | solution.py:33
  18.6 0.0 copy-start
  18.6 0.2 collective-permute-start.6
  18.8 0.4 %shard_map.81 = f32[128,512]{1,0:T(8,128)S(1)} custom-call(bf16[128,1344]{1,0:T(8,128)(2,1)S(1)} %get-tuple-element.25.hidden_ref, bf16[1344,1024]{1,0:T(8,128)(2,1)S(1)} %shard_map.77.down_ref), custom_call_target="tpu_custom_call" | custom-call | flops 176160768 | bytes 1376256 | tf_op jit(solution)/shard_map/pallas_call | solution.py:33
  19.2 0.8 %collective-permute-done.6 = bf16[128,512]{1,0:T(8,128)(2,1)S(1)} collective-permute-done((bf16[128,512]{1,0:T(8,128)(2,1)S(1)}, bf16[128,512]{1,0:T(8,128)(2,1)S(1)}, u32[]{:S(2)}, u32[]{:S(2)}) %collective-permute-start.6) | collective-permute-done | bytes 131104 | tf_op jit(solution)/shard_map/ppermute | solution.py:224
  20.0 1.6 %collective-permute-start.7 = (bf16[32,512]{1,0:T(8,128)(2,1)S(1)}, bf16[32,512]{1,0:T(8,128)(2,1)S(1)}, u32[]{:S(2)}, u32[]{:S(2)}) collective-permute-start(bf16[32,512]{1,0:T(8,128)(2,1)S(1)} %get-tuple-element.27), channel_id=1, source_target_pairs={{0,13},{1,12},{2,15},{3,14},{4,9},{5,8},{6,11},{7,10},{8,5},{9,4},... | collective-permute-start | bytes 98312 | tf_op jit(solution)/shard_map/ppermute | solution.py:230
  21.6 0.4 %collective-permute-start.9 = (bf16[32,512]{1,0:T(8,128)(2,1)S(1)}, bf16[32,512]{1,0:T(8,128)(2,1)S(1)}, u32[]{:S(2)}, u32[]{:S(2)}) collective-permute-start(bf16[32,512]{1,0:T(8,128)(2,1)S(1)} %get-tuple-element.28), channel_id=1, source_target_pairs={{0,5},{1,4},{2,7},{3,6},{4,1},{5,0},{6,3},{7,2},{8,13},{9,12},{10,... | collective-permute-start | bytes 98312 | tf_op jit(solution)/shard_map/ppermute | solution.py:230
  22.0 2.2 %collective-permute-start.8 = (bf16[32,512]{1,0:T(8,128)(2,1)S(1)}, bf16[32,512]{1,0:T(8,128)(2,1)S(1)}, u32[]{:S(2)}, u32[]{:S(2)}) collective-permute-start(bf16[32,512]{1,0:T(8,128)(2,1)S(1)} %get-tuple-element.29), channel_id=1, source_target_pairs={{0,8},{1,9},{2,10},{3,11},{4,12},{5,13},{6,14},{7,15},{8,0},{9,1},... | collective-permute-start | bytes 98312 | tf_op jit(solution)/shard_map/ppermute | solution.py:230
  24.2 1.1 %collective-permute-done.7 = bf16[32,512]{1,0:T(8,128)(2,1)S(1)} collective-permute-done((bf16[32,512]{1,0:T(8,128)(2,1)S(1)}, bf16[32,512]{1,0:T(8,128)(2,1)S(1)}, u32[]{:S(2)}, u32[]{:S(2)}) %collective-permute-start.7) | collective-permute-done | bytes 32800 | tf_op jit(solution)/shard_map/ppermute | solution.py:230
  25.3 1.8 %collective-permute-done.8 = bf16[32,512]{1,0:T(8,128)(2,1)S(1)} collective-permute-done((bf16[32,512]{1,0:T(8,128)(2,1)S(1)}, bf16[32,512]{1,0:T(8,128)(2,1)S(1)}, u32[]{:S(2)}, u32[]{:S(2)}) %collective-permute-start.8) | collective-permute-done | bytes 32800 | tf_op jit(solution)/shard_map/ppermute | solution.py:230
  27.2 0.2 collective-permute-start.10
  27.4 3.5 %collective-permute-done.10 = bf16[32,512]{1,0:T(8,128)(2,1)S(1)} collective-permute-done((bf16[32,512]{1,0:T(8,128)(2,1)S(1)}, bf16[32,512]{1,0:T(8,128)(2,1)S(1)}, u32[]{:S(2)}, u32[]{:S(2)}) %collective-permute-start.10) | collective-permute-done | bytes 32800 | tf_op jit(solution)/shard_map/ppermute | solution.py:224
  30.9 0.2 collective-permute-start.11
  31.1 0.3 shard_map.82.part_ref
  31.4 0.8 %collective-permute-done.11.other_ref = bf16[32,512]{1,0:T(8,128)(2,1)S(1)} collective-permute-done((bf16[32,512]{1,0:T(8,128)(2,1)S(1)}, bf16[32,512]{1,0:T(8,128)(2,1)S(1)}, u32[]{:S(2)}, u32[]{:S(2)}) %collective-permute-start.11) | collective-permute-done | bytes 32800 | tf_op jit(solution)/shard_map/ppermute | solution.py:224
  32.2 0.9 %shard_map.83 = bf16[32,1024]{1,0:T(8,128)(2,1)} custom-call(f32[32,1024]{1,0:T(8,128)S(1)} %shard_map.82.part_ref, bf16[32,512]{1,0:T(8,128)(2,1)S(1)} %collective-permute-done.11.other_ref, bf16[1024,1024]{1,0:T(8,128)(2,1)S(1)} %copy-done), custom_call_target="tpu_custom_call" | custom-call | flops 33554432 | bytes 1048576 | tf_op jit(solution)/shard_map/pallas_call | solution.py:33
  (11 shorter events, 0.1 us)
Async XLA Ops:
  1.7 1.4 %collective-permute-start = (bf16[32,512]{1,0:T(8,128)(2,1)S(1)}, bf16[32,512]{1,0:T(8,128)(2,1)S(1)}, u32[]{:S(2)}, u32[]{:S(2)}) collective-permute-start(bf16[32,512]{1,0:T(8,128)(2,1)S(1)} %get-tuple-element.18), channel_id=1, source_target_pairs={{0,1},{1,0},{2,3},{3,2},{4,5},{5,4},{6,7},{7,6},{8,9},{9,8},{10,11... | collective-permute-start | bytes 98312 | tf_op jit(solution)/shard_map/ppermute | solution.py:224
  3.1 4.5 %collective-permute-start.1 = (bf16[32,512]{1,0:T(8,128)(2,1)S(1)}, bf16[32,512]{1,0:T(8,128)(2,1)S(1)}, u32[]{:S(2)}, u32[]{:S(2)}) collective-permute-start(bf16[32,512]{1,0:T(8,128)(2,1)S(1)} %fusion.refs_0_), channel_id=1, source_target_pairs={{0,3},{1,2},{2,1},{3,0},{4,7},{5,6},{6,5},{7,4},{8,11},{9,10},{10,... | collective-permute-start | bytes 98312 | tf_op jit(solution)/shard_map/ppermute | solution.py:224
  7.7 5.8 %collective-permute-start.4 = (bf16[144,128]{1,0:T(8,128)(2,1)S(1)}, bf16[144,128]{1,0:T(8,128)(2,1)S(1)}, u32[]{:S(2)}, u32[]{:S(2)}) collective-permute-start(bf16[144,128]{1,0:T(8,128)(2,1)S(1)} %shard_map.76.after_ref.refs_0_), channel_id=1, source_target_pairs={{0,13},{1,12},{2,15},{3,14},{4,9},{5,8},{6,11},{7,10},{8,5},{9,4},... | collective-permute-start | bytes 110600 | tf_op jit(solution)/shard_map/ppermute | solution.py:230
  11.3 4.9 %collective-permute-start.3 = (bf16[144,128]{1,0:T(8,128)(2,1)S(1)}, bf16[144,128]{1,0:T(8,128)(2,1)S(1)}, u32[]{:S(2)}, u32[]{:S(2)}) collective-permute-start(bf16[144,128]{1,0:T(8,128)(2,1)S(1)} %shard_map.76.after_ref.refs_0_), channel_id=1, source_target_pairs={{0,8},{1,9},{2,10},{3,11},{4,12},{5,13},{6,14},{7,15},{8,0},{9,1},... | collective-permute-start | bytes 110600 | tf_op jit(solution)/shard_map/ppermute | solution.py:230
  11.3 4.9 %collective-permute-start.2 = (bf16[144,128]{1,0:T(8,128)(2,1)S(1)}, bf16[144,128]{1,0:T(8,128)(2,1)S(1)}, u32[]{:S(2)}, u32[]{:S(2)}) collective-permute-start(bf16[144,128]{1,0:T(8,128)(2,1)S(1)} %shard_map.76.after_ref.refs_0_), channel_id=1, source_target_pairs={{0,5},{1,4},{2,7},{3,6},{4,1},{5,0},{6,3},{7,2},{8,13},{9,12},{10,... | collective-permute-start | bytes 110600 | tf_op jit(solution)/shard_map/ppermute | solution.py:230
  16.2 1.4 %collective-permute-start.5 = (bf16[128,512]{1,0:T(8,128)(2,1)S(1)}, bf16[128,512]{1,0:T(8,128)(2,1)S(1)}, u32[]{:S(2)}, u32[]{:S(2)}) collective-permute-start(bf16[128,512]{1,0:T(8,128)(2,1)S(1)} %get-tuple-element.22.own_ref), channel_id=1, source_target_pairs={{0,1},{1,0},{2,3},{3,2},{4,5},{5,4},{6,7},{7,6},{8,9},{9,8},{10,11... | collective-permute-start | bytes 393224 | tf_op jit(solution)/shard_map/ppermute | solution.py:224
  18.6 12.5 %copy-start = (bf16[1024,1024]{1,0:T(8,128)(2,1)S(1)}, bf16[1024,1024]{1,0:T(8,128)(2,1)}, u32[]{:S(2)}) copy-start(bf16[1024,1024]{1,0:T(8,128)(2,1)} %weight_ref.3) | copy-start | bytes 6291460
  18.6 1.4 %collective-permute-start.6 = (bf16[128,512]{1,0:T(8,128)(2,1)S(1)}, bf16[128,512]{1,0:T(8,128)(2,1)S(1)}, u32[]{:S(2)}, u32[]{:S(2)}) collective-permute-start(bf16[128,512]{1,0:T(8,128)(2,1)S(1)} %get-tuple-element.26), channel_id=1, source_target_pairs={{0,1},{1,0},{2,3},{3,2},{4,5},{5,4},{6,7},{7,6},{8,9},{9,8},{10,11... | collective-permute-start | bytes 393224 | tf_op jit(solution)/shard_map/ppermute | solution.py:224
  20.0 5.3 %collective-permute-start.7 = (bf16[32,512]{1,0:T(8,128)(2,1)S(1)}, bf16[32,512]{1,0:T(8,128)(2,1)S(1)}, u32[]{:S(2)}, u32[]{:S(2)}) collective-permute-start(bf16[32,512]{1,0:T(8,128)(2,1)S(1)} %get-tuple-element.27), channel_id=1, source_target_pairs={{0,13},{1,12},{2,15},{3,14},{4,9},{5,8},{6,11},{7,10},{8,5},{9,4},... | collective-permute-start | bytes 98312 | tf_op jit(solution)/shard_map/ppermute | solution.py:230
  21.6 3.7 %collective-permute-start.9 = (bf16[32,512]{1,0:T(8,128)(2,1)S(1)}, bf16[32,512]{1,0:T(8,128)(2,1)S(1)}, u32[]{:S(2)}, u32[]{:S(2)}) collective-permute-start(bf16[32,512]{1,0:T(8,128)(2,1)S(1)} %get-tuple-element.28), channel_id=1, source_target_pairs={{0,5},{1,4},{2,7},{3,6},{4,1},{5,0},{6,3},{7,2},{8,13},{9,12},{10,... | collective-permute-start | bytes 98312 | tf_op jit(solution)/shard_map/ppermute | solution.py:230
  22.0 5.2 %collective-permute-start.8 = (bf16[32,512]{1,0:T(8,128)(2,1)S(1)}, bf16[32,512]{1,0:T(8,128)(2,1)S(1)}, u32[]{:S(2)}, u32[]{:S(2)}) collective-permute-start(bf16[32,512]{1,0:T(8,128)(2,1)S(1)} %get-tuple-element.29), channel_id=1, source_target_pairs={{0,8},{1,9},{2,10},{3,11},{4,12},{5,13},{6,14},{7,15},{8,0},{9,1},... | collective-permute-start | bytes 98312 | tf_op jit(solution)/shard_map/ppermute | solution.py:230
  27.2 3.7 %collective-permute-start.10 = (bf16[32,512]{1,0:T(8,128)(2,1)S(1)}, bf16[32,512]{1,0:T(8,128)(2,1)S(1)}, u32[]{:S(2)}, u32[]{:S(2)}) collective-permute-start(bf16[32,512]{1,0:T(8,128)(2,1)S(1)} %fusion.1), channel_id=1, source_target_pairs={{0,3},{1,2},{2,1},{3,0},{4,7},{5,6},{6,5},{7,4},{8,11},{9,10},{10,... | collective-permute-start | bytes 98312 | tf_op jit(solution)/shard_map/ppermute | solution.py:224
  30.9 1.3 %collective-permute-start.11 = (bf16[32,512]{1,0:T(8,128)(2,1)S(1)}, bf16[32,512]{1,0:T(8,128)(2,1)S(1)}, u32[]{:S(2)}, u32[]{:S(2)}) collective-permute-start(bf16[32,512]{1,0:T(8,128)(2,1)S(1)} %add_convert_fusion.1.own_ref), channel_id=1, source_target_pairs={{0,1},{1,0},{2,3},{3,2},{4,5},{5,4},{6,7},{7,6},{8,9},{9,8},{10,11... | collective-permute-start | bytes 98312 | tf_op jit(solution)/shard_map/ppermute | solution.py:224

commit v19 on v17

--- a/solution.py
+++ b/solution.py
@@ -56,8 +56,6 @@
 def down_kernel(tokens_hbm, weight_hbm, theirs_ref, tokens, mine_weight, weight, sems):
     half = theirs_ref.shape[1]
     size = half // CHUNKS
-    load = pltpu.make_async_copy(tokens_hbm, tokens, sems.at[0])
-    load.start()
     chunks = []
     for i in range(CHUNKS):
         start = pl.multiple_of(half_at(False, half) + i * size, size)
@@ -69,6 +67,8 @@
             )
         )
         chunks[i].start()
+    load = pltpu.make_async_copy(tokens_hbm, tokens, sems.at[0])
+    load.start()
     later = pltpu.make_async_copy(
         weight_hbm.at[pl.ds(half_at(True, half), half), :], mine_weight, sems.at[1]
     )
@@ -194,18 +194,13 @@
     out_ref[...] = dot(own_ref[...], weight_ref[pl.ds(half_at(True, half), half), :], NN)
 
 
-def up_kernel(part_ref, other_ref, weight_ref, out_hbm, out, sems):
+def up_kernel(part_ref, other_ref, weight_ref, out_hbm, out, sem):
     other = other_ref[...]
     at_rows = pl.ds(half_at(False, other.shape[1]), other.shape[1])
-    half = out.shape[1] // 2
-    copies = []
-    for i in range(2):
-        at = slice(i * half, (i + 1) * half)
-        out[:, at] = (part_ref[:, at] + dot(other, weight_ref[at_rows, at], NN)).astype(BF16)
-        copies.append(pltpu.make_async_copy(out.at[:, at], out_hbm.at[:, at], sems.at[i]))
-        copies[i].start()
-    for copy in copies:
-        copy.wait()
+    out[...] = (part_ref[...] + dot(other, weight_ref[at_rows, :], NN)).astype(BF16)
+    copy = pltpu.make_async_copy(out, out_hbm, sem)
+    copy.start()
+    copy.wait()
 
 
 def on_device(tokens, lat_down, lat_up, expert_up, expert_down, routes, route_weights):
@@ -352,7 +347,7 @@
         shaped(BF16, rows, out_len),
         (own_part, over_tp(mixed, 1), lat_up),
         (),
-        [pltpu.VMEM((rows, out_len), BF16), pltpu.SemaphoreType.DMA((2,))],
+        [pltpu.VMEM((rows, out_len), BF16), pltpu.SemaphoreType.DMA],
         rows * latent_len * out_len,
         latent_len * out_len,
         pltpu.HBM,

time: 33 us -> 32.9 us (level)
  no operation moved by 1% of the time
where the time goes in v19:
time: 32.9 us; the launch traced here: 32.7 us
  starting transfers between devices  12.8 us (39%)
  waiting for transfers between devices  10.8 us (33%)
  Pallas kernels  8.89 us (27%)
    pallas_call x11, Pallas kernels, kernel_call(): pl.pallas_call(body, out_shape=out_shape, in_specs=[spec(pltpu.HBM if i i...  8.89 us
    ppermute x6, starting transfers between devices, over_exp(): return lax.ppermute(x, ('exp', 'tp'), hops)  7.92 us
    ppermute x6, waiting for transfers between devices, over_exp(): return lax.ppermute(x, ('exp', 'tp'), hops)  5.76 us
    ppermute x6, waiting for transfers between devices, over_tp(): return lax.ppermute(x, 'tp', [(t, t ^ mask) for t in range(tp_count)])  5.07 us
    ppermute x6, starting transfers between devices, over_tp(): return lax.ppermute(x, 'tp', [(t, t ^ mask) for t in range(tp_count)])  4.85 us
  transfers between devices with their start and end apart: 12, of which 8 were waited for; matrix products, arithmetic and copies ran while one was open for 0% of the time, Pallas kernels for 16%

profile of v19, /device:TPU:0, one launch (start us, length us, event | category | flops | bytes accessed | tf_op | source)
XLA Modules:
  0.0 32.7 jit_solution(14969494891147386987)
XLA Ops:
  0.0 1.7 %shard_map.73 = (bf16[32,512]{1,0:T(8,128)(2,1)S(1)}, bf16[32,1024]{1,0:T(8,128)(2,1)S(1)}, bf16[512,1024]{1,0:T(8,128)(2,1)S(1)}) custom-call(bf16[32,1024]{1,0:T(8,128)(2,1)} %tokens_hbm.1, bf16[1024,1024]{1,0:T(8,128)(2,1)} %weight_hbm.1), custom_call_target="tpu_custom_call" | custom-call | flops 33554432 | bytes 2097152 | tf_op jit(solution)/shard_map/pallas_call | solution.py:33
  1.7 0.5 %collective-permute-start = (bf16[32,512]{1,0:T(8,128)(2,1)S(1)}, bf16[32,512]{1,0:T(8,128)(2,1)S(1)}, u32[]{:S(2)}, u32[]{:S(2)}) collective-permute-start(bf16[32,512]{1,0:T(8,128)(2,1)S(1)} %get-tuple-element.18), channel_id=1, source_target_pairs={{0,1},{1,0},{2,3},{3,2},{4,5},{5,4},{6,7},{7,6},{8,9},{9,8},{10,11... | collective-permute-start | bytes 98312 | tf_op jit(solution)/shard_map/ppermute | solution.py:220
  2.2 0.4 %shard_map.74 = f32[32,512]{1,0:T(8,128)S(1)} custom-call(bf16[32,1024]{1,0:T(8,128)(2,1)S(1)} %get-tuple-element.16.tokens_ref, bf16[512,1024]{1,0:T(8,128)(2,1)S(1)} %get-tuple-element.17.weight_ref), custom_call_target="tpu_custom_call" | custom-call | flops 33554432 | bytes 1048576 | tf_op jit(solution)/shard_map/pallas_call | solution.py:33
  2.6 0.5 %collective-permute-done = bf16[32,512]{1,0:T(8,128)(2,1)S(1)} collective-permute-done((bf16[32,512]{1,0:T(8,128)(2,1)S(1)}, bf16[32,512]{1,0:T(8,128)(2,1)S(1)}, u32[]{:S(2)}, u32[]{:S(2)}) %collective-permute-start) | collective-permute-done | bytes 32800 | tf_op jit(solution)/shard_map/ppermute | solution.py:220
  3.1 2.7 %collective-permute-start.1 = (bf16[32,512]{1,0:T(8,128)(2,1)S(1)}, bf16[32,512]{1,0:T(8,128)(2,1)S(1)}, u32[]{:S(2)}, u32[]{:S(2)}) collective-permute-start(bf16[32,512]{1,0:T(8,128)(2,1)S(1)} %fusion.refs_0_), channel_id=1, source_target_pairs={{0,3},{1,2},{2,1},{3,0},{4,7},{5,6},{6,5},{7,4},{8,11},{9,10},{10,... | collective-permute-start | bytes 98312 | tf_op jit(solution)/shard_map/ppermute | solution.py:220
  5.7 1.8 %shard_map.75 = (bf16[16,128]{1,0:T(8,128)(2,1)S(1)}, bf16[2,672,1024]{2,1,0:T(8,128)(2,1)S(1)}) custom-call(bf16[32,512]{1,0:T(8,128)(2,1)S(1)} %fusion.refs_0_, s32[4,32]{1,0:T(4,128)} %bitcast.4, f32[4,32]{1,0:T(4,128)} %bitcast.5, bf16[2,672,1024]{2,1,0:T(8,128)(2,1)} %refs_3_.1), custom_call_target="tpu_custom_call" | custom-call | bytes 2752512 | tf_op jit(solution)/shard_map/pallas_call | solution.py:33
  7.6 0.0 collective-permute-done.1
  7.6 3.7 %collective-permute-start.4 = (bf16[144,128]{1,0:T(8,128)(2,1)S(1)}, bf16[144,128]{1,0:T(8,128)(2,1)S(1)}, u32[]{:S(2)}, u32[]{:S(2)}) collective-permute-start(bf16[144,128]{1,0:T(8,128)(2,1)S(1)} %shard_map.76.after_ref.refs_0_), channel_id=1, source_target_pairs={{0,13},{1,12},{2,15},{3,14},{4,9},{5,8},{6,11},{7,10},{8,5},{9,4},... | collective-permute-start | bytes 110600 | tf_op jit(solution)/shard_map/ppermute | solution.py:226
  11.3 0.4 %collective-permute-start.2 = (bf16[144,128]{1,0:T(8,128)(2,1)S(1)}, bf16[144,128]{1,0:T(8,128)(2,1)S(1)}, u32[]{:S(2)}, u32[]{:S(2)}) collective-permute-start(bf16[144,128]{1,0:T(8,128)(2,1)S(1)} %shard_map.76.after_ref.refs_0_), channel_id=1, source_target_pairs={{0,5},{1,4},{2,7},{3,6},{4,1},{5,0},{6,3},{7,2},{8,13},{9,12},{10,... | collective-permute-start | bytes 110600 | tf_op jit(solution)/shard_map/ppermute | solution.py:226
  11.7 1.8 %shard_map.77.down_ref = bf16[1344,1024]{1,0:T(8,128)(2,1)S(1)} custom-call(bf16[144,128]{1,0:T(8,128)(2,1)S(1)} %shard_map.76.after_ref.refs_0_, bf16[1344,1024]{1,0:T(8,128)(2,1)} %bitcast.3), custom_call_target="tpu_custom_call" | custom-call | bytes 2752512 | tf_op jit(solution)/shard_map/pallas_call | solution.py:33
  13.5 0.0 collective-permute-done.4.refs_3_
  13.5 2.7 %collective-permute-done.3.refs_2_ = bf16[144,128]{1,0:T(8,128)(2,1)S(1)} collective-permute-done((bf16[144,128]{1,0:T(8,128)(2,1)S(1)}, bf16[144,128]{1,0:T(8,128)(2,1)S(1)}, u32[]{:S(2)}, u32[]{:S(2)}) %collective-permute-start.3) | collective-permute-done | bytes 36896 | tf_op jit(solution)/shard_map/ppermute | solution.py:226
  16.2 0.1 collective-permute-start.5
  16.3 0.7 %shard_map.79.pre_ref = f32[128,1344]{1,0:T(8,128)S(1)} custom-call(bf16[128,512]{1,0:T(8,128)(2,1)S(1)} %get-tuple-element.22.own_ref, bf16[2,672,1024]{2,1,0:T(8,128)(2,1)S(1)} %get-tuple-element.23.up_ref), custom_call_target="tpu_custom_call" | custom-call | flops 176160768 | bytes 1376256 | tf_op jit(solution)/shard_map/pallas_call | solution.py:33
  16.9 0.7 %collective-permute-done.5.other_ref = bf16[128,512]{1,0:T(8,128)(2,1)S(1)} collective-permute-done((bf16[128,512]{1,0:T(8,128)(2,1)S(1)}, bf16[128,512]{1,0:T(8,128)(2,1)S(1)}, u32[]{:S(2)}, u32[]{:S(2)}) %collective-permute-start.5) | collective-permute-done | bytes 131104 | tf_op jit(solution)/shard_map/ppermute | solution.py:220
  17.6 0.9 %shard_map.80 = (bf16[128,1344]{1,0:T(8,128)(2,1)S(1)}, bf16[128,512]{1,0:T(8,128)(2,1)S(1)}) custom-call(bf16[64,128]{1,0:T(8,128)(2,1)S(1)} %get-tuple-element.21.terms_ref, bf16[128,512]{1,0:T(8,128)(2,1)S(1)} %collective-permute-done.5.other_ref, f32[128,1344]{1,0:T(8,128)S(1)} %shard_map.79.pre_ref, bf16[2,672,1024]{2,1,0:T(8,128)(2,1)S(1)} %get-tuple-element.23.up_ref, ...), custom_call_target="tpu_custom_call" | custom-call | flops 352321536 | bytes 2752512 | tf_op jit(solution)/shard_map/pallas_call | solution.py:33
  18.5 0.0 copy-start
  18.5 0.2 collective-permute-start.6
  18.7 0.4 %shard_map.81 = f32[128,512]{1,0:T(8,128)S(1)} custom-call(bf16[128,1344]{1,0:T(8,128)(2,1)S(1)} %get-tuple-element.25.hidden_ref, bf16[1344,1024]{1,0:T(8,128)(2,1)S(1)} %shard_map.77.down_ref), custom_call_target="tpu_custom_call" | custom-call | flops 176160768 | bytes 1376256 | tf_op jit(solution)/shard_map/pallas_call | solution.py:33
  19.1 0.8 %collective-permute-done.6 = bf16[128,512]{1,0:T(8,128)(2,1)S(1)} collective-permute-done((bf16[128,512]{1,0:T(8,128)(2,1)S(1)}, bf16[128,512]{1,0:T(8,128)(2,1)S(1)}, u32[]{:S(2)}, u32[]{:S(2)}) %collective-permute-start.6) | collective-permute-done | bytes 131104 | tf_op jit(solution)/shard_map/ppermute | solution.py:220
  20.0 1.6 %collective-permute-start.7 = (bf16[32,512]{1,0:T(8,128)(2,1)S(1)}, bf16[32,512]{1,0:T(8,128)(2,1)S(1)}, u32[]{:S(2)}, u32[]{:S(2)}) collective-permute-start(bf16[32,512]{1,0:T(8,128)(2,1)S(1)} %get-tuple-element.27), channel_id=1, source_target_pairs={{0,13},{1,12},{2,15},{3,14},{4,9},{5,8},{6,11},{7,10},{8,5},{9,4},... | collective-permute-start | bytes 98312 | tf_op jit(solution)/shard_map/ppermute | solution.py:226
  21.6 0.2 collective-permute-start.9
  21.8 2.1 %collective-permute-start.8 = (bf16[32,512]{1,0:T(8,128)(2,1)S(1)}, bf16[32,512]{1,0:T(8,128)(2,1)S(1)}, u32[]{:S(2)}, u32[]{:S(2)}) collective-permute-start(bf16[32,512]{1,0:T(8,128)(2,1)S(1)} %get-tuple-element.29), channel_id=1, source_target_pairs={{0,5},{1,4},{2,7},{3,6},{4,1},{5,0},{6,3},{7,2},{8,13},{9,12},{10,... | collective-permute-start | bytes 98312 | tf_op jit(solution)/shard_map/ppermute | solution.py:226
  23.9 1.3 %collective-permute-done.7 = bf16[32,512]{1,0:T(8,128)(2,1)S(1)} collective-permute-done((bf16[32,512]{1,0:T(8,128)(2,1)S(1)}, bf16[32,512]{1,0:T(8,128)(2,1)S(1)}, u32[]{:S(2)}, u32[]{:S(2)}) %collective-permute-start.7) | collective-permute-done | bytes 32800 | tf_op jit(solution)/shard_map/ppermute | solution.py:226
  25.2 1.7 %collective-permute-done.9 = bf16[32,512]{1,0:T(8,128)(2,1)S(1)} collective-permute-done((bf16[32,512]{1,0:T(8,128)(2,1)S(1)}, bf16[32,512]{1,0:T(8,128)(2,1)S(1)}, u32[]{:S(2)}, u32[]{:S(2)}) %collective-permute-start.9) | collective-permute-done | bytes 32800 | tf_op jit(solution)/shard_map/ppermute | solution.py:226
  27.0 0.0 collective-permute-done.8
  27.0 1.2 %collective-permute-start.10 = (bf16[32,512]{1,0:T(8,128)(2,1)S(1)}, bf16[32,512]{1,0:T(8,128)(2,1)S(1)}, u32[]{:S(2)}, u32[]{:S(2)}) collective-permute-start(bf16[32,512]{1,0:T(8,128)(2,1)S(1)} %fusion.1), channel_id=1, source_target_pairs={{0,3},{1,2},{2,1},{3,0},{4,7},{5,6},{6,5},{7,4},{8,11},{9,10},{10,... | collective-permute-start | bytes 98312 | tf_op jit(solution)/shard_map/ppermute | solution.py:220
  28.2 2.3 %collective-permute-done.10 = bf16[32,512]{1,0:T(8,128)(2,1)S(1)} collective-permute-done((bf16[32,512]{1,0:T(8,128)(2,1)S(1)}, bf16[32,512]{1,0:T(8,128)(2,1)S(1)}, u32[]{:S(2)}, u32[]{:S(2)}) %collective-permute-start.10) | collective-permute-done | bytes 32800 | tf_op jit(solution)/shard_map/ppermute | solution.py:220
  30.5 0.2 collective-permute-start.11
  30.7 0.3 shard_map.82.part_ref
  31.0 0.8 %collective-permute-done.11.other_ref = bf16[32,512]{1,0:T(8,128)(2,1)S(1)} collective-permute-done((bf16[32,512]{1,0:T(8,128)(2,1)S(1)}, bf16[32,512]{1,0:T(8,128)(2,1)S(1)}, u32[]{:S(2)}, u32[]{:S(2)}) %collective-permute-start.11) | collective-permute-done | bytes 32800 | tf_op jit(solution)/shard_map/ppermute | solution.py:220
  31.8 0.9 %shard_map.83 = bf16[32,1024]{1,0:T(8,128)(2,1)} custom-call(f32[32,1024]{1,0:T(8,128)S(1)} %shard_map.82.part_ref, bf16[32,512]{1,0:T(8,128)(2,1)S(1)} %collective-permute-done.11.other_ref, bf16[1024,1024]{1,0:T(8,128)(2,1)S(1)} %copy-done), custom_call_target="tpu_custom_call" | custom-call | flops 33554432 | bytes 1048576 | tf_op jit(solution)/shard_map/pallas_call | solution.py:33
  (11 shorter events, 0.1 us)
Async XLA Ops:
  1.7 1.4 %collective-permute-start = (bf16[32,512]{1,0:T(8,128)(2,1)S(1)}, bf16[32,512]{1,0:T(8,128)(2,1)S(1)}, u32[]{:S(2)}, u32[]{:S(2)}) collective-permute-start(bf16[32,512]{1,0:T(8,128)(2,1)S(1)} %get-tuple-element.18), channel_id=1, source_target_pairs={{0,1},{1,0},{2,3},{3,2},{4,5},{5,4},{6,7},{7,6},{8,9},{9,8},{10,11... | collective-permute-start | bytes 98312 | tf_op jit(solution)/shard_map/ppermute | solution.py:220
  3.1 4.5 %collective-permute-start.1 = (bf16[32,512]{1,0:T(8,128)(2,1)S(1)}, bf16[32,512]{1,0:T(8,128)(2,1)S(1)}, u32[]{:S(2)}, u32[]{:S(2)}) collective-permute-start(bf16[32,512]{1,0:T(8,128)(2,1)S(1)} %fusion.refs_0_), channel_id=1, source_target_pairs={{0,3},{1,2},{2,1},{3,0},{4,7},{5,6},{6,5},{7,4},{8,11},{9,10},{10,... | collective-permute-start | bytes 98312 | tf_op jit(solution)/shard_map/ppermute | solution.py:220
  7.6 5.8 %collective-permute-start.4 = (bf16[144,128]{1,0:T(8,128)(2,1)S(1)}, bf16[144,128]{1,0:T(8,128)(2,1)S(1)}, u32[]{:S(2)}, u32[]{:S(2)}) collective-permute-start(bf16[144,128]{1,0:T(8,128)(2,1)S(1)} %shard_map.76.after_ref.refs_0_), channel_id=1, source_target_pairs={{0,13},{1,12},{2,15},{3,14},{4,9},{5,8},{6,11},{7,10},{8,5},{9,4},... | collective-permute-start | bytes 110600 | tf_op jit(solution)/shard_map/ppermute | solution.py:226
  11.3 4.9 %collective-permute-start.3 = (bf16[144,128]{1,0:T(8,128)(2,1)S(1)}, bf16[144,128]{1,0:T(8,128)(2,1)S(1)}, u32[]{:S(2)}, u32[]{:S(2)}) collective-permute-start(bf16[144,128]{1,0:T(8,128)(2,1)S(1)} %shard_map.76.after_ref.refs_0_), channel_id=1, source_target_pairs={{0,8},{1,9},{2,10},{3,11},{4,12},{5,13},{6,14},{7,15},{8,0},{9,1},... | collective-permute-start | bytes 110600 | tf_op jit(solution)/shard_map/ppermute | solution.py:226
  11.3 4.9 %collective-permute-start.2 = (bf16[144,128]{1,0:T(8,128)(2,1)S(1)}, bf16[144,128]{1,0:T(8,128)(2,1)S(1)}, u32[]{:S(2)}, u32[]{:S(2)}) collective-permute-start(bf16[144,128]{1,0:T(8,128)(2,1)S(1)} %shard_map.76.after_ref.refs_0_), channel_id=1, source_target_pairs={{0,5},{1,4},{2,7},{3,6},{4,1},{5,0},{6,3},{7,2},{8,13},{9,12},{10,... | collective-permute-start | bytes 110600 | tf_op jit(solution)/shard_map/ppermute | solution.py:226
  16.2 1.4 %collective-permute-start.5 = (bf16[128,512]{1,0:T(8,128)(2,1)S(1)}, bf16[128,512]{1,0:T(8,128)(2,1)S(1)}, u32[]{:S(2)}, u32[]{:S(2)}) collective-permute-start(bf16[128,512]{1,0:T(8,128)(2,1)S(1)} %get-tuple-element.22.own_ref), channel_id=1, source_target_pairs={{0,1},{1,0},{2,3},{3,2},{4,5},{5,4},{6,7},{7,6},{8,9},{9,8},{10,11... | collective-permute-start | bytes 393224 | tf_op jit(solution)/shard_map/ppermute | solution.py:220
  18.5 12.2 %copy-start = (bf16[1024,1024]{1,0:T(8,128)(2,1)S(1)}, bf16[1024,1024]{1,0:T(8,128)(2,1)}, u32[]{:S(2)}) copy-start(bf16[1024,1024]{1,0:T(8,128)(2,1)} %weight_ref.3) | copy-start | bytes 6291460
  18.5 1.4 %collective-permute-start.6 = (bf16[128,512]{1,0:T(8,128)(2,1)S(1)}, bf16[128,512]{1,0:T(8,128)(2,1)S(1)}, u32[]{:S(2)}, u32[]{:S(2)}) collective-permute-start(bf16[128,512]{1,0:T(8,128)(2,1)S(1)} %get-tuple-element.26), channel_id=1, source_target_pairs={{0,1},{1,0},{2,3},{3,2},{4,5},{5,4},{6,7},{7,6},{8,9},{9,8},{10,11... | collective-permute-start | bytes 393224 | tf_op jit(solution)/shard_map/ppermute | solution.py:220
  20.0 5.2 %collective-permute-start.7 = (bf16[32,512]{1,0:T(8,128)(2,1)S(1)}, bf16[32,512]{1,0:T(8,128)(2,1)S(1)}, u32[]{:S(2)}, u32[]{:S(2)}) collective-permute-start(bf16[32,512]{1,0:T(8,128)(2,1)S(1)} %get-tuple-element.27), channel_id=1, source_target_pairs={{0,13},{1,12},{2,15},{3,14},{4,9},{5,8},{6,11},{7,10},{8,5},{9,4},... | collective-permute-start | bytes 98312 | tf_op jit(solution)/shard_map/ppermute | solution.py:226
  21.6 5.4 %collective-permute-start.9 = (bf16[32,512]{1,0:T(8,128)(2,1)S(1)}, bf16[32,512]{1,0:T(8,128)(2,1)S(1)}, u32[]{:S(2)}, u32[]{:S(2)}) collective-permute-start(bf16[32,512]{1,0:T(8,128)(2,1)S(1)} %get-tuple-element.28), channel_id=1, source_target_pairs={{0,8},{1,9},{2,10},{3,11},{4,12},{5,13},{6,14},{7,15},{8,0},{9,1},... | collective-permute-start | bytes 98312 | tf_op jit(solution)/shard_map/ppermute | solution.py:226
  21.8 5.2 %collective-permute-start.8 = (bf16[32,512]{1,0:T(8,128)(2,1)S(1)}, bf16[32,512]{1,0:T(8,128)(2,1)S(1)}, u32[]{:S(2)}, u32[]{:S(2)}) collective-permute-start(bf16[32,512]{1,0:T(8,128)(2,1)S(1)} %get-tuple-element.29), channel_id=1, source_target_pairs={{0,5},{1,4},{2,7},{3,6},{4,1},{5,0},{6,3},{7,2},{8,13},{9,12},{10,... | collective-permute-start | bytes 98312 | tf_op jit(solution)/shard_map/ppermute | solution.py:226
  27.0 3.5 %collective-permute-start.10 = (bf16[32,512]{1,0:T(8,128)(2,1)S(1)}, bf16[32,512]{1,0:T(8,128)(2,1)S(1)}, u32[]{:S(2)}, u32[]{:S(2)}) collective-permute-start(bf16[32,512]{1,0:T(8,128)(2,1)S(1)} %fusion.1), channel_id=1, source_target_pairs={{0,3},{1,2},{2,1},{3,0},{4,7},{5,6},{6,5},{7,4},{8,11},{9,10},{10,... | collective-permute-start | bytes 98312 | tf_op jit(solution)/shard_map/ppermute | solution.py:220
  30.5 1.3 %collective-permute-start.11 = (bf16[32,512]{1,0:T(8,128)(2,1)S(1)}, bf16[32,512]{1,0:T(8,128)(2,1)S(1)}, u32[]{:S(2)}, u32[]{:S(2)}) collective-permute-start(bf16[32,512]{1,0:T(8,128)(2,1)S(1)} %add_convert_fusion.1.own_ref), channel_id=1, source_target_pairs={{0,1},{1,0},{2,3},{3,2},{4,5},{5,4},{6,7},{7,6},{8,9},{9,8},{10,11... | collective-permute-start | bytes 98312 | tf_op jit(solution)/shard_map/ppermute | solution.py:220

commit v20 on v19

--- a/solution.py
+++ b/solution.py
@@ -186,7 +186,8 @@
 
 def third_kernel(hidden_ref, down_ref, mine_ref):
     half = mine_ref.shape[1]
-    mine_ref[...] = dot(hidden_ref[...], down_ref[:, pl.ds(half_at(True, half), half)], NN)
+    mine = dot(hidden_ref[...], down_ref[:, pl.ds(half_at(True, half), half)], NN)
+    mine_ref[...] = mine.astype(BF16)
 
 
 def up_own_kernel(own_ref, weight_ref, out_ref):
@@ -319,14 +320,14 @@
     )
     mine = kernel_call(
         third_kernel,
-        shaped(F32, all_rows, half),
+        shaped(BF16, all_rows, half),
         (hidden, down_here),
         (),
         [],
         all_rows * latent_len * all_units,
         latent_len * all_units,
     )
-    part = (mine + over_tp(theirs, 1).astype(F32)).astype(BF16)
+    part = (mine.astype(F32) + over_tp(theirs, 1).astype(F32)).astype(BF16)
     blocks = part.reshape(exp_count, rows, half)
     mixed = blocks[0].astype(F32)
     for s in (exp_count - 1, *range(1, exp_count - 1)):

time: 32.9 us -> 32.9 us (level)
  no operation moved by 1% of the time
where the time goes in v20:
time: 32.9 us; the launch traced here: 32.7 us
  starting transfers between devices  12.8 us (39%)
  waiting for transfers between devices  10.8 us (33%)
  Pallas kernels  8.9 us (27%)
    pallas_call x11, Pallas kernels, kernel_call(): pl.pallas_call(body, out_shape=out_shape, in_specs=[spec(pltpu.HBM if i i...  8.9 us
    ppermute x6, starting transfers between devices, over_exp(): return lax.ppermute(x, ('exp', 'tp'), hops)  7.92 us
    ppermute x6, waiting for transfers between devices, over_exp(): return lax.ppermute(x, ('exp', 'tp'), hops)  5.76 us
    ppermute x6, waiting for transfers between devices, over_tp(): return lax.ppermute(x, 'tp', [(t, t ^ mask) for t in range(tp_count)])  5.06 us
    ppermute x6, starting transfers between devices, over_tp(): return lax.ppermute(x, 'tp', [(t, t ^ mask) for t in range(tp_count)])  4.85 us
  transfers between devices with their start and end apart: 12, of which 8 were waited for; matrix products, arithmetic and copies ran while one was open for 0% of the time, Pallas kernels for 16%

profile of v20, /device:TPU:0, one launch (start us, length us, event | category | flops | bytes accessed | tf_op | source)
XLA Modules:
  0.0 32.7 jit_solution(16815204692336031436)
XLA Ops:
  0.0 1.7 %shard_map.73 = (bf16[32,512]{1,0:T(8,128)(2,1)S(1)}, bf16[32,1024]{1,0:T(8,128)(2,1)S(1)}, bf16[512,1024]{1,0:T(8,128)(2,1)S(1)}) custom-call(bf16[32,1024]{1,0:T(8,128)(2,1)} %tokens_hbm.1, bf16[1024,1024]{1,0:T(8,128)(2,1)} %weight_hbm.1), custom_call_target="tpu_custom_call" | custom-call | flops 33554432 | bytes 2097152 | tf_op jit(solution)/shard_map/pallas_call | solution.py:33
  1.7 0.5 %collective-permute-start = (bf16[32,512]{1,0:T(8,128)(2,1)S(1)}, bf16[32,512]{1,0:T(8,128)(2,1)S(1)}, u32[]{:S(2)}, u32[]{:S(2)}) collective-permute-start(bf16[32,512]{1,0:T(8,128)(2,1)S(1)} %get-tuple-element.18), channel_id=1, source_target_pairs={{0,1},{1,0},{2,3},{3,2},{4,5},{5,4},{6,7},{7,6},{8,9},{9,8},{10,11... | collective-permute-start | bytes 98312 | tf_op jit(solution)/shard_map/ppermute | solution.py:221
  2.2 0.4 %shard_map.74 = f32[32,512]{1,0:T(8,128)S(1)} custom-call(bf16[32,1024]{1,0:T(8,128)(2,1)S(1)} %get-tuple-element.16.tokens_ref, bf16[512,1024]{1,0:T(8,128)(2,1)S(1)} %get-tuple-element.17.weight_ref), custom_call_target="tpu_custom_call" | custom-call | flops 33554432 | bytes 1048576 | tf_op jit(solution)/shard_map/pallas_call | solution.py:33
  2.6 0.5 %collective-permute-done = bf16[32,512]{1,0:T(8,128)(2,1)S(1)} collective-permute-done((bf16[32,512]{1,0:T(8,128)(2,1)S(1)}, bf16[32,512]{1,0:T(8,128)(2,1)S(1)}, u32[]{:S(2)}, u32[]{:S(2)}) %collective-permute-start) | collective-permute-done | bytes 32800 | tf_op jit(solution)/shard_map/ppermute | solution.py:221
  3.1 2.7 %collective-permute-start.1 = (bf16[32,512]{1,0:T(8,128)(2,1)S(1)}, bf16[32,512]{1,0:T(8,128)(2,1)S(1)}, u32[]{:S(2)}, u32[]{:S(2)}) collective-permute-start(bf16[32,512]{1,0:T(8,128)(2,1)S(1)} %fusion.refs_0_), channel_id=1, source_target_pairs={{0,3},{1,2},{2,1},{3,0},{4,7},{5,6},{6,5},{7,4},{8,11},{9,10},{10,... | collective-permute-start | bytes 98312 | tf_op jit(solution)/shard_map/ppermute | solution.py:221
  5.7 1.8 %shard_map.75 = (bf16[16,128]{1,0:T(8,128)(2,1)S(1)}, bf16[2,672,1024]{2,1,0:T(8,128)(2,1)S(1)}) custom-call(bf16[32,512]{1,0:T(8,128)(2,1)S(1)} %fusion.refs_0_, s32[4,32]{1,0:T(4,128)} %bitcast.4, f32[4,32]{1,0:T(4,128)} %bitcast.5, bf16[2,672,1024]{2,1,0:T(8,128)(2,1)} %refs_3_.1), custom_call_target="tpu_custom_call" | custom-call | bytes 2752512 | tf_op jit(solution)/shard_map/pallas_call | solution.py:33
  7.6 0.0 collective-permute-done.1
  7.6 3.7 %collective-permute-start.4 = (bf16[144,128]{1,0:T(8,128)(2,1)S(1)}, bf16[144,128]{1,0:T(8,128)(2,1)S(1)}, u32[]{:S(2)}, u32[]{:S(2)}) collective-permute-start(bf16[144,128]{1,0:T(8,128)(2,1)S(1)} %shard_map.76.after_ref.refs_0_), channel_id=1, source_target_pairs={{0,13},{1,12},{2,15},{3,14},{4,9},{5,8},{6,11},{7,10},{8,5},{9,4},... | collective-permute-start | bytes 110600 | tf_op jit(solution)/shard_map/ppermute | solution.py:227
  11.3 0.0 collective-permute-start.3
  11.3 0.4 %collective-permute-start.2 = (bf16[144,128]{1,0:T(8,128)(2,1)S(1)}, bf16[144,128]{1,0:T(8,128)(2,1)S(1)}, u32[]{:S(2)}, u32[]{:S(2)}) collective-permute-start(bf16[144,128]{1,0:T(8,128)(2,1)S(1)} %shard_map.76.after_ref.refs_0_), channel_id=1, source_target_pairs={{0,5},{1,4},{2,7},{3,6},{4,1},{5,0},{6,3},{7,2},{8,13},{9,12},{10,... | collective-permute-start | bytes 110600 | tf_op jit(solution)/shard_map/ppermute | solution.py:227
  11.7 1.8 %shard_map.77.down_ref = bf16[1344,1024]{1,0:T(8,128)(2,1)S(1)} custom-call(bf16[144,128]{1,0:T(8,128)(2,1)S(1)} %shard_map.76.after_ref.refs_0_, bf16[1344,1024]{1,0:T(8,128)(2,1)} %bitcast.3), custom_call_target="tpu_custom_call" | custom-call | bytes 2752512 | tf_op jit(solution)/shard_map/pallas_call | solution.py:33
  13.5 0.0 collective-permute-done.4.refs_3_
  13.5 2.7 %collective-permute-done.3.refs_2_ = bf16[144,128]{1,0:T(8,128)(2,1)S(1)} collective-permute-done((bf16[144,128]{1,0:T(8,128)(2,1)S(1)}, bf16[144,128]{1,0:T(8,128)(2,1)S(1)}, u32[]{:S(2)}, u32[]{:S(2)}) %collective-permute-start.3) | collective-permute-done | bytes 36896 | tf_op jit(solution)/shard_map/ppermute | solution.py:227
  16.2 0.1 collective-permute-start.5
  16.3 0.7 %shard_map.79.pre_ref = f32[128,1344]{1,0:T(8,128)S(1)} custom-call(bf16[128,512]{1,0:T(8,128)(2,1)S(1)} %get-tuple-element.22.own_ref, bf16[2,672,1024]{2,1,0:T(8,128)(2,1)S(1)} %get-tuple-element.23.up_ref), custom_call_target="tpu_custom_call" | custom-call | flops 176160768 | bytes 1376256 | tf_op jit(solution)/shard_map/pallas_call | solution.py:33
  16.9 0.7 %collective-permute-done.5.other_ref = bf16[128,512]{1,0:T(8,128)(2,1)S(1)} collective-permute-done((bf16[128,512]{1,0:T(8,128)(2,1)S(1)}, bf16[128,512]{1,0:T(8,128)(2,1)S(1)}, u32[]{:S(2)}, u32[]{:S(2)}) %collective-permute-start.5) | collective-permute-done | bytes 131104 | tf_op jit(solution)/shard_map/ppermute | solution.py:221
  17.6 0.9 %shard_map.80 = (bf16[128,1344]{1,0:T(8,128)(2,1)S(1)}, bf16[128,512]{1,0:T(8,128)(2,1)S(1)}) custom-call(bf16[64,128]{1,0:T(8,128)(2,1)S(1)} %get-tuple-element.21.terms_ref, bf16[128,512]{1,0:T(8,128)(2,1)S(1)} %collective-permute-done.5.other_ref, f32[128,1344]{1,0:T(8,128)S(1)} %shard_map.79.pre_ref, bf16[2,672,1024]{2,1,0:T(8,128)(2,1)S(1)} %get-tuple-element.23.up_ref, ...), custom_call_target="tpu_custom_call" | custom-call | flops 352321536 | bytes 2752512 | tf_op jit(solution)/shard_map/pallas_call | solution.py:33
  18.5 0.0 copy-start
  18.5 0.2 collective-permute-start.6
  18.7 0.4 %shard_map.81 = bf16[128,512]{1,0:T(8,128)(2,1)S(1)} custom-call(bf16[128,1344]{1,0:T(8,128)(2,1)S(1)} %get-tuple-element.25.hidden_ref, bf16[1344,1024]{1,0:T(8,128)(2,1)S(1)} %shard_map.77.down_ref), custom_call_target="tpu_custom_call" | custom-call | flops 176160768 | bytes 1376256 | tf_op jit(solution)/shard_map/pallas_call | solution.py:33
  19.1 0.8 %collective-permute-done.6 = bf16[128,512]{1,0:T(8,128)(2,1)S(1)} collective-permute-done((bf16[128,512]{1,0:T(8,128)(2,1)S(1)}, bf16[128,512]{1,0:T(8,128)(2,1)S(1)}, u32[]{:S(2)}, u32[]{:S(2)}) %collective-permute-start.6) | collective-permute-done | bytes 131104 | tf_op jit(solution)/shard_map/ppermute | solution.py:221
  20.0 1.6 %collective-permute-start.7 = (bf16[32,512]{1,0:T(8,128)(2,1)S(1)}, bf16[32,512]{1,0:T(8,128)(2,1)S(1)}, u32[]{:S(2)}, u32[]{:S(2)}) collective-permute-start(bf16[32,512]{1,0:T(8,128)(2,1)S(1)} %get-tuple-element.27), channel_id=1, source_target_pairs={{0,13},{1,12},{2,15},{3,14},{4,9},{5,8},{6,11},{7,10},{8,5},{9,4},... | collective-permute-start | bytes 98312 | tf_op jit(solution)/shard_map/ppermute | solution.py:227
  21.6 0.2 collective-permute-start.9
  21.8 2.1 %collective-permute-start.8 = (bf16[32,512]{1,0:T(8,128)(2,1)S(1)}, bf16[32,512]{1,0:T(8,128)(2,1)S(1)}, u32[]{:S(2)}, u32[]{:S(2)}) collective-permute-start(bf16[32,512]{1,0:T(8,128)(2,1)S(1)} %get-tuple-element.29), channel_id=1, source_target_pairs={{0,5},{1,4},{2,7},{3,6},{4,1},{5,0},{6,3},{7,2},{8,13},{9,12},{10,... | collective-permute-start | bytes 98312 | tf_op jit(solution)/shard_map/ppermute | solution.py:227
  23.9 1.3 %collective-permute-done.7 = bf16[32,512]{1,0:T(8,128)(2,1)S(1)} collective-permute-done((bf16[32,512]{1,0:T(8,128)(2,1)S(1)}, bf16[32,512]{1,0:T(8,128)(2,1)S(1)}, u32[]{:S(2)}, u32[]{:S(2)}) %collective-permute-start.7) | collective-permute-done | bytes 32800 | tf_op jit(solution)/shard_map/ppermute | solution.py:227
  25.2 1.7 %collective-permute-done.9 = bf16[32,512]{1,0:T(8,128)(2,1)S(1)} collective-permute-done((bf16[32,512]{1,0:T(8,128)(2,1)S(1)}, bf16[32,512]{1,0:T(8,128)(2,1)S(1)}, u32[]{:S(2)}, u32[]{:S(2)}) %collective-permute-start.9) | collective-permute-done | bytes 32800 | tf_op jit(solution)/shard_map/ppermute | solution.py:227
  27.0 1.2 %collective-permute-start.10 = (bf16[32,512]{1,0:T(8,128)(2,1)S(1)}, bf16[32,512]{1,0:T(8,128)(2,1)S(1)}, u32[]{:S(2)}, u32[]{:S(2)}) collective-permute-start(bf16[32,512]{1,0:T(8,128)(2,1)S(1)} %fusion.1), channel_id=1, source_target_pairs={{0,3},{1,2},{2,1},{3,0},{4,7},{5,6},{6,5},{7,4},{8,11},{9,10},{10,... | collective-permute-start | bytes 98312 | tf_op jit(solution)/shard_map/ppermute | solution.py:221
  28.2 2.3 %collective-permute-done.10 = bf16[32,512]{1,0:T(8,128)(2,1)S(1)} collective-permute-done((bf16[32,512]{1,0:T(8,128)(2,1)S(1)}, bf16[32,512]{1,0:T(8,128)(2,1)S(1)}, u32[]{:S(2)}, u32[]{:S(2)}) %collective-permute-start.10) | collective-permute-done | bytes 32800 | tf_op jit(solution)/shard_map/ppermute | solution.py:221
  30.5 0.2 collective-permute-start.11
  30.7 0.3 shard_map.82.part_ref
  31.0 0.8 %collective-permute-done.11.other_ref = bf16[32,512]{1,0:T(8,128)(2,1)S(1)} collective-permute-done((bf16[32,512]{1,0:T(8,128)(2,1)S(1)}, bf16[32,512]{1,0:T(8,128)(2,1)S(1)}, u32[]{:S(2)}, u32[]{:S(2)}) %collective-permute-start.11) | collective-permute-done | bytes 32800 | tf_op jit(solution)/shard_map/ppermute | solution.py:221
  31.8 0.9 %shard_map.83 = bf16[32,1024]{1,0:T(8,128)(2,1)} custom-call(f32[32,1024]{1,0:T(8,128)S(1)} %shard_map.82.part_ref, bf16[32,512]{1,0:T(8,128)(2,1)S(1)} %collective-permute-done.11.other_ref, bf16[1024,1024]{1,0:T(8,128)(2,1)S(1)} %copy-done), custom_call_target="tpu_custom_call" | custom-call | flops 33554432 | bytes 1048576 | tf_op jit(solution)/shard_map/pallas_call | solution.py:33
  (11 shorter events, 0.1 us)
Async XLA Ops:
  1.7 1.4 %collective-permute-start = (bf16[32,512]{1,0:T(8,128)(2,1)S(1)}, bf16[32,512]{1,0:T(8,128)(2,1)S(1)}, u32[]{:S(2)}, u32[]{:S(2)}) collective-permute-start(bf16[32,512]{1,0:T(8,128)(2,1)S(1)} %get-tuple-element.18), channel_id=1, source_target_pairs={{0,1},{1,0},{2,3},{3,2},{4,5},{5,4},{6,7},{7,6},{8,9},{9,8},{10,11... | collective-permute-start | bytes 98312 | tf_op jit(solution)/shard_map/ppermute | solution.py:221
  3.1 4.5 %collective-permute-start.1 = (bf16[32,512]{1,0:T(8,128)(2,1)S(1)}, bf16[32,512]{1,0:T(8,128)(2,1)S(1)}, u32[]{:S(2)}, u32[]{:S(2)}) collective-permute-start(bf16[32,512]{1,0:T(8,128)(2,1)S(1)} %fusion.refs_0_), channel_id=1, source_target_pairs={{0,3},{1,2},{2,1},{3,0},{4,7},{5,6},{6,5},{7,4},{8,11},{9,10},{10,... | collective-permute-start | bytes 98312 | tf_op jit(solution)/shard_map/ppermute | solution.py:221
  7.6 5.8 %collective-permute-start.4 = (bf16[144,128]{1,0:T(8,128)(2,1)S(1)}, bf16[144,128]{1,0:T(8,128)(2,1)S(1)}, u32[]{:S(2)}, u32[]{:S(2)}) collective-permute-start(bf16[144,128]{1,0:T(8,128)(2,1)S(1)} %shard_map.76.after_ref.refs_0_), channel_id=1, source_target_pairs={{0,13},{1,12},{2,15},{3,14},{4,9},{5,8},{6,11},{7,10},{8,5},{9,4},... | collective-permute-start | bytes 110600 | tf_op jit(solution)/shard_map/ppermute | solution.py:227
  11.3 4.9 %collective-permute-start.3 = (bf16[144,128]{1,0:T(8,128)(2,1)S(1)}, bf16[144,128]{1,0:T(8,128)(2,1)S(1)}, u32[]{:S(2)}, u32[]{:S(2)}) collective-permute-start(bf16[144,128]{1,0:T(8,128)(2,1)S(1)} %shard_map.76.after_ref.refs_0_), channel_id=1, source_target_pairs={{0,8},{1,9},{2,10},{3,11},{4,12},{5,13},{6,14},{7,15},{8,0},{9,1},... | collective-permute-start | bytes 110600 | tf_op jit(solution)/shard_map/ppermute | solution.py:227
  11.3 4.9 %collective-permute-start.2 = (bf16[144,128]{1,0:T(8,128)(2,1)S(1)}, bf16[144,128]{1,0:T(8,128)(2,1)S(1)}, u32[]{:S(2)}, u32[]{:S(2)}) collective-permute-start(bf16[144,128]{1,0:T(8,128)(2,1)S(1)} %shard_map.76.after_ref.refs_0_), channel_id=1, source_target_pairs={{0,5},{1,4},{2,7},{3,6},{4,1},{5,0},{6,3},{7,2},{8,13},{9,12},{10,... | collective-permute-start | bytes 110600 | tf_op jit(solution)/shard_map/ppermute | solution.py:227
  16.2 1.4 %collective-permute-start.5 = (bf16[128,512]{1,0:T(8,128)(2,1)S(1)}, bf16[128,512]{1,0:T(8,128)(2,1)S(1)}, u32[]{:S(2)}, u32[]{:S(2)}) collective-permute-start(bf16[128,512]{1,0:T(8,128)(2,1)S(1)} %get-tuple-element.22.own_ref), channel_id=1, source_target_pairs={{0,1},{1,0},{2,3},{3,2},{4,5},{5,4},{6,7},{7,6},{8,9},{9,8},{10,11... | collective-permute-start | bytes 393224 | tf_op jit(solution)/shard_map/ppermute | solution.py:221
  18.5 12.2 %copy-start = (bf16[1024,1024]{1,0:T(8,128)(2,1)S(1)}, bf16[1024,1024]{1,0:T(8,128)(2,1)}, u32[]{:S(2)}) copy-start(bf16[1024,1024]{1,0:T(8,128)(2,1)} %weight_ref.3) | copy-start | bytes 6291460
  18.5 1.4 %collective-permute-start.6 = (bf16[128,512]{1,0:T(8,128)(2,1)S(1)}, bf16[128,512]{1,0:T(8,128)(2,1)S(1)}, u32[]{:S(2)}, u32[]{:S(2)}) collective-permute-start(bf16[128,512]{1,0:T(8,128)(2,1)S(1)} %get-tuple-element.26), channel_id=1, source_target_pairs={{0,1},{1,0},{2,3},{3,2},{4,5},{5,4},{6,7},{7,6},{8,9},{9,8},{10,11... | collective-permute-start | bytes 393224 | tf_op jit(solution)/shard_map/ppermute | solution.py:221
  20.0 5.2 %collective-permute-start.7 = (bf16[32,512]{1,0:T(8,128)(2,1)S(1)}, bf16[32,512]{1,0:T(8,128)(2,1)S(1)}, u32[]{:S(2)}, u32[]{:S(2)}) collective-permute-start(bf16[32,512]{1,0:T(8,128)(2,1)S(1)} %get-tuple-element.27), channel_id=1, source_target_pairs={{0,13},{1,12},{2,15},{3,14},{4,9},{5,8},{6,11},{7,10},{8,5},{9,4},... | collective-permute-start | bytes 98312 | tf_op jit(solution)/shard_map/ppermute | solution.py:227
  21.6 5.4 %collective-permute-start.9 = (bf16[32,512]{1,0:T(8,128)(2,1)S(1)}, bf16[32,512]{1,0:T(8,128)(2,1)S(1)}, u32[]{:S(2)}, u32[]{:S(2)}) collective-permute-start(bf16[32,512]{1,0:T(8,128)(2,1)S(1)} %get-tuple-element.28), channel_id=1, source_target_pairs={{0,8},{1,9},{2,10},{3,11},{4,12},{5,13},{6,14},{7,15},{8,0},{9,1},... | collective-permute-start | bytes 98312 | tf_op jit(solution)/shard_map/ppermute | solution.py:227
  21.8 5.2 %collective-permute-start.8 = (bf16[32,512]{1,0:T(8,128)(2,1)S(1)}, bf16[32,512]{1,0:T(8,128)(2,1)S(1)}, u32[]{:S(2)}, u32[]{:S(2)}) collective-permute-start(bf16[32,512]{1,0:T(8,128)(2,1)S(1)} %get-tuple-element.29), channel_id=1, source_target_pairs={{0,5},{1,4},{2,7},{3,6},{4,1},{5,0},{6,3},{7,2},{8,13},{9,12},{10,... | collective-permute-start | bytes 98312 | tf_op jit(solution)/shard_map/ppermute | solution.py:227
  27.0 3.5 %collective-permute-start.10 = (bf16[32,512]{1,0:T(8,128)(2,1)S(1)}, bf16[32,512]{1,0:T(8,128)(2,1)S(1)}, u32[]{:S(2)}, u32[]{:S(2)}) collective-permute-start(bf16[32,512]{1,0:T(8,128)(2,1)S(1)} %fusion.1), channel_id=1, source_target_pairs={{0,3},{1,2},{2,1},{3,0},{4,7},{5,6},{6,5},{7,4},{8,11},{9,10},{10,... | collective-permute-start | bytes 98312 | tf_op jit(solution)/shard_map/ppermute | solution.py:221
  30.5 1.3 %collective-permute-start.11 = (bf16[32,512]{1,0:T(8,128)(2,1)S(1)}, bf16[32,512]{1,0:T(8,128)(2,1)S(1)}, u32[]{:S(2)}, u32[]{:S(2)}) collective-permute-start(bf16[32,512]{1,0:T(8,128)(2,1)S(1)} %add_convert_fusion.1.own_ref), channel_id=1, source_target_pairs={{0,1},{1,0},{2,3},{3,2},{4,5},{5,4},{6,7},{7,6},{8,9},{9,8},{10,11... | collective-permute-start | bytes 98312 | tf_op jit(solution)/shard_map/ppermute | solution.py:221
